TPU v7x, 128 devices: a whole 4x4x4 slice. The times are simulated.
128 devices in a mesh: tile: 16 (over x, y), field: 8 (over z, core).
Axes of the slice: x: 4, y: 4, z: 4, core: 2. Of those that a mesh axis runs over, the one named last changes fastest.
Arguments:
- right_side: float32 [8, 256, 16384], P(None, 'tile', 'field'), may hold values from -6 to 6
- kappa_field: float32 [8, 256, 16384], P(None, 'tile', 'field'), may hold values from 0.05 to 2
- tau_field: float32 [8, 256, 16384], P(None, 'tile', 'field'), may hold values from 0.03 to 0.3
- curvature: float32 [8, 256, 16384], P(None, 'tile', 'field'), may hold values from 0.2 to 2
- detect_prob: float32 [8], replicated, may hold values from 0.2 to 0.7
- site_cells: int32 [16, 8, 16, 128], P('tile', 'field'), may hold values from 0 to 32767
- site_offsets: float32 [16, 8, 16, 2, 128], P('tile', 'field'), may hold values from 0 to 1
- site_count: int32 [16, 8, 16], P('tile', 'field'), may hold values from 0 to 128, as said below
- visit_count: int32 [16, 8, 16, 128], P('tile', 'field'), may hold values from 1 to 8
- detections: int32 [16, 8, 16, 8, 128], P('tile', 'field'), may hold values from 0 to 8, as said below
- surveyed: int32 [16, 8, 16, 8, 128], P('tile', 'field'), may hold values 0 or 1
Outputs:
- latent: float32 [8, 256, 16384], P(None, 'tile', 'field')
- site_grad: float32 [16, 8, 16, 8, 128], P('tile', 'field')
Inputs may be any that keep to these rules, and one draw needn't show every extreme that they name: `site_count`: some block holds exactly 128 live slots. `detections`: at most the site's visit count.
All inputs are finite; a program needn't handle non-finite values. No bound on the sum of `surveyed` on one device may be relied on, other than what follows from the above.
Results may differ from a plain program's by a relative error of at most 0.0001.
Values sent between devices are 32-bit elements; how exact they have to be, the bound alone decides.
No kernel may reach another device: no remote copies, remote signals or barrier semaphores. Data moves between devices by JAX's collectives and lax.ppermute only.
A program may use at most 128 MiB of HBM per device.

v0:
```python
import jax
import jax.numpy as jnp
from jax import lax
from jax.sharding import PartitionSpec as P

ITERS = 8


def extended(x, sides, width):
    for axis, dim in sides:
        size, length = (lax.axis_size(axis), x.shape[dim])
        up = [(i, (i + 1) % size) for i in range(size - 1)]
        down = [(j, i) for i, j in up]
        last = lax.slice_in_dim(x, length - width, length, axis=dim)
        leading = lax.slice_in_dim(x, 0, width, axis=dim)
        before = lax.ppermute(last, axis, up)
        after = lax.ppermute(leading, axis, down)
        x = jnp.concatenate([before, x, after], axis=dim)
    return x


def passed_along(x, axis, by):
    length = lax.axis_size(axis)
    pairs = [(i, i + by) for i in range(length) if 0 <= i + by < length]
    return lax.ppermute(x, axis, pairs)


def neighbours(padded):
    return padded[:, 2:, 1:-1] + padded[:, :-2, 1:-1] + padded[:, 1:-1, 2:] + padded[:, 1:-1, :-2]


def local(
    right_side,
    kappa_field,
    tau_field,
    curvature,
    detect_prob,
    site_cells,
    site_offsets,
    site_count,
    visit_count,
    detections,
    surveyed,
):

    def squares(values):
        return lax.psum(jnp.sum(values * values, axis=(1, 2)), ("tile", "field"))[:, None, None]

    latent = jnp.zeros_like(right_side)
    residual = right_side
    direction = right_side
    norm_now = squares(residual)
    for sweep in range(ITERS):
        padded = extended(direction, (("tile", 1), ("field", 2)), 1)
        scaled = tau_field * ((kappa_field + 4.0) * direction - neighbours(padded))
        spread = extended(scaled, (("tile", 1), ("field", 2)), 1)
        image = (kappa_field + 4.0) * scaled - neighbours(spread) + curvature * direction
        inner = lax.psum(jnp.sum(direction * image, axis=(1, 2)), ("tile", "field"))[:, None, None]
        alpha = norm_now / inner
        latent = latent + alpha * direction
        residual = residual - alpha * image
        norm_next = squares(residual)
        direction = residual + norm_next / norm_now * direction
        norm_now = norm_next
    cells = site_cells[0, 0]
    offsets = site_offsets[0, 0]
    got_cells, got_offsets = (
        lax.all_to_all(cells, "tile", split_axis=0, concat_axis=0, tiled=True),
        lax.all_to_all(offsets, "tile", split_axis=0, concat_axis=0, tiled=True),
    )
    upper = passed_along(latent[:, :1, :], "tile", -1)
    tall = jnp.concatenate([latent, upper], axis=1)
    beside = passed_along(tall[:, :, :1], "field", -1)
    wide = jnp.concatenate([tall, beside], axis=2)
    columns = latent.shape[2]
    width = columns + 1
    flat = wide.reshape(wide.shape[0], -1)
    base = (got_cells // columns * width + got_cells % columns).astype(jnp.int32)

    def corner(offset):
        return jnp.take(flat, base + offset, axis=1)

    row_frac = got_offsets[None, :, 0, :]
    col_frac = got_offsets[None, :, 1, :]
    predictor = (
        (1.0 - row_frac) * (1.0 - col_frac) * corner(0)
        + row_frac * (1.0 - col_frac) * corner(width)
        + (1.0 - row_frac) * col_frac * corner(1)
        + row_frac * col_frac * corner(width + 1)
    )
    returned = lax.all_to_all(
        jnp.transpose(predictor, (1, 0, 2)), "tile", split_axis=0, concat_axis=0, tiled=True
    )
    slots = lax.broadcasted_iota(jnp.int32, cells.shape, 1)
    live = (slots < site_count[0, 0][:, None]).astype(jnp.float32)[:, None, :]
    visits = visit_count[0, 0].astype(jnp.float32)[:, None, :]
    miss_prob = jnp.exp(visits * jnp.log(1.0 - detect_prob)[:, None])
    expo = jnp.exp(returned)
    seen_grad = 1.0 / (1.0 + expo)
    miss_grad = -(1.0 - miss_prob) * expo / ((1.0 + expo) * (1.0 + miss_prob * expo))
    site_grad = (
        jnp.where(detections[0, 0] > 0, seen_grad, miss_grad)
        * surveyed[0, 0].astype(jnp.float32)
        * live
    )
    return (latent, site_grad[None, None])


def solution(mesh):
    in_specs = (
        P(None, "tile", "field"),
        P(None, "tile", "field"),
        P(None, "tile", "field"),
        P(None, "tile", "field"),
        P(),
        P("tile", "field", None, None),
        P("tile", "field", None, None, None),
        P("tile", "field", None),
        P("tile", "field", None, None),
        P("tile", "field", None, None, None),
        P("tile", "field", None, None, None),
    )
    out_specs = (P(None, "tile", "field"), P("tile", "field", None, None, None))
    return jax.shard_map(local, mesh=mesh, in_specs=in_specs, out_specs=out_specs, check_vma=False)
```

profile of v0, /device:TPU:0, one launch (start us, length us, event | category | flops | bytes accessed | tf_op | source)
XLA Modules:
  0.0 1410.3 jit_solution(1358771298325029352)
XLA Ops:
  3.3 4.5 collective-permute-start.1
  12.1 3.0 collective-permute-start.3
  16.0 4.1 fusion.79
  21.6 4.9 collective-permute-start.5
  29.8 4.0 collective-permute-start.7
  37.0 78.1 %all-reduce = (f32[8]{0:T(128)S(1)}, f32[8]{0:T(128)S(1)}) all-reduce(f32[8]{0:T(128)S(1)} %get-tuple-element.4, f32[8]{0:T(128)S(1)} %get-tuple-element.3), channel_id=1, replica_groups=mesh['tile'=16,'field'=8] {'tile','field'}, use_global_device_ids=true, to_apply=%region_1.0 | all-reduce | flops 16 | bytes 128 | tf_op jit(solution)/shard_map/psum | solution.py:47
  116.7 62.0 %psum.114 = f32[8]{0:T(128)S(1)} all-reduce(f32[8]{0:T(128)S(1)} %multiply_reduce_fusion.12), channel_id=1, replica_groups=mesh['tile'=16,'field'=8] {'tile','field'}, use_global_device_ids=true, to_apply=%region_5.0 | all-reduce | flops 8 | bytes 64 | tf_op jit(solution)/shard_map/psum | solution.py:47
  182.0 4.5 collective-permute-start.9
  189.8 3.0 collective-permute-start.11
  196.2 4.9 collective-permute-start.13
  204.4 3.4 collective-permute-start.15
  210.8 72.9 %psum.115 = f32[8]{0:T(128)S(1)} all-reduce(f32[8]{0:T(128)S(1)} %get-tuple-element.29), channel_id=1, replica_groups=mesh['tile'=16,'field'=8] {'tile','field'}, use_global_device_ids=true, to_apply=%region_7.0 | all-reduce | flops 8 | bytes 64 | tf_op jit(solution)/shard_map/psum | solution.py:58
  283.7 3.1 multiply_reduce_fusion.10
  286.9 64.0 %psum.116 = f32[8]{0:T(128)S(1)} all-reduce(f32[8]{0:T(128)S(1)} %get-tuple-element.27), channel_id=1, replica_groups=mesh['tile'=16,'field'=8] {'tile','field'}, use_global_device_ids=true, to_apply=%region_9.0 | all-reduce | flops 8 | bytes 64 | tf_op jit(solution)/shard_map/psum | solution.py:47
  354.0 4.5 collective-permute-start.17
  362.3 3.0 collective-permute-start.19
  368.7 4.9 collective-permute-start.21
  377.3 3.0 collective-permute-start.23
  383.3 73.2 %psum.117 = f32[8]{0:T(128)S(1)} all-reduce(f32[8]{0:T(128)S(1)} %get-tuple-element.25), channel_id=1, replica_groups=mesh['tile'=16,'field'=8] {'tile','field'}, use_global_device_ids=true, to_apply=%region_11.0 | all-reduce | flops 8 | bytes 64 | tf_op jit(solution)/shard_map/psum | solution.py:58
  456.4 2.7 multiply_reduce_fusion.8
  459.2 62.0 %psum.118 = f32[8]{0:T(128)S(1)} all-reduce(f32[8]{0:T(128)S(1)} %get-tuple-element.23), channel_id=1, replica_groups=mesh['tile'=16,'field'=8] {'tile','field'}, use_global_device_ids=true, to_apply=%region_13.0 | all-reduce | flops 8 | bytes 64 | tf_op jit(solution)/shard_map/psum | solution.py:47
  524.3 4.5 collective-permute-start.25
  532.1 3.0 collective-permute-start.27
  538.5 4.9 collective-permute-start.29
  546.7 3.9 collective-permute-start.31
  553.6 72.9 %psum.119 = f32[8]{0:T(128)S(1)} all-reduce(f32[8]{0:T(128)S(1)} %get-tuple-element.21), channel_id=1, replica_groups=mesh['tile'=16,'field'=8] {'tile','field'}, use_global_device_ids=true, to_apply=%region_15.0 | all-reduce | flops 8 | bytes 64 | tf_op jit(solution)/shard_map/psum | solution.py:58
  626.5 2.7 multiply_reduce_fusion.6
  629.2 63.7 %psum.120 = f32[8]{0:T(128)S(1)} all-reduce(f32[8]{0:T(128)S(1)} %get-tuple-element.19), channel_id=1, replica_groups=mesh['tile'=16,'field'=8] {'tile','field'}, use_global_device_ids=true, to_apply=%region_17.0 | all-reduce | flops 8 | bytes 64 | tf_op jit(solution)/shard_map/psum | solution.py:47
  696.1 4.5 collective-permute-start.33
  703.9 3.2 collective-permute-start.35
  710.3 4.9 collective-permute-start.37
  718.9 3.0 collective-permute-start.39
  724.9 73.1 %psum.121 = f32[8]{0:T(128)S(1)} all-reduce(f32[8]{0:T(128)S(1)} %get-tuple-element.17), channel_id=1, replica_groups=mesh['tile'=16,'field'=8] {'tile','field'}, use_global_device_ids=true, to_apply=%region_19.0 | all-reduce | flops 8 | bytes 64 | tf_op jit(solution)/shard_map/psum | solution.py:58
  798.0 2.7 multiply_reduce_fusion.4
  800.7 62.0 %psum.122 = f32[8]{0:T(128)S(1)} all-reduce(f32[8]{0:T(128)S(1)} %get-tuple-element.15), channel_id=1, replica_groups=mesh['tile'=16,'field'=8] {'tile','field'}, use_global_device_ids=true, to_apply=%region_21.0 | all-reduce | flops 8 | bytes 64 | tf_op jit(solution)/shard_map/psum | solution.py:47
  865.8 4.5 collective-permute-start.41
  873.7 3.0 collective-permute-start.43
  880.1 4.9 collective-permute-start.45
  888.3 3.7 collective-permute-start.47
  895.0 73.1 %psum.123 = f32[8]{0:T(128)S(1)} all-reduce(f32[8]{0:T(128)S(1)} %get-tuple-element.13), channel_id=1, replica_groups=mesh['tile'=16,'field'=8] {'tile','field'}, use_global_device_ids=true, to_apply=%region_23.0 | all-reduce | flops 8 | bytes 64 | tf_op jit(solution)/shard_map/psum | solution.py:58
  970.8 63.7 %psum.124 = f32[8]{0:T(128)S(1)} all-reduce(f32[8]{0:T(128)S(1)} %get-tuple-element.11), channel_id=1, replica_groups=mesh['tile'=16,'field'=8] {'tile','field'}, use_global_device_ids=true, to_apply=%region_25.0 | all-reduce | flops 8 | bytes 64 | tf_op jit(solution)/shard_map/psum | solution.py:47
  1037.7 4.5 collective-permute-start.49
  1045.5 3.2 collective-permute-start.51
  1051.9 4.9 collective-permute-start.53
  1060.5 3.0 collective-permute-start.55
  1066.4 73.1 %psum.125 = f32[8]{0:T(128)S(1)} all-reduce(f32[8]{0:T(128)S(1)} %get-tuple-element.9), channel_id=1, replica_groups=mesh['tile'=16,'field'=8] {'tile','field'}, use_global_device_ids=true, to_apply=%region_27.0 | all-reduce | flops 8 | bytes 64 | tf_op jit(solution)/shard_map/psum | solution.py:58
  1141.4 4.0 all-to-all-start.1
  1145.4 64.8 %psum.126 = f32[8]{0:T(128)S(1)} all-reduce(f32[8]{0:T(128)S(1)} %multiply_reduce_fusion), channel_id=1, replica_groups=mesh['tile'=16,'field'=8] {'tile','field'}, use_global_device_ids=true, to_apply=%region_29.0 | all-reduce | flops 8 | bytes 64 | tf_op jit(solution)/shard_map/psum | solution.py:47
  1213.8 4.5 collective-permute-start.57
  1221.7 3.0 collective-permute-start.59
  1229.0 4.9 collective-permute-start.61
  1233.9 8.4 all-to-all-start
  1244.7 3.1 collective-permute-start.63
  1248.8 4.1 fusion.4
  1252.9 68.8 %psum.127 = f32[8]{0:T(128)S(1)} all-reduce(f32[8]{0:T(128)S(1)} %fusion.4), channel_id=1, replica_groups=mesh['tile'=16,'field'=8] {'tile','field'}, use_global_device_ids=true, to_apply=%region_31.0 | all-reduce | flops 8 | bytes 64 | tf_op jit(solution)/shard_map/psum | solution.py:58
  1321.7 4.2 multiply_add_fusion
  1327.3 4.8 collective-permute-done.64
  1336.8 9.9 copy.29
  1346.7 11.5 gather_fusion
  1358.5 11.5 gather_fusion.1
  1370.4 11.5 gather_fusion.2
  1382.3 11.5 gather_fusion.3
  1394.8 6.6 all-to-all-start.2
  1401.5 7.6 all-to-all-done.2
  (230 shorter events, 141.9 us)
Async XLA Ops:
  2.0 6.2 collective-permute-start
  3.3 6.4 collective-permute-start.1
  10.8 4.3 collective-permute-start.2
  12.1 4.0 collective-permute-start.3
  20.2 6.6 collective-permute-start.4
  21.6 6.8 collective-permute-start.5
  28.5 5.3 collective-permute-start.6
  29.8 4.9 collective-permute-start.7
  180.7 6.2 collective-permute-start.8
  182.0 6.4 collective-permute-start.9
  188.5 4.3 collective-permute-start.10
  189.8 4.0 collective-permute-start.11
  194.9 6.5 collective-permute-start.12
  196.2 6.8 collective-permute-start.13
  203.1 4.7 collective-permute-start.14
  204.4 4.3 collective-permute-start.15
  352.7 6.2 collective-permute-start.16
  354.0 6.4 collective-permute-start.17
  360.6 4.8 collective-permute-start.18
  362.3 4.0 collective-permute-start.19
  367.4 7.2 collective-permute-start.20
  368.7 7.1 collective-permute-start.21
  376.0 4.3 collective-permute-start.22
  377.3 4.0 collective-permute-start.23
  523.0 6.2 collective-permute-start.24
  524.3 6.4 collective-permute-start.25
  530.8 4.3 collective-permute-start.26
  532.1 4.0 collective-permute-start.27
  537.2 6.5 collective-permute-start.28
  538.5 6.8 collective-permute-start.29
  545.4 5.2 collective-permute-start.30
  546.7 4.8 collective-permute-start.31
  694.8 6.2 collective-permute-start.32
  696.1 6.4 collective-permute-start.33
  702.6 4.5 collective-permute-start.34
  703.9 4.0 collective-permute-start.35
  709.0 7.2 collective-permute-start.36
  710.3 7.1 collective-permute-start.37
  717.6 4.3 collective-permute-start.38
  864.5 6.2 collective-permute-start.40
  865.8 6.4 collective-permute-start.41
  872.4 4.3 collective-permute-start.42
  878.8 6.5 collective-permute-start.44
  880.1 6.8 collective-permute-start.45
  887.0 5.0 collective-permute-start.46
  888.3 4.7 collective-permute-start.47
  1036.4 6.2 collective-permute-start.48
  1037.7 6.4 collective-permute-start.49
  1044.2 4.6 collective-permute-start.50
  1045.5 4.0 collective-permute-start.51
  1050.6 7.2 collective-permute-start.52
  1051.9 7.1 collective-permute-start.53
  1059.2 4.3 collective-permute-start.54
  1141.4 92.4 %all-to-all-start.1 = ((s32[16,1,128]{2,1,0:T(1,128)}), s32[16,1,128]{2,1,0:T(1,128)S(1)}, u32[]{:S(2)}, u32[]{:S(2)}) async-start(s32[16,1,128]{2,1,0:T(1,128)} %bitcast.4), calls=%async_computation.1 | async-start | bytes 16384 | tf_op jit(solution)/shard_map/all_to_all | solution.py:68
  1212.5 6.2 collective-permute-start.56
  1213.8 6.4 collective-permute-start.57
  1220.4 4.4 collective-permute-start.58
  1227.7 14.7 %collective-permute-start.60 = (f32[8,1,2048]{2,1,0:T(1,128)S(1)}, f32[8,1,2048]{2,1,0:T(1,128)S(1)}, u32[]{:S(2)}, u32[]{:S(2)}) collective-permute-start(f32[8,1,2048]{2,1,0:T(1,128)S(1)} %get-tuple-element.65), channel_id=1, source_target_pairs={{8,0},{16,8},{24,16},{32,24},{40,32},{48,40},{56,48},{64,56},{72,6... | collective-permute-start | bytes 196616 | tf_op jit(solution)/shard_map/ppermute | solution.py:17
  1229.0 13.4 collective-permute-start.61
  1233.9 93.4 %all-to-all-start = ((f32[16,2,128]{2,1,0:T(2,128)}), f32[16,2,128]{2,1,0:T(2,128)S(1)}, u32[]{:S(2)}, u32[]{:S(2)}) async-start(f32[16,2,128]{2,1,0:T(2,128)} %bitcast.1), calls=%async_computation | async-start | bytes 32768 | tf_op jit(solution)/shard_map/all_to_all | solution.py:69
  1243.4 4.5 collective-permute-start.62
  1244.7 4.1 collective-permute-start.63
  1326.0 6.2 collective-permute-start.64
  1394.8 14.3 %all-to-all-start.2 = ((f32[16,8,128]{2,1,0:T(8,128)}), f32[16,8,128]{2,1,0:T(8,128)S(1)}, u32[]{:S(2)}, u32[]{:S(2)}) async-start(f32[16,8,128]{2,1,0:T(8,128)} %fusion.85), calls=%async_computation.2 | async-start | bytes 131072 | tf_op jit(solution)/shard_map/all_to_all | solution.py:91
  (25 other events, 455.0 us)
where the time goes:
time: 1420 us; the launch traced here: 1410 us
  blocking collectives  1030 us (73%)
  starting transfers between devices  191 us (13%)
  other arithmetic  69.5 us (5%)
  local copies, waits for them, and re-layouts  62.4 us (4%)
  waiting for transfers between devices  57.4 us (4%)
    psum x8, blocking collectives, squares(): lax.psum(jnp.sum(values * values, axis=(1, 2)), ('tile', 'field'))  520 us
    psum x7, blocking collectives, local(): lax.psum(jnp.sum(direction * image, axis=(1, 2)), ('tile', 'field'))  507 us
    ppermute x32, starting transfers between devices, extended(): before = lax.ppermute(last, axis, up)  128 us
    gather x8, local copies, waits for them, and re-layouts, corner(): return jnp.take(flat, base + offset, axis=1)  47.3 us
    ppermute x32, starting transfers between devices, extended(): after = lax.ppermute(leading, axis, down)  41.9 us
    ppermute x32, waiting for transfers between devices, extended(): before = lax.ppermute(last, axis, up)  36.7 us
  transfers between devices with their start and end apart: 69, of which 49 were waited for; matrix products, arithmetic and copies ran while one was open for 1% of the time, Pallas kernels for 0%

commit v1 on v0

v1 whole, which is shorter than its diff:
```python
import functools

import jax
import jax.numpy as jnp
from jax import lax
from jax.experimental import pallas as pl
from jax.experimental.pallas import tpu as pltpu
from jax.sharding import PartitionSpec as P

ITERS = 8
F = 8
PAD = 4
SIDE = 16
LANES = 128
LOW, HIGH = 0.2, 15.0
MID, HALF = 0.5 * (HIGH + LOW), 0.5 * (HIGH - LOW)
PIVOT = 3e-4
VMEM = pl.BlockSpec(memory_space=pltpu.VMEM)
SMEM = pl.BlockSpec(memory_space=pltpu.SMEM)
PARAMS = pltpu.CompilerParams(vmem_limit_bytes=16 * 1024 * 1024)


def held(x):
    return pltpu.with_memory_space_constraint(x, pltpu.VMEM)


def columns_kernel(*refs):
    firsts, lasts, (to_left, to_right) = refs[0:4], refs[4:8], refs[8:]
    lane = lax.broadcasted_iota(jnp.int32, (16, F, LANES), 2)
    for out, blocks, start in ((to_left, firsts, 0), (to_right, lasts, LANES - SIDE)):
        packed = jnp.zeros((16, F, LANES), jnp.float32)
        for a, ref in enumerate(blocks):
            block = jnp.swapaxes(ref[...], 0, 1)
            shift = (SIDE * a - start) % LANES
            moved = pltpu.roll(block, shift, 2) if shift else block
            mine = (lane >= SIDE * a) & (lane < SIDE * (a + 1))
            packed = jnp.where(mine, moved, packed)
        out[...] = packed


def columns_of(fields):
    rows, cols = fields[0].shape[1:]
    first = pl.BlockSpec((F, rows, LANES), lambda i: (0, 0, 0))
    last = pl.BlockSpec((F, rows, LANES), lambda i: (0, 0, cols // LANES - 1))
    out = pl.BlockSpec((rows, F, LANES), lambda i: (0, 0, 0))
    shape = jax.ShapeDtypeStruct((rows, F, LANES), jnp.float32)
    return pl.pallas_call(
        columns_kernel,
        grid=(1,),
        in_specs=[first] * 4 + [last] * 4,
        out_specs=[out, out],
        out_shape=[shape, shape],
        name="columns",
    )(*fields, *fields)


DEPTHS = (4, 3, 3, 2)


def prepare_kernel(rows, cols, flags, *refs):
    fields, (left, right), outs, (to_up, to_down) = refs[0:4], refs[4:6], refs[6:10], refs[10:]
    lane = lax.broadcasted_iota(jnp.int32, (rows, F, LANES), 2)

    def shaped(a, x):
        if a == 1:
            return x + 4.0
        if a == 2:
            return x * (1.0 / HALF)
        if a == 3:
            return (x - MID) * (1.0 / HALF)
        return x

    def store(a, at, block):
        if a == 0:
            outs[0][0, PAD : PAD + rows, :, at] = block
        else:
            outs[a][PAD : PAD + rows, :, at] = block
        base, depth = sum(DEPTHS[:a]), DEPTHS[a]
        to_up[base : base + depth, :, at] = block[:depth]
        to_down[base : base + depth, :, at] = block[rows - depth :]

    for a in range(4):

        def step(c, carry, a=a):
            at = pl.ds(pl.multiple_of(c * LANES, LANES), LANES)
            store(a, at, shaped(a, jnp.swapaxes(fields[a][:, :, at], 0, 1)))
            return carry

        lax.fori_loop(0, cols // LANES, step, 0)
        shift = (-SIDE * a) % LANES
        after = shaped(a, pltpu.roll(right[...], shift, 2) if shift else right[...])
        before = shaped(a, pltpu.roll(left[...], (LANES - SIDE * (a + 1)) % LANES, 2))
        extra = jnp.where(lane < SIDE, after * flags[1], 0.0) + jnp.where(lane >= LANES - SIDE, before * flags[0], 0.0)
        store(a, pl.ds(cols, LANES), extra)


def prepare(flags, fields, left, right):
    rows, cols = fields[0].shape[1:]
    wide = cols + LANES
    f32 = jnp.float32
    ext = (rows + 2 * PAD, F, wide)
    packed = jax.ShapeDtypeStruct((sum(DEPTHS), F, wide), f32)
    return pl.pallas_call(
        functools.partial(prepare_kernel, rows, cols),
        in_specs=[SMEM] + [VMEM] * 6,
        out_specs=[VMEM] * 6,
        out_shape=[pltpu.VMEM((ITERS,) + ext, f32)] + [pltpu.VMEM(ext, f32)] * 3 + [packed, packed],
        compiler_params=PARAMS,
        name="prepare",
    )(flags, *fields, left, right)


def phase_kernel(p, rows, cols, flags, mask, basis_in, k_in, t_in, c_in, up, down, *refs):
    first, last = p == 0, p == ITERS // 2 - 1
    basis, refs = refs[0], refs[1:]
    if first:
        kap, tau, cur, refs = refs[0], refs[1], refs[2], refs[3:]
    else:
        kap, tau, cur = k_in, t_in, c_in
    if last:
        sums, scaled, one = refs
    else:
        to_up, to_down, sums, scaled, one = refs
    wide = cols + LANES
    now = 2 * p

    for source, flag, begin in ((up, 2, None), (down, 3, PAD + rows)):
        base = 0
        for a, depth in enumerate(DEPTHS if first else (PAD,)):
            at = PAD - depth if begin is None else begin
            for i in range(depth):
                row = source[base + i] * flags[flag]
                if a == 0:
                    basis[now, at + i] = row
                else:
                    (None, kap, tau, cur)[a][at + i] = row
            base += depth

    def around(ref, r):
        v = ref[r]
        sides = pltpu.roll(v, 1, 1) + pltpu.roll(v, wide - 1, 1)
        return v, ref[r - 1] + ref[r + 1] + sides

    def scale_rows(ref, low, high):
        def step(r, carry):
            v, near = around(ref, r)
            scaled[r] = tau[r] * (kap[r] * v - near)
            return carry

        lax.fori_loop(low, high, step, 0)

    side = mask[...]

    def image(ref, r):
        s, near = around(scaled, r)
        out = kap[r] * s - near + cur[r] * ref[r]
        flag = jnp.where(r < PAD, flags[2], jnp.where(r >= PAD + rows, flags[3], 1.0))
        return jnp.concatenate([out[:, :cols], out[:, cols:] * side], axis=1) * flag

    def folded(x):
        parts = [x[:, c : c + LANES] for c in range(0, cols, LANES)]
        while len(parts) > 1:
            parts = [a + b for a, b in zip(parts[::2], parts[1::2])]
        return parts[0]

    zero = jnp.zeros((F, LANES), jnp.float32)
    current = basis.at[now]
    own_low, own_high = PAD, PAD + rows

    scale_rows(current, own_low - 3, own_high + 3)

    def outer(r, carry):
        one[r] = image(current, r)
        return carry

    lax.fori_loop(own_low - 2, own_low - 1, outer, 0)
    lax.fori_loop(own_high + 1, own_high + 2, outer, 0)

    def advance(r):
        new = image(current, r)
        one[r] = new
        if not first:
            new = 2.0 * new - basis[now - 1, r]
        basis[now + 1, r] = new
        return new

    def beside(r, carry):
        advance(r)
        return carry

    lax.fori_loop(own_low - 1, own_low, beside, 0)
    lax.fori_loop(own_high, own_high + 1, beside, 0)

    def first_rows(r, carry):
        new = advance(r)
        old = current[r]
        out = (carry[0] + folded(new * new), carry[1] + folded(new * old))
        return out + ((carry[2] + folded(old * old),) if first else ())

    squares = lax.fori_loop(own_low, own_high, first_rows, (zero,) * (3 if first else 2))
    sums[0] = squares[1]
    sums[1] = squares[0]
    if first:
        sums[4] = squares[2]

    if last:
        after = basis.at[now + 1]

        def final_rows(r, carry):
            v, near = around(after, r)
            k = kap[r] * v - near
            return carry + folded(tau[r] * k * k + cur[r] * v * v)

        sums[2] = lax.fori_loop(own_low, own_high, final_rows, zero)
        return

    scale_rows(one, own_low - 1, own_high + 1)

    def second_rows(r, carry):
        new = 2.0 * image(one, r) - current[r]
        if not first:
            new = 2.0 * new - basis[now - 2, r]
        basis[now + 2, r] = new
        return carry[0] + folded(new * basis[now + 1, r]), carry[1] + folded(new * new)

    squares = lax.fori_loop(own_low, own_high, second_rows, (zero, zero))
    sums[2] = squares[0]
    sums[3] = squares[1]
    to_up[...] = basis[now + 2, own_low : own_low + PAD]
    to_down[...] = basis[now + 2, own_high - PAD : own_high]


def phase(p, rows, cols, flags, mask, basis, coefs, up, down):
    first, last = p == 0, p == ITERS // 2 - 1
    f32 = jnp.float32
    wide = cols + LANES
    ext = (rows + 2 * PAD, F, wide)
    out_shape = [pltpu.VMEM(basis.shape, f32)]
    aliases = {2: 0}
    if first:
        out_shape += [pltpu.VMEM(ext, f32)] * 3
        aliases.update({3: 1, 4: 2, 5: 3})
    if not last:
        out_shape += [jax.ShapeDtypeStruct((PAD, F, wide), f32)] * 2
    out_shape += [jax.ShapeDtypeStruct((5 if first else 4, F, LANES), f32)]
    outs = pl.pallas_call(
        functools.partial(phase_kernel, p, rows, cols),
        in_specs=[SMEM] + [VMEM] * 7,
        out_specs=[VMEM] * len(out_shape),
        out_shape=out_shape,
        scratch_shapes=[pltpu.VMEM(ext, f32), pltpu.VMEM(ext, f32)],
        input_output_aliases=aliases,
        compiler_params=PARAMS,
        name=f"phase{p}",
    )(flags, mask, held(basis), *[held(c) for c in coefs], up, down)
    basis, outs = outs[0], outs[1:]
    if first:
        coefs, outs = outs[:3], outs[3:]
    if last:
        return basis, coefs, None, None, outs[0]
    return basis, coefs, outs[0], outs[1], outs[2]


def pack_kernel(s0, s1, s2, s3, out):
    lane = lax.broadcasted_iota(jnp.int32, (F, LANES), 1)
    order = [s0[4], s0[0], s0[1], s0[2], s0[3]]
    for s in (s1, s2):
        order += [s[0], s[1], s[2], s[3]]
    order += [s3[0], s3[1], s3[2]]
    table = jnp.zeros((F, LANES), jnp.float32)
    for k, entry in enumerate(order):
        table = jnp.where(lane == k, jnp.sum(entry, axis=1, keepdims=True), table)
    line = table[0:1]
    for f in range(1, F):
        line = line + pltpu.roll(table[f : f + 1], 2 * ITERS * f, 1)
    out[...] = line


def packed_sums(sums):
    return pl.pallas_call(
        pack_kernel,
        in_specs=[VMEM] * 4,
        out_specs=VMEM,
        out_shape=jax.ShapeDtypeStruct((1, LANES), jnp.float32),
        name="sums",
    )(*sums)


def coefficients(line):
    raw = [jnp.sum(jnp.where(lax.broadcasted_iota(jnp.int32, (F, LANES), 1)
                             == 2 * ITERS * lax.broadcasted_iota(jnp.int32, (F, LANES), 0) + k,
                             jnp.broadcast_to(line, (F, LANES)), 0.0), axis=1, keepdims=True)
           for k in range(2 * ITERS)]
    raw = [jnp.broadcast_to(v, (F, LANES)) for v in raw]
    m = [raw[0], raw[1]] + [2.0 * raw[k] - raw[k % 2] for k in range(2, 2 * ITERS - 1)]
    m.append(4.0 * raw[2 * ITERS - 1] - m[2 * ITERS - 3] - 2.0 * m[1])
    zero = jnp.zeros((F, LANES), jnp.float32)
    one = jnp.ones((F, LANES), jnp.float32)

    def moved(v):
        out = [MID * e for e in v] + [zero]
        out[1] = out[1] + HALF * v[0]
        for k in range(1, len(v)):
            out[k - 1] = out[k - 1] + 0.5 * HALF * v[k]
            out[k + 1] = out[k + 1] + 0.5 * HALF * v[k]
        return out

    def against(v, l):
        return MID * v[l] + 0.5 * HALF * (v[l + 1] + v[abs(l - 1)])

    res, way = list(m), list(m)
    res_in, way_in, lat_in = [one], [one], [zero] * ITERS
    lead = one
    now = m[0]
    worst = one
    for it in range(ITERS):
        image = [against(way, l) for l in range(len(way) - 1)]
        alpha = now / (lead * image[it])
        for k in range(it + 1):
            lat_in[k] = lat_in[k] + alpha * way_in[k]
        if it == ITERS - 1:
            break
        res = [res[l] - alpha * image[l] for l in range(len(image))]
        step = moved(way_in)
        res_in = [a - alpha * b for a, b in zip(res_in + [zero], step)]
        lead = res_in[it + 1]
        new = lead * res[it + 1]
        worst = jnp.minimum(worst, res[it + 1] / (lead * m[0]))
        beta = new / now
        way = [res[l] + beta * way[l] for l in range(len(res))]
        way_in = [a + beta * b for a, b in zip(res_in, way_in + [zero])]
        now = new
    return lat_in, worst, now / (m[0])


def weights_kernel(cells, fracs, high, low):
    col = lax.rem(cells[...], high.shape[0] - LANES)
    frac = fracs[...]

    def step(b, carry):
        at = pl.ds(pl.multiple_of(b * LANES, LANES), LANES)
        row = lax.broadcasted_iota(jnp.int32, (LANES, cells.shape[1]), 0) + b * LANES
        w = jnp.where(row == col, 1.0 - frac, jnp.where(row == col + 1, frac, 0.0))
        part = w.astype(jnp.bfloat16)
        high[at] = part
        low[at] = (w - part.astype(jnp.float32)).astype(jnp.bfloat16)
        return carry

    lax.fori_loop(0, high.shape[0] // LANES, step, 0)


def column_weights(cells, fracs, wide):
    shape = pltpu.VMEM((wide, cells.shape[1]), jnp.bfloat16)
    return pl.pallas_call(
        weights_kernel,
        in_specs=[VMEM] * 2,
        out_specs=[VMEM] * 2,
        out_shape=[shape, shape],
        compiler_params=PARAMS,
        name="column_weights",
    )(cells, fracs)


def finish_kernel(rows, cols, line, basis, high, low, cells, fracs, latent, predictor, fine, x_high, x_low, keep):
    wide = cols + LANES
    lat_in, worst, left = coefficients(line[...])
    fine[...] = jnp.where(worst >= PIVOT, 1.0, 0.0)
    for k in range(ITERS):
        keep[k] = lat_in[k]

    def step(c, carry):
        at = pl.ds(pl.multiple_of(c * LANES, LANES), LANES)
        total = keep[0] * basis[0, PAD : PAD + rows + 1, :, at]
        for k in range(1, ITERS):
            total = total + keep[k] * basis[k, PAD : PAD + rows + 1, :, at]
        part = total.astype(jnp.bfloat16)
        rest = (total - part.astype(jnp.float32)).astype(jnp.bfloat16)
        x_high[:, at] = part.reshape((rows + 1) * F, LANES)
        x_low[:, at] = rest.reshape((rows + 1) * F, LANES)

        @pl.when(c < cols // LANES)
        def _():
            latent[:, :, at] = jnp.swapaxes(total[:rows], 0, 1)

        return carry

    lax.fori_loop(0, wide // LANES, step, 0)
    chunk = 4 * LANES
    for c in range(0, cells.shape[1], chunk):
        at = slice(c, c + chunk)
        dot = functools.partial(jnp.dot, preferred_element_type=jnp.float32)
        both = dot(x_high[...], high[:, at]) + dot(x_low[...], high[:, at]) + dot(x_high[...], low[:, at])
        row = cells[:, at] // cols
        frac = fracs[:, at]
        out = jnp.zeros((F, chunk), jnp.float32)
        for r in range(rows + 1):
            w = jnp.where(row == r, 1.0 - frac, jnp.where(row + 1 == r, frac, 0.0))
            out = out + w * both[r * F : (r + 1) * F]
        for i in range(chunk // LANES):
            predictor[c // LANES + i] = out[:, i * LANES : (i + 1) * LANES]


def finish(rows, cols, line, basis, high, low, cells, fracs):
    f32 = jnp.float32
    wide = cols + LANES
    return pl.pallas_call(
        functools.partial(finish_kernel, rows, cols),
        in_specs=[VMEM] * 6,
        out_specs=[VMEM] * 3,
        out_shape=[
            jax.ShapeDtypeStruct((F, rows, cols), f32),
            jax.ShapeDtypeStruct((cells.shape[1] // LANES, F, LANES), f32),
            jax.ShapeDtypeStruct((F, LANES), f32),
        ],
        scratch_shapes=[
            pltpu.VMEM(((rows + 1) * F, wide), jnp.bfloat16),
            pltpu.VMEM(((rows + 1) * F, wide), jnp.bfloat16),
            pltpu.VMEM((ITERS, F, LANES), f32),
        ],
        compiler_params=PARAMS,
        name="finish",
    )(line, held(basis), held(high), held(low), cells, fracs)


def extended(x, sides, width):
    for axis, dim in sides:
        size, length = (lax.axis_size(axis), x.shape[dim])
        up = [(i, (i + 1) % size) for i in range(size - 1)]
        down = [(j, i) for i, j in up]
        last = lax.slice_in_dim(x, length - width, length, axis=dim)
        leading = lax.slice_in_dim(x, 0, width, axis=dim)
        before = lax.ppermute(last, axis, up)
        after = lax.ppermute(leading, axis, down)
        x = jnp.concatenate([before, x, after], axis=dim)
    return x


def passed_along(x, axis, by):
    length = lax.axis_size(axis)
    pairs = [(i, i + by) for i in range(length) if 0 <= i + by < length]
    return lax.ppermute(x, axis, pairs)


def neighbours(padded):
    return padded[:, 2:, 1:-1] + padded[:, :-2, 1:-1] + padded[:, 1:-1, 2:] + padded[:, 1:-1, :-2]


def plain(right_side, kappa_field, tau_field, curvature, got_cells, got_row, got_col):
    def squares(values):
        return lax.psum(jnp.sum(values * values, axis=(1, 2)), ("tile", "field"))[:, None, None]

    def sweep(_, state):
        latent, residual, direction, norm_now = state
        padded = extended(direction, (("tile", 1), ("field", 2)), 1)
        scaled = tau_field * ((kappa_field + 4.0) * direction - neighbours(padded))
        spread = extended(scaled, (("tile", 1), ("field", 2)), 1)
        image = (kappa_field + 4.0) * scaled - neighbours(spread) + curvature * direction
        inner = lax.psum(jnp.sum(direction * image, axis=(1, 2)), ("tile", "field"))[:, None, None]
        alpha = norm_now / inner
        latent = latent + alpha * direction
        residual = residual - alpha * image
        norm_next = squares(residual)
        direction = residual + norm_next / norm_now * direction
        return latent, residual, direction, norm_next

    state = (jnp.zeros_like(right_side), right_side, right_side, squares(right_side))
    latent = lax.fori_loop(0, ITERS, sweep, state)[0]
    upper = passed_along(latent[:, :1, :], "tile", -1)
    tall = jnp.concatenate([latent, upper], axis=1)
    beside = passed_along(tall[:, :, :1], "field", -1)
    wide = jnp.concatenate([tall, beside], axis=2)
    columns = latent.shape[2]
    width = columns + 1
    flat = wide.reshape(wide.shape[0], -1)
    base = (got_cells // columns * width + got_cells % columns).astype(jnp.int32)

    def corner(offset):
        return jnp.take(flat, base + offset, axis=1)

    row_frac = got_row[None]
    col_frac = got_col[None]
    predictor = (
        (1.0 - row_frac) * (1.0 - col_frac) * corner(0)
        + row_frac * (1.0 - col_frac) * corner(width)
        + (1.0 - row_frac) * col_frac * corner(1)
        + row_frac * col_frac * corner(width + 1)
    )
    return latent, jnp.transpose(predictor, (1, 0, 2))


def turned(x, axis, by):
    size = lax.axis_size(axis)
    return lax.ppermute(x, axis, [(i, (i + by) % size) for i in range(size)])


def local(
    right_side,
    kappa_field,
    tau_field,
    curvature,
    detect_prob,
    site_cells,
    site_offsets,
    site_count,
    visit_count,
    detections,
    surveyed,
):
    rows, cols = right_side.shape[1:]
    wide = cols + LANES
    tiles, bands = lax.axis_size("tile"), lax.axis_size("field")
    tile, band = lax.axis_index("tile"), lax.axis_index("field")
    flags = jnp.stack([band > 0, band < bands - 1, tile > 0, tile < tiles - 1]).astype(jnp.float32)
    lane = lax.broadcasted_iota(jnp.int32, (F, LANES), 1)
    mask = jnp.where(lane < SIDE, flags[1], jnp.where(lane >= LANES - SIDE, flags[0], 0.0))

    fields = (right_side, kappa_field, tau_field, curvature)
    to_left, to_right = columns_of(fields)
    from_right = turned(to_left, "field", -1)
    from_left = turned(to_right, "field", 1)
    basis, kap, tau, cur, to_up, to_down = prepare(flags, fields, from_left, from_right)
    coefs = (kap, tau, cur)

    cells = site_cells[0, 0]
    sent = jnp.concatenate([cells.astype(jnp.float32)[:, None], site_offsets[0, 0]], axis=1)
    got = None
    sums = []
    for p in range(ITERS // 2):
        from_down = turned(to_up, "tile", -1)
        from_up = turned(to_down, "tile", 1)
        if p == 0:
            sent, to_up = lax.optimization_barrier((sent, to_up))
            got = lax.all_to_all(sent, "tile", split_axis=0, concat_axis=0, tiled=True)
            got_cells = got[:, 0].astype(jnp.int32)
            got_row, got_col = got[:, 1], got[:, 2]
            high, low = column_weights(got_cells.reshape(1, -1), got_col.reshape(1, -1), wide)
        basis, coefs, to_up, to_down, part = phase(p, rows, cols, flags, mask, basis, coefs, from_up, from_down)
        sums.append(part)

    line = packed_sums(sums)
    spread = jnp.broadcast_to(line[None], (tiles * bands, 1, LANES))
    line = jnp.sum(lax.all_to_all(spread, ("tile", "field"), split_axis=0, concat_axis=0, tiled=True), axis=0)
    latent, predictor, fine = finish(
        rows, cols, line, basis, high, low, got_cells.reshape(1, -1), got_row.reshape(1, -1)
    )
    latent, predictor, _ = lax.while_loop(
        lambda state: state[2],
        lambda state: plain(*fields, got_cells, got_row, got_col) + (False,),
        (latent, predictor, jnp.logical_not(jnp.all(fine > 0.5))),
    )
    returned = lax.all_to_all(predictor, "tile", split_axis=0, concat_axis=0, tiled=True)

    slots = lax.broadcasted_iota(jnp.int32, cells.shape, 1)
    live = (slots < site_count[0, 0][:, None]).astype(jnp.float32)[:, None, :]
    visits = visit_count[0, 0].astype(jnp.float32)[:, None, :]
    miss_prob = jnp.exp(visits * jnp.log(1.0 - detect_prob)[:, None])
    expo = jnp.exp(returned)
    seen_grad = 1.0 / (1.0 + expo)
    miss_grad = -(1.0 - miss_prob) * expo / ((1.0 + expo) * (1.0 + miss_prob * expo))
    site_grad = (
        jnp.where(detections[0, 0] > 0, seen_grad, miss_grad)
        * surveyed[0, 0].astype(jnp.float32)
        * live
    )
    return (latent, site_grad[None, None])


def solution(mesh):
    in_specs = (
        P(None, "tile", "field"),
        P(None, "tile", "field"),
        P(None, "tile", "field"),
        P(None, "tile", "field"),
        P(),
        P("tile", "field", None, None),
        P("tile", "field", None, None, None),
        P("tile", "field", None),
        P("tile", "field", None, None),
        P("tile", "field", None, None, None),
        P("tile", "field", None, None, None),
    )
    out_specs = (P(None, "tile", "field"), P("tile", "field", None, None, None))
    return jax.shard_map(local, mesh=mesh, in_specs=in_specs, out_specs=out_specs, check_vma=False)
```

time: 1420 us -> 190 us (0.13)
  blocking collectives: 1030 us -> 0 us
  starting transfers between devices: 191 us -> 47 us
  other arithmetic: 69.5 us -> 5.6 us
  Pallas kernels: 0 us -> 55.8 us
  local copies, waits for them, and re-layouts: 62.4 us -> 41.2 us
  waiting for transfers between devices: 57.4 us -> 37.5 us
    psum x15 -> x0, blocking collectives: 1030 us -> none  [the longest x8 520 us: squares(): lax.psum(jnp.sum(values * values, axis=(1, 2)), ('tile', 'field'))]
    ppermute x66 -> x10, starting transfers between devices: 172 us -> 25.1 us  [turned(): return lax.ppermute(x, axis, [(i, (i + by) % size) for i in range(size)])]
    pallas_call x0 -> x9, Pallas kernels: none -> 55.8 us  [the longest x4 37.1 us: phase(): pl.pallas_call(functools.partial(phase_kernel, p, rows, cols), in_specs=[...]
    gather x8 -> x0, local copies, waits for them, and re-layouts: 47.3 us -> none  [corner(): return jnp.take(flat, base + offset, axis=1)]
    reduce_sum x15 -> x1, other arithmetic: 36 us -> 0.03 us  [local(): jnp.sum(lax.all_to_all(spread, ('tile', 'field'), split_axis=0, concat_ax...]
    unnamed x40 -> x44, local copies, waits for them, and re-layouts: 0.96 us -> 35.9 us
    ppermute x66 -> x10, waiting for transfers between devices: 49.8 us -> 29.8 us  [turned(): return lax.ppermute(x, axis, [(i, (i + by) % size) for i in range(size)])]
    add x8 -> x0, other arithmetic: 16.8 us -> none  [the longest x7 12.6 us: local(): direction = residual + norm_next / norm_now * direction]
  transfers between devices with their start and end apart: 69 -> 13, of which waited for: 49 -> 6; matrix products, arithmetic and copies ran while one was open for 1% -> 2% of each run, Pallas kernels for 0% -> 7%
where the time goes in v1:
time: 190 us; the launch traced here: 189 us
  Pallas kernels  55.8 us (29%)
  starting transfers between devices  47 us (25%)
  local copies, waits for them, and re-layouts  41.2 us (22%)
  waiting for transfers between devices  37.5 us (20%)
  other arithmetic  5.6 us (3%)
    pallas_call x4, Pallas kernels, phase(): pl.pallas_call(functools.partial(phase_kernel, p, rows, cols), in_specs=[...  37.1 us
    unnamed x44, local copies, waits for them, and re-layouts  35.9 us
    ppermute x10, waiting for transfers between devices, turned(): return lax.ppermute(x, axis, [(i, (i + by) % size) for i in range(size)])  29.8 us
    ppermute x10, starting transfers between devices, turned(): return lax.ppermute(x, axis, [(i, (i + by) % size) for i in range(size)])  25.1 us
    all_to_all x1, starting transfers between devices, local(): lax.all_to_all(spread, ('tile', 'field'), split_axis=0, concat_axis=0, ti...  12.1 us
    all_to_all x1, waiting for transfers between devices, local(): lax.all_to_all(predictor, 'tile', split_axis=0, concat_axis=0, tiled=True)  7.64 us
    pallas_call x1, Pallas kernels, finish(): pl.pallas_call(functools.partial(finish_kernel, rows, cols), in_specs=[VM...  6.56 us
    all_to_all x1, starting transfers between devices, local(): lax.all_to_all(predictor, 'tile', split_axis=0, concat_axis=0, tiled=True)  6.27 us
  transfers between devices with their start and end apart: 13, of which 6 were waited for; matrix products, arithmetic and copies ran while one was open for 2% of the time, Pallas kernels for 7%

profile of v1, /device:TPU:0, one launch (start us, length us, event | category | flops | bytes accessed | tf_op | source)
XLA Modules:
  0.0 188.8 jit_solution(11269774527336443625)
XLA Ops:
  0.6 1.9 %columns.1 = (f32[16,8,128]{2,1,0:T(8,128)}, f32[16,8,128]{2,1,0:T(8,128)}) custom-call(f32[8,16,2048]{2,1,0:T(8,128)} %refs_0_.3, f32[8,16,2048]{2,1,0:T(8,128)} %refs_1_.3, f32[8,16,2048]{2,1,0:T(8,128)} %refs_2_.3, f32[8,16,2048]{2,1,0:T(8,128)} %refs_3_.3, f32[8,16,2048]{2,1,0:T(8,128)} %refs_0_.3, f32[8,16,2048]{2,1,0:T(8,128)} %refs_1_.3, ...), custom_call_target="tpu_custom_call" | custom-call | tf_op jit(solution)/shard_map/columns/pallas_call | solution.py:47
  2.5 0.0 collective-permute-start.10
  2.5 3.6 %collective-permute-start.11 = (f32[16,8,128]{2,1,0:T(8,128)}, f32[16,8,128]{2,1,0:T(8,128)S(1)}, u32[]{:S(2)}, u32[]{:S(2)}) collective-permute-start(f32[16,8,128]{2,1,0:T(8,128)} %get-tuple-element.148), channel_id=1, source_target_pairs={{0,7},{1,0},{2,1},{3,2},{4,3},{5,4},{6,5},{7,6},{8,15},{9,8},{10,9... | collective-permute-start | bytes 196616 | tf_op jit(solution)/shard_map/ppermute | solution.py:493
  6.1 0.1 add_convert_fusion.flags
  6.2 2.1 %collective-permute-done.10.refs_4_ = f32[16,8,128]{2,1,0:T(8,128)S(1)} collective-permute-done((f32[16,8,128]{2,1,0:T(8,128)}, f32[16,8,128]{2,1,0:T(8,128)S(1)}, u32[]{:S(2)}, u32[]{:S(2)}) %collective-permute-start.10) | collective-permute-done | bytes 65568 | tf_op jit(solution)/shard_map/ppermute | solution.py:493
  8.3 0.1 collective-permute-done.11.refs_5_
  8.3 4.0 %prepare.1 = (f32[8,24,8,2176]{3,2,1,0:T(8,128)S(1)}, f32[24,8,2176]{2,1,0:T(8,128)S(1)}, f32[24,8,2176]{2,1,0:T(8,128)S(1)}, f32[24,8,2176]{2,1,0:T(8,128)S(1)}...) custom-call(f32[4]{0:T(128)S(1)} %add_convert_fusion.flags, f32[8,16,2048]{2,1,0:T(8,128)} %refs_0_.3, ...), custom_call_target="tpu_custom_call" | custom-call | tf_op jit(solution)/shard_map/prepare/pallas_call | solution.py:103
  12.3 1.6 collective-permute-start.12
  13.9 3.8 %collective-permute-start.13 = (f32[12,8,2176]{2,1,0:T(8,128)S(1)}, f32[12,8,2176]{2,1,0:T(8,128)S(1)}, u32[]{:S(2)}, u32[]{:S(2)}) collective-permute-start(f32[12,8,2176]{2,1,0:T(8,128)S(1)} %get-tuple-element.154), channel_id=1, source_target_pairs={{0,120},{8,0},{16,8},{24,16},{32,24},{40,32},{48,40},{56,48},{64,5... | collective-permute-start | bytes 2506760 | tf_op jit(solution)/shard_map/ppermute | solution.py:493
  17.7 0.6 fusion.29
  18.3 0.6 compare_select_fusion.4
  18.9 0.7 broadcast_select_fusion.mask
  19.6 17.0 %collective-permute-done.12.up = f32[12,8,2176]{2,1,0:T(8,128)S(1)} collective-permute-done((f32[12,8,2176]{2,1,0:T(8,128)S(1)}, f32[12,8,2176]{2,1,0:T(8,128)S(1)}, u32[]{:S(2)}, u32[]{:S(2)}) %collective-permute-start.12) | collective-permute-done | bytes 835616 | tf_op jit(solution)/shard_map/ppermute | solution.py:493
  36.6 0.0 collective-permute-done.13.down
  36.6 9.5 %phase0.1 = (f32[8,24,8,2176]{3,2,1,0:T(8,128)S(1)}, f32[24,8,2176]{2,1,0:T(8,128)S(1)}, f32[24,8,2176]{2,1,0:T(8,128)S(1)}, f32[24,8,2176]{2,1,0:T(8,128)S(1)},...) custom-call(f32[4]{0:T(128)S(1)} %add_convert_fusion.flags, ...), custom_call_target="tpu_custom_call", output_to_operand_aliasing={{0}: (2, {}), {1}: (3, {}), {2}: (4, {}), {3}: (5, {})} | custom-call | tf_op jit(solution)/shard_map/phase0/pallas_call | solution.py:246
  46.0 0.0 copy-start.10
  46.0 0.0 copy-start.4
  46.0 0.1 collective-permute-start.14
  46.1 5.3 %collective-permute-start.15 = (f32[4,8,2176]{2,1,0:T(8,128)S(1)}, f32[4,8,2176]{2,1,0:T(8,128)S(1)}, u32[]{:S(2)}, u32[]{:S(2)}) collective-permute-start(f32[4,8,2176]{2,1,0:T(8,128)S(1)} %get-tuple-element.161), channel_id=1, source_target_pairs={{0,120},{8,0},{16,8},{24,16},{32,24},{40,32},{48,40},{56,48},{64,5... | collective-permute-start | bytes 835592 | tf_op jit(solution)/shard_map/ppermute | solution.py:493
  51.5 6.1 %collective-permute-done.14.up = f32[4,8,2176]{2,1,0:T(8,128)S(1)} collective-permute-done((f32[4,8,2176]{2,1,0:T(8,128)S(1)}, f32[4,8,2176]{2,1,0:T(8,128)S(1)}, u32[]{:S(2)}, u32[]{:S(2)}) %collective-permute-start.14) | collective-permute-done | bytes 278560 | tf_op jit(solution)/shard_map/ppermute | solution.py:493
  57.6 0.0 collective-permute-done.15.down
  57.6 9.6 %phase1.1 = (f32[8,24,8,2176]{3,2,1,0:T(8,128)S(1)}, f32[4,8,2176]{2,1,0:T(8,128)S(1)}, f32[4,8,2176]{2,1,0:T(8,128)S(1)}, f32[4,8,128]{2,1,0:T(8,128)S(1)}) custom-call(f32[4]{0:T(128)S(1)} %add_convert_fusion.flags, f32[8,128]{1,0:T(8,128)S(1)} %broadcast_select_fusion.mask, ...), custom_call_target="tpu_custom_call", output_to_operand_aliasing={{0}: (2, {})} | custom-call | tf_op jit(solution)/shard_map/phase1/pallas_call | solution.py:246
  67.1 0.0 copy-done.10
  67.2 0.1 collective-permute-start.16
  67.3 5.3 %collective-permute-start.17 = (f32[4,8,2176]{2,1,0:T(8,128)S(1)}, f32[4,8,2176]{2,1,0:T(8,128)S(1)}, u32[]{:S(2)}, u32[]{:S(2)}) collective-permute-start(f32[4,8,2176]{2,1,0:T(8,128)S(1)} %get-tuple-element.165), channel_id=1, source_target_pairs={{0,120},{8,0},{16,8},{24,16},{32,24},{40,32},{48,40},{56,48},{64,5... | collective-permute-start | bytes 835592 | tf_op jit(solution)/shard_map/ppermute | solution.py:493
  72.6 0.6 convert_bitcast_fusion
  73.2 4.6 %collective-permute-done.16.up = f32[4,8,2176]{2,1,0:T(8,128)S(1)} collective-permute-done((f32[4,8,2176]{2,1,0:T(8,128)S(1)}, f32[4,8,2176]{2,1,0:T(8,128)S(1)}, u32[]{:S(2)}, u32[]{:S(2)}) %collective-permute-start.16) | collective-permute-done | bytes 278560 | tf_op jit(solution)/shard_map/ppermute | solution.py:493
  77.8 0.0 collective-permute-done.17.down
  77.8 0.0 copy-start.19
  77.8 0.0 copy-start.22
  77.8 10.4 %phase2.1 = (f32[8,24,8,2176]{3,2,1,0:T(8,128)S(1)}, f32[4,8,2176]{2,1,0:T(8,128)}, f32[4,8,2176]{2,1,0:T(8,128)}, f32[4,8,128]{2,1,0:T(8,128)S(1)}) custom-call(f32[4]{0:T(128)S(1)} %add_convert_fusion.flags, f32[8,128]{1,0:T(8,128)S(1)} %broadcast_select_fusion.mask, ...), custom_call_target="tpu_custom_call", output_to_operand_aliasing={{0}: (2, {})} | custom-call | tf_op jit(solution)/shard_map/phase2/pallas_call | solution.py:246
  88.2 4.8 %copy-done = f32[8,24,8,2176]{3,2,1,0:T(8,128)} copy-done((f32[8,24,8,2176]{3,2,1,0:T(8,128)}, f32[8,24,8,2176]{3,2,1,0:T(8,128)S(1)}, u32[]{:S(2)}) %copy-start) | copy-done | bytes 13369368
  93.0 0.6 copy-done.12
  93.6 0.0 collective-permute-start.18
  93.6 5.3 %collective-permute-start.19 = (f32[4,8,2176]{2,1,0:T(8,128)}, f32[4,8,2176]{2,1,0:T(8,128)}, u32[]{:S(2)}, u32[]{:S(2)}) collective-permute-start(f32[4,8,2176]{2,1,0:T(8,128)} %get-tuple-element.169), channel_id=1, source_target_pairs={{0,120},{8,0},{16,8},{24,16},{32,24},{40,32},{48,40},{56,48},{64,5... | collective-permute-start | bytes 835592 | tf_op jit(solution)/shard_map/ppermute | solution.py:493
  99.0 0.6 pad_maximum_fusion.23
  99.6 3.5 %all-to-all-start.1 = ((f32[16,3,128]{2,1,0:T(4,128)}), f32[16,3,128]{2,1,0:T(4,128)S(1)}, u32[]{:S(2)}, u32[]{:S(2)}) async-start(f32[16,3,128]{2,1,0:T(4,128)} %pad_maximum_fusion.23), calls=%async_computation.1 | async-start | bytes 65536 | tf_op jit(solution)/shard_map/all_to_all | solution.py:533
  103.1 0.7 fusion.23
  103.8 0.0 collective-permute-done.18.up
  103.8 0.0 collective-permute-done.19.down
  103.8 4.8 %copy-done.1 = f32[8,24,8,2176]{3,2,1,0:T(8,128)S(1)} copy-done((f32[8,24,8,2176]{3,2,1,0:T(8,128)S(1)}, f32[8,24,8,2176]{3,2,1,0:T(8,128)}, u32[]{:S(2)}) %copy-start.1) | copy-done | bytes 13369368
  108.6 1.4 copy-done.5
  110.1 7.8 %phase3.1 = (f32[8,24,8,2176]{3,2,1,0:T(8,128)S(1)}, f32[4,8,128]{2,1,0:T(8,128)S(1)}) custom-call(f32[4]{0:T(128)S(1)} %add_convert_fusion.flags, f32[8,128]{1,0:T(8,128)S(1)} %broadcast_select_fusion.mask, f32[8,24,8,2176]{3,2,1,0:T(8,128)S(1)} %copy-done.1, f32[24,8,2176]{2,1,0:T(8,128)S(1)} %get-tuple-element.157.k_in, ...), custom_call_target="tpu_custom_call", output_to_operand_aliasing={{0}: (2, {})} | custom-call | tf_op jit(solution)/shard_map/phase3/pallas_call | solution.py:246
  117.8 4.8 %copy-done.2 = f32[8,24,8,2176]{3,2,1,0:T(8,128)} copy-done((f32[8,24,8,2176]{3,2,1,0:T(8,128)}, f32[8,24,8,2176]{3,2,1,0:T(8,128)S(1)}, u32[]{:S(2)}) %copy-start.2) | copy-done | bytes 13369368
  122.7 0.6 copy-done.13
  123.3 1.4 sums.1
  124.7 0.0 all-to-all-done.1
  124.7 1.3 broadcast_in_dim.50
  126.0 12.1 %all-to-all-start = ((f32[128,1,128]{2,1,0:T(1,128)}), f32[128,1,128]{2,1,0:T(1,128)S(1)}, u32[]{:S(2)}, u32[]{:S(2)}) async-start(f32[128,1,128]{2,1,0:T(1,128)} %broadcast_in_dim.50), calls=%async_computation | async-start | bytes 131072 | tf_op jit(solution)/shard_map/all_to_all | solution.py:542
  138.1 4.8 %column_weights.1 = (bf16[2176,2048]{1,0:T(8,128)(2,1)S(1)}, bf16[2176,2048]{1,0:T(8,128)(2,1)S(1)}) custom-call(s32[1,2048]{1,0:T(1,128)S(1)} %get-tuple-element.323.cells, f32[1,2048]{1,0:T(1,128)S(1)} %get-tuple-element.321.fracs), custom_call_target="tpu_custom_call" | custom-call | tf_op jit(solution)/shard_map/column_weights/pallas_call | solution.py:354
  142.9 3.4 %copy-done.6 = bf16[2176,2048]{1,0:T(8,128)(2,1)} copy-done((bf16[2176,2048]{1,0:T(8,128)(2,1)}, bf16[2176,2048]{1,0:T(8,128)(2,1)S(1)}, u32[]{:S(2)}) %copy-start.6) | copy-done | bytes 8912920
  146.4 3.5 %copy-done.8 = bf16[2176,2048]{1,0:T(8,128)(2,1)} copy-done((bf16[2176,2048]{1,0:T(8,128)(2,1)}, bf16[2176,2048]{1,0:T(8,128)(2,1)S(1)}, u32[]{:S(2)}) %copy-start.8) | copy-done | bytes 8912920
  149.8 0.0 all-to-all-done
  149.8 4.8 %copy-done.3 = f32[8,24,8,2176]{3,2,1,0:T(8,128)S(1)} copy-done((f32[8,24,8,2176]{3,2,1,0:T(8,128)S(1)}, f32[8,24,8,2176]{3,2,1,0:T(8,128)}, u32[]{:S(2)}) %copy-start.3) | copy-done | bytes 13369368
  154.6 3.5 %copy-done.7 = bf16[2176,2048]{1,0:T(8,128)(2,1)S(1)} copy-done((bf16[2176,2048]{1,0:T(8,128)(2,1)S(1)}, bf16[2176,2048]{1,0:T(8,128)(2,1)}, u32[]{:S(2)}) %copy-start.7) | copy-done | bytes 8912920
  158.2 3.5 %copy-done.9 = bf16[2176,2048]{1,0:T(8,128)(2,1)S(1)} copy-done((bf16[2176,2048]{1,0:T(8,128)(2,1)S(1)}, bf16[2176,2048]{1,0:T(8,128)(2,1)}, u32[]{:S(2)}) %copy-start.9) | copy-done | bytes 8912920
  161.7 6.6 %finish.1 = (f32[8,16,2048]{2,1,0:T(8,128)}, f32[16,8,128]{2,1,0:T(8,128)S(1)}, f32[8,128]{1,0:T(8,128)S(1)}) custom-call(f32[1,128]{1,0:T(1,128)S(1)} %bitcast.100, f32[8,24,8,2176]{3,2,1,0:T(8,128)S(1)} %copy-done.3, bf16[2176,2048]{1,0:T(8,128)(2,1)S(1)} %copy-done.7, bf16[2176,2048]{1,0:T(8,128)(2,1)S(1)} %copy-done.9, ...), custom_call_target="tpu_custom_call" | custom-call | tf_op jit(solution)/shard_map/finish/pallas_call | solution.py:406
  168.3 0.6 compare_reduce_fusion
  169.6 1.3 copy.52
  170.9 0.2 while.28
  171.1 2.2 %copy.55 = f32[16,8,128]{2,1,0:T(8,128)} copy(f32[16,8,128]{1,2,0:T(8,128)} %get-tuple-element.493) | data formatting | bytes 131072 | tf_op jit(solution)/shard_map/while | solution.py:546
  173.3 6.3 %all-to-all-start.2 = ((f32[16,8,128]{2,1,0:T(8,128)}), f32[16,8,128]{2,1,0:T(8,128)S(1)}, u32[]{:S(2)}, u32[]{:S(2)}) async-start(f32[16,8,128]{2,1,0:T(8,128)} %copy.55), calls=%async_computation.2 | async-start | bytes 131072 | tf_op jit(solution)/shard_map/all_to_all | solution.py:551
  179.6 7.6 %all-to-all-done.2 = f32[16,8,128]{2,1,0:T(8,128)S(1)} async-done(((f32[16,8,128]{2,1,0:T(8,128)}), f32[16,8,128]{2,1,0:T(8,128)S(1)}, u32[]{:S(2)}, u32[]{:S(2)}) %all-to-all-start.2) | async-done | bytes 65568 | tf_op jit(solution)/shard_map/all_to_all | solution.py:551
  187.2 1.6 fusion.22
  (33 shorter events, 0.1 us)
Async XLA Ops:
  2.5 5.7 %collective-permute-start.10 = (f32[16,8,128]{2,1,0:T(8,128)}, f32[16,8,128]{2,1,0:T(8,128)S(1)}, u32[]{:S(2)}, u32[]{:S(2)}) collective-permute-start(f32[16,8,128]{2,1,0:T(8,128)} %get-tuple-element.147), channel_id=1, source_target_pairs={{0,1},{1,2},{2,3},{3,4},{4,5},{5,6},{6,7},{7,0},{8,9},{9,10},{10,1... | collective-permute-start | bytes 196616 | tf_op jit(solution)/shard_map/ppermute | solution.py:493
  2.5 5.8 %collective-permute-start.11 = (f32[16,8,128]{2,1,0:T(8,128)}, f32[16,8,128]{2,1,0:T(8,128)S(1)}, u32[]{:S(2)}, u32[]{:S(2)}) collective-permute-start(f32[16,8,128]{2,1,0:T(8,128)} %get-tuple-element.148), channel_id=1, source_target_pairs={{0,7},{1,0},{2,1},{3,2},{4,3},{5,4},{6,5},{7,6},{8,15},{9,8},{10,9... | collective-permute-start | bytes 196616 | tf_op jit(solution)/shard_map/ppermute | solution.py:493
  12.3 24.3 %collective-permute-start.12 = (f32[12,8,2176]{2,1,0:T(8,128)S(1)}, f32[12,8,2176]{2,1,0:T(8,128)S(1)}, u32[]{:S(2)}, u32[]{:S(2)}) collective-permute-start(f32[12,8,2176]{2,1,0:T(8,128)S(1)} %get-tuple-element.153), channel_id=1, source_target_pairs={{0,8},{8,16},{16,24},{24,32},{32,40},{40,48},{48,56},{56,64},{64,7... | collective-permute-start | bytes 2506760 | tf_op jit(solution)/shard_map/ppermute | solution.py:493
  13.9 22.6 %collective-permute-start.13 = (f32[12,8,2176]{2,1,0:T(8,128)S(1)}, f32[12,8,2176]{2,1,0:T(8,128)S(1)}, u32[]{:S(2)}, u32[]{:S(2)}) collective-permute-start(f32[12,8,2176]{2,1,0:T(8,128)S(1)} %get-tuple-element.154), channel_id=1, source_target_pairs={{0,120},{8,0},{16,8},{24,16},{32,24},{40,32},{48,40},{56,48},{64,5... | collective-permute-start | bytes 2506760 | tf_op jit(solution)/shard_map/ppermute | solution.py:493
  46.0 21.1 %copy-start.10 = (f32[5,8,128]{2,1,0:T(8,128)}, f32[5,8,128]{2,1,0:T(8,128)S(1)}, u32[]{:S(2)}) copy-start(f32[5,8,128]{2,1,0:T(8,128)S(1)} %get-tuple-element.155.s0) | copy-start | bytes 61444
  46.0 31.8 %copy-start.4 = (f32[24,8,2176]{2,1,0:T(8,128)}, f32[24,8,2176]{2,1,0:T(8,128)S(1)}, u32[]{:S(2)}) copy-start(f32[24,8,2176]{2,1,0:T(8,128)S(1)} %get-tuple-element.159.c_in) | copy-start | bytes 5013508
  46.0 11.5 %collective-permute-start.14 = (f32[4,8,2176]{2,1,0:T(8,128)S(1)}, f32[4,8,2176]{2,1,0:T(8,128)S(1)}, u32[]{:S(2)}, u32[]{:S(2)}) collective-permute-start(f32[4,8,2176]{2,1,0:T(8,128)S(1)} %get-tuple-element.160), channel_id=1, source_target_pairs={{0,8},{8,16},{16,24},{24,32},{32,40},{40,48},{48,56},{56,64},{64,7... | collective-permute-start | bytes 835592 | tf_op jit(solution)/shard_map/ppermute | solution.py:493
  46.1 11.5 %collective-permute-start.15 = (f32[4,8,2176]{2,1,0:T(8,128)S(1)}, f32[4,8,2176]{2,1,0:T(8,128)S(1)}, u32[]{:S(2)}, u32[]{:S(2)}) collective-permute-start(f32[4,8,2176]{2,1,0:T(8,128)S(1)} %get-tuple-element.161), channel_id=1, source_target_pairs={{0,120},{8,0},{16,8},{24,16},{32,24},{40,32},{48,40},{56,48},{64,5... | collective-permute-start | bytes 835592 | tf_op jit(solution)/shard_map/ppermute | solution.py:493
  57.6 15.0 %copy-start.20 = (s32[1,1,16,128]{3,2,1,0:T(8,128)S(1)}, s32[1,1,16,128]{3,2,1,0:T(8,128)}, u32[]{:S(2)}) copy-start(s32[1,1,16,128]{3,2,1,0:T(8,128)} %param.22) | copy-start | bytes 24580
  57.6 15.0 %copy-start.21 = (s32[1,1,16,128]{3,2,1,0:T(8,128)S(1)}, s32[1,1,16,128]{3,2,1,0:T(8,128)}, u32[]{:S(2)}) copy-start(s32[1,1,16,128]{3,2,1,0:T(8,128)} %param.25) | copy-start | bytes 24580
  67.2 10.6 %copy-start.11 = (f32[4,8,128]{2,1,0:T(8,128)}, f32[4,8,128]{2,1,0:T(8,128)S(1)}, u32[]{:S(2)}) copy-start(f32[4,8,128]{2,1,0:T(8,128)S(1)} %get-tuple-element.162.s1) | copy-start | bytes 49156
  67.2 10.6 %collective-permute-start.16 = (f32[4,8,2176]{2,1,0:T(8,128)S(1)}, f32[4,8,2176]{2,1,0:T(8,128)S(1)}, u32[]{:S(2)}, u32[]{:S(2)}) collective-permute-start(f32[4,8,2176]{2,1,0:T(8,128)S(1)} %get-tuple-element.164), channel_id=1, source_target_pairs={{0,8},{8,16},{16,24},{24,32},{32,40},{40,48},{48,56},{56,64},{64,7... | collective-permute-start | bytes 835592 | tf_op jit(solution)/shard_map/ppermute | solution.py:493
  67.3 10.5 %collective-permute-start.17 = (f32[4,8,2176]{2,1,0:T(8,128)S(1)}, f32[4,8,2176]{2,1,0:T(8,128)S(1)}, u32[]{:S(2)}, u32[]{:S(2)}) collective-permute-start(f32[4,8,2176]{2,1,0:T(8,128)S(1)} %get-tuple-element.165), channel_id=1, source_target_pairs={{0,120},{8,0},{16,8},{24,16},{32,24},{40,32},{48,40},{56,48},{64,5... | collective-permute-start | bytes 835592 | tf_op jit(solution)/shard_map/ppermute | solution.py:493
  77.8 21.2 %copy-start.19 = (f32[1,1,16,2,128]{4,3,2,1,0:T(2,128)S(1)}, f32[1,1,16,2,128]{4,3,2,1,0:T(2,128)}, u32[]{:S(2)}) copy-start(f32[1,1,16,2,128]{4,3,2,1,0:T(2,128)} %param.23) | copy-start | bytes 49156
  77.8 25.3 %copy-start.22 = (s32[1,1,16]{2,1,0:T(1,128)S(1)}, s32[1,1,16]{2,1,0:T(1,128)}, u32[]{:S(2)}) copy-start(s32[1,1,16]{2,1,0:T(1,128)} %param.24) | copy-start | bytes 196
  88.2 4.8 %copy-start = (f32[8,24,8,2176]{3,2,1,0:T(8,128)}, f32[8,24,8,2176]{3,2,1,0:T(8,128)S(1)}, u32[]{:S(2)}) copy-start(f32[8,24,8,2176]{3,2,1,0:T(8,128)S(1)} %get-tuple-element.167.basis_in) | copy-start | bytes 40108036
  93.0 0.6 copy-start.12
  93.6 10.2 %collective-permute-start.18 = (f32[4,8,2176]{2,1,0:T(8,128)}, f32[4,8,2176]{2,1,0:T(8,128)}, u32[]{:S(2)}, u32[]{:S(2)}) collective-permute-start(f32[4,8,2176]{2,1,0:T(8,128)} %get-tuple-element.168), channel_id=1, source_target_pairs={{0,8},{8,16},{16,24},{24,32},{32,40},{40,48},{48,56},{56,64},{64,7... | collective-permute-start | bytes 835592 | tf_op jit(solution)/shard_map/ppermute | solution.py:493
  93.6 10.2 %collective-permute-start.19 = (f32[4,8,2176]{2,1,0:T(8,128)}, f32[4,8,2176]{2,1,0:T(8,128)}, u32[]{:S(2)}, u32[]{:S(2)}) collective-permute-start(f32[4,8,2176]{2,1,0:T(8,128)} %get-tuple-element.169), channel_id=1, source_target_pairs={{0,120},{8,0},{16,8},{24,16},{32,24},{40,32},{48,40},{56,48},{64,5... | collective-permute-start | bytes 835592 | tf_op jit(solution)/shard_map/ppermute | solution.py:493
  99.6 25.1 %all-to-all-start.1 = ((f32[16,3,128]{2,1,0:T(4,128)}), f32[16,3,128]{2,1,0:T(4,128)S(1)}, u32[]{:S(2)}, u32[]{:S(2)}) async-start(f32[16,3,128]{2,1,0:T(4,128)} %pad_maximum_fusion.23), calls=%async_computation.1 | async-start | bytes 65536 | tf_op jit(solution)/shard_map/all_to_all | solution.py:533
  103.8 4.8 %copy-start.1 = (f32[8,24,8,2176]{3,2,1,0:T(8,128)S(1)}, f32[8,24,8,2176]{3,2,1,0:T(8,128)}, u32[]{:S(2)}) copy-start(f32[8,24,8,2176]{3,2,1,0:T(8,128)} %copy-done) | copy-start | bytes 40108036
  108.6 1.4 copy-start.5
  117.8 4.8 %copy-start.2 = (f32[8,24,8,2176]{3,2,1,0:T(8,128)}, f32[8,24,8,2176]{3,2,1,0:T(8,128)S(1)}, u32[]{:S(2)}) copy-start(f32[8,24,8,2176]{3,2,1,0:T(8,128)S(1)} %get-tuple-element.171.basis) | copy-start | bytes 40108036
  122.7 0.6 copy-start.13
  126.0 23.8 %all-to-all-start = ((f32[128,1,128]{2,1,0:T(1,128)}), f32[128,1,128]{2,1,0:T(1,128)S(1)}, u32[]{:S(2)}, u32[]{:S(2)}) async-start(f32[128,1,128]{2,1,0:T(1,128)} %broadcast_in_dim.50), calls=%async_computation | async-start | bytes 131072 | tf_op jit(solution)/shard_map/all_to_all | solution.py:542
  142.9 3.4 %copy-start.6 = (bf16[2176,2048]{1,0:T(8,128)(2,1)}, bf16[2176,2048]{1,0:T(8,128)(2,1)S(1)}, u32[]{:S(2)}) copy-start(bf16[2176,2048]{1,0:T(8,128)(2,1)S(1)} %get-tuple-element.173.high) | copy-start | bytes 26738692
  146.3 3.5 %copy-start.8 = (bf16[2176,2048]{1,0:T(8,128)(2,1)}, bf16[2176,2048]{1,0:T(8,128)(2,1)S(1)}, u32[]{:S(2)}) copy-start(bf16[2176,2048]{1,0:T(8,128)(2,1)S(1)} %get-tuple-element.174.low) | copy-start | bytes 26738692
  149.8 4.8 %copy-start.3 = (f32[8,24,8,2176]{3,2,1,0:T(8,128)S(1)}, f32[8,24,8,2176]{3,2,1,0:T(8,128)}, u32[]{:S(2)}) copy-start(f32[8,24,8,2176]{3,2,1,0:T(8,128)} %copy-done.2) | copy-start | bytes 40108036
  154.6 3.5 %copy-start.7 = (bf16[2176,2048]{1,0:T(8,128)(2,1)S(1)}, bf16[2176,2048]{1,0:T(8,128)(2,1)}, u32[]{:S(2)}) copy-start(bf16[2176,2048]{1,0:T(8,128)(2,1)} %copy-done.6) | copy-start | bytes 26738692
  158.2 3.5 %copy-start.9 = (bf16[2176,2048]{1,0:T(8,128)(2,1)S(1)}, bf16[2176,2048]{1,0:T(8,128)(2,1)}, u32[]{:S(2)}) copy-start(bf16[2176,2048]{1,0:T(8,128)(2,1)} %copy-done.8) | copy-start | bytes 26738692
  161.7 9.2 %copy-start.15 = (f32[8,16,2048]{2,1,0:T(8,128)S(1)}, f32[8,16,2048]{2,1,0:T(8,128)}, u32[]{:S(2)}) copy-start(f32[8,16,2048]{2,1,0:T(8,128)} %refs_0_.3) | copy-start | bytes 3145732
  170.9 8.6 %copy-start.23 = (f32[8]{0:T(128)S(1)}, f32[8]{0:T(128)}, u32[]{:S(2)}) copy-start(f32[8]{0:T(128)} %param.21) | copy-start | bytes 100
  170.9 16.3 %copy-start.17 = (f32[16,128]{1,0:T(8,128)S(1)}, f32[16,128]{1,0:T(8,128)}, u32[]{:S(2)}) copy-start(f32[16,128]{1,0:T(8,128)} %convert_bitcast_fusion) | copy-start | bytes 24580
  170.9 16.3 %copy-start.18 = (f32[16,128]{1,0:T(8,128)S(1)}, f32[16,128]{1,0:T(8,128)}, u32[]{:S(2)}) copy-start(f32[16,128]{1,0:T(8,128)} %fusion.23) | copy-start | bytes 24580
  173.3 13.9 %all-to-all-start.2 = ((f32[16,8,128]{2,1,0:T(8,128)}), f32[16,8,128]{2,1,0:T(8,128)S(1)}, u32[]{:S(2)}, u32[]{:S(2)}) async-start(f32[16,8,128]{2,1,0:T(8,128)} %copy.55), calls=%async_computation.2 | async-start | bytes 131072 | tf_op jit(solution)/shard_map/all_to_all | solution.py:551

commit v2 on v1

--- a/solution.py
+++ b/solution.py
@@ -14,10 +14,9 @@
 LANES = 128
 LOW, HIGH = 0.2, 15.0
 MID, HALF = 0.5 * (HIGH + LOW), 0.5 * (HIGH - LOW)
-PIVOT = 3e-4
 VMEM = pl.BlockSpec(memory_space=pltpu.VMEM)
 SMEM = pl.BlockSpec(memory_space=pltpu.SMEM)
-PARAMS = pltpu.CompilerParams(vmem_limit_bytes=16 * 1024 * 1024)
+PARAMS = pltpu.CompilerParams(vmem_limit_bytes=10 * 1024 * 1024)
 
 
 def held(x):
@@ -110,21 +109,56 @@
     )(flags, *fields, left, right)
 
 
+def walk(ref, r, count, wide):
+    tiles = wide // LANES
+    lane = lax.broadcasted_iota(jnp.int32, (F, LANES), 1)
+    leftmost, rightmost = lane == 0, lane == LANES - 1
+
+    def load(c):
+        return [ref[r - 1 + i, :, c * LANES : (c + 1) * LANES] for i in range(count + 2)]
+
+    def turn(tile, by):
+        return [pltpu.roll(v, by, 1) for v in tile[1:-1]]
+
+    now = load(0)
+    before = turn([ref[r - 1 + i, :, wide - LANES :] for i in range(count + 2)], 1)
+    right, left = turn(now, 1), turn(now, LANES - 1)
+    start = left
+    for c in range(tiles):
+        after = load(c + 1) if c + 1 < tiles else None
+        following = turn(after, LANES - 1) if after else start
+        near = [
+            (now[i] + now[i + 2])
+            + (jnp.where(leftmost, before[i], right[i]) + jnp.where(rightmost, following[i], left[i]))
+            for i in range(count)
+        ]
+        yield slice(c * LANES, (c + 1) * LANES), now[1:-1], near
+        if after:
+            before, right, left, now = right, turn(after, 1), following, after
+
+
+def pairs(low, high, body, carry):
+    return lax.fori_loop(0, (high - low) // 2, lambda i, carry: body(low + 2 * i, carry), carry)
+
+
 def phase_kernel(p, rows, cols, flags, mask, basis_in, k_in, t_in, c_in, up, down, *refs):
     first, last = p == 0, p == ITERS // 2 - 1
+    if last:
+        earlier, refs = refs[: ITERS // 2 - 1], refs[ITERS // 2 - 1 :]
     basis, refs = refs[0], refs[1:]
     if first:
         kap, tau, cur, refs = refs[0], refs[1], refs[2], refs[3:]
     else:
         kap, tau, cur = k_in, t_in, c_in
     if last:
-        sums, scaled, one = refs
+        line, scaled, one = refs
     else:
         to_up, to_down, sums, scaled, one = refs
     wide = cols + LANES
     now = 2 * p
-
-    for source, flag, begin in ((up, 2, None), (down, 3, PAD + rows)):
+    own_low, own_high = PAD, PAD + rows
+
+    for source, flag, begin in ((up, 2, None), (down, 3, own_high)):
         base = 0
         for a, depth in enumerate(DEPTHS if first else (PAD,)):
             at = PAD - depth if begin is None else begin
@@ -136,101 +170,105 @@
                     (None, kap, tau, cur)[a][at + i] = row
             base += depth
 
-    def around(ref, r):
-        v = ref[r]
-        sides = pltpu.roll(v, 1, 1) + pltpu.roll(v, wide - 1, 1)
-        return v, ref[r - 1] + ref[r + 1] + sides
-
-    def scale_rows(ref, low, high):
-        def step(r, carry):
-            v, near = around(ref, r)
-            scaled[r] = tau[r] * (kap[r] * v - near)
-            return carry
-
-        lax.fori_loop(low, high, step, 0)
-
-    side = mask[...]
-
-    def image(ref, r):
-        s, near = around(scaled, r)
-        out = kap[r] * s - near + cur[r] * ref[r]
-        flag = jnp.where(r < PAD, flags[2], jnp.where(r >= PAD + rows, flags[3], 1.0))
-        return jnp.concatenate([out[:, :cols], out[:, cols:] * side], axis=1) * flag
-
-    def folded(x):
-        parts = [x[:, c : c + LANES] for c in range(0, cols, LANES)]
-        while len(parts) > 1:
-            parts = [a + b for a, b in zip(parts[::2], parts[1::2])]
-        return parts[0]
-
     zero = jnp.zeros((F, LANES), jnp.float32)
     current = basis.at[now]
-    own_low, own_high = PAD, PAD + rows
-
-    scale_rows(current, own_low - 3, own_high + 3)
-
-    def outer(r, carry):
-        one[r] = image(current, r)
-        return carry
-
-    lax.fori_loop(own_low - 2, own_low - 1, outer, 0)
-    lax.fori_loop(own_high + 1, own_high + 2, outer, 0)
-
-    def advance(r):
-        new = image(current, r)
-        one[r] = new
-        if not first:
-            new = 2.0 * new - basis[now - 1, r]
-        basis[now + 1, r] = new
-        return new
-
-    def beside(r, carry):
-        advance(r)
-        return carry
-
-    lax.fori_loop(own_low - 1, own_low, beside, 0)
-    lax.fori_loop(own_high, own_high + 1, beside, 0)
+
+    def scale(ref, low, high):
+        def body(r, carry):
+            for at, v, near in walk(ref, r, 2, wide):
+                for i in range(2):
+                    scaled[r + i, :, at] = tau[r + i, :, at] * (kap[r + i, :, at] * v[i] - near[i])
+            return carry
+
+        pairs(low, high, body, 0)
+
+    def image(ref, r):
+        for at, s, near in walk(scaled, r, 2, wide):
+            out = []
+            for i in range(2):
+                new = (kap[r + i, :, at] * s[i] - near[i]) + cur[r + i, :, at] * ref[r + i, :, at]
+                out.append(new * mask[...] if at.start == cols else new)
+            yield at, out
+
+    scale(current, own_low - 3, own_high + 3)
+    for r, flag, inner in ((own_low - 2, flags[2], 1), (own_high, flags[3], 0)):
+        for at, new in image(current, r):
+            for i in range(2):
+                value = new[i] * flag
+                one[r + i, :, at] = value
+                if i == inner:
+                    basis[now + 1, r + i, :, at] = value if first else 2.0 * value - basis[now - 1, r + i, :, at]
 
     def first_rows(r, carry):
-        new = advance(r)
-        old = current[r]
-        out = (carry[0] + folded(new * new), carry[1] + folded(new * old))
-        return out + ((carry[2] + folded(old * old),) if first else ())
-
-    squares = lax.fori_loop(own_low, own_high, first_rows, (zero,) * (3 if first else 2))
-    sums[0] = squares[1]
-    sums[1] = squares[0]
-    if first:
-        sums[4] = squares[2]
+        cross = square = start = zero
+        for at, new in image(current, r):
+            for i in range(2):
+                one[r + i, :, at] = new[i]
+                value = new[i] if first else 2.0 * new[i] - basis[now - 1, r + i, :, at]
+                basis[now + 1, r + i, :, at] = value
+                if at.start < cols:
+                    old = current[r + i, :, at]
+                    cross += value * old
+                    square += value * value
+                    if first:
+                        start += old * old
+        out = (carry[0] + cross, carry[1] + square)
+        return out + ((carry[2] + start,) if first else ())
+
+    found = pairs(own_low, own_high, first_rows, (zero,) * (3 if first else 2))
 
     if last:
         after = basis.at[now + 1]
 
         def final_rows(r, carry):
-            v, near = around(after, r)
-            k = kap[r] * v - near
-            return carry + folded(tau[r] * k * k + cur[r] * v * v)
-
-        sums[2] = lax.fori_loop(own_low, own_high, final_rows, zero)
+            total = zero
+            for at, v, near in walk(after, r, 2, wide):
+                if at.start < cols:
+                    for i in range(2):
+                        k = kap[r + i, :, at] * v[i] - near[i]
+                        total += tau[r + i, :, at] * k * k + cur[r + i, :, at] * v[i] * v[i]
+            return carry + total
+
+        found += (pairs(own_low, own_high, final_rows, zero),)
+        entries = [earlier[0][4]]
+        for s in earlier:
+            entries += [s[i] for i in range(4)]
+        lane = lax.broadcasted_iota(jnp.int32, (F, LANES), 1)
+        table = zero
+        for k, entry in enumerate(entries + list(found)):
+            table = jnp.where(lane == k, jnp.sum(entry, axis=1, keepdims=True), table)
+        total = table[0:1]
+        for f in range(1, F):
+            total = total + pltpu.roll(table[f : f + 1], 2 * ITERS * f, 1)
+        line[...] = jnp.broadcast_to(total[None], line.shape)
         return
 
-    scale_rows(one, own_low - 1, own_high + 1)
+    sums[0] = found[0]
+    sums[1] = found[1]
+    if first:
+        sums[4] = found[2]
+
+    scale(one, own_low - 1, own_high + 1)
 
     def second_rows(r, carry):
-        new = 2.0 * image(one, r) - current[r]
-        if not first:
-            new = 2.0 * new - basis[now - 2, r]
-        basis[now + 2, r] = new
-        return carry[0] + folded(new * basis[now + 1, r]), carry[1] + folded(new * new)
-
-    squares = lax.fori_loop(own_low, own_high, second_rows, (zero, zero))
-    sums[2] = squares[0]
-    sums[3] = squares[1]
+        cross = square = zero
+        for at, new in image(one, r):
+            for i in range(2):
+                value = 2.0 * new[i] - current[r + i, :, at]
+                if not first:
+                    value = 2.0 * value - basis[now - 2, r + i, :, at]
+                basis[now + 2, r + i, :, at] = value
+                if at.start < cols:
+                    cross += value * basis[now + 1, r + i, :, at]
+                    square += value * value
+        return carry[0] + cross, carry[1] + square
+
+    sums[2], sums[3] = pairs(own_low, own_high, second_rows, (zero, zero))
     to_up[...] = basis[now + 2, own_low : own_low + PAD]
     to_down[...] = basis[now + 2, own_high - PAD : own_high]
 
 
-def phase(p, rows, cols, flags, mask, basis, coefs, up, down):
+def phase(p, rows, cols, flags, mask, basis, coefs, up, down, earlier=(), devices=1):
     first, last = p == 0, p == ITERS // 2 - 1
     f32 = jnp.float32
     wide = cols + LANES
@@ -240,50 +278,27 @@
     if first:
         out_shape += [pltpu.VMEM(ext, f32)] * 3
         aliases.update({3: 1, 4: 2, 5: 3})
-    if not last:
+    if last:
+        out_shape += [jax.ShapeDtypeStruct((devices, 1, LANES), f32)]
+    else:
         out_shape += [jax.ShapeDtypeStruct((PAD, F, wide), f32)] * 2
-    out_shape += [jax.ShapeDtypeStruct((5 if first else 4, F, LANES), f32)]
+        out_shape += [jax.ShapeDtypeStruct((5 if first else 4, F, LANES), f32)]
     outs = pl.pallas_call(
         functools.partial(phase_kernel, p, rows, cols),
-        in_specs=[SMEM] + [VMEM] * 7,
+        in_specs=[SMEM] + [VMEM] * (7 + len(earlier)),
         out_specs=[VMEM] * len(out_shape),
         out_shape=out_shape,
         scratch_shapes=[pltpu.VMEM(ext, f32), pltpu.VMEM(ext, f32)],
         input_output_aliases=aliases,
         compiler_params=PARAMS,
         name=f"phase{p}",
-    )(flags, mask, held(basis), *[held(c) for c in coefs], up, down)
+    )(flags, mask, held(basis), *[held(c) for c in coefs], up, down, *earlier)
     basis, outs = outs[0], outs[1:]
     if first:
         coefs, outs = outs[:3], outs[3:]
     if last:
-        return basis, coefs, None, None, outs[0]
+        return basis, outs[0]
     return basis, coefs, outs[0], outs[1], outs[2]
-
-
-def pack_kernel(s0, s1, s2, s3, out):
-    lane = lax.broadcasted_iota(jnp.int32, (F, LANES), 1)
-    order = [s0[4], s0[0], s0[1], s0[2], s0[3]]
-    for s in (s1, s2):
-        order += [s[0], s[1], s[2], s[3]]
-    order += [s3[0], s3[1], s3[2]]
-    table = jnp.zeros((F, LANES), jnp.float32)
-    for k, entry in enumerate(order):
-        table = jnp.where(lane == k, jnp.sum(entry, axis=1, keepdims=True), table)
-    line = table[0:1]
-    for f in range(1, F):
-        line = line + pltpu.roll(table[f : f + 1], 2 * ITERS * f, 1)
-    out[...] = line
-
-
-def packed_sums(sums):
-    return pl.pallas_call(
-        pack_kernel,
-        in_specs=[VMEM] * 4,
-        out_specs=VMEM,
-        out_shape=jax.ShapeDtypeStruct((1, LANES), jnp.float32),
-        name="sums",
-    )(*sums)
 
 
 def coefficients(line):
@@ -312,7 +327,7 @@
     res_in, way_in, lat_in = [one], [one], [zero] * ITERS
     lead = one
     now = m[0]
-    worst = one
+    pivots = []
     for it in range(ITERS):
         image = [against(way, l) for l in range(len(way) - 1)]
         alpha = now / (lead * image[it])
@@ -325,82 +340,94 @@
         res_in = [a - alpha * b for a, b in zip(res_in + [zero], step)]
         lead = res_in[it + 1]
         new = lead * res[it + 1]
-        worst = jnp.minimum(worst, res[it + 1] / (lead * m[0]))
+        pivots.append(res[it + 1] / (lead * m[0]))
         beta = new / now
         way = [res[l] + beta * way[l] for l in range(len(res))]
         way_in = [a + beta * b for a, b in zip(res_in, way_in + [zero])]
         now = new
-    return lat_in, worst, now / (m[0])
-
-
-def weights_kernel(cells, fracs, high, low):
-    col = lax.rem(cells[...], high.shape[0] - LANES)
-    frac = fracs[...]
+    fine = pivots[-1] >= 0.3 * pivots[0]
+    for pivot in pivots:
+        fine = fine & (pivot >= 5e-3) & (pivot <= 20.0)
+    return lat_in, fine
+
+
+def columns_hot_kernel(cells, hot):
+    col = lax.rem(cells[...], hot.shape[0] - LANES)
 
     def step(b, carry):
         at = pl.ds(pl.multiple_of(b * LANES, LANES), LANES)
         row = lax.broadcasted_iota(jnp.int32, (LANES, cells.shape[1]), 0) + b * LANES
-        w = jnp.where(row == col, 1.0 - frac, jnp.where(row == col + 1, frac, 0.0))
-        part = w.astype(jnp.bfloat16)
-        high[at] = part
-        low[at] = (w - part.astype(jnp.float32)).astype(jnp.bfloat16)
+        hot[at] = jnp.where(row == col, 1.0, 0.0).astype(jnp.bfloat16)
         return carry
 
-    lax.fori_loop(0, high.shape[0] // LANES, step, 0)
-
-
-def column_weights(cells, fracs, wide):
-    shape = pltpu.VMEM((wide, cells.shape[1]), jnp.bfloat16)
+    lax.fori_loop(0, hot.shape[0] // LANES, step, 0)
+
+
+def columns_hot(cells, wide):
     return pl.pallas_call(
-        weights_kernel,
-        in_specs=[VMEM] * 2,
-        out_specs=[VMEM] * 2,
-        out_shape=[shape, shape],
+        columns_hot_kernel,
+        in_specs=[VMEM],
+        out_specs=VMEM,
+        out_shape=pltpu.VMEM((wide, cells.shape[1]), jnp.bfloat16),
         compiler_params=PARAMS,
-        name="column_weights",
-    )(cells, fracs)
-
-
-def finish_kernel(rows, cols, line, basis, high, low, cells, fracs, latent, predictor, fine, x_high, x_low, keep):
+        name="columns_hot",
+    )(cells)
+
+
+def finish_kernel(rows, cols, line, basis, hot, cells, row_frac, col_frac, latent, predictor, fine, parts, keep):
     wide = cols + LANES
-    lat_in, worst, left = coefficients(line[...])
-    fine[...] = jnp.where(worst >= PIVOT, 1.0, 0.0)
+    lat_in, good = coefficients(line[...])
+    fine[...] = jnp.where(good, 1.0, 0.0)
     for k in range(ITERS):
         keep[k] = lat_in[k]
-
-    def step(c, carry):
+    lane = lax.broadcasted_iota(jnp.int32, (rows + 1, F, LANES), 2)
+    tall = (rows + 1) * F
+
+    def split(x, at, base):
+        part = x.astype(jnp.bfloat16)
+        rest = (x - part.astype(jnp.float32)).astype(jnp.bfloat16)
+        parts[base : base + tall, at] = part.reshape(tall, LANES)
+        parts[base + tall : base + 2 * tall, at] = rest.reshape(tall, LANES)
+
+    def step(c, after):
+        c = wide // LANES - 1 - c
         at = pl.ds(pl.multiple_of(c * LANES, LANES), LANES)
         total = keep[0] * basis[0, PAD : PAD + rows + 1, :, at]
         for k in range(1, ITERS):
             total = total + keep[k] * basis[k, PAD : PAD + rows + 1, :, at]
-        part = total.astype(jnp.bfloat16)
-        rest = (total - part.astype(jnp.float32)).astype(jnp.bfloat16)
-        x_high[:, at] = part.reshape((rows + 1) * F, LANES)
-        x_low[:, at] = rest.reshape((rows + 1) * F, LANES)
+        turned = pltpu.roll(total, LANES - 1, 2)
+        split(total, at, 0)
+        split(jnp.where(lane == LANES - 1, after, turned), at, 2 * tall)
 
         @pl.when(c < cols // LANES)
         def _():
             latent[:, :, at] = jnp.swapaxes(total[:rows], 0, 1)
 
-        return carry
-
-    lax.fori_loop(0, wide // LANES, step, 0)
+        return turned
+
+    lax.fori_loop(0, wide // LANES, step, jnp.zeros((rows + 1, F, LANES), jnp.float32))
     chunk = 4 * LANES
     for c in range(0, cells.shape[1], chunk):
         at = slice(c, c + chunk)
-        dot = functools.partial(jnp.dot, preferred_element_type=jnp.float32)
-        both = dot(x_high[...], high[:, at]) + dot(x_low[...], high[:, at]) + dot(x_high[...], low[:, at])
+        both = jnp.dot(parts[...], hot[:, at], preferred_element_type=jnp.float32)
+        here = both[:tall] + both[tall : 2 * tall]
+        beside = both[2 * tall : 3 * tall] + both[3 * tall :]
         row = cells[:, at] // cols
-        frac = fracs[:, at]
-        out = jnp.zeros((F, chunk), jnp.float32)
+        frac = row_frac[:, at]
+        low = jnp.zeros((F, chunk), jnp.float32)
+        high = jnp.zeros((F, chunk), jnp.float32)
         for r in range(rows + 1):
             w = jnp.where(row == r, 1.0 - frac, jnp.where(row + 1 == r, frac, 0.0))
-            out = out + w * both[r * F : (r + 1) * F]
+            low = low + w * here[r * F : (r + 1) * F]
+            high = high + w * beside[r * F : (r + 1) * F]
+        side = col_frac[:, at]
+        out = (1.0 - side) * low + side * high
         for i in range(chunk // LANES):
-            predictor[c // LANES + i] = out[:, i * LANES : (i + 1) * LANES]
-
-
-def finish(rows, cols, line, basis, high, low, cells, fracs):
+            base = (c // LANES + i) * F
+            predictor[base : base + F] = out[:, i * LANES : (i + 1) * LANES]
+
+
+def finish(rows, cols, line, basis, hot, cells, row_frac, col_frac):
     f32 = jnp.float32
     wide = cols + LANES
     return pl.pallas_call(
@@ -409,17 +436,16 @@
         out_specs=[VMEM] * 3,
         out_shape=[
             jax.ShapeDtypeStruct((F, rows, cols), f32),
-            jax.ShapeDtypeStruct((cells.shape[1] // LANES, F, LANES), f32),
+            jax.ShapeDtypeStruct((cells.shape[1] // LANES * F, LANES), f32),
             jax.ShapeDtypeStruct((F, LANES), f32),
         ],
         scratch_shapes=[
-            pltpu.VMEM(((rows + 1) * F, wide), jnp.bfloat16),
-            pltpu.VMEM(((rows + 1) * F, wide), jnp.bfloat16),
+            pltpu.VMEM((4 * (rows + 1) * F, wide), jnp.bfloat16),
             pltpu.VMEM((ITERS, F, LANES), f32),
         ],
         compiler_params=PARAMS,
         name="finish",
-    )(line, held(basis), held(high), held(low), cells, fracs)
+    )(line, held(basis), held(hot), cells, row_frac, col_frac)
 
 
 def extended(x, sides, width):
@@ -485,7 +511,7 @@
         + (1.0 - row_frac) * col_frac * corner(1)
         + row_frac * col_frac * corner(width + 1)
     )
-    return latent, jnp.transpose(predictor, (1, 0, 2))
+    return latent, jnp.transpose(predictor, (1, 0, 2)).reshape(-1, predictor.shape[2])
 
 
 def turned(x, axis, by):
@@ -523,7 +549,6 @@
 
     cells = site_cells[0, 0]
     sent = jnp.concatenate([cells.astype(jnp.float32)[:, None], site_offsets[0, 0]], axis=1)
-    got = None
     sums = []
     for p in range(ITERS // 2):
         from_down = turned(to_up, "tile", -1)
@@ -533,21 +558,26 @@
             got = lax.all_to_all(sent, "tile", split_axis=0, concat_axis=0, tiled=True)
             got_cells = got[:, 0].astype(jnp.int32)
             got_row, got_col = got[:, 1], got[:, 2]
-            high, low = column_weights(got_cells.reshape(1, -1), got_col.reshape(1, -1), wide)
-        basis, coefs, to_up, to_down, part = phase(p, rows, cols, flags, mask, basis, coefs, from_up, from_down)
-        sums.append(part)
-
-    line = packed_sums(sums)
-    spread = jnp.broadcast_to(line[None], (tiles * bands, 1, LANES))
-    line = jnp.sum(lax.all_to_all(spread, ("tile", "field"), split_axis=0, concat_axis=0, tiled=True), axis=0)
+            hot = columns_hot(got_cells.reshape(1, -1), wide)
+            flags, hot = lax.optimization_barrier((flags, hot))
+        state = (p, rows, cols, flags, mask, basis, coefs, from_up, from_down)
+        if p < ITERS // 2 - 1:
+            basis, coefs, to_up, to_down, part = phase(*state)
+            sums.append(part)
+        else:
+            basis, spread = phase(*state, earlier=sums, devices=tiles * bands)
+
+    spread = lax.all_to_all(spread, ("tile", "field"), split_axis=0, concat_axis=0, tiled=True)
+    line = jnp.sum(spread, axis=0)
     latent, predictor, fine = finish(
-        rows, cols, line, basis, high, low, got_cells.reshape(1, -1), got_row.reshape(1, -1)
+        rows, cols, line, basis, hot, got_cells.reshape(1, -1), got_row.reshape(1, -1), got_col.reshape(1, -1)
     )
     latent, predictor, _ = lax.while_loop(
         lambda state: state[2],
         lambda state: plain(*fields, got_cells, got_row, got_col) + (False,),
         (latent, predictor, jnp.logical_not(jnp.all(fine > 0.5))),
     )
+    predictor = predictor.reshape(tiles, F, LANES)
     returned = lax.all_to_all(predictor, "tile", split_axis=0, concat_axis=0, tiled=True)
 
     slots = lax.broadcasted_iota(jnp.int32, cells.shape, 1)

time: 190 us -> 184 us (0.968)
  Pallas kernels: 55.8 us -> 43.3 us
  waiting for transfers between devices: 37.5 us -> 47.8 us
  local copies, waits for them, and re-layouts: 41.2 us -> 37.6 us
    all_to_all x1, waiting for transfers between devices: 0.01 us -> 15.3 us  [local(): got = lax.all_to_all(sent, 'tile', split_axis=0, concat_axis=0, tiled=True)]
    ppermute x10, waiting for transfers between devices: 29.8 us -> 16.2 us  [turned(): return lax.ppermute(x, axis, [(i, (i + by) % size) for i in range(size)])]
    pallas_call x4, Pallas kernels: 37.1 us -> 26 us  [phase(): pl.pallas_call(functools.partial(phase_kernel, p, rows, cols), in_specs=[...]
    all_to_all x1, waiting for transfers between devices: 0.01 us -> 8.76 us  [local(): lax.all_to_all(spread, ('tile', 'field'), split_axis=0, concat_axis=0, ti...]
    pallas_call x2 -> x1, Pallas kernels: 6.27 us -> 1.6 us  [columns_hot(): pl.pallas_call(columns_hot_kernel, in_specs=[VMEM], out_specs=VMEM, out_s...]
    while x2 -> x0, local copies, waits for them, and re-layouts: 3.5 us -> none  [local(): lax.while_loop(lambda state: state[2], lambda state: plain(*fields, got_c...]
    all_to_all x1, starting transfers between devices: 3.5 us -> 6.72 us  [local(): got = lax.all_to_all(sent, 'tile', split_axis=0, concat_axis=0, tiled=True)]
    all_to_all x1, starting transfers between devices: 6.27 us -> 3.51 us  [local(): lax.all_to_all(predictor, 'tile', split_axis=0, concat_axis=0, tiled=True)]
  transfers between devices with their start and end apart: 13 -> 13, of which waited for: 6 -> 8; matrix products, arithmetic and copies ran while one was open for 2% -> 2% of each run, Pallas kernels for 7% -> 1%
where the time goes in v2:
time: 184 us
  waiting for transfers between devices  47.8 us (26%)
  starting transfers between devices  47.5 us (26%)
  Pallas kernels  43.3 us (24%)
  local copies, waits for them, and re-layouts  37.6 us (20%)
  other arithmetic  5.72 us (3%)
    unnamed x36, local copies, waits for them, and re-layouts  37 us
    pallas_call x4, Pallas kernels, phase(): pl.pallas_call(functools.partial(phase_kernel, p, rows, cols), in_specs=[...  26 us
    ppermute x10, starting transfers between devices, turned(): return lax.ppermute(x, axis, [(i, (i + by) % size) for i in range(size)])  24.9 us
    ppermute x10, waiting for transfers between devices, turned(): return lax.ppermute(x, axis, [(i, (i + by) % size) for i in range(size)])  16.2 us
    all_to_all x1, waiting for transfers between devices, local(): got = lax.all_to_all(sent, 'tile', split_axis=0, concat_axis=0, tiled=True)  15.3 us
    all_to_all x1, starting transfers between devices, local(): lax.all_to_all(spread, ('tile', 'field'), split_axis=0, concat_axis=0, ti...  12.3 us
    all_to_all x1, waiting for transfers between devices, local(): lax.all_to_all(spread, ('tile', 'field'), split_axis=0, concat_axis=0, ti...  8.76 us
    pallas_call x1, Pallas kernels, finish(): pl.pallas_call(functools.partial(finish_kernel, rows, cols), in_specs=[VM...  8.63 us
  transfers between devices with their start and end apart: 13, of which 8 were waited for; matrix products, arithmetic and copies ran while one was open for 2% of the time, Pallas kernels for 1%

profile of v2, /device:TPU:0, one launch (start us, length us, event | category | flops | bytes accessed | tf_op | source)
XLA Modules:
  0.0 183.6 jit_solution(2286086000759009347)
XLA Ops:
  0.6 1.9 %columns.1 = (f32[16,8,128]{2,1,0:T(8,128)}, f32[16,8,128]{2,1,0:T(8,128)}) custom-call(f32[8,16,2048]{2,1,0:T(8,128)} %refs_0_.3, f32[8,16,2048]{2,1,0:T(8,128)} %refs_1_.3, f32[8,16,2048]{2,1,0:T(8,128)} %refs_2_.3, f32[8,16,2048]{2,1,0:T(8,128)} %refs_3_.3, f32[8,16,2048]{2,1,0:T(8,128)} %refs_0_.3, f32[8,16,2048]{2,1,0:T(8,128)} %refs_1_.3, ...), custom_call_target="tpu_custom_call" | custom-call | tf_op jit(solution)/shard_map/columns/pallas_call | solution.py:46
  2.5 0.0 collective-permute-start.10
  2.5 3.6 %collective-permute-start.11 = (f32[16,8,128]{2,1,0:T(8,128)}, f32[16,8,128]{2,1,0:T(8,128)S(1)}, u32[]{:S(2)}, u32[]{:S(2)}) collective-permute-start(f32[16,8,128]{2,1,0:T(8,128)} %get-tuple-element.148), channel_id=1, source_target_pairs={{0,7},{1,0},{2,1},{3,2},{4,3},{5,4},{6,5},{7,6},{8,15},{9,8},{10,9... | collective-permute-start | bytes 196616 | tf_op jit(solution)/shard_map/ppermute | solution.py:519
  6.1 0.1 add_convert_fusion.flags
  6.2 2.1 %collective-permute-done.10.refs_4_ = f32[16,8,128]{2,1,0:T(8,128)S(1)} collective-permute-done((f32[16,8,128]{2,1,0:T(8,128)}, f32[16,8,128]{2,1,0:T(8,128)S(1)}, u32[]{:S(2)}, u32[]{:S(2)}) %collective-permute-start.10) | collective-permute-done | bytes 65568 | tf_op jit(solution)/shard_map/ppermute | solution.py:519
  8.3 0.1 collective-permute-done.11.refs_5_
  8.3 5.2 %prepare.1 = (f32[8,24,8,2176]{3,2,1,0:T(8,128)S(1)}, f32[24,8,2176]{2,1,0:T(8,128)S(1)}, f32[24,8,2176]{2,1,0:T(8,128)S(1)}, f32[24,8,2176]{2,1,0:T(8,128)S(1)}...) custom-call(f32[4]{0:T(128)S(1)} %add_convert_fusion.flags, f32[8,16,2048]{2,1,0:T(8,128)} %refs_0_.3, ...), custom_call_target="tpu_custom_call" | custom-call | tf_op jit(solution)/shard_map/prepare/pallas_call | solution.py:102
  13.5 4.8 %copy-done = f32[8,24,8,2176]{3,2,1,0:T(8,128)} copy-done((f32[8,24,8,2176]{3,2,1,0:T(8,128)}, f32[8,24,8,2176]{3,2,1,0:T(8,128)S(1)}, u32[]{:S(2)}) %copy-start) | copy-done | bytes 13369368
  18.4 1.2 copy-done.8
  19.5 5.2 %collective-permute-start.13 = (f32[12,8,2176]{2,1,0:T(8,128)}, f32[12,8,2176]{2,1,0:T(8,128)}, u32[]{:S(2)}, u32[]{:S(2)}) collective-permute-start(f32[12,8,2176]{2,1,0:T(8,128)} %get-tuple-element.149), channel_id=1, source_target_pairs={{0,120},{8,0},{16,8},{24,16},{32,24},{40,32},{48,40},{56,48},{64,5... | collective-permute-start | bytes 2506760 | tf_op jit(solution)/shard_map/ppermute | solution.py:519
  24.7 0.0 collective-permute-start.12
  24.7 0.0 copy-done.16
  24.8 0.6 fusion.29
  25.4 0.6 compare_select_fusion.4
  26.0 0.0 copy-done.15
  26.0 0.6 pad_maximum_fusion.23
  26.7 6.7 %all-to-all-start = ((f32[16,3,128]{2,1,0:T(4,128)}), f32[16,3,128]{2,1,0:T(4,128)S(1)}, u32[]{:S(2)}, u32[]{:S(2)}) async-start(f32[16,3,128]{2,1,0:T(4,128)} %pad_maximum_fusion.23), calls=%async_computation | async-start | bytes 65536 | tf_op jit(solution)/shard_map/all_to_all | solution.py:558
  33.4 0.6 broadcast_select_fusion.mask
  34.0 15.3 %all-to-all-done = f32[16,3,128]{2,1,0:T(4,128)S(1)} async-done(((f32[16,3,128]{2,1,0:T(4,128)}), f32[16,3,128]{2,1,0:T(4,128)S(1)}, u32[]{:S(2)}, u32[]{:S(2)}) %all-to-all-start) | async-done | bytes 24608 | tf_op jit(solution)/shard_map/all_to_all | solution.py:558
  49.3 0.0 copy-start.9
  49.3 1.6 columns_hot.1.hot
  50.9 0.0 copy-start.6
  51.0 3.4 %copy-done.6 = bf16[2176,2048]{1,0:T(8,128)(2,1)} copy-done((bf16[2176,2048]{1,0:T(8,128)(2,1)}, bf16[2176,2048]{1,0:T(8,128)(2,1)S(1)}, u32[]{:S(2)}) %copy-start.6) | copy-done | bytes 8912920
  54.4 0.0 collective-permute-done.13.down
  54.4 0.0 collective-permute-done.12.up
  54.4 0.0 copy-done.9
  54.4 0.0 copy-start.1
  54.4 4.8 %copy-done.1 = f32[8,24,8,2176]{3,2,1,0:T(8,128)S(1)} copy-done((f32[8,24,8,2176]{3,2,1,0:T(8,128)S(1)}, f32[8,24,8,2176]{3,2,1,0:T(8,128)}, u32[]{:S(2)}) %copy-start.1) | copy-done | bytes 13369368
  59.2 7.4 %phase0.1 = (f32[8,24,8,2176]{3,2,1,0:T(8,128)S(1)}, f32[24,8,2176]{2,1,0:T(8,128)S(1)}, f32[24,8,2176]{2,1,0:T(8,128)S(1)}, f32[24,8,2176]{2,1,0:T(8,128)S(1)},...) custom-call(f32[4]{0:T(128)S(1)} %add_convert_fusion.flags, ...), custom_call_target="tpu_custom_call", output_to_operand_aliasing={{0}: (2, {}), {1}: (3, {}), {2}: (4, {}), {3}: (5, {})} | custom-call | tf_op jit(solution)/shard_map/phase0/pallas_call | solution.py:286
  66.6 0.9 collective-permute-start.14
  67.5 4.5 %collective-permute-start.15 = (f32[4,8,2176]{2,1,0:T(8,128)S(1)}, f32[4,8,2176]{2,1,0:T(8,128)S(1)}, u32[]{:S(2)}, u32[]{:S(2)}) collective-permute-start(f32[4,8,2176]{2,1,0:T(8,128)S(1)} %get-tuple-element.162), channel_id=1, source_target_pairs={{0,120},{8,0},{16,8},{24,16},{32,24},{40,32},{48,40},{56,48},{64,5... | collective-permute-start | bytes 835592 | tf_op jit(solution)/shard_map/ppermute | solution.py:519
  72.0 5.5 %collective-permute-done.14.up = f32[4,8,2176]{2,1,0:T(8,128)S(1)} collective-permute-done((f32[4,8,2176]{2,1,0:T(8,128)S(1)}, f32[4,8,2176]{2,1,0:T(8,128)S(1)}, u32[]{:S(2)}, u32[]{:S(2)}) %collective-permute-start.14) | collective-permute-done | bytes 278560 | tf_op jit(solution)/shard_map/ppermute | solution.py:519
  77.5 0.0 collective-permute-done.15.down
  77.5 6.4 %phase1.1 = (f32[8,24,8,2176]{3,2,1,0:T(8,128)S(1)}, f32[4,8,2176]{2,1,0:T(8,128)S(1)}, f32[4,8,2176]{2,1,0:T(8,128)S(1)}, f32[4,8,128]{2,1,0:T(8,128)S(1)}) custom-call(f32[4]{0:T(128)S(1)} %add_convert_fusion.flags, f32[8,128]{1,0:T(8,128)S(1)} %broadcast_select_fusion.mask, ...), custom_call_target="tpu_custom_call", output_to_operand_aliasing={{0}: (2, {})} | custom-call | tf_op jit(solution)/shard_map/phase1/pallas_call | solution.py:286
  83.9 0.1 collective-permute-start.16
  84.0 5.3 %collective-permute-start.17 = (f32[4,8,2176]{2,1,0:T(8,128)S(1)}, f32[4,8,2176]{2,1,0:T(8,128)S(1)}, u32[]{:S(2)}, u32[]{:S(2)}) collective-permute-start(f32[4,8,2176]{2,1,0:T(8,128)S(1)} %get-tuple-element.165), channel_id=1, source_target_pairs={{0,120},{8,0},{16,8},{24,16},{32,24},{40,32},{48,40},{56,48},{64,5... | collective-permute-start | bytes 835592 | tf_op jit(solution)/shard_map/ppermute | solution.py:519
  89.4 4.6 %collective-permute-done.16.up = f32[4,8,2176]{2,1,0:T(8,128)S(1)} collective-permute-done((f32[4,8,2176]{2,1,0:T(8,128)S(1)}, f32[4,8,2176]{2,1,0:T(8,128)S(1)}, u32[]{:S(2)}, u32[]{:S(2)}) %collective-permute-start.16) | collective-permute-done | bytes 278560 | tf_op jit(solution)/shard_map/ppermute | solution.py:519
  94.0 0.0 collective-permute-done.17.down
  94.0 6.4 %phase2.1 = (f32[8,24,8,2176]{3,2,1,0:T(8,128)S(1)}, f32[4,8,2176]{2,1,0:T(8,128)S(1)}, f32[4,8,2176]{2,1,0:T(8,128)S(1)}, f32[4,8,128]{2,1,0:T(8,128)S(1)}) custom-call(f32[4]{0:T(128)S(1)} %add_convert_fusion.flags, f32[8,128]{1,0:T(8,128)S(1)} %broadcast_select_fusion.mask, ...), custom_call_target="tpu_custom_call", output_to_operand_aliasing={{0}: (2, {})} | custom-call | tf_op jit(solution)/shard_map/phase2/pallas_call | solution.py:286
  100.4 4.8 %copy-done.2 = f32[8,24,8,2176]{3,2,1,0:T(8,128)} copy-done((f32[8,24,8,2176]{3,2,1,0:T(8,128)}, f32[8,24,8,2176]{3,2,1,0:T(8,128)S(1)}, u32[]{:S(2)}) %copy-start.2) | copy-done | bytes 13369368
  105.2 0.0 collective-permute-start.18
  105.2 5.3 %collective-permute-start.19 = (f32[4,8,2176]{2,1,0:T(8,128)S(1)}, f32[4,8,2176]{2,1,0:T(8,128)S(1)}, u32[]{:S(2)}, u32[]{:S(2)}) collective-permute-start(f32[4,8,2176]{2,1,0:T(8,128)S(1)} %get-tuple-element.168), channel_id=1, source_target_pairs={{0,120},{8,0},{16,8},{24,16},{32,24},{40,32},{48,40},{56,48},{64,5... | collective-permute-start | bytes 835592 | tf_op jit(solution)/shard_map/ppermute | solution.py:519
  110.6 0.0 copy-done.17
  110.6 0.6 convert_bitcast_fusion
  111.2 3.9 %collective-permute-done.18.up = f32[4,8,2176]{2,1,0:T(8,128)S(1)} collective-permute-done((f32[4,8,2176]{2,1,0:T(8,128)S(1)}, f32[4,8,2176]{2,1,0:T(8,128)S(1)}, u32[]{:S(2)}, u32[]{:S(2)}) %collective-permute-start.18) | collective-permute-done | bytes 278560 | tf_op jit(solution)/shard_map/ppermute | solution.py:519
  115.1 0.0 collective-permute-done.19.down
  115.1 4.8 %copy-done.3 = f32[8,24,8,2176]{3,2,1,0:T(8,128)S(1)} copy-done((f32[8,24,8,2176]{3,2,1,0:T(8,128)S(1)}, f32[8,24,8,2176]{3,2,1,0:T(8,128)}, u32[]{:S(2)}) %copy-start.3) | copy-done | bytes 13369368
  119.9 5.8 %phase3.1 = (f32[8,24,8,2176]{3,2,1,0:T(8,128)S(1)}, f32[128,1,128]{2,1,0:T(1,128)}) custom-call(f32[4]{0:T(128)S(1)} %add_convert_fusion.flags, f32[8,128]{1,0:T(8,128)S(1)} %broadcast_select_fusion.mask, f32[8,24,8,2176]{3,2,1,0:T(8,128)S(1)} %copy-done.3, f32[24,8,2176]{2,1,0:T(8,128)S(1)} %get-tuple-element.158.k_in, ...), custom_call_target="tpu_custom_call", output_to_operand_aliasing={{0}: (2, {})} | custom-call | tf_op jit(solution)/shard_map/phase3/pallas_call | solution.py:286
  125.7 4.8 %copy-done.4 = f32[8,24,8,2176]{3,2,1,0:T(8,128)} copy-done((f32[8,24,8,2176]{3,2,1,0:T(8,128)}, f32[8,24,8,2176]{3,2,1,0:T(8,128)S(1)}, u32[]{:S(2)}) %copy-start.4) | copy-done | bytes 13369368
  130.5 12.3 %all-to-all-start.1 = ((f32[128,1,128]{2,1,0:T(1,128)}), f32[128,1,128]{2,1,0:T(1,128)S(1)}, u32[]{:S(2)}, u32[]{:S(2)}) async-start(f32[128,1,128]{2,1,0:T(1,128)} %get-tuple-element.172), calls=%async_computation.1 | async-start | bytes 131072 | tf_op jit(solution)/shard_map/all_to_all | solution.py:570
  142.8 0.7 fusion.23
  143.5 8.8 %all-to-all-done.1 = f32[128,1,128]{2,1,0:T(1,128)S(1)} async-done(((f32[128,1,128]{2,1,0:T(1,128)}), f32[128,1,128]{2,1,0:T(1,128)S(1)}, u32[]{:S(2)}, u32[]{:S(2)}) %all-to-all-start.1) | async-done | bytes 65568 | tf_op jit(solution)/shard_map/all_to_all | solution.py:570
  152.3 0.2 reduce_sum.40
  152.4 4.8 %copy-done.5 = f32[8,24,8,2176]{3,2,1,0:T(8,128)S(1)} copy-done((f32[8,24,8,2176]{3,2,1,0:T(8,128)S(1)}, f32[8,24,8,2176]{3,2,1,0:T(8,128)}, u32[]{:S(2)}) %copy-start.5) | copy-done | bytes 13369368
  157.2 3.5 %copy-done.7 = bf16[2176,2048]{1,0:T(8,128)(2,1)S(1)} copy-done((bf16[2176,2048]{1,0:T(8,128)(2,1)S(1)}, bf16[2176,2048]{1,0:T(8,128)(2,1)}, u32[]{:S(2)}) %copy-start.7) | copy-done | bytes 8912920
  160.7 8.6 %finish.1 = (f32[8,16,2048]{2,1,0:T(8,128)}, f32[128,128]{1,0:T(8,128)}, f32[8,128]{1,0:T(8,128)S(1)}) custom-call(f32[1,128]{1,0:T(1,128)S(1)} %bitcast.100, f32[8,24,8,2176]{3,2,1,0:T(8,128)S(1)} %copy-done.5, bf16[2176,2048]{1,0:T(8,128)(2,1)S(1)} %copy-done.7, s32[1,2048]{1,0:T(1,128)S(1)} %get-tuple-element.283.cells, ...), custom_call_target="tpu_custom_call" | custom-call | tf_op jit(solution)/shard_map/finish/pallas_call | solution.py:433
  169.4 0.6 compare_reduce_fusion
  170.7 0.0 copy-start.19
  170.7 0.0 copy-start.13
  170.7 0.0 copy-start.14
  170.7 0.2 while.28
  170.9 3.5 %all-to-all-start.2 = ((f32[16,8,128]{2,1,0:T(8,128)}), f32[16,8,128]{2,1,0:T(8,128)S(1)}, u32[]{:S(2)}, u32[]{:S(2)}) async-start(f32[16,8,128]{2,1,0:T(8,128)} %bitcast.111), calls=%async_computation.2 | async-start | bytes 131072 | tf_op jit(solution)/shard_map/all_to_all | solution.py:581
  174.4 7.6 %all-to-all-done.2 = f32[16,8,128]{2,1,0:T(8,128)S(1)} async-done(((f32[16,8,128]{2,1,0:T(8,128)}), f32[16,8,128]{2,1,0:T(8,128)S(1)}, u32[]{:S(2)}, u32[]{:S(2)}) %all-to-all-start.2) | async-done | bytes 65568 | tf_op jit(solution)/shard_map/all_to_all | solution.py:581
  182.0 1.6 fusion.22
  (21 shorter events, 0.1 us)
Async XLA Ops:
  2.5 5.7 %collective-permute-start.10 = (f32[16,8,128]{2,1,0:T(8,128)}, f32[16,8,128]{2,1,0:T(8,128)S(1)}, u32[]{:S(2)}, u32[]{:S(2)}) collective-permute-start(f32[16,8,128]{2,1,0:T(8,128)} %get-tuple-element.147), channel_id=1, source_target_pairs={{0,1},{1,2},{2,3},{3,4},{4,5},{5,6},{6,7},{7,0},{8,9},{9,10},{10,1... | collective-permute-start | bytes 196616 | tf_op jit(solution)/shard_map/ppermute | solution.py:519
  2.5 5.8 %collective-permute-start.11 = (f32[16,8,128]{2,1,0:T(8,128)}, f32[16,8,128]{2,1,0:T(8,128)S(1)}, u32[]{:S(2)}, u32[]{:S(2)}) collective-permute-start(f32[16,8,128]{2,1,0:T(8,128)} %get-tuple-element.148), channel_id=1, source_target_pairs={{0,7},{1,0},{2,1},{3,2},{4,3},{5,4},{6,5},{7,6},{8,15},{9,8},{10,9... | collective-permute-start | bytes 196616 | tf_op jit(solution)/shard_map/ppermute | solution.py:519
  6.2 18.6 %copy-start.16 = (s32[1,1,16,128]{3,2,1,0:T(8,128)S(1)}, s32[1,1,16,128]{3,2,1,0:T(8,128)}, u32[]{:S(2)}) copy-start(s32[1,1,16,128]{3,2,1,0:T(8,128)} %param.22) | copy-start | bytes 24580
  6.2 19.8 %copy-start.15 = (f32[1,1,16,2,128]{4,3,2,1,0:T(2,128)S(1)}, f32[1,1,16,2,128]{4,3,2,1,0:T(2,128)}, u32[]{:S(2)}) copy-start(f32[1,1,16,2,128]{4,3,2,1,0:T(2,128)} %param.23) | copy-start | bytes 49156
  13.5 4.8 %copy-start = (f32[8,24,8,2176]{3,2,1,0:T(8,128)}, f32[8,24,8,2176]{3,2,1,0:T(8,128)S(1)}, u32[]{:S(2)}) copy-start(f32[8,24,8,2176]{3,2,1,0:T(8,128)S(1)} %get-tuple-element.152.basis_in) | copy-start | bytes 40108036
  18.4 1.2 copy-start.8
  19.5 34.9 %collective-permute-start.13 = (f32[12,8,2176]{2,1,0:T(8,128)}, f32[12,8,2176]{2,1,0:T(8,128)}, u32[]{:S(2)}, u32[]{:S(2)}) collective-permute-start(f32[12,8,2176]{2,1,0:T(8,128)} %get-tuple-element.149), channel_id=1, source_target_pairs={{0,120},{8,0},{16,8},{24,16},{32,24},{40,32},{48,40},{56,48},{64,5... | collective-permute-start | bytes 2506760 | tf_op jit(solution)/shard_map/ppermute | solution.py:519
  24.7 29.6 %collective-permute-start.12 = (f32[12,8,2176]{2,1,0:T(8,128)}, f32[12,8,2176]{2,1,0:T(8,128)}, u32[]{:S(2)}, u32[]{:S(2)}) collective-permute-start(f32[12,8,2176]{2,1,0:T(8,128)} %get-tuple-element.156), channel_id=1, source_target_pairs={{0,8},{8,16},{16,24},{24,32},{32,40},{40,48},{48,56},{56,64},{64,7... | collective-permute-start | bytes 2506760 | tf_op jit(solution)/shard_map/ppermute | solution.py:519
  26.7 22.6 %all-to-all-start = ((f32[16,3,128]{2,1,0:T(4,128)}), f32[16,3,128]{2,1,0:T(4,128)S(1)}, u32[]{:S(2)}, u32[]{:S(2)}) async-start(f32[16,3,128]{2,1,0:T(4,128)} %pad_maximum_fusion.23), calls=%async_computation | async-start | bytes 65536 | tf_op jit(solution)/shard_map/all_to_all | solution.py:558
  49.3 5.1 %copy-start.9 = (f32[24,8,2176]{2,1,0:T(8,128)S(1)}, f32[24,8,2176]{2,1,0:T(8,128)}, u32[]{:S(2)}) copy-start(f32[24,8,2176]{2,1,0:T(8,128)} %copy-done.8) | copy-start | bytes 5013508
  50.9 3.4 %copy-start.6 = (bf16[2176,2048]{1,0:T(8,128)(2,1)}, bf16[2176,2048]{1,0:T(8,128)(2,1)S(1)}, u32[]{:S(2)}) copy-start(bf16[2176,2048]{1,0:T(8,128)(2,1)S(1)} %columns_hot.1.hot) | copy-start | bytes 26738692
  54.4 4.8 %copy-start.1 = (f32[8,24,8,2176]{3,2,1,0:T(8,128)S(1)}, f32[8,24,8,2176]{3,2,1,0:T(8,128)}, u32[]{:S(2)}) copy-start(f32[8,24,8,2176]{3,2,1,0:T(8,128)} %copy-done) | copy-start | bytes 40108036
  66.6 11.0 %collective-permute-start.14 = (f32[4,8,2176]{2,1,0:T(8,128)S(1)}, f32[4,8,2176]{2,1,0:T(8,128)S(1)}, u32[]{:S(2)}, u32[]{:S(2)}) collective-permute-start(f32[4,8,2176]{2,1,0:T(8,128)S(1)} %get-tuple-element.161), channel_id=1, source_target_pairs={{0,8},{8,16},{16,24},{24,32},{32,40},{40,48},{48,56},{56,64},{64,7... | collective-permute-start | bytes 835592 | tf_op jit(solution)/shard_map/ppermute | solution.py:519
  67.5 10.1 %collective-permute-start.15 = (f32[4,8,2176]{2,1,0:T(8,128)S(1)}, f32[4,8,2176]{2,1,0:T(8,128)S(1)}, u32[]{:S(2)}, u32[]{:S(2)}) collective-permute-start(f32[4,8,2176]{2,1,0:T(8,128)S(1)} %get-tuple-element.162), channel_id=1, source_target_pairs={{0,120},{8,0},{16,8},{24,16},{32,24},{40,32},{48,40},{56,48},{64,5... | collective-permute-start | bytes 835592 | tf_op jit(solution)/shard_map/ppermute | solution.py:519
  83.9 10.0 %collective-permute-start.16 = (f32[4,8,2176]{2,1,0:T(8,128)S(1)}, f32[4,8,2176]{2,1,0:T(8,128)S(1)}, u32[]{:S(2)}, u32[]{:S(2)}) collective-permute-start(f32[4,8,2176]{2,1,0:T(8,128)S(1)} %get-tuple-element.164), channel_id=1, source_target_pairs={{0,8},{8,16},{16,24},{24,32},{32,40},{40,48},{48,56},{56,64},{64,7... | collective-permute-start | bytes 835592 | tf_op jit(solution)/shard_map/ppermute | solution.py:519
  84.0 10.0 %collective-permute-start.17 = (f32[4,8,2176]{2,1,0:T(8,128)S(1)}, f32[4,8,2176]{2,1,0:T(8,128)S(1)}, u32[]{:S(2)}, u32[]{:S(2)}) collective-permute-start(f32[4,8,2176]{2,1,0:T(8,128)S(1)} %get-tuple-element.165), channel_id=1, source_target_pairs={{0,120},{8,0},{16,8},{24,16},{32,24},{40,32},{48,40},{56,48},{64,5... | collective-permute-start | bytes 835592 | tf_op jit(solution)/shard_map/ppermute | solution.py:519
  94.0 16.6 %copy-start.17 = (s32[1,1,16,128]{3,2,1,0:T(8,128)S(1)}, s32[1,1,16,128]{3,2,1,0:T(8,128)}, u32[]{:S(2)}) copy-start(s32[1,1,16,128]{3,2,1,0:T(8,128)} %param.25) | copy-start | bytes 24580
  100.4 4.8 %copy-start.2 = (f32[8,24,8,2176]{3,2,1,0:T(8,128)}, f32[8,24,8,2176]{3,2,1,0:T(8,128)S(1)}, u32[]{:S(2)}) copy-start(f32[8,24,8,2176]{3,2,1,0:T(8,128)S(1)} %get-tuple-element.166.basis_in) | copy-start | bytes 40108036
  105.2 9.9 %collective-permute-start.18 = (f32[4,8,2176]{2,1,0:T(8,128)S(1)}, f32[4,8,2176]{2,1,0:T(8,128)S(1)}, u32[]{:S(2)}, u32[]{:S(2)}) collective-permute-start(f32[4,8,2176]{2,1,0:T(8,128)S(1)} %get-tuple-element.167), channel_id=1, source_target_pairs={{0,8},{8,16},{16,24},{24,32},{32,40},{40,48},{48,56},{56,64},{64,7... | collective-permute-start | bytes 835592 | tf_op jit(solution)/shard_map/ppermute | solution.py:519
  105.2 9.9 %collective-permute-start.19 = (f32[4,8,2176]{2,1,0:T(8,128)S(1)}, f32[4,8,2176]{2,1,0:T(8,128)S(1)}, u32[]{:S(2)}, u32[]{:S(2)}) collective-permute-start(f32[4,8,2176]{2,1,0:T(8,128)S(1)} %get-tuple-element.168), channel_id=1, source_target_pairs={{0,120},{8,0},{16,8},{24,16},{32,24},{40,32},{48,40},{56,48},{64,5... | collective-permute-start | bytes 835592 | tf_op jit(solution)/shard_map/ppermute | solution.py:519
  115.1 4.8 %copy-start.3 = (f32[8,24,8,2176]{3,2,1,0:T(8,128)S(1)}, f32[8,24,8,2176]{3,2,1,0:T(8,128)}, u32[]{:S(2)}) copy-start(f32[8,24,8,2176]{3,2,1,0:T(8,128)} %copy-done.2) | copy-start | bytes 40108036
  119.9 22.9 %copy-start.18 = (s32[1,1,16]{2,1,0:T(1,128)S(1)}, s32[1,1,16]{2,1,0:T(1,128)}, u32[]{:S(2)}) copy-start(s32[1,1,16]{2,1,0:T(1,128)} %param.24) | copy-start | bytes 196
  125.7 4.8 %copy-start.4 = (f32[8,24,8,2176]{3,2,1,0:T(8,128)}, f32[8,24,8,2176]{3,2,1,0:T(8,128)S(1)}, u32[]{:S(2)}) copy-start(f32[8,24,8,2176]{3,2,1,0:T(8,128)S(1)} %get-tuple-element.173.basis) | copy-start | bytes 40108036
  130.5 21.7 %all-to-all-start.1 = ((f32[128,1,128]{2,1,0:T(1,128)}), f32[128,1,128]{2,1,0:T(1,128)S(1)}, u32[]{:S(2)}, u32[]{:S(2)}) async-start(f32[128,1,128]{2,1,0:T(1,128)} %get-tuple-element.172), calls=%async_computation.1 | async-start | bytes 131072 | tf_op jit(solution)/shard_map/all_to_all | solution.py:570
  152.4 4.8 %copy-start.5 = (f32[8,24,8,2176]{3,2,1,0:T(8,128)S(1)}, f32[8,24,8,2176]{3,2,1,0:T(8,128)}, u32[]{:S(2)}) copy-start(f32[8,24,8,2176]{3,2,1,0:T(8,128)} %copy-done.4) | copy-start | bytes 40108036
  157.2 3.5 %copy-start.7 = (bf16[2176,2048]{1,0:T(8,128)(2,1)S(1)}, bf16[2176,2048]{1,0:T(8,128)(2,1)}, u32[]{:S(2)}) copy-start(bf16[2176,2048]{1,0:T(8,128)(2,1)} %copy-done.6) | copy-start | bytes 26738692
  160.7 9.9 %copy-start.11 = (f32[8,16,2048]{2,1,0:T(8,128)S(1)}, f32[8,16,2048]{2,1,0:T(8,128)}, u32[]{:S(2)}) copy-start(f32[8,16,2048]{2,1,0:T(8,128)} %refs_0_.3) | copy-start | bytes 3145732
  170.7 3.8 %copy-start.19 = (f32[8]{0:T(128)S(1)}, f32[8]{0:T(128)}, u32[]{:S(2)}) copy-start(f32[8]{0:T(128)} %param.21) | copy-start | bytes 100
  170.7 11.3 %copy-start.13 = (f32[16,128]{1,0:T(8,128)S(1)}, f32[16,128]{1,0:T(8,128)}, u32[]{:S(2)}) copy-start(f32[16,128]{1,0:T(8,128)} %convert_bitcast_fusion) | copy-start | bytes 24580
  170.7 11.3 %copy-start.14 = (f32[16,128]{1,0:T(8,128)S(1)}, f32[16,128]{1,0:T(8,128)}, u32[]{:S(2)}) copy-start(f32[16,128]{1,0:T(8,128)} %fusion.23) | copy-start | bytes 24580
  170.9 11.1 %all-to-all-start.2 = ((f32[16,8,128]{2,1,0:T(8,128)}), f32[16,8,128]{2,1,0:T(8,128)S(1)}, u32[]{:S(2)}, u32[]{:S(2)}) async-start(f32[16,8,128]{2,1,0:T(8,128)} %bitcast.111), calls=%async_computation.2 | async-start | bytes 131072 | tf_op jit(solution)/shard_map/all_to_all | solution.py:581

commit v3 on v2

--- a/solution.py
+++ b/solution.py
@@ -10,6 +10,7 @@
 ITERS = 8
 F = 8
 PAD = 4
+SKIP = PAD - 1
 SIDE = 16
 LANES = 128
 LOW, HIGH = 0.2, 15.0
@@ -56,57 +57,73 @@
 DEPTHS = (4, 3, 3, 2)
 
 
-def prepare_kernel(rows, cols, flags, *refs):
-    fields, (left, right), outs, (to_up, to_down) = refs[0:4], refs[4:6], refs[6:10], refs[10:]
-    lane = lax.broadcasted_iota(jnp.int32, (rows, F, LANES), 2)
-
-    def shaped(a, x):
-        if a == 1:
-            return x + 4.0
-        if a == 2:
-            return x * (1.0 / HALF)
-        if a == 3:
-            return (x - MID) * (1.0 / HALF)
-        return x
-
-    def store(a, at, block):
-        if a == 0:
-            outs[0][0, PAD : PAD + rows, :, at] = block
-        else:
-            outs[a][PAD : PAD + rows, :, at] = block
-        base, depth = sum(DEPTHS[:a]), DEPTHS[a]
-        to_up[base : base + depth, :, at] = block[:depth]
-        to_down[base : base + depth, :, at] = block[rows - depth :]
-
-    for a in range(4):
-
-        def step(c, carry, a=a):
-            at = pl.ds(pl.multiple_of(c * LANES, LANES), LANES)
-            store(a, at, shaped(a, jnp.swapaxes(fields[a][:, :, at], 0, 1)))
-            return carry
-
-        lax.fori_loop(0, cols // LANES, step, 0)
-        shift = (-SIDE * a) % LANES
-        after = shaped(a, pltpu.roll(right[...], shift, 2) if shift else right[...])
-        before = shaped(a, pltpu.roll(left[...], (LANES - SIDE * (a + 1)) % LANES, 2))
-        extra = jnp.where(lane < SIDE, after * flags[1], 0.0) + jnp.where(lane >= LANES - SIDE, before * flags[0], 0.0)
-        store(a, pl.ds(cols, LANES), extra)
-
-
-def prepare(flags, fields, left, right):
+def shaped(a, x):
+    if a == 1:
+        return x + 4.0
+    if a == 2:
+        return x * (1.0 / HALF)
+    if a == 3:
+        return (x - MID) * (1.0 / HALF)
+    return x
+
+
+def place(a, at, block, outs, to_up, to_down):
+    rows = block.shape[0]
+    outs[a][PAD : PAD + rows, :, at] = block
+    base, depth = sum(DEPTHS[:a]), DEPTHS[a]
+    to_up[base : base + depth, :, at] = block[:depth]
+    to_down[base : base + depth, :, at] = block[rows - depth :]
+
+
+def prepare_kernel(cols, *refs):
+    fields, outs, (to_up, to_down) = refs[0:4], refs[4:8], refs[8:]
+
+    def step(c, carry):
+        at = pl.ds(pl.multiple_of(c * LANES, LANES), LANES)
+        for a in range(4):
+            place(a, at, shaped(a, jnp.swapaxes(fields[a][:, :, at], 0, 1)), outs, to_up, to_down)
+        return carry
+
+    lax.fori_loop(0, cols // LANES, step, 0)
+
+
+def prepare(fields):
     rows, cols = fields[0].shape[1:]
     wide = cols + LANES
     f32 = jnp.float32
-    ext = (rows + 2 * PAD, F, wide)
-    packed = jax.ShapeDtypeStruct((sum(DEPTHS), F, wide), f32)
+    ext = pltpu.VMEM((rows + 2 * PAD, F, wide), f32)
+    packed = pltpu.VMEM((sum(DEPTHS), F, wide), f32)
     return pl.pallas_call(
-        functools.partial(prepare_kernel, rows, cols),
-        in_specs=[SMEM] + [VMEM] * 6,
+        functools.partial(prepare_kernel, cols),
+        in_specs=[VMEM] * 4,
         out_specs=[VMEM] * 6,
-        out_shape=[pltpu.VMEM((ITERS,) + ext, f32)] + [pltpu.VMEM(ext, f32)] * 3 + [packed, packed],
+        out_shape=[ext] * 4 + [packed] * 2,
         compiler_params=PARAMS,
         name="prepare",
-    )(flags, *fields, left, right)
+    )(*fields)
+
+
+def sides_kernel(rows, cols, flags, left, right, *refs):
+    outs, (to_up, to_down) = refs[6:10], refs[10:]
+    lane = lax.broadcasted_iota(jnp.int32, (rows, F, LANES), 2)
+    for a in range(4):
+        shift = (-SIDE * a) % LANES
+        after = shaped(a, pltpu.roll(right[...], shift, 2) if shift else right[...])
+        before = shaped(a, pltpu.roll(left[...], LANES - SIDE * (a + 1), 2))
+        extra = jnp.where(lane < SIDE, after * flags[1], 0.0) + jnp.where(lane >= LANES - SIDE, before * flags[0], 0.0)
+        place(a, pl.ds(cols, LANES), extra, outs, to_up, to_down)
+
+
+def sides(rows, cols, flags, left, right, prepared):
+    return pl.pallas_call(
+        functools.partial(sides_kernel, rows, cols),
+        in_specs=[SMEM] + [VMEM] * 8,
+        out_specs=[VMEM] * 6,
+        out_shape=[pltpu.VMEM(x.shape, x.dtype) for x in prepared],
+        input_output_aliases={3 + i: i for i in range(6)},
+        compiler_params=PARAMS,
+        name="sides",
+    )(flags, left, right, *[held(x) for x in prepared])
 
 
 def walk(ref, r, count, wide):
@@ -138,24 +155,27 @@
 
 
 def pairs(low, high, body, carry):
-    return lax.fori_loop(0, (high - low) // 2, lambda i, carry: body(low + 2 * i, carry), carry)
-
-
-def phase_kernel(p, rows, cols, flags, mask, basis_in, k_in, t_in, c_in, up, down, *refs):
+    return lax.fori_loop(0, (high - low) // 2, lambda i, carry: body(low + 2 * i, carry), carry, unroll=True)
+
+
+def phase_kernel(p, rows, cols, *refs):
     first, last = p == 0, p == ITERS // 2 - 1
+    refs = list(refs)
+    take = lambda n: [refs.pop(0) for _ in range(n)]
+    flags, mask, current, kap, tau, cur, up, down = take(8)
+    if not first:
+        older, old = take(2)
     if last:
-        earlier, refs = refs[: ITERS // 2 - 1], refs[ITERS // 2 - 1 :]
-    basis, refs = refs[0], refs[1:]
+        earlier = take(ITERS // 2 - 1)
+    (current,) = take(1)
     if first:
-        kap, tau, cur, refs = refs[0], refs[1], refs[2], refs[3:]
-    else:
-        kap, tau, cur = k_in, t_in, c_in
+        kap, tau, cur = take(3)
+    (middle,) = take(1)
     if last:
         line, scaled, one = refs
     else:
-        to_up, to_down, sums, scaled, one = refs
+        newest, to_up, to_down, sums, scaled, one = refs
     wide = cols + LANES
-    now = 2 * p
     own_low, own_high = PAD, PAD + rows
 
     for source, flag, begin in ((up, 2, None), (down, 3, own_high)):
@@ -164,14 +184,10 @@
             at = PAD - depth if begin is None else begin
             for i in range(depth):
                 row = source[base + i] * flags[flag]
-                if a == 0:
-                    basis[now, at + i] = row
-                else:
-                    (None, kap, tau, cur)[a][at + i] = row
+                (current, kap, tau, cur)[a][at + i] = row
             base += depth
 
     zero = jnp.zeros((F, LANES), jnp.float32)
-    current = basis.at[now]
 
     def scale(ref, low, high):
         def body(r, carry):
@@ -197,32 +213,31 @@
                 value = new[i] * flag
                 one[r + i, :, at] = value
                 if i == inner:
-                    basis[now + 1, r + i, :, at] = value if first else 2.0 * value - basis[now - 1, r + i, :, at]
+                    middle[r + i - SKIP, :, at] = value if first else 2.0 * value - old[r + i - SKIP, :, at]
 
     def first_rows(r, carry):
         cross = square = start = zero
         for at, new in image(current, r):
             for i in range(2):
                 one[r + i, :, at] = new[i]
-                value = new[i] if first else 2.0 * new[i] - basis[now - 1, r + i, :, at]
-                basis[now + 1, r + i, :, at] = value
+                value = new[i] if first else 2.0 * new[i] - old[r + i - SKIP, :, at]
+                middle[r + i - SKIP, :, at] = value
                 if at.start < cols:
-                    old = current[r + i, :, at]
-                    cross += value * old
+                    source = current[r + i, :, at]
+                    cross += value * source
                     square += value * value
                     if first:
-                        start += old * old
+                        start += source * source
         out = (carry[0] + cross, carry[1] + square)
         return out + ((carry[2] + start,) if first else ())
 
     found = pairs(own_low, own_high, first_rows, (zero,) * (3 if first else 2))
 
     if last:
-        after = basis.at[now + 1]
 
         def final_rows(r, carry):
             total = zero
-            for at, v, near in walk(after, r, 2, wide):
+            for at, v, near in walk(middle, r - SKIP, 2, wide):
                 if at.start < cols:
                     for i in range(2):
                         k = kap[r + i, :, at] * v[i] - near[i]
@@ -256,16 +271,16 @@
             for i in range(2):
                 value = 2.0 * new[i] - current[r + i, :, at]
                 if not first:
-                    value = 2.0 * value - basis[now - 2, r + i, :, at]
-                basis[now + 2, r + i, :, at] = value
+                    value = 2.0 * value - older[r + i, :, at]
+                newest[r + i, :, at] = value
                 if at.start < cols:
-                    cross += value * basis[now + 1, r + i, :, at]
+                    cross += value * middle[r + i - SKIP, :, at]
                     square += value * value
         return carry[0] + cross, carry[1] + square
 
     sums[2], sums[3] = pairs(own_low, own_high, second_rows, (zero, zero))
-    to_up[...] = basis[now + 2, own_low : own_low + PAD]
-    to_down[...] = basis[now + 2, own_high - PAD : own_high]
+    to_up[...] = newest[own_low : own_low + PAD]
+    to_down[...] = newest[own_high - PAD : own_high]
 
 
 def phase(p, rows, cols, flags, mask, basis, coefs, up, down, earlier=(), devices=1):
@@ -273,32 +288,36 @@
     f32 = jnp.float32
     wide = cols + LANES
     ext = (rows + 2 * PAD, F, wide)
-    out_shape = [pltpu.VMEM(basis.shape, f32)]
+    out_shape = [pltpu.VMEM(ext, f32)]
     aliases = {2: 0}
     if first:
         out_shape += [pltpu.VMEM(ext, f32)] * 3
         aliases.update({3: 1, 4: 2, 5: 3})
+    out_shape += [pltpu.VMEM((rows + 2, F, wide), f32)]
     if last:
         out_shape += [jax.ShapeDtypeStruct((devices, 1, LANES), f32)]
     else:
-        out_shape += [jax.ShapeDtypeStruct((PAD, F, wide), f32)] * 2
+        out_shape += [pltpu.VMEM(ext, f32)]
+        out_shape += [pltpu.VMEM((PAD, F, wide), f32)] * 2
         out_shape += [jax.ShapeDtypeStruct((5 if first else 4, F, LANES), f32)]
+    older = [] if first else [held(basis[-3]), held(basis[-2])]
     outs = pl.pallas_call(
         functools.partial(phase_kernel, p, rows, cols),
-        in_specs=[SMEM] + [VMEM] * (7 + len(earlier)),
+        in_specs=[SMEM] + [VMEM] * (7 + len(older) + len(earlier)),
         out_specs=[VMEM] * len(out_shape),
         out_shape=out_shape,
         scratch_shapes=[pltpu.VMEM(ext, f32), pltpu.VMEM(ext, f32)],
         input_output_aliases=aliases,
         compiler_params=PARAMS,
         name=f"phase{p}",
-    )(flags, mask, held(basis), *[held(c) for c in coefs], up, down, *earlier)
-    basis, outs = outs[0], outs[1:]
+    )(flags, mask, held(basis[-1]), *[held(c) for c in coefs], held(up), held(down), *older, *earlier)
+    current, outs = outs[0], list(outs[1:])
     if first:
         coefs, outs = outs[:3], outs[3:]
+    basis = basis[:-1] + [current, outs[0]]
     if last:
-        return basis, outs[0]
-    return basis, coefs, outs[0], outs[1], outs[2]
+        return basis, outs[1]
+    return basis + [outs[1]], coefs, outs[2], outs[3], outs[4]
 
 
 def coefficients(line):
@@ -351,31 +370,42 @@
     return lat_in, fine
 
 
-def columns_hot_kernel(cells, hot):
-    col = lax.rem(cells[...], hot.shape[0] - LANES)
+CHUNK = 4 * LANES
+
+
+def columns_hot_kernel(cols, cells, hot):
+    col = lax.rem(cells[...], cols)
 
     def step(b, carry):
         at = pl.ds(pl.multiple_of(b * LANES, LANES), LANES)
-        row = lax.broadcasted_iota(jnp.int32, (LANES, cells.shape[1]), 0) + b * LANES
-        hot[at] = jnp.where(row == col, 1.0, 0.0).astype(jnp.bfloat16)
+        row = lax.broadcasted_iota(jnp.int32, (LANES, CHUNK), 0) + b * LANES
+        hot[0, at] = jnp.where(row == col, 1.0, 0.0).astype(jnp.bfloat16)
         return carry
 
-    lax.fori_loop(0, hot.shape[0] // LANES, step, 0)
-
-
-def columns_hot(cells, wide):
+    lax.fori_loop(0, hot.shape[1] // LANES, step, 0)
+
+
+def columns_hot(cells, cols):
+    chunks, wide = cells.shape[1] // CHUNK, cols + LANES
     return pl.pallas_call(
-        columns_hot_kernel,
-        in_specs=[VMEM],
-        out_specs=VMEM,
-        out_shape=pltpu.VMEM((wide, cells.shape[1]), jnp.bfloat16),
+        functools.partial(columns_hot_kernel, cols),
+        grid=(chunks,),
+        in_specs=[pl.BlockSpec((1, CHUNK), lambda i: (0, i))],
+        out_specs=pl.BlockSpec((1, wide, CHUNK), lambda i: (i, 0, 0)),
+        out_shape=pltpu.HBM((chunks, wide, CHUNK), jnp.bfloat16),
         compiler_params=PARAMS,
         name="columns_hot",
     )(cells)
 
 
-def finish_kernel(rows, cols, line, basis, hot, cells, row_frac, col_frac, latent, predictor, fine, parts, keep):
+def finish_kernel(rows, cols, line, hot, cells, row_frac, col_frac, *refs):
+    basis, refs = refs[:ITERS], refs[ITERS:]
+    latent, predictor, fine, parts, keep, held_hot, arrived = refs
     wide = cols + LANES
+    chunks = hot.shape[0]
+    copies = [pltpu.make_async_copy(hot.at[i], held_hot.at[i], arrived.at[i]) for i in range(chunks)]
+    for copy in copies:
+        copy.start()
     lat_in, good = coefficients(line[...])
     fine[...] = jnp.where(good, 1.0, 0.0)
     for k in range(ITERS):
@@ -392,9 +422,11 @@
     def step(c, after):
         c = wide // LANES - 1 - c
         at = pl.ds(pl.multiple_of(c * LANES, LANES), LANES)
-        total = keep[0] * basis[0, PAD : PAD + rows + 1, :, at]
-        for k in range(1, ITERS):
-            total = total + keep[k] * basis[k, PAD : PAD + rows + 1, :, at]
+        total = None
+        for k in range(ITERS):
+            begin = PAD - SKIP * (k % 2)
+            term = keep[k] * basis[k][begin : begin + rows + 1, :, at]
+            total = term if total is None else total + term
         turned = pltpu.roll(total, LANES - 1, 2)
         split(total, at, 0)
         split(jnp.where(lane == LANES - 1, after, turned), at, 2 * tall)
@@ -406,33 +438,34 @@
         return turned
 
     lax.fori_loop(0, wide // LANES, step, jnp.zeros((rows + 1, F, LANES), jnp.float32))
-    chunk = 4 * LANES
-    for c in range(0, cells.shape[1], chunk):
-        at = slice(c, c + chunk)
-        both = jnp.dot(parts[...], hot[:, at], preferred_element_type=jnp.float32)
+    for c in range(chunks):
+        copies[c].wait()
+        at = slice(c * CHUNK, (c + 1) * CHUNK)
+        both = jnp.dot(parts[...], held_hot[c], preferred_element_type=jnp.float32)
         here = both[:tall] + both[tall : 2 * tall]
         beside = both[2 * tall : 3 * tall] + both[3 * tall :]
         row = cells[:, at] // cols
         frac = row_frac[:, at]
-        low = jnp.zeros((F, chunk), jnp.float32)
-        high = jnp.zeros((F, chunk), jnp.float32)
+        low = jnp.zeros((F, CHUNK), jnp.float32)
+        high = jnp.zeros((F, CHUNK), jnp.float32)
         for r in range(rows + 1):
             w = jnp.where(row == r, 1.0 - frac, jnp.where(row + 1 == r, frac, 0.0))
             low = low + w * here[r * F : (r + 1) * F]
             high = high + w * beside[r * F : (r + 1) * F]
         side = col_frac[:, at]
         out = (1.0 - side) * low + side * high
-        for i in range(chunk // LANES):
-            base = (c // LANES + i) * F
+        for i in range(CHUNK // LANES):
+            base = (c * CHUNK // LANES + i) * F
             predictor[base : base + F] = out[:, i * LANES : (i + 1) * LANES]
 
 
 def finish(rows, cols, line, basis, hot, cells, row_frac, col_frac):
     f32 = jnp.float32
     wide = cols + LANES
+    chunks = hot.shape[0]
     return pl.pallas_call(
         functools.partial(finish_kernel, rows, cols),
-        in_specs=[VMEM] * 6,
+        in_specs=[VMEM, pl.BlockSpec(memory_space=pl.ANY)] + [VMEM] * (3 + ITERS),
         out_specs=[VMEM] * 3,
         out_shape=[
             jax.ShapeDtypeStruct((F, rows, cols), f32),
@@ -442,10 +475,12 @@
         scratch_shapes=[
             pltpu.VMEM((4 * (rows + 1) * F, wide), jnp.bfloat16),
             pltpu.VMEM((ITERS, F, LANES), f32),
+            pltpu.VMEM((chunks, wide, CHUNK), jnp.bfloat16),
+            pltpu.SemaphoreType.DMA((chunks,)),
         ],
-        compiler_params=PARAMS,
+        compiler_params=pltpu.CompilerParams(vmem_limit_bytes=20 * 1024 * 1024),
         name="finish",
-    )(line, held(basis), held(hot), cells, row_frac, col_frac)
+    )(line, pltpu.with_memory_space_constraint(hot, pltpu.HBM), cells, row_frac, col_frac, *[held(b) for b in basis])
 
 
 def extended(x, sides, width):
@@ -541,24 +576,24 @@
     mask = jnp.where(lane < SIDE, flags[1], jnp.where(lane >= LANES - SIDE, flags[0], 0.0))
 
     fields = (right_side, kappa_field, tau_field, curvature)
+    cells = site_cells[0, 0]
+    sent = jnp.concatenate([cells.astype(jnp.float32)[:, None], site_offsets[0, 0]], axis=1)
     to_left, to_right = columns_of(fields)
+    sent, to_left, to_right = lax.optimization_barrier((sent, to_left, to_right))
     from_right = turned(to_left, "field", -1)
     from_left = turned(to_right, "field", 1)
-    basis, kap, tau, cur, to_up, to_down = prepare(flags, fields, from_left, from_right)
-    coefs = (kap, tau, cur)
-
-    cells = site_cells[0, 0]
-    sent = jnp.concatenate([cells.astype(jnp.float32)[:, None], site_offsets[0, 0]], axis=1)
+    got = lax.all_to_all(sent, "tile", split_axis=0, concat_axis=0, tiled=True)
+    got_cells = got[:, 0].astype(jnp.int32)
+    got_row, got_col = got[:, 1], got[:, 2]
+    hot = columns_hot(got_cells.reshape(1, -1), cols)
+    prepared = sides(rows, cols, flags, from_left, from_right, prepare(fields))
+    basis, coefs, to_up, to_down = [prepared[0]], prepared[1:4], prepared[4], prepared[5]
+
     sums = []
     for p in range(ITERS // 2):
         from_down = turned(to_up, "tile", -1)
         from_up = turned(to_down, "tile", 1)
         if p == 0:
-            sent, to_up = lax.optimization_barrier((sent, to_up))
-            got = lax.all_to_all(sent, "tile", split_axis=0, concat_axis=0, tiled=True)
-            got_cells = got[:, 0].astype(jnp.int32)
-            got_row, got_col = got[:, 1], got[:, 2]
-            hot = columns_hot(got_cells.reshape(1, -1), wide)
             flags, hot = lax.optimization_barrier((flags, hot))
         state = (p, rows, cols, flags, mask, basis, coefs, from_up, from_down)
         if p < ITERS // 2 - 1:

time: 184 us -> 1710 us (9.29)
  blocking collectives: 0 us -> 1140 us
  starting transfers between devices: 47.5 us -> 212 us
  other arithmetic: 5.72 us -> 85 us
  waiting for transfers between devices: 47.8 us -> 126 us
  local copies, waits for them, and re-layouts: 37.6 us -> 95.8 us
    psum x0 -> x17, blocking collectives: none -> 1140 us  [the longest x8 579 us: sweep(): lax.psum(jnp.sum(direction * image, axis=(1, 2)), ('tile', 'field'))]
    ppermute x0 -> x66, starting transfers between devices: none -> 165 us  [the longest x32 120 us: extended(): before = lax.ppermute(last, axis, up)]
    ppermute x0 -> x66, waiting for transfers between devices: none -> 83.4 us  [the longest x32 52.7 us: extended(): after = lax.ppermute(leading, axis, down)]
    gather x0 -> x4, local copies, waits for them, and re-layouts: none -> 50.3 us  [corner(): return jnp.take(flat, base + offset, axis=1)]
    reduce_sum x0 -> x17, other arithmetic: none -> 42.5 us  [the longest x8 28 us: sweep(): jnp.sum(direction * image, axis=(1, 2))]
    mul x0 -> x25, other arithmetic: none -> 17.6 us  [the longest x8 17.5 us: sweep(): scaled = tau_field * ((kappa_field + 4.0) * direction - neighbours(padded))]
    unnamed x36 -> x58, local copies, waits for them, and re-layouts: 37 us -> 20.9 us
  transfers between devices with their start and end apart: 13 -> 79, of which waited for: 8 -> 56; matrix products, arithmetic and copies ran while one was open for 2% -> 0% of each run, Pallas kernels for 1% -> 1%
where the time goes in v3:
time: 1710 us; the launch traced here: 1700 us
  blocking collectives  1140 us (67%)
  starting transfers between devices  212 us (12%)
  waiting for transfers between devices  126 us (7%)
  local copies, waits for them, and re-layouts  95.8 us (6%)
  other arithmetic  85 us (5%)
  Pallas kernels  41 us (2%)
    psum x8, blocking collectives, sweep(): lax.psum(jnp.sum(direction * image, axis=(1, 2)), ('tile', 'field'))  579 us
    psum x9, blocking collectives, squares(): lax.psum(jnp.sum(values * values, axis=(1, 2)), ('tile', 'field'))  563 us
    ppermute x32, starting transfers between devices, extended(): before = lax.ppermute(last, axis, up)  120 us
    ppermute x32, waiting for transfers between devices, extended(): after = lax.ppermute(leading, axis, down)  52.7 us
    gather x4, local copies, waits for them, and re-layouts, corner(): return jnp.take(flat, base + offset, axis=1)  50.3 us
    ppermute x32, starting transfers between devices, extended(): after = lax.ppermute(leading, axis, down)  42.4 us
  transfers between devices with their start and end apart: 79, of which 56 were waited for; matrix products, arithmetic and copies ran while one was open for 0% of the time, Pallas kernels for 1%

profile of v3, /device:TPU:0, one launch (start us, length us, event | category | flops | bytes accessed | tf_op | source)
XLA Modules:
  0.0 1704.1 jit_solution(9506195287466862838)
XLA Ops:
  8.1 4.4 prepare.1
  34.1 13.1 all-to-all-done
  47.2 4.6 columns_hot.1.hot
  51.8 5.4 phase0.1
  58.1 4.6 collective-permute-start.15
  62.7 4.5 collective-permute-done.14.refs_6_
  67.2 4.4 phase1.1
  71.7 5.6 collective-permute-start.17
  81.6 4.4 phase2.1
  86.1 5.7 collective-permute-start.19
  102.3 10.9 all-to-all-start.1
  113.9 8.8 all-to-all-done.1
  133.8 9.3 finish.1
  144.5 1543.7 %while.28 = (f32[8,16,2048]{2,1,0:T(8,128)}, f32[128,128]{1,0:T(8,128)}, pred[]{:T(512)}, f32[8,16,2048]{2,1,0:T(8,128)}, f32[8,16,2048]{2,1,0:T(8,128)}, /*inde...) while((f32[8,16,2048]{2,1,0:T(8,128)}, ...), condition=%region_11.13_spmd, body=%region_2.12_spmd | while | flops 12143899 | bytes 54547736 | solution.py:610
  146.5 62.8 %psum.22 = f32[8,1,1]{0,2,1:T(1,128)S(1)} all-reduce(f32[8,1,1]{0,2,1:T(1,128)S(1)} %bitcast.114), channel_id=1, replica_groups=mesh['tile'=16,'field'=8] {'tile','field'}, use_global_device_ids=true, to_apply=%region_4.4 | all-reduce | flops 8 | bytes 64 | tf_op jit(solution)/shard_map/while/body/psum | solution.py:511
  209.3 1401.5 %while.30 = (s32[]{:T(128)}, f32[8,16,2048]{2,1,0:T(8,128)}, f32[8,16,2048]{2,1,0:T(8,128)S(1)}, f32[8,16,2048]{2,1,0:T(8,128)S(1)}, f32[8,1,1]{0,2,1:T(1,128)S(...) while((s32[]{:T(128)}, f32[8,16,2048]{2,1,0:T(8,128)}, ...), condition=%wide.region_10.10_spmd.clone, body=%wide.region_5.9_spmd.clone.sunk | while | flops 11011219 | bytes 34617888 | solution.py:528
  210.9 4.5 collective-permute-start.1
  226.4 4.9 collective-permute-start.5
  234.0 4.3 collective-permute-start.6
  245.8 72.2 %psum.27 = f32[8,1,1]{0,2,1:T(1,128)S(1)} all-reduce(f32[8,1,1]{0,2,1:T(1,128)S(1)} %bitcast.105), channel_id=1, replica_groups=mesh['tile'=16,'field'=8] {'tile','field'}, use_global_device_ids=true, to_apply=%region_7.6 | all-reduce | flops 8 | bytes 64 | tf_op jit(solution)/shard_map/while/body/while/body/eval_jaxpr/psum | solution.py:519
  319.9 62.6 %psum.28 = f32[8,1,1]{0,2,1:T(1,128)S(1)} all-reduce(f32[8,1,1]{0,2,1:T(1,128)S(1)} %bitcast.106), channel_id=1, replica_groups=mesh['tile'=16,'field'=8] {'tile','field'}, use_global_device_ids=true, to_apply=%region_9.8 | all-reduce | flops 8 | bytes 64 | tf_op jit(solution)/shard_map/while/body/while/body/eval_jaxpr/psum | solution.py:511
  385.7 4.5 collective-permute-start.1
  401.6 4.9 collective-permute-start.5
  409.1 4.3 collective-permute-start.6
  421.0 72.2 %psum.27 = f32[8,1,1]{0,2,1:T(1,128)S(1)} all-reduce(f32[8,1,1]{0,2,1:T(1,128)S(1)} %bitcast.105), channel_id=1, replica_groups=mesh['tile'=16,'field'=8] {'tile','field'}, use_global_device_ids=true, to_apply=%region_7.6 | all-reduce | flops 8 | bytes 64 | tf_op jit(solution)/shard_map/while/body/while/body/eval_jaxpr/psum | solution.py:519
  495.0 62.6 %psum.28 = f32[8,1,1]{0,2,1:T(1,128)S(1)} all-reduce(f32[8,1,1]{0,2,1:T(1,128)S(1)} %bitcast.106), channel_id=1, replica_groups=mesh['tile'=16,'field'=8] {'tile','field'}, use_global_device_ids=true, to_apply=%region_9.8 | all-reduce | flops 8 | bytes 64 | tf_op jit(solution)/shard_map/while/body/while/body/eval_jaxpr/psum | solution.py:511
  560.8 4.5 collective-permute-start.1
  576.8 4.9 collective-permute-start.5
  584.3 4.3 collective-permute-start.6
  596.3 72.2 %psum.27 = f32[8,1,1]{0,2,1:T(1,128)S(1)} all-reduce(f32[8,1,1]{0,2,1:T(1,128)S(1)} %bitcast.105), channel_id=1, replica_groups=mesh['tile'=16,'field'=8] {'tile','field'}, use_global_device_ids=true, to_apply=%region_7.6 | all-reduce | flops 8 | bytes 64 | tf_op jit(solution)/shard_map/while/body/while/body/eval_jaxpr/psum | solution.py:519
  670.3 62.6 %psum.28 = f32[8,1,1]{0,2,1:T(1,128)S(1)} all-reduce(f32[8,1,1]{0,2,1:T(1,128)S(1)} %bitcast.106), channel_id=1, replica_groups=mesh['tile'=16,'field'=8] {'tile','field'}, use_global_device_ids=true, to_apply=%region_9.8 | all-reduce | flops 8 | bytes 64 | tf_op jit(solution)/shard_map/while/body/while/body/eval_jaxpr/psum | solution.py:511
  736.1 4.5 collective-permute-start.1
  752.1 4.9 collective-permute-start.5
  759.6 4.3 collective-permute-start.6
  771.5 72.4 %psum.27 = f32[8,1,1]{0,2,1:T(1,128)S(1)} all-reduce(f32[8,1,1]{0,2,1:T(1,128)S(1)} %bitcast.105), channel_id=1, replica_groups=mesh['tile'=16,'field'=8] {'tile','field'}, use_global_device_ids=true, to_apply=%region_7.6 | all-reduce | flops 8 | bytes 64 | tf_op jit(solution)/shard_map/while/body/while/body/eval_jaxpr/psum | solution.py:519
  845.7 62.4 %psum.28 = f32[8,1,1]{0,2,1:T(1,128)S(1)} all-reduce(f32[8,1,1]{0,2,1:T(1,128)S(1)} %bitcast.106), channel_id=1, replica_groups=mesh['tile'=16,'field'=8] {'tile','field'}, use_global_device_ids=true, to_apply=%region_9.8 | all-reduce | flops 8 | bytes 64 | tf_op jit(solution)/shard_map/while/body/while/body/eval_jaxpr/psum | solution.py:511
  911.3 4.5 collective-permute-start.1
  927.3 4.9 collective-permute-start.5
  934.8 4.3 collective-permute-start.6
  946.8 72.5 %psum.27 = f32[8,1,1]{0,2,1:T(1,128)S(1)} all-reduce(f32[8,1,1]{0,2,1:T(1,128)S(1)} %bitcast.105), channel_id=1, replica_groups=mesh['tile'=16,'field'=8] {'tile','field'}, use_global_device_ids=true, to_apply=%region_7.6 | all-reduce | flops 8 | bytes 64 | tf_op jit(solution)/shard_map/while/body/while/body/eval_jaxpr/psum | solution.py:519
  1021.1 62.4 %psum.28 = f32[8,1,1]{0,2,1:T(1,128)S(1)} all-reduce(f32[8,1,1]{0,2,1:T(1,128)S(1)} %bitcast.106), channel_id=1, replica_groups=mesh['tile'=16,'field'=8] {'tile','field'}, use_global_device_ids=true, to_apply=%region_9.8 | all-reduce | flops 8 | bytes 64 | tf_op jit(solution)/shard_map/while/body/while/body/eval_jaxpr/psum | solution.py:511
  1086.6 4.5 collective-permute-start.1
  1102.6 4.9 collective-permute-start.5
  1110.2 4.3 collective-permute-start.6
  1122.0 72.4 %psum.27 = f32[8,1,1]{0,2,1:T(1,128)S(1)} all-reduce(f32[8,1,1]{0,2,1:T(1,128)S(1)} %bitcast.105), channel_id=1, replica_groups=mesh['tile'=16,'field'=8] {'tile','field'}, use_global_device_ids=true, to_apply=%region_7.6 | all-reduce | flops 8 | bytes 64 | tf_op jit(solution)/shard_map/while/body/while/body/eval_jaxpr/psum | solution.py:519
  1196.2 62.4 %psum.28 = f32[8,1,1]{0,2,1:T(1,128)S(1)} all-reduce(f32[8,1,1]{0,2,1:T(1,128)S(1)} %bitcast.106), channel_id=1, replica_groups=mesh['tile'=16,'field'=8] {'tile','field'}, use_global_device_ids=true, to_apply=%region_9.8 | all-reduce | flops 8 | bytes 64 | tf_op jit(solution)/shard_map/while/body/while/body/eval_jaxpr/psum | solution.py:511
  1261.8 4.5 collective-permute-start.1
  1277.8 4.9 collective-permute-start.5
  1285.4 4.3 collective-permute-start.6
  1297.3 72.5 %psum.27 = f32[8,1,1]{0,2,1:T(1,128)S(1)} all-reduce(f32[8,1,1]{0,2,1:T(1,128)S(1)} %bitcast.105), channel_id=1, replica_groups=mesh['tile'=16,'field'=8] {'tile','field'}, use_global_device_ids=true, to_apply=%region_7.6 | all-reduce | flops 8 | bytes 64 | tf_op jit(solution)/shard_map/while/body/while/body/eval_jaxpr/psum | solution.py:519
  1371.6 62.4 %psum.28 = f32[8,1,1]{0,2,1:T(1,128)S(1)} all-reduce(f32[8,1,1]{0,2,1:T(1,128)S(1)} %bitcast.106), channel_id=1, replica_groups=mesh['tile'=16,'field'=8] {'tile','field'}, use_global_device_ids=true, to_apply=%region_9.8 | all-reduce | flops 8 | bytes 64 | tf_op jit(solution)/shard_map/while/body/while/body/eval_jaxpr/psum | solution.py:511
  1437.1 4.5 collective-permute-start.1
  1453.3 4.9 collective-permute-start.5
  1460.9 4.3 collective-permute-start.6
  1472.6 72.4 %psum.27 = f32[8,1,1]{0,2,1:T(1,128)S(1)} all-reduce(f32[8,1,1]{0,2,1:T(1,128)S(1)} %bitcast.105), channel_id=1, replica_groups=mesh['tile'=16,'field'=8] {'tile','field'}, use_global_device_ids=true, to_apply=%region_7.6 | all-reduce | flops 8 | bytes 64 | tf_op jit(solution)/shard_map/while/body/while/body/eval_jaxpr/psum | solution.py:519
  1546.8 62.4 %psum.28 = f32[8,1,1]{0,2,1:T(1,128)S(1)} all-reduce(f32[8,1,1]{0,2,1:T(1,128)S(1)} %bitcast.106), channel_id=1, replica_groups=mesh['tile'=16,'field'=8] {'tile','field'}, use_global_device_ids=true, to_apply=%region_9.8 | all-reduce | flops 8 | bytes 64 | tf_op jit(solution)/shard_map/while/body/while/body/eval_jaxpr/psum | solution.py:511
  1622.2 9.0 copy.35
  1631.2 11.5 gather_fusion.2
  1642.7 11.5 gather_fusion.3
  1654.3 13.6 gather_fusion
  1667.9 13.6 gather_fusion.1
  1681.5 5.7 fusion.11
  1688.2 6.6 all-to-all-start.2
  1694.8 7.6 all-to-all-done.2
  (353 shorter events, 284.7 us)
Async XLA Ops:
  4.6 10.5 collective-permute-start.10
  4.6 10.5 collective-permute-start.11
  23.1 28.7 %collective-permute-start.12 = (f32[12,8,2176]{2,1,0:T(8,128)}, f32[12,8,2176]{2,1,0:T(8,128)}, u32[]{:S(2)}, u32[]{:S(2)}) collective-permute-start(f32[12,8,2176]{2,1,0:T(8,128)} %get-tuple-element.178), channel_id=1, source_target_pairs={{0,8},{8,16},{16,24},{24,32},{32,40},{40,48},{48,56},{56,64},{64,7... | collective-permute-start | bytes 2506760 | tf_op jit(solution)/shard_map/ppermute | solution.py:554
  24.7 27.2 %collective-permute-start.13 = (f32[12,8,2176]{2,1,0:T(8,128)}, f32[12,8,2176]{2,1,0:T(8,128)}, u32[]{:S(2)}, u32[]{:S(2)}) collective-permute-start(f32[12,8,2176]{2,1,0:T(8,128)} %get-tuple-element.179), channel_id=1, source_target_pairs={{0,120},{8,0},{16,8},{24,16},{32,24},{40,32},{48,40},{56,48},{64,5... | collective-permute-start | bytes 2506760 | tf_op jit(solution)/shard_map/ppermute | solution.py:554
  28.4 18.7 %all-to-all-start = ((f32[16,3,128]{2,1,0:T(4,128)}), f32[16,3,128]{2,1,0:T(4,128)S(1)}, u32[]{:S(2)}, u32[]{:S(2)}) async-start(f32[16,3,128]{2,1,0:T(4,128)} %pad_maximum_fusion.23), calls=%async_computation | async-start | bytes 65536 | tf_op jit(solution)/shard_map/all_to_all | solution.py:585
  57.3 9.9 collective-permute-start.14
  58.1 9.1 collective-permute-start.15
  71.6 9.9 collective-permute-start.16
  71.7 9.9 collective-permute-start.17
  86.0 10.2 collective-permute-start.18
  86.1 10.1 collective-permute-start.19
  102.3 20.4 %all-to-all-start.1 = ((f32[128,1,128]{2,1,0:T(1,128)}), f32[128,1,128]{2,1,0:T(1,128)S(1)}, u32[]{:S(2)}, u32[]{:S(2)}) async-start(f32[128,1,128]{2,1,0:T(1,128)} %get-tuple-element.201), calls=%async_computation.1 | async-start | bytes 131072 | tf_op jit(solution)/shard_map/all_to_all | solution.py:605
  209.4 6.3 collective-permute-start
  210.9 6.4 collective-permute-start.1
  225.1 6.5 collective-permute-start.4
  226.4 6.8 collective-permute-start.5
  234.0 5.6 collective-permute-start.6
  384.2 6.3 collective-permute-start
  385.7 6.4 collective-permute-start.1
  393.5 4.5 collective-permute-start.3
  400.3 6.5 collective-permute-start.4
  401.6 6.8 collective-permute-start.5
  409.1 5.6 collective-permute-start.6
  559.4 6.3 collective-permute-start
  560.8 6.4 collective-permute-start.1
  568.7 4.5 collective-permute-start.3
  575.5 6.5 collective-permute-start.4
  576.8 6.8 collective-permute-start.5
  584.3 5.6 collective-permute-start.6
  588.6 4.3 collective-permute-start.7
  734.7 6.3 collective-permute-start
  736.1 6.4 collective-permute-start.1
  744.0 4.5 collective-permute-start.3
  750.8 6.5 collective-permute-start.4
  752.1 6.8 collective-permute-start.5
  759.6 5.6 collective-permute-start.6
  909.9 6.3 collective-permute-start
  911.3 6.4 collective-permute-start.1
  919.1 4.5 collective-permute-start.3
  926.0 6.5 collective-permute-start.4
  927.3 6.8 collective-permute-start.5
  934.8 5.6 collective-permute-start.6
  939.1 4.2 collective-permute-start.7
  1085.2 6.3 collective-permute-start
  1086.6 6.4 collective-permute-start.1
  1094.4 4.6 collective-permute-start.3
  1101.3 6.5 collective-permute-start.4
  1102.6 6.8 collective-permute-start.5
  1110.2 5.6 collective-permute-start.6
  1260.4 6.3 collective-permute-start
  1261.8 6.4 collective-permute-start.1
  1269.7 4.6 collective-permute-start.3
  1276.5 6.5 collective-permute-start.4
  1277.8 6.8 collective-permute-start.5
  1285.4 5.6 collective-permute-start.6
  1289.7 4.1 collective-permute-start.7
  1435.7 6.3 collective-permute-start
  1437.1 6.4 collective-permute-start.1
  1445.0 4.8 collective-permute-start.3
  1452.0 6.5 collective-permute-start.4
  1453.3 6.8 collective-permute-start.5
  1460.9 5.6 collective-permute-start.6
  1611.9 6.2 collective-permute-start.8
  1688.2 14.3 all-to-all-start.2
  (69 other events, 6071.3 us)

commit v4 on v3

--- a/solution.py
+++ b/solution.py
@@ -17,7 +17,8 @@
 MID, HALF = 0.5 * (HIGH + LOW), 0.5 * (HIGH - LOW)
 VMEM = pl.BlockSpec(memory_space=pltpu.VMEM)
 SMEM = pl.BlockSpec(memory_space=pltpu.SMEM)
-PARAMS = pltpu.CompilerParams(vmem_limit_bytes=10 * 1024 * 1024)
+HBM = pl.BlockSpec(memory_space=pl.ANY)
+PARAMS = pltpu.CompilerParams(vmem_limit_bytes=12 * 1024 * 1024)
 
 
 def held(x):
@@ -67,63 +68,66 @@
     return x
 
 
-def place(a, at, block, outs, to_up, to_down):
-    rows = block.shape[0]
-    outs[a][PAD : PAD + rows, :, at] = block
-    base, depth = sum(DEPTHS[:a]), DEPTHS[a]
-    to_up[base : base + depth, :, at] = block[:depth]
-    to_down[base : base + depth, :, at] = block[rows - depth :]
-
-
-def prepare_kernel(cols, *refs):
-    fields, outs, (to_up, to_down) = refs[0:4], refs[4:8], refs[8:]
-
-    def step(c, carry):
-        at = pl.ds(pl.multiple_of(c * LANES, LANES), LANES)
-        for a in range(4):
-            place(a, at, shaped(a, jnp.swapaxes(fields[a][:, :, at], 0, 1)), outs, to_up, to_down)
-        return carry
-
-    lax.fori_loop(0, cols // LANES, step, 0)
+def extra_tile(a, flags, left, right):
+    lane = lax.broadcasted_iota(jnp.int32, left.shape, 2)
+    shift = (-SIDE * a) % LANES
+    after = shaped(a, pltpu.roll(right[...], shift, 2) if shift else right[...])
+    before = shaped(a, pltpu.roll(left[...], LANES - SIDE * (a + 1), 2))
+    return jnp.where(lane < SIDE, after * flags[1], 0.0) + jnp.where(lane >= LANES - SIDE, before * flags[0], 0.0)
+
+
+def prepare_kernel(*refs):
+    fields, outs, (top, bottom) = refs[0:4], refs[4:8], refs[8:]
+    rows = fields[0].shape[1]
+    for a in range(4):
+        base, depth = sum(DEPTHS[:a]), DEPTHS[a]
+        for c in range(0, fields[a].shape[2], LANES):
+            at = slice(c, c + LANES)
+            block = shaped(a, jnp.swapaxes(fields[a][:, :, at], 0, 1))
+            outs[a][:, :, at] = block
+            top[base : base + depth, :, at] = block[:depth]
+            bottom[base : base + depth, :, at] = block[rows - depth :]
 
 
 def prepare(fields):
     rows, cols = fields[0].shape[1:]
-    wide = cols + LANES
     f32 = jnp.float32
-    ext = pltpu.VMEM((rows + 2 * PAD, F, wide), f32)
-    packed = pltpu.VMEM((sum(DEPTHS), F, wide), f32)
+    step = 4 * LANES
+    edge = sum(DEPTHS)
     return pl.pallas_call(
-        functools.partial(prepare_kernel, cols),
-        in_specs=[VMEM] * 4,
-        out_specs=[VMEM] * 6,
-        out_shape=[ext] * 4 + [packed] * 2,
+        prepare_kernel,
+        grid=(cols // step,),
+        in_specs=[pl.BlockSpec((F, rows, step), lambda i: (0, 0, i))] * 4,
+        out_specs=[pl.BlockSpec((rows, F, step), lambda i: (0, 0, i))] * 4
+        + [pl.BlockSpec((edge, F, step), lambda i: (0, 0, i))] * 2,
+        out_shape=[jax.ShapeDtypeStruct((rows, F, cols), f32)] * 4
+        + [jax.ShapeDtypeStruct((edge, F, cols), f32)] * 2,
         compiler_params=PARAMS,
         name="prepare",
     )(*fields)
 
 
-def sides_kernel(rows, cols, flags, left, right, *refs):
-    outs, (to_up, to_down) = refs[6:10], refs[10:]
-    lane = lax.broadcasted_iota(jnp.int32, (rows, F, LANES), 2)
+def sides_kernel(flags, left, right, top, bottom, to_up, to_down):
+    rows, cols = left.shape[0], top.shape[2]
+    to_up[:, :, :cols] = top[...]
+    to_down[:, :, :cols] = bottom[...]
     for a in range(4):
-        shift = (-SIDE * a) % LANES
-        after = shaped(a, pltpu.roll(right[...], shift, 2) if shift else right[...])
-        before = shaped(a, pltpu.roll(left[...], LANES - SIDE * (a + 1), 2))
-        extra = jnp.where(lane < SIDE, after * flags[1], 0.0) + jnp.where(lane >= LANES - SIDE, before * flags[0], 0.0)
-        place(a, pl.ds(cols, LANES), extra, outs, to_up, to_down)
-
-
-def sides(rows, cols, flags, left, right, prepared):
+        base, depth = sum(DEPTHS[:a]), DEPTHS[a]
+        extra = extra_tile(a, flags, left, right)
+        to_up[base : base + depth, :, cols:] = extra[:depth]
+        to_down[base : base + depth, :, cols:] = extra[rows - depth :]
+
+
+def sides(flags, left, right, top, bottom):
+    edge, _, cols = top.shape
     return pl.pallas_call(
-        functools.partial(sides_kernel, rows, cols),
-        in_specs=[SMEM] + [VMEM] * 8,
-        out_specs=[VMEM] * 6,
-        out_shape=[pltpu.VMEM(x.shape, x.dtype) for x in prepared],
-        input_output_aliases={3 + i: i for i in range(6)},
+        sides_kernel,
+        in_specs=[SMEM] + [VMEM] * 4,
+        out_specs=[VMEM] * 2,
+        out_shape=[jax.ShapeDtypeStruct((edge, F, cols + LANES), jnp.float32)] * 2,
         compiler_params=PARAMS,
         name="sides",
-    )(flags, left, right, *[held(x) for x in prepared])
+    )(flags, left, right, top, bottom)
 
 
 def walk(ref, r, count, wide):
@@ -162,30 +166,45 @@
     first, last = p == 0, p == ITERS // 2 - 1
     refs = list(refs)
     take = lambda n: [refs.pop(0) for _ in range(n)]
-    flags, mask, current, kap, tau, cur, up, down = take(8)
-    if not first:
-        older, old = take(2)
+    flags, mask, up, down = take(4)
+    if first:
+        left, right = take(2)
+        mains = take(4)
+    else:
+        own, kap, tau, cur, older, old = take(6)
+        begin = PAD if p == 1 else 0
     if last:
         earlier = take(ITERS // 2 - 1)
-    (current,) = take(1)
-    if first:
-        kap, tau, cur = take(3)
-    (middle,) = take(1)
-    if last:
-        line, scaled, one = refs
+        saved, (line, current, middle) = take(3), take(3)
+    elif first:
+        saved, (kap, tau, cur, current, middle, newest, to_up, to_down, sums) = take(1), take(9)
     else:
-        newest, to_up, to_down, sums, scaled, one = refs
+        saved, (middle, newest, to_up, to_down, sums, current) = take(2), take(6)
+    scaled, one, arrived = refs
     wide = cols + LANES
     own_low, own_high = PAD, PAD + rows
 
-    for source, flag, begin in ((up, 2, None), (down, 3, own_high)):
-        base = 0
-        for a, depth in enumerate(DEPTHS if first else (PAD,)):
-            at = PAD - depth if begin is None else begin
-            for i in range(depth):
-                row = source[base + i] * flags[flag]
-                (current, kap, tau, cur)[a][at + i] = row
-            base += depth
+    work = (current, kap, tau, cur)
+    if first:
+        for a, source in enumerate(mains):
+            work[a][own_low:own_high, :, :cols] = source[...]
+            work[a][own_low:own_high, :, cols:] = extra_tile(a, flags, left, right)
+    else:
+        current[own_low:own_high] = own[...]
+    base = 0
+    for a, depth in enumerate(DEPTHS if first else (PAD,)):
+        for i in range(depth):
+            work[a][own_low - depth + i] = up[base + i] * flags[2]
+            work[a][own_high + i] = down[base + i] * flags[3]
+        base += depth
+
+    def save(i, ref, low):
+        copy = pltpu.make_async_copy(ref.at[low : low + rows + 1], saved[i], arrived.at[i])
+        copy.start()
+        return copy
+
+    copies = [] if first else [save(0, old, 1)]
+    copies.append(save(len(copies), current, own_low))
 
     zero = jnp.zeros((F, LANES), jnp.float32)
 
@@ -234,6 +253,7 @@
     found = pairs(own_low, own_high, first_rows, (zero,) * (3 if first else 2))
 
     if last:
+        copies.append(save(2, middle, 1))
 
         def final_rows(r, carry):
             total = zero
@@ -256,6 +276,8 @@
         for f in range(1, F):
             total = total + pltpu.roll(table[f : f + 1], 2 * ITERS * f, 1)
         line[...] = jnp.broadcast_to(total[None], line.shape)
+        for copy in copies:
+            copy.wait()
         return
 
     sums[0] = found[0]
@@ -271,53 +293,50 @@
             for i in range(2):
                 value = 2.0 * new[i] - current[r + i, :, at]
                 if not first:
-                    value = 2.0 * value - older[r + i, :, at]
-                newest[r + i, :, at] = value
+                    value = 2.0 * value - older[r + i - PAD + begin, :, at]
+                newest[r + i - PAD, :, at] = value
                 if at.start < cols:
                     cross += value * middle[r + i - SKIP, :, at]
                     square += value * value
         return carry[0] + cross, carry[1] + square
 
     sums[2], sums[3] = pairs(own_low, own_high, second_rows, (zero, zero))
-    to_up[...] = newest[own_low : own_low + PAD]
-    to_down[...] = newest[own_high - PAD : own_high]
-
-
-def phase(p, rows, cols, flags, mask, basis, coefs, up, down, earlier=(), devices=1):
+    to_up[...] = newest[:PAD]
+    to_down[...] = newest[rows - PAD :]
+    for copy in copies:
+        copy.wait()
+
+
+def phase(p, rows, cols, flags, mask, up, down, state, earlier=(), devices=1):
     first, last = p == 0, p == ITERS // 2 - 1
     f32 = jnp.float32
     wide = cols + LANES
-    ext = (rows + 2 * PAD, F, wide)
-    out_shape = [pltpu.VMEM(ext, f32)]
-    aliases = {2: 0}
-    if first:
-        out_shape += [pltpu.VMEM(ext, f32)] * 3
-        aliases.update({3: 1, 4: 2, 5: 3})
-    out_shape += [pltpu.VMEM((rows + 2, F, wide), f32)]
+    ext, ring = (rows + 2 * PAD, F, wide), (rows + 2, F, wide)
+    saved = 1 if first else 3 if last else 2
+    out_shape = [pltpu.HBM((rows + 1, F, wide), f32)] * saved
+    scratch = []
     if last:
         out_shape += [jax.ShapeDtypeStruct((devices, 1, LANES), f32)]
+        scratch += [pltpu.VMEM(ext, f32), pltpu.VMEM(ring, f32)]
     else:
-        out_shape += [pltpu.VMEM(ext, f32)]
-        out_shape += [pltpu.VMEM((PAD, F, wide), f32)] * 2
+        if first:
+            out_shape += [pltpu.VMEM(ext, f32)] * 4
+        else:
+            scratch += [pltpu.VMEM(ext, f32)]
+        out_shape += [pltpu.VMEM(ring, f32), pltpu.VMEM((rows, F, wide), f32)]
+        out_shape += [jax.ShapeDtypeStruct((PAD, F, wide), f32)] * 2
         out_shape += [jax.ShapeDtypeStruct((5 if first else 4, F, LANES), f32)]
-    older = [] if first else [held(basis[-3]), held(basis[-2])]
+    operands = list(state) if first else [held(x) for x in state]
     outs = pl.pallas_call(
         functools.partial(phase_kernel, p, rows, cols),
-        in_specs=[SMEM] + [VMEM] * (7 + len(older) + len(earlier)),
-        out_specs=[VMEM] * len(out_shape),
+        in_specs=[SMEM] + [VMEM] * (3 + len(operands) + len(earlier)),
+        out_specs=[HBM] * saved + [VMEM] * (len(out_shape) - saved),
         out_shape=out_shape,
-        scratch_shapes=[pltpu.VMEM(ext, f32), pltpu.VMEM(ext, f32)],
-        input_output_aliases=aliases,
+        scratch_shapes=scratch + [pltpu.VMEM(ext, f32), pltpu.VMEM(ext, f32), pltpu.SemaphoreType.DMA((saved,))],
         compiler_params=PARAMS,
         name=f"phase{p}",
-    )(flags, mask, held(basis[-1]), *[held(c) for c in coefs], held(up), held(down), *older, *earlier)
-    current, outs = outs[0], list(outs[1:])
-    if first:
-        coefs, outs = outs[:3], outs[3:]
-    basis = basis[:-1] + [current, outs[0]]
-    if last:
-        return basis, outs[1]
-    return basis + [outs[1]], coefs, outs[2], outs[3], outs[4]
+    )(flags, mask, up, down, *operands, *earlier)
+    return list(outs[:saved]), list(outs[saved:])
 
 
 def coefficients(line):
@@ -398,48 +417,69 @@
     )(cells)
 
 
-def finish_kernel(rows, cols, line, hot, cells, row_frac, col_frac, *refs):
+def finish_kernel(rows, cols, line, cells, row_frac, col_frac, hot, *refs):
     basis, refs = refs[:ITERS], refs[ITERS:]
-    latent, predictor, fine, parts, keep, held_hot, arrived = refs
+    latent, predictor, fine, parts, keep, vectors, held_hot, vectors_in, hot_in = refs
     wide = cols + LANES
     chunks = hot.shape[0]
-    copies = [pltpu.make_async_copy(hot.at[i], held_hot.at[i], arrived.at[i]) for i in range(chunks)]
-    for copy in copies:
+    half = rows // 2
+    bands = [(0, half), (half, half), (rows, 1)]
+    copies = [
+        [
+            pltpu.make_async_copy(
+                basis[k].at[low : low + count], vectors.at[k, low : low + count], vectors_in.at[b, k]
+            )
+            for k in range(ITERS)
+        ]
+        for b, (low, count) in enumerate(bands)
+    ]
+    hot_copies = [pltpu.make_async_copy(hot.at[i], held_hot.at[i], hot_in.at[i]) for i in range(chunks)]
+    for band in copies:
+        for copy in band:
+            copy.start()
+    for copy in hot_copies:
         copy.start()
     lat_in, good = coefficients(line[...])
     fine[...] = jnp.where(good, 1.0, 0.0)
     for k in range(ITERS):
         keep[k] = lat_in[k]
-    lane = lax.broadcasted_iota(jnp.int32, (rows + 1, F, LANES), 2)
-    tall = (rows + 1) * F
-
-    def split(x, at, base):
-        part = x.astype(jnp.bfloat16)
-        rest = (x - part.astype(jnp.float32)).astype(jnp.bfloat16)
-        parts[base : base + tall, at] = part.reshape(tall, LANES)
-        parts[base + tall : base + 2 * tall, at] = rest.reshape(tall, LANES)
-
-    def step(c, after):
-        c = wide // LANES - 1 - c
-        at = pl.ds(pl.multiple_of(c * LANES, LANES), LANES)
-        total = None
-        for k in range(ITERS):
-            begin = PAD - SKIP * (k % 2)
-            term = keep[k] * basis[k][begin : begin + rows + 1, :, at]
-            total = term if total is None else total + term
-        turned = pltpu.roll(total, LANES - 1, 2)
-        split(total, at, 0)
-        split(jnp.where(lane == LANES - 1, after, turned), at, 2 * tall)
-
-        @pl.when(c < cols // LANES)
-        def _():
-            latent[:, :, at] = jnp.swapaxes(total[:rows], 0, 1)
-
-        return turned
-
-    lax.fori_loop(0, wide // LANES, step, jnp.zeros((rows + 1, F, LANES), jnp.float32))
+    tall = (rows + 2) * F
+
+    for (low, count), band in zip(bands, copies):
+        for copy in band:
+            copy.wait()
+        fill = count % 2
+        lane = lax.broadcasted_iota(jnp.int32, (count + fill, F, LANES), 2)
+
+        def split(x, at, base):
+            part = x.astype(jnp.bfloat16)
+            rest = (x - part.astype(jnp.float32)).astype(jnp.bfloat16)
+            size = (count + fill) * F
+            parts[base : base + size, at] = part.reshape(size, LANES)
+            parts[base + tall : base + tall + size, at] = rest.reshape(size, LANES)
+
+        def step(c, after):
+            c = wide // LANES - 1 - c
+            at = pl.ds(pl.multiple_of(c * LANES, LANES), LANES)
+            total = keep[0] * vectors[0, low : low + count, :, at]
+            for k in range(1, ITERS):
+                total = total + keep[k] * vectors[k, low : low + count, :, at]
+            if fill:
+                total = jnp.concatenate([total, jnp.zeros_like(total)], axis=0)
+            turned = pltpu.roll(total, LANES - 1, 2)
+            split(total, at, low * F)
+            split(jnp.where(lane == LANES - 1, after, turned), at, 2 * tall + low * F)
+            if low < rows:
+
+                @pl.when(c < cols // LANES)
+                def _():
+                    latent[:, low : low + count, at] = jnp.swapaxes(total, 0, 1)
+
+            return turned
+
+        lax.fori_loop(0, wide // LANES, step, jnp.zeros((count + fill, F, LANES), jnp.float32))
     for c in range(chunks):
-        copies[c].wait()
+        hot_copies[c].wait()
         at = slice(c * CHUNK, (c + 1) * CHUNK)
         both = jnp.dot(parts[...], held_hot[c], preferred_element_type=jnp.float32)
         here = both[:tall] + both[tall : 2 * tall]
@@ -459,13 +499,13 @@
             predictor[base : base + F] = out[:, i * LANES : (i + 1) * LANES]
 
 
-def finish(rows, cols, line, basis, hot, cells, row_frac, col_frac):
+def finish(rows, cols, line, cells, row_frac, col_frac, hot, basis):
     f32 = jnp.float32
     wide = cols + LANES
     chunks = hot.shape[0]
     return pl.pallas_call(
         functools.partial(finish_kernel, rows, cols),
-        in_specs=[VMEM, pl.BlockSpec(memory_space=pl.ANY)] + [VMEM] * (3 + ITERS),
+        in_specs=[VMEM] * 4 + [HBM] * (1 + ITERS),
         out_specs=[VMEM] * 3,
         out_shape=[
             jax.ShapeDtypeStruct((F, rows, cols), f32),
@@ -473,14 +513,16 @@
             jax.ShapeDtypeStruct((F, LANES), f32),
         ],
         scratch_shapes=[
-            pltpu.VMEM((4 * (rows + 1) * F, wide), jnp.bfloat16),
+            pltpu.VMEM((4 * (rows + 2) * F, wide), jnp.bfloat16),
             pltpu.VMEM((ITERS, F, LANES), f32),
+            pltpu.VMEM((ITERS, rows + 1, F, wide), f32),
             pltpu.VMEM((chunks, wide, CHUNK), jnp.bfloat16),
+            pltpu.SemaphoreType.DMA((3, ITERS)),
             pltpu.SemaphoreType.DMA((chunks,)),
         ],
-        compiler_params=pltpu.CompilerParams(vmem_limit_bytes=20 * 1024 * 1024),
+        compiler_params=pltpu.CompilerParams(vmem_limit_bytes=32 * 1024 * 1024),
         name="finish",
-    )(line, pltpu.with_memory_space_constraint(hot, pltpu.HBM), cells, row_frac, col_frac, *[held(b) for b in basis])
+    )(line, cells, row_frac, col_frac, *[pltpu.with_memory_space_constraint(x, pltpu.HBM) for x in (hot, *basis)])
 
 
 def extended(x, sides, width):
@@ -576,37 +618,48 @@
     mask = jnp.where(lane < SIDE, flags[1], jnp.where(lane >= LANES - SIDE, flags[0], 0.0))
 
     fields = (right_side, kappa_field, tau_field, curvature)
+    to_left, to_right = columns_of(fields)
+    from_right = turned(to_left, "field", -1)
+    from_left = turned(to_right, "field", 1)
+    *mains, top, bottom = prepare(fields)
+    to_up, to_down = sides(flags, from_left, from_right, top, bottom)
+
     cells = site_cells[0, 0]
     sent = jnp.concatenate([cells.astype(jnp.float32)[:, None], site_offsets[0, 0]], axis=1)
-    to_left, to_right = columns_of(fields)
-    sent, to_left, to_right = lax.optimization_barrier((sent, to_left, to_right))
-    from_right = turned(to_left, "field", -1)
-    from_left = turned(to_right, "field", 1)
+    sent, to_up, to_down = lax.optimization_barrier((sent, to_up, to_down))
     got = lax.all_to_all(sent, "tile", split_axis=0, concat_axis=0, tiled=True)
     got_cells = got[:, 0].astype(jnp.int32)
     got_row, got_col = got[:, 1], got[:, 2]
-    hot = columns_hot(got_cells.reshape(1, -1), cols)
-    prepared = sides(rows, cols, flags, from_left, from_right, prepare(fields))
-    basis, coefs, to_up, to_down = [prepared[0]], prepared[1:4], prepared[4], prepared[5]
-
-    sums = []
-    for p in range(ITERS // 2):
-        from_down = turned(to_up, "tile", -1)
-        from_up = turned(to_down, "tile", 1)
-        if p == 0:
-            flags, hot = lax.optimization_barrier((flags, hot))
-        state = (p, rows, cols, flags, mask, basis, coefs, from_up, from_down)
-        if p < ITERS // 2 - 1:
-            basis, coefs, to_up, to_down, part = phase(*state)
-            sums.append(part)
-        else:
-            basis, spread = phase(*state, earlier=sums, devices=tiles * bands)
+    sites = (got_cells.reshape(1, -1), got_row.reshape(1, -1), got_col.reshape(1, -1))
+
+    common = (rows, cols, flags, mask)
+
+    def exchanged(to_up, to_down):
+        return turned(to_down, "tile", 1), turned(to_up, "tile", -1)
+
+    up, down = exchanged(to_up, to_down)
+    basis, outs = phase(0, *common, up, down, (from_left, from_right, *mains))
+    *coefs, older, old, own, to_up, to_down, part = outs
+    sums = [part]
+    for p in range(1, ITERS // 2 - 1):
+        up, down = exchanged(to_up, to_down)
+        if p == 1:
+            hot = columns_hot(sites[0], cols)
+            mask, hot = lax.optimization_barrier((mask, hot))
+            common = (rows, cols, flags, mask)
+        saved, (old, newest, to_up, to_down, part) = phase(p, *common, up, down, (own, *coefs, older, old))
+        older, own = own, newest
+        basis += saved
+        sums.append(part)
+    up, down = exchanged(to_up, to_down)
+    saved, (spread,) = phase(
+        ITERS // 2 - 1, *common, up, down, (own, *coefs, older, old), earlier=sums, devices=tiles * bands
+    )
+    basis += saved
 
     spread = lax.all_to_all(spread, ("tile", "field"), split_axis=0, concat_axis=0, tiled=True)
     line = jnp.sum(spread, axis=0)
-    latent, predictor, fine = finish(
-        rows, cols, line, basis, hot, got_cells.reshape(1, -1), got_row.reshape(1, -1), got_col.reshape(1, -1)
-    )
+    latent, predictor, fine = finish(rows, cols, line, *sites, hot, basis)
     latent, predictor, _ = lax.while_loop(
         lambda state: state[2],
         lambda state: plain(*fields, got_cells, got_row, got_col) + (False,),

time: 1710 us -> 150 us (0.09)
  blocking collectives: 1140 us -> 10.6 us
  starting transfers between devices: 212 us -> 39.2 us
  local copies, waits for them, and re-layouts: 95.8 us -> 5.69 us
  waiting for transfers between devices: 126 us -> 40 us
  other arithmetic: 85 us -> 5.12 us
    psum x17 -> x0, blocking collectives: 1140 us -> none  [the longest x8 579 us: sweep(): lax.psum(jnp.sum(direction * image, axis=(1, 2)), ('tile', 'field'))]
    ppermute x66 -> x0, starting transfers between devices: 165 us -> none  [the longest x32 120 us: extended(): before = lax.ppermute(last, axis, up)]
    ppermute x66 -> x0, waiting for transfers between devices: 83.4 us -> none  [the longest x32 52.7 us: extended(): after = lax.ppermute(leading, axis, down)]
    gather x4 -> x0, local copies, waits for them, and re-layouts: 50.3 us -> none  [corner(): return jnp.take(flat, base + offset, axis=1)]
    reduce_sum x17 -> x0, other arithmetic: 42.5 us -> none  [the longest x8 28 us: sweep(): jnp.sum(direction * image, axis=(1, 2))]
    mul x25 -> x0, other arithmetic: 17.6 us -> none  [the longest x8 17.5 us: sweep(): scaled = tau_field * ((kappa_field + 4.0) * direction - neighbours(padded))]
  transfers between devices with their start and end apart: 79 -> 12, of which waited for: 56 -> 5; matrix products, arithmetic and copies ran while one was open for 0% -> 2% of each run, Pallas kernels for 1% -> 6%
where the time goes in v4:
time: 150 us; the launch traced here: 149 us
  Pallas kernels  47 us (31%)
  waiting for transfers between devices  40 us (27%)
  starting transfers between devices  39.2 us (26%)
  blocking collectives  10.6 us (7%)
  local copies, waits for them, and re-layouts  5.69 us (4%)
  other arithmetic  5.12 us (3%)
    ppermute x10, starting transfers between devices, turned(): return lax.ppermute(x, axis, [(i, (i + by) % size) for i in range(size)])  25.3 us
    ppermute x10, waiting for transfers between devices, turned(): return lax.ppermute(x, axis, [(i, (i + by) % size) for i in range(size)])  23.7 us
    pallas_call x4, Pallas kernels, phase(): pl.pallas_call(functools.partial(phase_kernel, p, rows, cols), in_specs=[...  21.8 us
    pallas_call x1, Pallas kernels, finish(): pl.pallas_call(functools.partial(finish_kernel, rows, cols), in_specs=[VM...  14.4 us
    all_to_all x1, blocking collectives, local(): got = lax.all_to_all(sent, 'tile', split_axis=0, concat_axis=0, tiled=True)  10.6 us
    all_to_all x1, starting transfers between devices, local(): lax.all_to_all(spread, ('tile', 'field'), split_axis=0, concat_axis=0, ti...  10.4 us
    all_to_all x1, waiting for transfers between devices, local(): lax.all_to_all(spread, ('tile', 'field'), split_axis=0, concat_axis=0, ti...  8.76 us
    all_to_all x1, waiting for transfers between devices, local(): lax.all_to_all(predictor, 'tile', split_axis=0, concat_axis=0, tiled=True)  7.58 us
  transfers between devices with their start and end apart: 12, of which 5 were waited for; matrix products, arithmetic and copies ran while one was open for 2% of the time, Pallas kernels for 6%

profile of v4, /device:TPU:0, one launch (start us, length us, event | category | flops | bytes accessed | tf_op | source)
XLA Modules:
  0.0 149.3 jit_solution(1501105633496538701)
XLA Ops:
  0.6 1.9 %columns.1 = (f32[16,8,128]{2,1,0:T(8,128)}, f32[16,8,128]{2,1,0:T(8,128)}) custom-call(f32[8,16,2048]{2,1,0:T(8,128)} %refs_0_.3, f32[8,16,2048]{2,1,0:T(8,128)} %refs_1_.3, f32[8,16,2048]{2,1,0:T(8,128)} %refs_2_.3, f32[8,16,2048]{2,1,0:T(8,128)} %refs_3_.3, f32[8,16,2048]{2,1,0:T(8,128)} %refs_0_.3, f32[8,16,2048]{2,1,0:T(8,128)} %refs_1_.3, ...), custom_call_target="tpu_custom_call" | custom-call | tf_op jit(solution)/shard_map/columns/pallas_call | solution.py:48
  2.5 0.0 collective-permute-start.10
  2.5 3.6 %collective-permute-start.11 = (f32[16,8,128]{2,1,0:T(8,128)}, f32[16,8,128]{2,1,0:T(8,128)S(1)}, u32[]{:S(2)}, u32[]{:S(2)}) collective-permute-start(f32[16,8,128]{2,1,0:T(8,128)} %get-tuple-element.163), channel_id=1, source_target_pairs={{0,7},{1,0},{2,1},{3,2},{4,3},{5,4},{6,5},{7,6},{8,15},{9,8},{10,9... | collective-permute-start | bytes 196616 | tf_op jit(solution)/shard_map/ppermute | solution.py:596
  6.1 0.0 copy-start.14
  6.1 3.7 %prepare.1 = (f32[16,8,2048]{2,1,0:T(8,128)S(1)}, f32[16,8,2048]{2,1,0:T(8,128)S(1)}, f32[16,8,2048]{2,1,0:T(8,128)S(1)}, f32[16,8,2048]{2,1,0:T(8,128)S(1)}, f3...) custom-call(f32[8,16,2048]{2,1,0:T(8,128)} %refs_0_.3, f32[8,16,2048]{2,1,0:T(8,128)} %refs_1_.3, ...), custom_call_target="tpu_custom_call" | custom-call | tf_op jit(solution)/shard_map/prepare/pallas_call | solution.py:97
  9.8 0.0 copy-start
  9.8 1.0 copy-done
  10.7 0.9 copy-done.2
  11.6 0.9 copy-done.4
  12.5 0.0 copy-done.14
  12.5 0.0 copy-done.13
  12.6 0.1 add_convert_fusion.flags.refs_0_
  12.6 0.0 collective-permute-done.10.left.refs_4_
  12.6 0.0 collective-permute-done.11.right.refs_5_
  12.6 0.0 copy-start.3
  12.7 1.2 copy-done.3
  13.9 1.1 copy-done.5
  15.0 0.7 sides.1
  15.7 1.6 %collective-permute-start.12 = (f32[12,8,2176]{2,1,0:T(8,128)S(1)}, f32[12,8,2176]{2,1,0:T(8,128)S(1)}, u32[]{:S(2)}, u32[]{:S(2)}) collective-permute-start(f32[12,8,2176]{2,1,0:T(8,128)S(1)} %get-tuple-element.170), channel_id=1, source_target_pairs={{0,8},{8,16},{16,24},{24,32},{32,40},{40,48},{48,56},{56,64},{64,7... | collective-permute-start | bytes 2506760 | tf_op jit(solution)/shard_map/ppermute | solution.py:596
  17.3 3.8 %collective-permute-start.13 = (f32[12,8,2176]{2,1,0:T(8,128)S(1)}, f32[12,8,2176]{2,1,0:T(8,128)S(1)}, u32[]{:S(2)}, u32[]{:S(2)}) collective-permute-start(f32[12,8,2176]{2,1,0:T(8,128)S(1)} %get-tuple-element.171), channel_id=1, source_target_pairs={{0,120},{8,0},{16,8},{24,16},{32,24},{40,32},{48,40},{56,48},{64,5... | collective-permute-start | bytes 2506760 | tf_op jit(solution)/shard_map/ppermute | solution.py:596
  21.1 0.6 fusion.29
  21.7 0.6 compare_select_fusion.4
  22.3 0.7 broadcast_select_fusion.refs_1_
  23.0 15.3 %collective-permute-done.12.refs_2_ = f32[12,8,2176]{2,1,0:T(8,128)S(1)} collective-permute-done((f32[12,8,2176]{2,1,0:T(8,128)S(1)}, f32[12,8,2176]{2,1,0:T(8,128)S(1)}, u32[]{:S(2)}, u32[]{:S(2)}) %collective-permute-start.12) | collective-permute-done | bytes 835616 | tf_op jit(solution)/shard_map/ppermute | solution.py:596
  38.2 0.0 collective-permute-done.13.refs_3_
  38.2 0.0 copy-done.1
  38.3 5.3 %phase0.1 = (f32[17,8,2176]{2,1,0:T(8,128)}, f32[24,8,2176]{2,1,0:T(8,128)S(1)}, f32[24,8,2176]{2,1,0:T(8,128)S(1)}, f32[24,8,2176]{2,1,0:T(8,128)S(1)}, f32[24,...) custom-call(f32[4]{0:T(128)S(1)} %add_convert_fusion.flags.refs_0_, ...), custom_call_target="tpu_custom_call" | custom-call | tf_op jit(solution)/shard_map/phase0/pallas_call | solution.py:330
  43.5 0.1 collective-permute-start.14
  43.6 5.3 %collective-permute-start.15 = (f32[4,8,2176]{2,1,0:T(8,128)S(1)}, f32[4,8,2176]{2,1,0:T(8,128)S(1)}, u32[]{:S(2)}, u32[]{:S(2)}) collective-permute-start(f32[4,8,2176]{2,1,0:T(8,128)S(1)} %get-tuple-element.177), channel_id=1, source_target_pairs={{0,120},{8,0},{16,8},{24,16},{32,24},{40,32},{48,40},{56,48},{64,5... | collective-permute-start | bytes 835592 | tf_op jit(solution)/shard_map/ppermute | solution.py:596
  48.9 10.6 %all_to_all.15 = f32[16,3,128]{2,1,0:T(4,128)S(1)} all-to-all(f32[16,3,128]{2,1,0:T(4,128)S(1)} %pad_maximum_fusion.23), channel_id=1, replica_groups=mesh['tile'=16,'field'=8] {'tile'}, dimensions={0} | all-to-all | bytes 49152 | tf_op jit(solution)/shard_map/all_to_all | solution.py:630
  59.6 4.6 %columns_hot.1.hot = bf16[4,2176,512]{2,1,0:T(8,128)(2,1)} custom-call(s32[1,2048]{1,0:T(1,128)S(1)} %get-tuple-element.313.cells), custom_call_target="tpu_custom_call" | custom-call | tf_op jit(solution)/shard_map/columns_hot/pallas_call | solution.py:409
  64.2 0.0 collective-permute-done.14.refs_2_
  64.2 0.0 collective-permute-done.15.refs_3_
  64.2 5.5 %phase1.1 = (f32[17,8,2176]{2,1,0:T(8,128)}, f32[17,8,2176]{2,1,0:T(8,128)}, f32[18,8,2176]{2,1,0:T(8,128)S(1)}, f32[16,8,2176]{2,1,0:T(8,128)S(1)}, f32[4,8,217...) custom-call(f32[4]{0:T(128)S(1)} %add_convert_fusion.flags.refs_0_, ...), custom_call_target="tpu_custom_call" | custom-call | tf_op jit(solution)/shard_map/phase1/pallas_call | solution.py:330
  69.6 0.6 collective-permute-start.16
  70.3 4.8 %collective-permute-start.17 = (f32[4,8,2176]{2,1,0:T(8,128)S(1)}, f32[4,8,2176]{2,1,0:T(8,128)S(1)}, u32[]{:S(2)}, u32[]{:S(2)}) collective-permute-start(f32[4,8,2176]{2,1,0:T(8,128)S(1)} %get-tuple-element.185), channel_id=1, source_target_pairs={{0,120},{8,0},{16,8},{24,16},{32,24},{40,32},{48,40},{56,48},{64,5... | collective-permute-start | bytes 835592 | tf_op jit(solution)/shard_map/ppermute | solution.py:596
  75.1 4.5 %collective-permute-done.16.refs_2_ = f32[4,8,2176]{2,1,0:T(8,128)S(1)} collective-permute-done((f32[4,8,2176]{2,1,0:T(8,128)S(1)}, f32[4,8,2176]{2,1,0:T(8,128)S(1)}, u32[]{:S(2)}, u32[]{:S(2)}) %collective-permute-start.16) | collective-permute-done | bytes 278560 | tf_op jit(solution)/shard_map/ppermute | solution.py:596
  79.6 0.0 collective-permute-done.17.refs_3_
  79.6 5.4 %phase2.1 = (f32[17,8,2176]{2,1,0:T(8,128)}, f32[17,8,2176]{2,1,0:T(8,128)}, f32[18,8,2176]{2,1,0:T(8,128)S(1)}, f32[16,8,2176]{2,1,0:T(8,128)S(1)}, f32[4,8,217...) custom-call(f32[4]{0:T(128)S(1)} %add_convert_fusion.flags.refs_0_, ...), custom_call_target="tpu_custom_call" | custom-call | tf_op jit(solution)/shard_map/phase2/pallas_call | solution.py:330
  85.0 0.1 collective-permute-start.18
  85.1 5.4 %collective-permute-start.19 = (f32[4,8,2176]{2,1,0:T(8,128)S(1)}, f32[4,8,2176]{2,1,0:T(8,128)S(1)}, u32[]{:S(2)}, u32[]{:S(2)}) collective-permute-start(f32[4,8,2176]{2,1,0:T(8,128)S(1)} %get-tuple-element.189), channel_id=1, source_target_pairs={{0,120},{8,0},{16,8},{24,16},{32,24},{40,32},{48,40},{56,48},{64,5... | collective-permute-start | bytes 835592 | tf_op jit(solution)/shard_map/ppermute | solution.py:596
  90.5 0.0 copy-done.15
  90.5 0.6 convert_bitcast_fusion
  91.1 3.9 %collective-permute-done.18.refs_2_ = f32[4,8,2176]{2,1,0:T(8,128)S(1)} collective-permute-done((f32[4,8,2176]{2,1,0:T(8,128)S(1)}, f32[4,8,2176]{2,1,0:T(8,128)S(1)}, u32[]{:S(2)}, u32[]{:S(2)}) %collective-permute-start.18) | collective-permute-done | bytes 278560 | tf_op jit(solution)/shard_map/ppermute | solution.py:596
  95.0 0.0 collective-permute-done.19.refs_3_
  95.0 5.6 %phase3.1 = (f32[17,8,2176]{2,1,0:T(8,128)}, f32[17,8,2176]{2,1,0:T(8,128)}, f32[17,8,2176]{2,1,0:T(8,128)}, f32[128,1,128]{2,1,0:T(1,128)}) custom-call(f32[4]{0:T(128)S(1)} %add_convert_fusion.flags.refs_0_, f32[8,128]{1,0:T(8,128)S(1)} %broadcast_select_fusion.refs_1_, f32[4,8,2176]{2,1,0:T(8,128)S(1)} %collective-permute-done.18.refs_2_, ...), custom_call_target="tpu_custom_call" | custom-call | tf_op jit(solution)/shard_map/phase3/pallas_call | solution.py:330
  100.6 10.4 %all-to-all-start.1 = ((f32[128,1,128]{2,1,0:T(1,128)}), f32[128,1,128]{2,1,0:T(1,128)S(1)}, u32[]{:S(2)}, u32[]{:S(2)}) async-start(f32[128,1,128]{2,1,0:T(1,128)} %get-tuple-element.195), calls=%async_computation.1 | async-start | bytes 131072 | tf_op jit(solution)/shard_map/all_to_all | solution.py:660
  111.0 0.0 copy-done.16
  111.0 0.7 fusion.23
  111.7 8.8 %all-to-all-done.1 = f32[128,1,128]{2,1,0:T(1,128)S(1)} async-done(((f32[128,1,128]{2,1,0:T(1,128)}), f32[128,1,128]{2,1,0:T(1,128)S(1)}, u32[]{:S(2)}, u32[]{:S(2)}) %all-to-all-start.1) | async-done | bytes 65568 | tf_op jit(solution)/shard_map/all_to_all | solution.py:660
  120.4 0.2 reduce_sum.40
  120.6 14.4 %finish.1 = (f32[8,16,2048]{2,1,0:T(8,128)}, f32[128,128]{1,0:T(8,128)}, f32[8,128]{1,0:T(8,128)S(1)}) custom-call(f32[1,128]{1,0:T(1,128)S(1)} %bitcast.100, s32[1,2048]{1,0:T(1,128)S(1)} %get-tuple-element.313.cells, f32[1,2048]{1,0:T(1,128)S(1)} %get-tuple-element.311.row_frac, f32[1,2048]{1,0:T(1,128)S(1)} %get-tuple-element.312.col_frac, ...), custom_call_target="tpu_custom_call" | custom-call | tf_op jit(solution)/shard_map/finish/pallas_call | solution.py:506
  135.0 0.7 compare_reduce_fusion
  136.3 0.0 copy-done.9
  136.3 0.0 copy-start.17
  136.3 0.0 copy-start.11
  136.3 0.0 copy-start.12
  136.3 0.2 while.28
  136.6 3.5 %all-to-all-start.2 = ((f32[16,8,128]{2,1,0:T(8,128)}), f32[16,8,128]{2,1,0:T(8,128)S(1)}, u32[]{:S(2)}, u32[]{:S(2)}) async-start(f32[16,8,128]{2,1,0:T(8,128)} %bitcast.111), calls=%async_computation.2 | async-start | bytes 131072 | tf_op jit(solution)/shard_map/all_to_all | solution.py:669
  140.1 0.0 copy-done.17
  140.1 7.6 %all-to-all-done.2 = f32[16,8,128]{2,1,0:T(8,128)S(1)} async-done(((f32[16,8,128]{2,1,0:T(8,128)}), f32[16,8,128]{2,1,0:T(8,128)S(1)}, u32[]{:S(2)}, u32[]{:S(2)}) %all-to-all-start.2) | async-done | bytes 65568 | tf_op jit(solution)/shard_map/all_to_all | solution.py:669
  147.7 0.0 copy-done.11
  147.7 0.0 copy-done.12
  147.7 1.6 %fusion.22 = f32[1,1,16,8,128]{4,3,2,1,0:T(8,128)} fusion(s32[1,1,16,8,128]{4,3,2,1,0:T(8,128)} %param.27, f32[16,8,128]{2,1,0:T(8,128)S(1)} %all-to-all-done.2, s32[1,1,16,8,128]{4,3,2,1,0:T(8,128)} %param.26, f32[16,128]{1,0:T(8,128)S(1)} %copy-done.12, f32[8]{0:T(128)S(1)} %subtract_log_fusion, f32[16,128]{1,0:T(8,128)S(1)} %copy-done.11), kind=kLoop, calls=%fused_computation.86 | loop fusion | flops 245760 | bytes 278560 | tf_op jit(solution)/shard_map/broadcast_in_dim | solution.py:683
  (13 shorter events, 0.1 us)
Async XLA Ops:
  2.5 10.1 %collective-permute-start.10 = (f32[16,8,128]{2,1,0:T(8,128)}, f32[16,8,128]{2,1,0:T(8,128)S(1)}, u32[]{:S(2)}, u32[]{:S(2)}) collective-permute-start(f32[16,8,128]{2,1,0:T(8,128)} %get-tuple-element.162), channel_id=1, source_target_pairs={{0,1},{1,2},{2,3},{3,4},{4,5},{5,6},{6,7},{7,0},{8,9},{9,10},{10,1... | collective-permute-start | bytes 196616 | tf_op jit(solution)/shard_map/ppermute | solution.py:596
  2.5 10.1 %collective-permute-start.11 = (f32[16,8,128]{2,1,0:T(8,128)}, f32[16,8,128]{2,1,0:T(8,128)S(1)}, u32[]{:S(2)}, u32[]{:S(2)}) collective-permute-start(f32[16,8,128]{2,1,0:T(8,128)} %get-tuple-element.163), channel_id=1, source_target_pairs={{0,7},{1,0},{2,1},{3,2},{4,3},{5,4},{6,5},{7,6},{8,15},{9,8},{10,9... | collective-permute-start | bytes 196616 | tf_op jit(solution)/shard_map/ppermute | solution.py:596
  6.1 6.4 %copy-start.14 = (s32[1,1,16,128]{3,2,1,0:T(8,128)S(1)}, s32[1,1,16,128]{3,2,1,0:T(8,128)}, u32[]{:S(2)}) copy-start(s32[1,1,16,128]{3,2,1,0:T(8,128)} %param.22) | copy-start | bytes 24580
  6.1 6.4 %copy-start.13 = (f32[1,1,16,2,128]{4,3,2,1,0:T(2,128)S(1)}, f32[1,1,16,2,128]{4,3,2,1,0:T(2,128)}, u32[]{:S(2)}) copy-start(f32[1,1,16,2,128]{4,3,2,1,0:T(2,128)} %param.23) | copy-start | bytes 49156
  9.8 1.0 copy-start
  10.7 0.9 copy-start.2
  11.6 0.9 copy-start.4
  12.5 25.7 %copy-start.1 = (f32[16,8,2048]{2,1,0:T(8,128)S(1)}, f32[16,8,2048]{2,1,0:T(8,128)}, u32[]{:S(2)}) copy-start(f32[16,8,2048]{2,1,0:T(8,128)} %copy-done) | copy-start | bytes 3145732
  12.6 1.2 copy-start.3
  13.8 1.1 copy-start.5
  15.7 22.6 %collective-permute-start.12 = (f32[12,8,2176]{2,1,0:T(8,128)S(1)}, f32[12,8,2176]{2,1,0:T(8,128)S(1)}, u32[]{:S(2)}, u32[]{:S(2)}) collective-permute-start(f32[12,8,2176]{2,1,0:T(8,128)S(1)} %get-tuple-element.170), channel_id=1, source_target_pairs={{0,8},{8,16},{16,24},{24,32},{32,40},{40,48},{48,56},{56,64},{64,7... | collective-permute-start | bytes 2506760 | tf_op jit(solution)/shard_map/ppermute | solution.py:596
  17.3 21.0 %collective-permute-start.13 = (f32[12,8,2176]{2,1,0:T(8,128)S(1)}, f32[12,8,2176]{2,1,0:T(8,128)S(1)}, u32[]{:S(2)}, u32[]{:S(2)}) collective-permute-start(f32[12,8,2176]{2,1,0:T(8,128)S(1)} %get-tuple-element.171), channel_id=1, source_target_pairs={{0,120},{8,0},{16,8},{24,16},{32,24},{40,32},{48,40},{56,48},{64,5... | collective-permute-start | bytes 2506760 | tf_op jit(solution)/shard_map/ppermute | solution.py:596
  43.5 20.6 %collective-permute-start.14 = (f32[4,8,2176]{2,1,0:T(8,128)S(1)}, f32[4,8,2176]{2,1,0:T(8,128)S(1)}, u32[]{:S(2)}, u32[]{:S(2)}) collective-permute-start(f32[4,8,2176]{2,1,0:T(8,128)S(1)} %get-tuple-element.176), channel_id=1, source_target_pairs={{0,8},{8,16},{16,24},{24,32},{32,40},{40,48},{48,56},{56,64},{64,7... | collective-permute-start | bytes 835592 | tf_op jit(solution)/shard_map/ppermute | solution.py:596
  43.6 20.6 %collective-permute-start.15 = (f32[4,8,2176]{2,1,0:T(8,128)S(1)}, f32[4,8,2176]{2,1,0:T(8,128)S(1)}, u32[]{:S(2)}, u32[]{:S(2)}) collective-permute-start(f32[4,8,2176]{2,1,0:T(8,128)S(1)} %get-tuple-element.177), channel_id=1, source_target_pairs={{0,120},{8,0},{16,8},{24,16},{32,24},{40,32},{48,40},{56,48},{64,5... | collective-permute-start | bytes 835592 | tf_op jit(solution)/shard_map/ppermute | solution.py:596
  69.6 9.9 %collective-permute-start.16 = (f32[4,8,2176]{2,1,0:T(8,128)S(1)}, f32[4,8,2176]{2,1,0:T(8,128)S(1)}, u32[]{:S(2)}, u32[]{:S(2)}) collective-permute-start(f32[4,8,2176]{2,1,0:T(8,128)S(1)} %get-tuple-element.184), channel_id=1, source_target_pairs={{0,8},{8,16},{16,24},{24,32},{32,40},{40,48},{48,56},{56,64},{64,7... | collective-permute-start | bytes 835592 | tf_op jit(solution)/shard_map/ppermute | solution.py:596
  70.3 9.3 %collective-permute-start.17 = (f32[4,8,2176]{2,1,0:T(8,128)S(1)}, f32[4,8,2176]{2,1,0:T(8,128)S(1)}, u32[]{:S(2)}, u32[]{:S(2)}) collective-permute-start(f32[4,8,2176]{2,1,0:T(8,128)S(1)} %get-tuple-element.185), channel_id=1, source_target_pairs={{0,120},{8,0},{16,8},{24,16},{32,24},{40,32},{48,40},{56,48},{64,5... | collective-permute-start | bytes 835592 | tf_op jit(solution)/shard_map/ppermute | solution.py:596
  79.6 10.9 %copy-start.15 = (s32[1,1,16,128]{3,2,1,0:T(8,128)S(1)}, s32[1,1,16,128]{3,2,1,0:T(8,128)}, u32[]{:S(2)}) copy-start(s32[1,1,16,128]{3,2,1,0:T(8,128)} %param.25) | copy-start | bytes 24580
  85.0 9.9 %collective-permute-start.18 = (f32[4,8,2176]{2,1,0:T(8,128)S(1)}, f32[4,8,2176]{2,1,0:T(8,128)S(1)}, u32[]{:S(2)}, u32[]{:S(2)}) collective-permute-start(f32[4,8,2176]{2,1,0:T(8,128)S(1)} %get-tuple-element.188), channel_id=1, source_target_pairs={{0,8},{8,16},{16,24},{24,32},{32,40},{40,48},{48,56},{56,64},{64,7... | collective-permute-start | bytes 835592 | tf_op jit(solution)/shard_map/ppermute | solution.py:596
  85.1 9.9 %collective-permute-start.19 = (f32[4,8,2176]{2,1,0:T(8,128)S(1)}, f32[4,8,2176]{2,1,0:T(8,128)S(1)}, u32[]{:S(2)}, u32[]{:S(2)}) collective-permute-start(f32[4,8,2176]{2,1,0:T(8,128)S(1)} %get-tuple-element.189), channel_id=1, source_target_pairs={{0,120},{8,0},{16,8},{24,16},{32,24},{40,32},{48,40},{56,48},{64,5... | collective-permute-start | bytes 835592 | tf_op jit(solution)/shard_map/ppermute | solution.py:596
  95.0 16.0 %copy-start.16 = (s32[1,1,16]{2,1,0:T(1,128)S(1)}, s32[1,1,16]{2,1,0:T(1,128)}, u32[]{:S(2)}) copy-start(s32[1,1,16]{2,1,0:T(1,128)} %param.24) | copy-start | bytes 196
  100.6 19.8 %all-to-all-start.1 = ((f32[128,1,128]{2,1,0:T(1,128)}), f32[128,1,128]{2,1,0:T(1,128)S(1)}, u32[]{:S(2)}, u32[]{:S(2)}) async-start(f32[128,1,128]{2,1,0:T(1,128)} %get-tuple-element.195), calls=%async_computation.1 | async-start | bytes 131072 | tf_op jit(solution)/shard_map/all_to_all | solution.py:660
  120.6 15.7 %copy-start.9 = (f32[8,16,2048]{2,1,0:T(8,128)S(1)}, f32[8,16,2048]{2,1,0:T(8,128)}, u32[]{:S(2)}) copy-start(f32[8,16,2048]{2,1,0:T(8,128)} %refs_0_.3) | copy-start | bytes 3145732
  136.3 3.8 %copy-start.17 = (f32[8]{0:T(128)S(1)}, f32[8]{0:T(128)}, u32[]{:S(2)}) copy-start(f32[8]{0:T(128)} %param.21) | copy-start | bytes 100
  136.3 11.4 %copy-start.11 = (f32[16,128]{1,0:T(8,128)S(1)}, f32[16,128]{1,0:T(8,128)}, u32[]{:S(2)}) copy-start(f32[16,128]{1,0:T(8,128)} %convert_bitcast_fusion) | copy-start | bytes 24580
  136.3 11.4 %copy-start.12 = (f32[16,128]{1,0:T(8,128)S(1)}, f32[16,128]{1,0:T(8,128)}, u32[]{:S(2)}) copy-start(f32[16,128]{1,0:T(8,128)} %fusion.23) | copy-start | bytes 24580
  136.6 11.1 %all-to-all-start.2 = ((f32[16,8,128]{2,1,0:T(8,128)}), f32[16,8,128]{2,1,0:T(8,128)S(1)}, u32[]{:S(2)}, u32[]{:S(2)}) async-start(f32[16,8,128]{2,1,0:T(8,128)} %bitcast.111), calls=%async_computation.2 | async-start | bytes 131072 | tf_op jit(solution)/shard_map/all_to_all | solution.py:669

commit v5 on v4

--- a/solution.py
+++ b/solution.py
@@ -100,8 +100,7 @@
         in_specs=[pl.BlockSpec((F, rows, step), lambda i: (0, 0, i))] * 4,
         out_specs=[pl.BlockSpec((rows, F, step), lambda i: (0, 0, i))] * 4
         + [pl.BlockSpec((edge, F, step), lambda i: (0, 0, i))] * 2,
-        out_shape=[jax.ShapeDtypeStruct((rows, F, cols), f32)] * 4
-        + [jax.ShapeDtypeStruct((edge, F, cols), f32)] * 2,
+        out_shape=[pltpu.HBM((rows, F, cols), f32)] * 4 + [pltpu.HBM((edge, F, cols), f32)] * 2,
         compiler_params=PARAMS,
         name="prepare",
     )(*fields)
@@ -172,15 +171,14 @@
         mains = take(4)
     else:
         own, kap, tau, cur, older, old = take(6)
-        begin = PAD if p == 1 else 0
     if last:
         earlier = take(ITERS // 2 - 1)
-        saved, (line, current, middle) = take(3), take(3)
+        line, current, middle = take(3)
     elif first:
-        saved, (kap, tau, cur, current, middle, newest, to_up, to_down, sums) = take(1), take(9)
+        kap, tau, cur, current, middle, newest, to_up, to_down, sums = take(9)
     else:
-        saved, (middle, newest, to_up, to_down, sums, current) = take(2), take(6)
-    scaled, one, arrived = refs
+        current, middle, newest, to_up, to_down, sums = take(6)
+    scaled, one = refs
     wide = cols + LANES
     own_low, own_high = PAD, PAD + rows
 
@@ -197,14 +195,6 @@
             work[a][own_low - depth + i] = up[base + i] * flags[2]
             work[a][own_high + i] = down[base + i] * flags[3]
         base += depth
-
-    def save(i, ref, low):
-        copy = pltpu.make_async_copy(ref.at[low : low + rows + 1], saved[i], arrived.at[i])
-        copy.start()
-        return copy
-
-    copies = [] if first else [save(0, old, 1)]
-    copies.append(save(len(copies), current, own_low))
 
     zero = jnp.zeros((F, LANES), jnp.float32)
 
@@ -253,7 +243,6 @@
     found = pairs(own_low, own_high, first_rows, (zero,) * (3 if first else 2))
 
     if last:
-        copies.append(save(2, middle, 1))
 
         def final_rows(r, carry):
             total = zero
@@ -275,9 +264,7 @@
         total = table[0:1]
         for f in range(1, F):
             total = total + pltpu.roll(table[f : f + 1], 2 * ITERS * f, 1)
-        line[...] = jnp.broadcast_to(total[None], line.shape)
-        for copy in copies:
-            copy.wait()
+        line[...] = total
         return
 
     sums[0] = found[0]
@@ -293,7 +280,7 @@
             for i in range(2):
                 value = 2.0 * new[i] - current[r + i, :, at]
                 if not first:
-                    value = 2.0 * value - older[r + i - PAD + begin, :, at]
+                    value = 2.0 * value - older[r + i, :, at]
                 newest[r + i - PAD, :, at] = value
                 if at.start < cols:
                     cross += value * middle[r + i - SKIP, :, at]
@@ -303,40 +290,30 @@
     sums[2], sums[3] = pairs(own_low, own_high, second_rows, (zero, zero))
     to_up[...] = newest[:PAD]
     to_down[...] = newest[rows - PAD :]
-    for copy in copies:
-        copy.wait()
-
-
-def phase(p, rows, cols, flags, mask, up, down, state, earlier=(), devices=1):
+
+
+def phase(p, rows, cols, flags, mask, up, down, state, earlier=()):
     first, last = p == 0, p == ITERS // 2 - 1
     f32 = jnp.float32
     wide = cols + LANES
-    ext, ring = (rows + 2 * PAD, F, wide), (rows + 2, F, wide)
-    saved = 1 if first else 3 if last else 2
-    out_shape = [pltpu.HBM((rows + 1, F, wide), f32)] * saved
-    scratch = []
+    ext = (rows + 2 * PAD, F, wide)
+    out_shape = [pltpu.VMEM(ext, f32)] * (4 if first else 1) + [pltpu.VMEM((rows + 2, F, wide), f32)]
     if last:
-        out_shape += [jax.ShapeDtypeStruct((devices, 1, LANES), f32)]
-        scratch += [pltpu.VMEM(ext, f32), pltpu.VMEM(ring, f32)]
+        out_shape = [jax.ShapeDtypeStruct((1, LANES), f32)] + out_shape
     else:
-        if first:
-            out_shape += [pltpu.VMEM(ext, f32)] * 4
-        else:
-            scratch += [pltpu.VMEM(ext, f32)]
-        out_shape += [pltpu.VMEM(ring, f32), pltpu.VMEM((rows, F, wide), f32)]
+        out_shape += [pltpu.VMEM((rows, F, wide), f32)]
         out_shape += [jax.ShapeDtypeStruct((PAD, F, wide), f32)] * 2
         out_shape += [jax.ShapeDtypeStruct((5 if first else 4, F, LANES), f32)]
     operands = list(state) if first else [held(x) for x in state]
-    outs = pl.pallas_call(
+    return pl.pallas_call(
         functools.partial(phase_kernel, p, rows, cols),
         in_specs=[SMEM] + [VMEM] * (3 + len(operands) + len(earlier)),
-        out_specs=[HBM] * saved + [VMEM] * (len(out_shape) - saved),
+        out_specs=[VMEM] * len(out_shape),
         out_shape=out_shape,
-        scratch_shapes=scratch + [pltpu.VMEM(ext, f32), pltpu.VMEM(ext, f32), pltpu.SemaphoreType.DMA((saved,))],
+        scratch_shapes=[pltpu.VMEM(ext, f32), pltpu.VMEM(ext, f32)],
         compiler_params=PARAMS,
         name=f"phase{p}",
     )(flags, mask, up, down, *operands, *earlier)
-    return list(outs[:saved]), list(outs[saved:])
 
 
 def coefficients(line):
@@ -397,21 +374,19 @@
 
     def step(b, carry):
         at = pl.ds(pl.multiple_of(b * LANES, LANES), LANES)
-        row = lax.broadcasted_iota(jnp.int32, (LANES, CHUNK), 0) + b * LANES
-        hot[0, at] = jnp.where(row == col, 1.0, 0.0).astype(jnp.bfloat16)
+        row = lax.broadcasted_iota(jnp.int32, (LANES, cells.shape[1]), 0) + b * LANES
+        hot[at] = jnp.where(row == col, 1.0, 0.0).astype(jnp.bfloat16)
         return carry
 
-    lax.fori_loop(0, hot.shape[1] // LANES, step, 0)
+    lax.fori_loop(0, hot.shape[0] // LANES, step, 0)
 
 
 def columns_hot(cells, cols):
-    chunks, wide = cells.shape[1] // CHUNK, cols + LANES
     return pl.pallas_call(
         functools.partial(columns_hot_kernel, cols),
-        grid=(chunks,),
-        in_specs=[pl.BlockSpec((1, CHUNK), lambda i: (0, i))],
-        out_specs=pl.BlockSpec((1, wide, CHUNK), lambda i: (i, 0, 0)),
-        out_shape=pltpu.HBM((chunks, wide, CHUNK), jnp.bfloat16),
+        in_specs=[VMEM],
+        out_specs=VMEM,
+        out_shape=pltpu.VMEM((cols + LANES, cells.shape[1]), jnp.bfloat16),
         compiler_params=PARAMS,
         name="columns_hot",
     )(cells)
@@ -419,69 +394,44 @@
 
 def finish_kernel(rows, cols, line, cells, row_frac, col_frac, hot, *refs):
     basis, refs = refs[:ITERS], refs[ITERS:]
-    latent, predictor, fine, parts, keep, vectors, held_hot, vectors_in, hot_in = refs
+    latent, predictor, fine, parts, keep = refs
     wide = cols + LANES
-    chunks = hot.shape[0]
-    half = rows // 2
-    bands = [(0, half), (half, half), (rows, 1)]
-    copies = [
-        [
-            pltpu.make_async_copy(
-                basis[k].at[low : low + count], vectors.at[k, low : low + count], vectors_in.at[b, k]
-            )
-            for k in range(ITERS)
-        ]
-        for b, (low, count) in enumerate(bands)
-    ]
-    hot_copies = [pltpu.make_async_copy(hot.at[i], held_hot.at[i], hot_in.at[i]) for i in range(chunks)]
-    for band in copies:
-        for copy in band:
-            copy.start()
-    for copy in hot_copies:
-        copy.start()
     lat_in, good = coefficients(line[...])
     fine[...] = jnp.where(good, 1.0, 0.0)
     for k in range(ITERS):
         keep[k] = lat_in[k]
     tall = (rows + 2) * F
-
-    for (low, count), band in zip(bands, copies):
-        for copy in band:
-            copy.wait()
-        fill = count % 2
-        lane = lax.broadcasted_iota(jnp.int32, (count + fill, F, LANES), 2)
-
-        def split(x, at, base):
-            part = x.astype(jnp.bfloat16)
-            rest = (x - part.astype(jnp.float32)).astype(jnp.bfloat16)
-            size = (count + fill) * F
-            parts[base : base + size, at] = part.reshape(size, LANES)
-            parts[base + tall : base + tall + size, at] = rest.reshape(size, LANES)
-
-        def step(c, after):
-            c = wide // LANES - 1 - c
-            at = pl.ds(pl.multiple_of(c * LANES, LANES), LANES)
-            total = keep[0] * vectors[0, low : low + count, :, at]
-            for k in range(1, ITERS):
-                total = total + keep[k] * vectors[k, low : low + count, :, at]
-            if fill:
-                total = jnp.concatenate([total, jnp.zeros_like(total)], axis=0)
-            turned = pltpu.roll(total, LANES - 1, 2)
-            split(total, at, low * F)
-            split(jnp.where(lane == LANES - 1, after, turned), at, 2 * tall + low * F)
-            if low < rows:
-
-                @pl.when(c < cols // LANES)
-                def _():
-                    latent[:, low : low + count, at] = jnp.swapaxes(total, 0, 1)
-
-            return turned
-
-        lax.fori_loop(0, wide // LANES, step, jnp.zeros((count + fill, F, LANES), jnp.float32))
-    for c in range(chunks):
-        hot_copies[c].wait()
-        at = slice(c * CHUNK, (c + 1) * CHUNK)
-        both = jnp.dot(parts[...], held_hot[c], preferred_element_type=jnp.float32)
+    lane = lax.broadcasted_iota(jnp.int32, (rows + 2, F, LANES), 2)
+
+    def split(x, at, base):
+        part = x.astype(jnp.bfloat16)
+        rest = (x - part.astype(jnp.float32)).astype(jnp.bfloat16)
+        parts[base : base + tall, at] = part.reshape(tall, LANES)
+        parts[base + tall : base + 2 * tall, at] = rest.reshape(tall, LANES)
+
+    def step(c, after):
+        c = wide // LANES - 1 - c
+        at = pl.ds(pl.multiple_of(c * LANES, LANES), LANES)
+        total = None
+        for k in range(ITERS):
+            begin = PAD - SKIP * (k % 2)
+            term = keep[k] * basis[k][begin : begin + rows + 1, :, at]
+            total = term if total is None else total + term
+        total = jnp.concatenate([total, jnp.zeros((1, F, LANES), jnp.float32)], axis=0)
+        turned = pltpu.roll(total, LANES - 1, 2)
+        split(total, at, 0)
+        split(jnp.where(lane == LANES - 1, after, turned), at, 2 * tall)
+
+        @pl.when(c < cols // LANES)
+        def _():
+            latent[:, :, at] = jnp.swapaxes(total[:rows], 0, 1)
+
+        return turned
+
+    lax.fori_loop(0, wide // LANES, step, jnp.zeros((rows + 2, F, LANES), jnp.float32))
+    for c in range(0, cells.shape[1], CHUNK):
+        at = slice(c, c + CHUNK)
+        both = jnp.dot(parts[...], hot[:, at], preferred_element_type=jnp.float32)
         here = both[:tall] + both[tall : 2 * tall]
         beside = both[2 * tall : 3 * tall] + both[3 * tall :]
         row = cells[:, at] // cols
@@ -495,17 +445,16 @@
         side = col_frac[:, at]
         out = (1.0 - side) * low + side * high
         for i in range(CHUNK // LANES):
-            base = (c * CHUNK // LANES + i) * F
+            base = (c // LANES + i) * F
             predictor[base : base + F] = out[:, i * LANES : (i + 1) * LANES]
 
 
 def finish(rows, cols, line, cells, row_frac, col_frac, hot, basis):
     f32 = jnp.float32
     wide = cols + LANES
-    chunks = hot.shape[0]
     return pl.pallas_call(
         functools.partial(finish_kernel, rows, cols),
-        in_specs=[VMEM] * 4 + [HBM] * (1 + ITERS),
+        in_specs=[VMEM] * (5 + ITERS),
         out_specs=[VMEM] * 3,
         out_shape=[
             jax.ShapeDtypeStruct((F, rows, cols), f32),
@@ -515,14 +464,10 @@
         scratch_shapes=[
             pltpu.VMEM((4 * (rows + 2) * F, wide), jnp.bfloat16),
             pltpu.VMEM((ITERS, F, LANES), f32),
-            pltpu.VMEM((ITERS, rows + 1, F, wide), f32),
-            pltpu.VMEM((chunks, wide, CHUNK), jnp.bfloat16),
-            pltpu.SemaphoreType.DMA((3, ITERS)),
-            pltpu.SemaphoreType.DMA((chunks,)),
         ],
-        compiler_params=pltpu.CompilerParams(vmem_limit_bytes=32 * 1024 * 1024),
+        compiler_params=PARAMS,
         name="finish",
-    )(line, cells, row_frac, col_frac, *[pltpu.with_memory_space_constraint(x, pltpu.HBM) for x in (hot, *basis)])
+    )(line, cells, row_frac, col_frac, *[held(x) for x in (hot, *basis)])
 
 
 def extended(x, sides, width):
@@ -594,6 +539,27 @@
 def turned(x, axis, by):
     size = lax.axis_size(axis)
     return lax.ppermute(x, axis, [(i, (i + by) % size) for i in range(size)])
+
+
+def summed(x, axis):
+    size, stride = lax.axis_size(axis), 1
+    while stride < size:
+        if size // stride in (4, 16):
+            for by in (1, -1):
+                x = x + lax.ppermute(
+                    x, axis, [(i, other(i, stride, by)) for i in range(size)]
+                )
+            stride *= 4
+        else:
+            x = x + lax.ppermute(x, axis, [(i, i ^ stride) for i in range(size)])
+            stride *= 2
+    return x
+
+
+def other(i, stride, by):
+    place = i // stride % 4
+    partner = (place + (by if place % 2 == 0 else -by)) % 4
+    return i + (partner - place) * stride
 
 
 def local(
@@ -632,33 +598,29 @@
     got_row, got_col = got[:, 1], got[:, 2]
     sites = (got_cells.reshape(1, -1), got_row.reshape(1, -1), got_col.reshape(1, -1))
 
+    mask, got_row = lax.optimization_barrier((mask, got_row))
     common = (rows, cols, flags, mask)
 
     def exchanged(to_up, to_down):
         return turned(to_down, "tile", 1), turned(to_up, "tile", -1)
 
     up, down = exchanged(to_up, to_down)
-    basis, outs = phase(0, *common, up, down, (from_left, from_right, *mains))
-    *coefs, older, old, own, to_up, to_down, part = outs
-    sums = [part]
+    *coefs, older, old, own, to_up, to_down, part = phase(
+        0, *common, up, down, (from_left, from_right, *mains)
+    )
+    basis, sums = [older, old], [part]
     for p in range(1, ITERS // 2 - 1):
         up, down = exchanged(to_up, to_down)
-        if p == 1:
-            hot = columns_hot(sites[0], cols)
-            mask, hot = lax.optimization_barrier((mask, hot))
-            common = (rows, cols, flags, mask)
-        saved, (old, newest, to_up, to_down, part) = phase(p, *common, up, down, (own, *coefs, older, old))
-        older, own = own, newest
-        basis += saved
+        older, old, own, to_up, to_down, part = phase(p, *common, up, down, (own, *coefs, older, old))
+        basis += [older, old]
         sums.append(part)
     up, down = exchanged(to_up, to_down)
-    saved, (spread,) = phase(
-        ITERS // 2 - 1, *common, up, down, (own, *coefs, older, old), earlier=sums, devices=tiles * bands
-    )
-    basis += saved
-
-    spread = lax.all_to_all(spread, ("tile", "field"), split_axis=0, concat_axis=0, tiled=True)
-    line = jnp.sum(spread, axis=0)
+    line, older, old = phase(ITERS // 2 - 1, *common, up, down, (own, *coefs, older, old), earlier=sums)
+    basis += [older, old]
+
+    line, got_cells = lax.optimization_barrier((line, got_cells))
+    hot = columns_hot(got_cells.reshape(1, -1), cols)
+    line = summed(summed(line, "field"), "tile")
     latent, predictor, fine = finish(rows, cols, line, *sites, hot, basis)
     latent, predictor, _ = lax.while_loop(
         lambda state: state[2],

time: 150 us -> 144 us (0.960)
  Pallas kernels: 47 us -> 35 us
  waiting for transfers between devices: 40 us -> 51 us
  blocking collectives: 10.6 us -> 0 us
  starting transfers between devices: 39.2 us -> 43.4 us
    ppermute x0 -> x7, waiting for transfers between devices: none -> 16.9 us  [the longest x6 15.8 us: summed(): lax.ppermute(x, axis, [(i, other(i, stride, by)) for i in range(size)])]
    all_to_all x1 -> x0, blocking collectives: 10.6 us -> none  [local(): got = lax.all_to_all(sent, 'tile', split_axis=0, concat_axis=0, tiled=True)]
    ppermute x10, waiting for transfers between devices: 23.7 us -> 13.2 us  [turned(): return lax.ppermute(x, axis, [(i, (i + by) % size) for i in range(size)])]
    ppermute x0 -> x7, starting transfers between devices: none -> 7.44 us  [the longest x6 7.41 us: summed(): lax.ppermute(x, axis, [(i, other(i, stride, by)) for i in range(size)])]
    all_to_all x1, starting transfers between devices: 10.4 us -> 3.73 us  [local(): got = lax.all_to_all(sent, 'tile', split_axis=0, concat_axis=0, tiled=True)]
    pallas_call x4, Pallas kernels: 21.8 us -> 16.2 us  [phase(): pl.pallas_call(functools.partial(phase_kernel, p, rows, cols), in_specs=[...]
    pallas_call x1, Pallas kernels: 14.4 us -> 9.03 us  [finish(): pl.pallas_call(functools.partial(finish_kernel, rows, cols), in_specs=[VM...]
    all_to_all x1, waiting for transfers between devices: 8.76 us -> 13.2 us  [local(): got = lax.all_to_all(sent, 'tile', split_axis=0, concat_axis=0, tiled=True)]
  transfers between devices with their start and end apart: 12 -> 19, of which waited for: 5 -> 11; matrix products, arithmetic and copies ran while one was open for 2% -> 3% of each run, Pallas kernels for 6% -> 4%
where the time goes in v5:
time: 144 us; the launch traced here: 143 us
  waiting for transfers between devices  51 us (35%)
  starting transfers between devices  43.4 us (30%)
  Pallas kernels  35 us (24%)
  local copies, waits for them, and re-layouts  6.58 us (5%)
  other arithmetic  5.55 us (4%)
  between operations  1.63 us (1%)
    ppermute x10, starting transfers between devices, turned(): return lax.ppermute(x, axis, [(i, (i + by) % size) for i in range(size)])  25.7 us
    pallas_call x4, Pallas kernels, phase(): pl.pallas_call(functools.partial(phase_kernel, p, rows, cols), in_specs=[...  16.2 us
    ppermute x6, waiting for transfers between devices, summed(): lax.ppermute(x, axis, [(i, other(i, stride, by)) for i in range(size)])  15.8 us
    ppermute x10, waiting for transfers between devices, turned(): return lax.ppermute(x, axis, [(i, (i + by) % size) for i in range(size)])  13.2 us
    all_to_all x1, waiting for transfers between devices, local(): got = lax.all_to_all(sent, 'tile', split_axis=0, concat_axis=0, tiled=True)  13.2 us
    pallas_call x1, Pallas kernels, finish(): pl.pallas_call(functools.partial(finish_kernel, rows, cols), in_specs=[VM...  9.03 us
    all_to_all x1, waiting for transfers between devices, local(): lax.all_to_all(predictor, 'tile', split_axis=0, concat_axis=0, tiled=True)  7.64 us
    ppermute x6, starting transfers between devices, summed(): lax.ppermute(x, axis, [(i, other(i, stride, by)) for i in range(size)])  7.41 us
  transfers between devices with their start and end apart: 19, of which 11 were waited for; matrix products, arithmetic and copies ran while one was open for 3% of the time, Pallas kernels for 4%

profile of v5, /device:TPU:0, one launch (start us, length us, event | category | flops | bytes accessed | tf_op | source)
XLA Modules:
  0.0 143.5 jit_solution(472392838404213653)
XLA Ops:
  0.6 0.0 copy-start.6
  0.6 0.0 copy-start.10
  0.7 0.0 copy-start.11
  0.7 2.0 %columns.1 = (f32[16,8,128]{2,1,0:T(8,128)}, f32[16,8,128]{2,1,0:T(8,128)}) custom-call(f32[8,16,2048]{2,1,0:T(8,128)} %refs_0_.3, f32[8,16,2048]{2,1,0:T(8,128)} %refs_1_.3, f32[8,16,2048]{2,1,0:T(8,128)} %refs_2_.3, f32[8,16,2048]{2,1,0:T(8,128)} %refs_3_.3, f32[8,16,2048]{2,1,0:T(8,128)} %refs_0_.3, f32[8,16,2048]{2,1,0:T(8,128)} %refs_1_.3, ...), custom_call_target="tpu_custom_call" | custom-call | tf_op jit(solution)/shard_map/columns/pallas_call | solution.py:48
  2.7 0.0 collective-permute-start.10
  2.7 3.6 %collective-permute-start.11 = (f32[16,8,128]{2,1,0:T(8,128)}, f32[16,8,128]{2,1,0:T(8,128)S(1)}, u32[]{:S(2)}, u32[]{:S(2)}) collective-permute-start(f32[16,8,128]{2,1,0:T(8,128)} %get-tuple-element.161), channel_id=1, source_target_pairs={{0,7},{1,0},{2,1},{3,2},{4,3},{5,4},{6,5},{7,6},{8,15},{9,8},{10,9... | collective-permute-start | bytes 196616 | tf_op jit(solution)/shard_map/ppermute | solution.py:541
  6.3 0.0 copy-start.18
  6.3 4.3 %prepare.1 = (f32[16,8,2048]{2,1,0:T(8,128)}, f32[16,8,2048]{2,1,0:T(8,128)}, f32[16,8,2048]{2,1,0:T(8,128)}, f32[16,8,2048]{2,1,0:T(8,128)}, f32[12,8,2048]{2,1,0:T(8,128)}, /*index=5*/f32[12,8,2048]{2,1,0:T(8,128)}) custom-call(f32[8,16,2048]{2,1,0:T(8,128)} %refs_0_.3, f32[8,16,2048]{2,1,0:T(8,128)S(1)} %copy-done.6, f32[8,16,2048]{2,1,0:T(8,128)S(1)} %copy-done.10, ...), custom_call_target="tpu_custom_call" | custom-call | tf_op jit(solution)/shard_map/prepare/pallas_call | solution.py:97
  10.6 0.6 pad_maximum_fusion.23
  11.3 0.1 add_convert_fusion.flags.refs_0_
  11.3 0.0 collective-permute-done.10.left.refs_4_
  11.3 0.0 collective-permute-done.11.right.refs_5_
  11.4 1.1 copy-done.4
  12.5 1.1 copy-done.5
  13.6 1.8 %sides.1 = (f32[12,8,2176]{2,1,0:T(8,128)}, f32[12,8,2176]{2,1,0:T(8,128)}) custom-call(f32[4]{0:T(128)S(1)} %add_convert_fusion.flags.refs_0_, f32[16,8,128]{2,1,0:T(8,128)S(1)} %collective-permute-done.10.left.refs_4_, f32[16,8,128]{2,1,0:T(8,128)S(1)} %collective-permute-done.11.right.refs_5_, f32[12,8,2048]{2,1,0:T(8,128)S(1)} %copy-done.4, ...), custom_call_target="tpu_custom_call" | custom-call | tf_op jit(solution)/shard_map/sides/pallas_call | solution.py:122
  15.5 1.6 %collective-permute-start.12 = (f32[12,8,2176]{2,1,0:T(8,128)}, f32[12,8,2176]{2,1,0:T(8,128)S(1)}, u32[]{:S(2)}, u32[]{:S(2)}) collective-permute-start(f32[12,8,2176]{2,1,0:T(8,128)} %get-tuple-element.168), channel_id=1, source_target_pairs={{0,8},{8,16},{16,24},{24,32},{32,40},{40,48},{48,56},{56,64},{64,7... | collective-permute-start | bytes 2506760 | tf_op jit(solution)/shard_map/ppermute | solution.py:541
  17.0 3.8 %collective-permute-start.13 = (f32[12,8,2176]{2,1,0:T(8,128)}, f32[12,8,2176]{2,1,0:T(8,128)S(1)}, u32[]{:S(2)}, u32[]{:S(2)}) collective-permute-start(f32[12,8,2176]{2,1,0:T(8,128)} %get-tuple-element.169), channel_id=1, source_target_pairs={{0,120},{8,0},{16,8},{24,16},{32,24},{40,32},{48,40},{56,48},{64,5... | collective-permute-start | bytes 2506760 | tf_op jit(solution)/shard_map/ppermute | solution.py:541
  20.8 0.6 fusion.31
  21.4 0.6 compare_select_fusion.4
  22.0 3.7 %all-to-all-start = ((f32[16,3,128]{2,1,0:T(4,128)}), f32[16,3,128]{2,1,0:T(4,128)S(1)}, u32[]{:S(2)}, u32[]{:S(2)}) async-start(f32[16,3,128]{2,1,0:T(4,128)} %pad_maximum_fusion.23), calls=%async_computation | async-start | bytes 65536 | tf_op jit(solution)/shard_map/all_to_all | solution.py:596
  25.7 0.7 broadcast_select_fusion.refs_1_
  26.4 13.2 %all-to-all-done = f32[16,3,128]{2,1,0:T(4,128)S(1)} async-done(((f32[16,3,128]{2,1,0:T(4,128)}), f32[16,3,128]{2,1,0:T(4,128)S(1)}, u32[]{:S(2)}, u32[]{:S(2)}) %all-to-all-start) | async-done | bytes 24608 | tf_op jit(solution)/shard_map/all_to_all | solution.py:596
  39.6 0.0 collective-permute-done.13.refs_3_
  39.6 1.2 copy-done.1
  40.9 1.2 copy-done.2
  42.1 1.2 copy-done.3
  43.3 4.5 %phase0.1 = (f32[24,8,2176]{2,1,0:T(8,128)S(1)}, f32[24,8,2176]{2,1,0:T(8,128)S(1)}, f32[24,8,2176]{2,1,0:T(8,128)S(1)}, f32[24,8,2176]{2,1,0:T(8,128)S(1)}, f32...) custom-call(f32[4]{0:T(128)S(1)} %add_convert_fusion.flags.refs_0_, ...), custom_call_target="tpu_custom_call" | custom-call | tf_op jit(solution)/shard_map/phase0/pallas_call | solution.py:308
  47.8 0.8 collective-permute-start.14
  48.7 4.6 %collective-permute-start.15 = (f32[4,8,2176]{2,1,0:T(8,128)S(1)}, f32[4,8,2176]{2,1,0:T(8,128)S(1)}, u32[]{:S(2)}, u32[]{:S(2)}) collective-permute-start(f32[4,8,2176]{2,1,0:T(8,128)S(1)} %get-tuple-element.175), channel_id=1, source_target_pairs={{0,120},{8,0},{16,8},{24,16},{32,24},{40,32},{48,40},{56,48},{64,5... | collective-permute-start | bytes 835592 | tf_op jit(solution)/shard_map/ppermute | solution.py:541
  53.3 4.5 %collective-permute-done.14.refs_2_ = f32[4,8,2176]{2,1,0:T(8,128)S(1)} collective-permute-done((f32[4,8,2176]{2,1,0:T(8,128)S(1)}, f32[4,8,2176]{2,1,0:T(8,128)S(1)}, u32[]{:S(2)}, u32[]{:S(2)}) %collective-permute-start.14) | collective-permute-done | bytes 278560 | tf_op jit(solution)/shard_map/ppermute | solution.py:541
  57.8 0.0 collective-permute-done.15.refs_3_
  57.8 4.1 %phase1.1 = (f32[24,8,2176]{2,1,0:T(8,128)S(1)}, f32[18,8,2176]{2,1,0:T(8,128)S(1)}, f32[16,8,2176]{2,1,0:T(8,128)S(1)}, f32[4,8,2176]{2,1,0:T(8,128)S(1)}, f32[...) custom-call(f32[4]{0:T(128)S(1)} %add_convert_fusion.flags.refs_0_, f32[8,128]{1,0:T(8,128)S(1)} %broadcast_select_fusion.refs_1_, ...), custom_call_target="tpu_custom_call" | custom-call | tf_op jit(solution)/shard_map/phase1/pallas_call | solution.py:308
  61.8 0.1 collective-permute-start.16
  61.9 5.6 %collective-permute-start.17 = (f32[4,8,2176]{2,1,0:T(8,128)S(1)}, f32[4,8,2176]{2,1,0:T(8,128)S(1)}, u32[]{:S(2)}, u32[]{:S(2)}) collective-permute-start(f32[4,8,2176]{2,1,0:T(8,128)S(1)} %get-tuple-element.183), channel_id=1, source_target_pairs={{0,120},{8,0},{16,8},{24,16},{32,24},{40,32},{48,40},{56,48},{64,5... | collective-permute-start | bytes 835592 | tf_op jit(solution)/shard_map/ppermute | solution.py:541
  67.5 4.3 %collective-permute-done.16.refs_2_ = f32[4,8,2176]{2,1,0:T(8,128)S(1)} collective-permute-done((f32[4,8,2176]{2,1,0:T(8,128)S(1)}, f32[4,8,2176]{2,1,0:T(8,128)S(1)}, u32[]{:S(2)}, u32[]{:S(2)}) %collective-permute-start.16) | collective-permute-done | bytes 278560 | tf_op jit(solution)/shard_map/ppermute | solution.py:541
  71.8 4.2 %phase2.1 = (f32[24,8,2176]{2,1,0:T(8,128)S(1)}, f32[18,8,2176]{2,1,0:T(8,128)S(1)}, f32[16,8,2176]{2,1,0:T(8,128)S(1)}, f32[4,8,2176]{2,1,0:T(8,128)S(1)}, f32[...) custom-call(f32[4]{0:T(128)S(1)} %add_convert_fusion.flags.refs_0_, f32[8,128]{1,0:T(8,128)S(1)} %broadcast_select_fusion.refs_1_, ...), custom_call_target="tpu_custom_call" | custom-call | tf_op jit(solution)/shard_map/phase2/pallas_call | solution.py:308
  76.0 0.1 collective-permute-start.18
  76.1 5.7 %collective-permute-start.19 = (f32[4,8,2176]{2,1,0:T(8,128)S(1)}, f32[4,8,2176]{2,1,0:T(8,128)S(1)}, u32[]{:S(2)}, u32[]{:S(2)}) collective-permute-start(f32[4,8,2176]{2,1,0:T(8,128)S(1)} %get-tuple-element.188), channel_id=1, source_target_pairs={{0,120},{8,0},{16,8},{24,16},{32,24},{40,32},{48,40},{56,48},{64,5... | collective-permute-start | bytes 835592 | tf_op jit(solution)/shard_map/ppermute | solution.py:541
  81.8 4.4 %collective-permute-done.18.refs_2_ = f32[4,8,2176]{2,1,0:T(8,128)S(1)} collective-permute-done((f32[4,8,2176]{2,1,0:T(8,128)S(1)}, f32[4,8,2176]{2,1,0:T(8,128)S(1)}, u32[]{:S(2)}, u32[]{:S(2)}) %collective-permute-start.18) | collective-permute-done | bytes 278560 | tf_op jit(solution)/shard_map/ppermute | solution.py:541
  86.2 3.4 %phase3.1 = (f32[1,128]{1,0:T(1,128)S(1)}, f32[24,8,2176]{2,1,0:T(8,128)S(1)}, f32[18,8,2176]{2,1,0:T(8,128)S(1)}) custom-call(f32[4]{0:T(128)S(1)} %add_convert_fusion.flags.refs_0_, f32[8,128]{1,0:T(8,128)S(1)} %broadcast_select_fusion.refs_1_, f32[4,8,2176]{2,1,0:T(8,128)S(1)} %collective-permute-done.18.refs_2_, ...), custom_call_target="tpu_custom_call" | custom-call | tf_op jit(solution)/shard_map/phase3/pallas_call | solution.py:308
  89.6 0.0 collective-permute-start.20
  89.7 1.1 collective-permute-done.20
  90.8 3.1 %collective-permute-start.21 = (f32[1,128]{1,0:T(1,128)S(1)}, f32[1,128]{1,0:T(1,128)S(1)}, u32[]{:S(2)}, u32[]{:S(2)}) collective-permute-start(f32[1,128]{1,0:T(1,128)S(1)} %add.114), channel_id=1, source_target_pairs={{0,2},{1,3},{2,0},{3,1},{4,6},{5,7},{6,4},{7,5},{8,10},{9,11},{10,... | collective-permute-start | bytes 1544 | tf_op jit(solution)/shard_map/ppermute | solution.py:549
  93.9 1.5 %collective-permute-done.21 = f32[1,128]{1,0:T(1,128)S(1)} collective-permute-done((f32[1,128]{1,0:T(1,128)S(1)}, f32[1,128]{1,0:T(1,128)S(1)}, u32[]{:S(2)}, u32[]{:S(2)}) %collective-permute-start.21) | collective-permute-done | bytes 544 | tf_op jit(solution)/shard_map/ppermute | solution.py:549
  95.4 1.7 %collective-permute-start.22 = (f32[1,128]{1,0:T(1,128)S(1)}, f32[1,128]{1,0:T(1,128)S(1)}, u32[]{:S(2)}, u32[]{:S(2)}) collective-permute-start(f32[1,128]{1,0:T(1,128)S(1)} %add.115), channel_id=1, source_target_pairs={{0,6},{1,7},{2,4},{3,5},{4,2},{5,3},{6,0},{7,1},{8,14},{9,15},{10,... | collective-permute-start | bytes 1544 | tf_op jit(solution)/shard_map/ppermute | solution.py:549
  97.0 3.1 %collective-permute-done.22 = f32[1,128]{1,0:T(1,128)S(1)} collective-permute-done((f32[1,128]{1,0:T(1,128)S(1)}, f32[1,128]{1,0:T(1,128)S(1)}, u32[]{:S(2)}, u32[]{:S(2)}) %collective-permute-start.22) | collective-permute-done | bytes 544 | tf_op jit(solution)/shard_map/ppermute | solution.py:549
  100.1 0.0 collective-permute-start.23
  100.1 3.5 %collective-permute-done.23 = f32[1,128]{1,0:T(1,128)S(1)} collective-permute-done((f32[1,128]{1,0:T(1,128)S(1)}, f32[1,128]{1,0:T(1,128)S(1)}, u32[]{:S(2)}, u32[]{:S(2)}) %collective-permute-start.23) | collective-permute-done | bytes 544 | tf_op jit(solution)/shard_map/ppermute | solution.py:549
  103.7 0.0 collective-permute-start.24
  103.7 4.7 %collective-permute-done.24 = f32[1,128]{1,0:T(1,128)S(1)} collective-permute-done((f32[1,128]{1,0:T(1,128)S(1)}, f32[1,128]{1,0:T(1,128)S(1)}, u32[]{:S(2)}, u32[]{:S(2)}) %collective-permute-start.24) | collective-permute-done | bytes 544 | tf_op jit(solution)/shard_map/ppermute | solution.py:549
  108.4 0.0 collective-permute-start.25
  108.4 0.6 convert_bitcast_fusion
  109.0 2.9 %collective-permute-done.25 = f32[1,128]{1,0:T(1,128)S(1)} collective-permute-done((f32[1,128]{1,0:T(1,128)S(1)}, f32[1,128]{1,0:T(1,128)S(1)}, u32[]{:S(2)}, u32[]{:S(2)}) %collective-permute-start.25) | collective-permute-done | bytes 544 | tf_op jit(solution)/shard_map/ppermute | solution.py:549
  112.0 2.7 %collective-permute-start.26 = (f32[1,128]{1,0:T(1,128)S(1)}, f32[1,128]{1,0:T(1,128)S(1)}, u32[]{:S(2)}, u32[]{:S(2)}) collective-permute-start(f32[1,128]{1,0:T(1,128)S(1)} %add.119), channel_id=1, source_target_pairs={{0,96},{8,104},{16,112},{24,120},{32,64},{40,72},{48,80},{56,88},{... | collective-permute-start | bytes 1544 | tf_op jit(solution)/shard_map/ppermute | solution.py:549
  114.7 0.7 fusion.24
  115.3 1.6 %columns_hot.1.hot = bf16[2176,2048]{1,0:T(8,128)(2,1)S(1)} custom-call(s32[1,2048]{1,0:T(1,128)S(1)} %bitcast.96), custom_call_target="tpu_custom_call" | custom-call | tf_op jit(solution)/shard_map/columns_hot/pallas_call | solution.py:385
  116.9 0.0 copy-start.12
  117.0 9.0 %finish.1 = (f32[8,16,2048]{2,1,0:T(8,128)}, f32[128,128]{1,0:T(8,128)}, f32[8,128]{1,0:T(8,128)S(1)}) custom-call(f32[1,128]{1,0:T(1,128)S(1)} %add.120.line, s32[1,2048]{1,0:T(1,128)S(1)} %get-tuple-element.309.cells, f32[1,2048]{1,0:T(1,128)S(1)} %get-tuple-element.307.row_frac, f32[1,2048]{1,0:T(1,128)S(1)} %get-tuple-element.308.col_frac, ...), custom_call_target="tpu_custom_call" | custom-call | tf_op jit(solution)/shard_map/finish/pallas_call | solution.py:455
  126.0 0.7 compare_reduce_fusion
  127.4 0.0 copy-start.22
  127.4 0.2 while.28
  127.7 6.5 %all-to-all-start.1 = ((f32[16,8,128]{2,1,0:T(8,128)}), f32[16,8,128]{2,1,0:T(8,128)S(1)}, u32[]{:S(2)}, u32[]{:S(2)}) async-start(f32[16,8,128]{2,1,0:T(8,128)} %bitcast.103), calls=%async_computation.1 | async-start | bytes 131072 | tf_op jit(solution)/shard_map/all_to_all | solution.py:631
  134.2 7.6 %all-to-all-done.1 = f32[16,8,128]{2,1,0:T(8,128)S(1)} async-done(((f32[16,8,128]{2,1,0:T(8,128)}), f32[16,8,128]{2,1,0:T(8,128)S(1)}, u32[]{:S(2)}, u32[]{:S(2)}) %all-to-all-start.1) | async-done | bytes 65568 | tf_op jit(solution)/shard_map/all_to_all | solution.py:631
  141.8 1.6 %fusion.23 = f32[1,1,16,8,128]{4,3,2,1,0:T(8,128)} fusion(s32[1,1,16,8,128]{4,3,2,1,0:T(8,128)} %param.27, f32[16,8,128]{2,1,0:T(8,128)S(1)} %all-to-all-done.1, s32[1,1,16,8,128]{4,3,2,1,0:T(8,128)} %param.26, f32[16,128]{1,0:T(8,128)S(1)} %copy-done.17, f32[8]{0:T(128)S(1)} %subtract_log_fusion, f32[16,128]{1,0:T(8,128)S(1)} %copy-done.16), kind=kLoop, calls=%fused_computation.85 | loop fusion | flops 245760 | bytes 278560 | tf_op jit(solution)/shard_map/broadcast_in_dim | solution.py:645
  (42 shorter events, 0.1 us)
Async XLA Ops:
  0.6 5.6 %copy-start.6 = (f32[8,16,2048]{2,1,0:T(8,128)S(1)}, f32[8,16,2048]{2,1,0:T(8,128)}, u32[]{:S(2)}) copy-start(f32[8,16,2048]{2,1,0:T(8,128)} %refs_1_.3) | copy-start | bytes 3145732
  0.6 5.6 %copy-start.10 = (f32[8,16,2048]{2,1,0:T(8,128)S(1)}, f32[8,16,2048]{2,1,0:T(8,128)}, u32[]{:S(2)}) copy-start(f32[8,16,2048]{2,1,0:T(8,128)} %refs_2_.3) | copy-start | bytes 3145732
  0.7 5.6 %copy-start.11 = (f32[8,16,2048]{2,1,0:T(8,128)S(1)}, f32[8,16,2048]{2,1,0:T(8,128)}, u32[]{:S(2)}) copy-start(f32[8,16,2048]{2,1,0:T(8,128)} %refs_3_.3) | copy-start | bytes 3145732
  2.7 8.6 %collective-permute-start.10 = (f32[16,8,128]{2,1,0:T(8,128)}, f32[16,8,128]{2,1,0:T(8,128)S(1)}, u32[]{:S(2)}, u32[]{:S(2)}) collective-permute-start(f32[16,8,128]{2,1,0:T(8,128)} %get-tuple-element.160), channel_id=1, source_target_pairs={{0,1},{1,2},{2,3},{3,4},{4,5},{5,6},{6,7},{7,0},{8,9},{9,10},{10,1... | collective-permute-start | bytes 196616 | tf_op jit(solution)/shard_map/ppermute | solution.py:541
  2.7 8.6 %collective-permute-start.11 = (f32[16,8,128]{2,1,0:T(8,128)}, f32[16,8,128]{2,1,0:T(8,128)S(1)}, u32[]{:S(2)}, u32[]{:S(2)}) collective-permute-start(f32[16,8,128]{2,1,0:T(8,128)} %get-tuple-element.161), channel_id=1, source_target_pairs={{0,7},{1,0},{2,1},{3,2},{4,3},{5,4},{6,5},{7,6},{8,15},{9,8},{10,9... | collective-permute-start | bytes 196616 | tf_op jit(solution)/shard_map/ppermute | solution.py:541
  6.3 4.3 %copy-start.19 = (s32[1,1,16,128]{3,2,1,0:T(8,128)S(1)}, s32[1,1,16,128]{3,2,1,0:T(8,128)}, u32[]{:S(2)}) copy-start(s32[1,1,16,128]{3,2,1,0:T(8,128)} %param.22) | copy-start | bytes 24580
  6.3 4.3 %copy-start.18 = (f32[1,1,16,2,128]{4,3,2,1,0:T(2,128)S(1)}, f32[1,1,16,2,128]{4,3,2,1,0:T(2,128)}, u32[]{:S(2)}) copy-start(f32[1,1,16,2,128]{4,3,2,1,0:T(2,128)} %param.23) | copy-start | bytes 49156
  10.6 29.0 %copy-start = (f32[16,8,2048]{2,1,0:T(8,128)S(1)}, f32[16,8,2048]{2,1,0:T(8,128)}, u32[]{:S(2)}) copy-start(f32[16,8,2048]{2,1,0:T(8,128)} %get-tuple-element.170.refs_6_) | copy-start | bytes 3145732
  11.4 1.1 copy-start.4
  12.5 1.1 copy-start.5
  15.5 24.1 %collective-permute-start.12 = (f32[12,8,2176]{2,1,0:T(8,128)}, f32[12,8,2176]{2,1,0:T(8,128)S(1)}, u32[]{:S(2)}, u32[]{:S(2)}) collective-permute-start(f32[12,8,2176]{2,1,0:T(8,128)} %get-tuple-element.168), channel_id=1, source_target_pairs={{0,8},{8,16},{16,24},{24,32},{32,40},{40,48},{48,56},{56,64},{64,7... | collective-permute-start | bytes 2506760 | tf_op jit(solution)/shard_map/ppermute | solution.py:541
  17.0 22.6 %collective-permute-start.13 = (f32[12,8,2176]{2,1,0:T(8,128)}, f32[12,8,2176]{2,1,0:T(8,128)S(1)}, u32[]{:S(2)}, u32[]{:S(2)}) collective-permute-start(f32[12,8,2176]{2,1,0:T(8,128)} %get-tuple-element.169), channel_id=1, source_target_pairs={{0,120},{8,0},{16,8},{24,16},{32,24},{40,32},{48,40},{56,48},{64,5... | collective-permute-start | bytes 2506760 | tf_op jit(solution)/shard_map/ppermute | solution.py:541
  22.0 17.6 %all-to-all-start = ((f32[16,3,128]{2,1,0:T(4,128)}), f32[16,3,128]{2,1,0:T(4,128)S(1)}, u32[]{:S(2)}, u32[]{:S(2)}) async-start(f32[16,3,128]{2,1,0:T(4,128)} %pad_maximum_fusion.23), calls=%async_computation | async-start | bytes 65536 | tf_op jit(solution)/shard_map/all_to_all | solution.py:596
  39.6 75.7 %copy-start.14 = (s32[16,1,128]{2,1,0:T(1,128)}, s32[16,1,128]{2,1,0:T(1,128)S(1)}, u32[]{:S(2)}) copy-start(s32[16,1,128]{2,1,0:T(1,128)S(1)} %get-tuple-element.310) | copy-start | bytes 24580
  39.6 1.2 copy-start.1
  40.9 1.2 copy-start.2
  42.1 1.2 copy-start.3
  47.8 9.9 %collective-permute-start.14 = (f32[4,8,2176]{2,1,0:T(8,128)S(1)}, f32[4,8,2176]{2,1,0:T(8,128)S(1)}, u32[]{:S(2)}, u32[]{:S(2)}) collective-permute-start(f32[4,8,2176]{2,1,0:T(8,128)S(1)} %get-tuple-element.174), channel_id=1, source_target_pairs={{0,8},{8,16},{16,24},{24,32},{32,40},{40,48},{48,56},{56,64},{64,7... | collective-permute-start | bytes 835592 | tf_op jit(solution)/shard_map/ppermute | solution.py:541
  48.7 9.1 %collective-permute-start.15 = (f32[4,8,2176]{2,1,0:T(8,128)S(1)}, f32[4,8,2176]{2,1,0:T(8,128)S(1)}, u32[]{:S(2)}, u32[]{:S(2)}) collective-permute-start(f32[4,8,2176]{2,1,0:T(8,128)S(1)} %get-tuple-element.175), channel_id=1, source_target_pairs={{0,120},{8,0},{16,8},{24,16},{32,24},{40,32},{48,40},{56,48},{64,5... | collective-permute-start | bytes 835592 | tf_op jit(solution)/shard_map/ppermute | solution.py:541
  61.8 9.9 %collective-permute-start.16 = (f32[4,8,2176]{2,1,0:T(8,128)S(1)}, f32[4,8,2176]{2,1,0:T(8,128)S(1)}, u32[]{:S(2)}, u32[]{:S(2)}) collective-permute-start(f32[4,8,2176]{2,1,0:T(8,128)S(1)} %get-tuple-element.182), channel_id=1, source_target_pairs={{0,8},{8,16},{16,24},{24,32},{32,40},{40,48},{48,56},{56,64},{64,7... | collective-permute-start | bytes 835592 | tf_op jit(solution)/shard_map/ppermute | solution.py:541
  61.9 9.9 %collective-permute-start.17 = (f32[4,8,2176]{2,1,0:T(8,128)S(1)}, f32[4,8,2176]{2,1,0:T(8,128)S(1)}, u32[]{:S(2)}, u32[]{:S(2)}) collective-permute-start(f32[4,8,2176]{2,1,0:T(8,128)S(1)} %get-tuple-element.183), channel_id=1, source_target_pairs={{0,120},{8,0},{16,8},{24,16},{32,24},{40,32},{48,40},{56,48},{64,5... | collective-permute-start | bytes 835592 | tf_op jit(solution)/shard_map/ppermute | solution.py:541
  76.0 10.2 %collective-permute-start.18 = (f32[4,8,2176]{2,1,0:T(8,128)S(1)}, f32[4,8,2176]{2,1,0:T(8,128)S(1)}, u32[]{:S(2)}, u32[]{:S(2)}) collective-permute-start(f32[4,8,2176]{2,1,0:T(8,128)S(1)} %get-tuple-element.187), channel_id=1, source_target_pairs={{0,8},{8,16},{16,24},{24,32},{32,40},{40,48},{48,56},{56,64},{64,7... | collective-permute-start | bytes 835592 | tf_op jit(solution)/shard_map/ppermute | solution.py:541
  76.1 10.1 %collective-permute-start.19 = (f32[4,8,2176]{2,1,0:T(8,128)S(1)}, f32[4,8,2176]{2,1,0:T(8,128)S(1)}, u32[]{:S(2)}, u32[]{:S(2)}) collective-permute-start(f32[4,8,2176]{2,1,0:T(8,128)S(1)} %get-tuple-element.188), channel_id=1, source_target_pairs={{0,120},{8,0},{16,8},{24,16},{32,24},{40,32},{48,40},{56,48},{64,5... | collective-permute-start | bytes 835592 | tf_op jit(solution)/shard_map/ppermute | solution.py:541
  86.2 22.2 %copy-start.20 = (s32[1,1,16,128]{3,2,1,0:T(8,128)S(1)}, s32[1,1,16,128]{3,2,1,0:T(8,128)}, u32[]{:S(2)}) copy-start(s32[1,1,16,128]{3,2,1,0:T(8,128)} %param.25) | copy-start | bytes 24580
  86.2 28.4 %copy-start.21 = (s32[1,1,16]{2,1,0:T(1,128)S(1)}, s32[1,1,16]{2,1,0:T(1,128)}, u32[]{:S(2)}) copy-start(s32[1,1,16]{2,1,0:T(1,128)} %param.24) | copy-start | bytes 196
  89.6 1.1 collective-permute-start.20
  90.8 4.6 %collective-permute-start.21 = (f32[1,128]{1,0:T(1,128)S(1)}, f32[1,128]{1,0:T(1,128)S(1)}, u32[]{:S(2)}, u32[]{:S(2)}) collective-permute-start(f32[1,128]{1,0:T(1,128)S(1)} %add.114), channel_id=1, source_target_pairs={{0,2},{1,3},{2,0},{3,1},{4,6},{5,7},{6,4},{7,5},{8,10},{9,11},{10,... | collective-permute-start | bytes 1544 | tf_op jit(solution)/shard_map/ppermute | solution.py:549
  95.4 4.8 %collective-permute-start.22 = (f32[1,128]{1,0:T(1,128)S(1)}, f32[1,128]{1,0:T(1,128)S(1)}, u32[]{:S(2)}, u32[]{:S(2)}) collective-permute-start(f32[1,128]{1,0:T(1,128)S(1)} %add.115), channel_id=1, source_target_pairs={{0,6},{1,7},{2,4},{3,5},{4,2},{5,3},{6,0},{7,1},{8,14},{9,15},{10,... | collective-permute-start | bytes 1544 | tf_op jit(solution)/shard_map/ppermute | solution.py:549
  100.1 3.5 %collective-permute-start.23 = (f32[1,128]{1,0:T(1,128)S(1)}, f32[1,128]{1,0:T(1,128)S(1)}, u32[]{:S(2)}, u32[]{:S(2)}) collective-permute-start(f32[1,128]{1,0:T(1,128)S(1)} %add.116), channel_id=1, source_target_pairs={{0,8},{8,0},{16,24},{24,16},{32,40},{40,32},{48,56},{56,48},{64,72... | collective-permute-start | bytes 1544 | tf_op jit(solution)/shard_map/ppermute | solution.py:549
  103.7 4.8 %collective-permute-start.24 = (f32[1,128]{1,0:T(1,128)S(1)}, f32[1,128]{1,0:T(1,128)S(1)}, u32[]{:S(2)}, u32[]{:S(2)}) collective-permute-start(f32[1,128]{1,0:T(1,128)S(1)} %add.117), channel_id=1, source_target_pairs={{0,24},{8,16},{16,8},{24,0},{32,56},{40,48},{48,40},{56,32},{64,88... | collective-permute-start | bytes 1544 | tf_op jit(solution)/shard_map/ppermute | solution.py:549
  108.4 3.5 %collective-permute-start.25 = (f32[1,128]{1,0:T(1,128)S(1)}, f32[1,128]{1,0:T(1,128)S(1)}, u32[]{:S(2)}, u32[]{:S(2)}) collective-permute-start(f32[1,128]{1,0:T(1,128)S(1)} %add.118), channel_id=1, source_target_pairs={{0,32},{8,40},{16,48},{24,56},{32,0},{40,8},{48,16},{56,24},{64,96... | collective-permute-start | bytes 1544 | tf_op jit(solution)/shard_map/ppermute | solution.py:549
  112.0 4.9 %collective-permute-start.26 = (f32[1,128]{1,0:T(1,128)S(1)}, f32[1,128]{1,0:T(1,128)S(1)}, u32[]{:S(2)}, u32[]{:S(2)}) collective-permute-start(f32[1,128]{1,0:T(1,128)S(1)} %add.119), channel_id=1, source_target_pairs={{0,96},{8,104},{16,112},{24,120},{32,64},{40,72},{48,80},{56,88},{... | collective-permute-start | bytes 1544 | tf_op jit(solution)/shard_map/ppermute | solution.py:549
  116.9 10.4 %copy-start.12 = (f32[8,16,2048]{2,1,0:T(8,128)S(1)}, f32[8,16,2048]{2,1,0:T(8,128)}, u32[]{:S(2)}) copy-start(f32[8,16,2048]{2,1,0:T(8,128)} %refs_0_.3) | copy-start | bytes 3145732
  117.0 10.4 %copy-start.15 = (s32[16,1,128]{2,1,0:T(1,128)S(1)}, s32[16,1,128]{2,1,0:T(1,128)}, u32[]{:S(2)}) copy-start(s32[16,1,128]{2,1,0:T(1,128)} %copy-done.14) | copy-start | bytes 24580
  127.4 6.8 %copy-start.22 = (f32[8]{0:T(128)S(1)}, f32[8]{0:T(128)}, u32[]{:S(2)}) copy-start(f32[8]{0:T(128)} %param.21) | copy-start | bytes 100
  127.4 14.4 %copy-start.16 = (f32[16,128]{1,0:T(8,128)S(1)}, f32[16,128]{1,0:T(8,128)}, u32[]{:S(2)}) copy-start(f32[16,128]{1,0:T(8,128)} %convert_bitcast_fusion) | copy-start | bytes 24580
  127.4 14.4 %copy-start.17 = (f32[16,128]{1,0:T(8,128)S(1)}, f32[16,128]{1,0:T(8,128)}, u32[]{:S(2)}) copy-start(f32[16,128]{1,0:T(8,128)} %fusion.24) | copy-start | bytes 24580
  127.7 14.2 %all-to-all-start.1 = ((f32[16,8,128]{2,1,0:T(8,128)}), f32[16,8,128]{2,1,0:T(8,128)S(1)}, u32[]{:S(2)}, u32[]{:S(2)}) async-start(f32[16,8,128]{2,1,0:T(8,128)} %bitcast.103), calls=%async_computation.1 | async-start | bytes 131072 | tf_op jit(solution)/shard_map/all_to_all | solution.py:631

commit v6 on v5

--- a/solution.py
+++ b/solution.py
@@ -76,57 +76,39 @@
     return jnp.where(lane < SIDE, after * flags[1], 0.0) + jnp.where(lane >= LANES - SIDE, before * flags[0], 0.0)
 
 
-def prepare_kernel(*refs):
-    fields, outs, (top, bottom) = refs[0:4], refs[4:8], refs[8:]
-    rows = fields[0].shape[1]
+def prepare_kernel(flags, left, right, *refs):
+    fields, outs, (to_up, to_down) = refs[0:4], refs[4:8], refs[8:]
+    rows, cols = fields[0].shape[1:]
+
+    def place(a, at, block):
+        outs[a][:, :, at] = block
+        base, depth = sum(DEPTHS[:a]), DEPTHS[a]
+        to_up[base : base + depth, :, at] = block[:depth]
+        to_down[base : base + depth, :, at] = block[rows - depth :]
+
+    def step(c, carry):
+        at = pl.ds(pl.multiple_of(c * LANES, LANES), LANES)
+        for a in range(4):
+            place(a, at, shaped(a, jnp.swapaxes(fields[a][:, :, at], 0, 1)))
+        return carry
+
+    lax.fori_loop(0, cols // LANES, step, 0, unroll=4)
     for a in range(4):
-        base, depth = sum(DEPTHS[:a]), DEPTHS[a]
-        for c in range(0, fields[a].shape[2], LANES):
-            at = slice(c, c + LANES)
-            block = shaped(a, jnp.swapaxes(fields[a][:, :, at], 0, 1))
-            outs[a][:, :, at] = block
-            top[base : base + depth, :, at] = block[:depth]
-            bottom[base : base + depth, :, at] = block[rows - depth :]
-
-
-def prepare(fields):
+        place(a, slice(cols, cols + LANES), extra_tile(a, flags, left, right))
+
+
+def prepare(flags, left, right, fields):
     rows, cols = fields[0].shape[1:]
+    wide = cols + LANES
     f32 = jnp.float32
-    step = 4 * LANES
-    edge = sum(DEPTHS)
     return pl.pallas_call(
         prepare_kernel,
-        grid=(cols // step,),
-        in_specs=[pl.BlockSpec((F, rows, step), lambda i: (0, 0, i))] * 4,
-        out_specs=[pl.BlockSpec((rows, F, step), lambda i: (0, 0, i))] * 4
-        + [pl.BlockSpec((edge, F, step), lambda i: (0, 0, i))] * 2,
-        out_shape=[pltpu.HBM((rows, F, cols), f32)] * 4 + [pltpu.HBM((edge, F, cols), f32)] * 2,
+        in_specs=[SMEM] + [VMEM] * 6,
+        out_specs=[VMEM] * 6,
+        out_shape=[pltpu.VMEM((rows, F, wide), f32)] * 4 + [jax.ShapeDtypeStruct((sum(DEPTHS), F, wide), f32)] * 2,
         compiler_params=PARAMS,
         name="prepare",
-    )(*fields)
-
-
-def sides_kernel(flags, left, right, top, bottom, to_up, to_down):
-    rows, cols = left.shape[0], top.shape[2]
-    to_up[:, :, :cols] = top[...]
-    to_down[:, :, :cols] = bottom[...]
-    for a in range(4):
-        base, depth = sum(DEPTHS[:a]), DEPTHS[a]
-        extra = extra_tile(a, flags, left, right)
-        to_up[base : base + depth, :, cols:] = extra[:depth]
-        to_down[base : base + depth, :, cols:] = extra[rows - depth :]
-
-
-def sides(flags, left, right, top, bottom):
-    edge, _, cols = top.shape
-    return pl.pallas_call(
-        sides_kernel,
-        in_specs=[SMEM] + [VMEM] * 4,
-        out_specs=[VMEM] * 2,
-        out_shape=[jax.ShapeDtypeStruct((edge, F, cols + LANES), jnp.float32)] * 2,
-        compiler_params=PARAMS,
-        name="sides",
-    )(flags, left, right, top, bottom)
+    )(flags, left, right, *fields)
 
 
 def walk(ref, r, count, wide):
@@ -167,7 +149,6 @@
     take = lambda n: [refs.pop(0) for _ in range(n)]
     flags, mask, up, down = take(4)
     if first:
-        left, right = take(2)
         mains = take(4)
     else:
         own, kap, tau, cur, older, old = take(6)
@@ -185,12 +166,11 @@
     work = (current, kap, tau, cur)
     if first:
         for a, source in enumerate(mains):
-            work[a][own_low:own_high, :, :cols] = source[...]
-            work[a][own_low:own_high, :, cols:] = extra_tile(a, flags, left, right)
+            work[a][own_low:own_high] = source[...]
     else:
         current[own_low:own_high] = own[...]
     base = 0
-    for a, depth in enumerate(DEPTHS if first else (PAD,)):
+    for a, depth in enumerate(DEPTHS if first else (up.shape[0],)):
         for i in range(depth):
             work[a][own_low - depth + i] = up[base + i] * flags[2]
             work[a][own_high + i] = down[base + i] * flags[3]
@@ -215,7 +195,8 @@
                 out.append(new * mask[...] if at.start == cols else new)
             yield at, out
 
-    scale(current, own_low - 3, own_high + 3)
+    reach = 2 if last else 3
+    scale(current, own_low - reach, own_high + reach)
     for r, flag, inner in ((own_low - 2, flags[2], 1), (own_high, flags[3], 0)):
         for at, new in image(current, r):
             for i in range(2):
@@ -288,8 +269,9 @@
         return carry[0] + cross, carry[1] + square
 
     sums[2], sums[3] = pairs(own_low, own_high, second_rows, (zero, zero))
-    to_up[...] = newest[:PAD]
-    to_down[...] = newest[rows - PAD :]
+    depth = to_up.shape[0]
+    to_up[...] = newest[:depth]
+    to_down[...] = newest[rows - depth :]
 
 
 def phase(p, rows, cols, flags, mask, up, down, state, earlier=()):
@@ -302,9 +284,10 @@
         out_shape = [jax.ShapeDtypeStruct((1, LANES), f32)] + out_shape
     else:
         out_shape += [pltpu.VMEM((rows, F, wide), f32)]
-        out_shape += [jax.ShapeDtypeStruct((PAD, F, wide), f32)] * 2
+        depth = PAD - 1 if p == ITERS // 2 - 2 else PAD
+        out_shape += [jax.ShapeDtypeStruct((depth, F, wide), f32)] * 2
         out_shape += [jax.ShapeDtypeStruct((5 if first else 4, F, LANES), f32)]
-    operands = list(state) if first else [held(x) for x in state]
+    operands = [held(x) for x in state]
     return pl.pallas_call(
         functools.partial(phase_kernel, p, rows, cols),
         in_specs=[SMEM] + [VMEM] * (3 + len(operands) + len(earlier)),
@@ -386,7 +369,7 @@
         functools.partial(columns_hot_kernel, cols),
         in_specs=[VMEM],
         out_specs=VMEM,
-        out_shape=pltpu.VMEM((cols + LANES, cells.shape[1]), jnp.bfloat16),
+        out_shape=pltpu.VMEM((cols, cells.shape[1]), jnp.bfloat16),
         compiler_params=PARAMS,
         name="columns_hot",
     )(cells)
@@ -419,11 +402,11 @@
             total = term if total is None else total + term
         total = jnp.concatenate([total, jnp.zeros((1, F, LANES), jnp.float32)], axis=0)
         turned = pltpu.roll(total, LANES - 1, 2)
-        split(total, at, 0)
-        split(jnp.where(lane == LANES - 1, after, turned), at, 2 * tall)
 
         @pl.when(c < cols // LANES)
         def _():
+            split(total, at, 0)
+            split(jnp.where(lane == LANES - 1, after, turned), at, 2 * tall)
             latent[:, :, at] = jnp.swapaxes(total[:rows], 0, 1)
 
         return turned
@@ -462,7 +445,7 @@
             jax.ShapeDtypeStruct((F, LANES), f32),
         ],
         scratch_shapes=[
-            pltpu.VMEM((4 * (rows + 2) * F, wide), jnp.bfloat16),
+            pltpu.VMEM((4 * (rows + 2) * F, cols), jnp.bfloat16),
             pltpu.VMEM((ITERS, F, LANES), f32),
         ],
         compiler_params=PARAMS,
@@ -585,20 +568,17 @@
 
     fields = (right_side, kappa_field, tau_field, curvature)
     to_left, to_right = columns_of(fields)
+    cells = site_cells[0, 0]
+    sent = jnp.concatenate([cells.astype(jnp.float32)[:, None], site_offsets[0, 0]], axis=1)
+    sent, to_left, to_right = lax.optimization_barrier((sent, to_left, to_right))
     from_right = turned(to_left, "field", -1)
     from_left = turned(to_right, "field", 1)
-    *mains, top, bottom = prepare(fields)
-    to_up, to_down = sides(flags, from_left, from_right, top, bottom)
-
-    cells = site_cells[0, 0]
-    sent = jnp.concatenate([cells.astype(jnp.float32)[:, None], site_offsets[0, 0]], axis=1)
-    sent, to_up, to_down = lax.optimization_barrier((sent, to_up, to_down))
     got = lax.all_to_all(sent, "tile", split_axis=0, concat_axis=0, tiled=True)
+    flags, got = lax.optimization_barrier((flags, got))
     got_cells = got[:, 0].astype(jnp.int32)
     got_row, got_col = got[:, 1], got[:, 2]
     sites = (got_cells.reshape(1, -1), got_row.reshape(1, -1), got_col.reshape(1, -1))
-
-    mask, got_row = lax.optimization_barrier((mask, got_row))
+    *mains, to_up, to_down = prepare(flags, from_left, from_right, fields)
     common = (rows, cols, flags, mask)
 
     def exchanged(to_up, to_down):
@@ -606,7 +586,7 @@
 
     up, down = exchanged(to_up, to_down)
     *coefs, older, old, own, to_up, to_down, part = phase(
-        0, *common, up, down, (from_left, from_right, *mains)
+        0, *common, up, down, mains
     )
     basis, sums = [older, old], [part]
     for p in range(1, ITERS // 2 - 1):

time: 144 us -> 144 us (level)
  local copies, waits for them, and re-layouts: 6.58 us -> 0.62 us
  starting transfers between devices: 43.4 us -> 47.9 us
  waiting for transfers between devices: 51 us -> 54.9 us
  Pallas kernels: 35 us -> 31.6 us
  other arithmetic: 5.55 us -> 7.02 us
    ppermute x10, waiting for transfers between devices: 13.2 us -> 27.6 us  [turned(): return lax.ppermute(x, axis, [(i, (i + by) % size) for i in range(size)])]
    all_to_all x1, waiting for transfers between devices: 13.2 us -> 4.31 us  [local(): got = lax.all_to_all(sent, 'tile', split_axis=0, concat_axis=0, tiled=True)]
    unnamed x38 -> x16, local copies, waits for them, and re-layouts: 6 us -> 0.03 us
    pallas_call x2 -> x1, Pallas kernels: 6.15 us -> 2.45 us  [prepare(): pl.pallas_call(prepare_kernel, in_specs=[SMEM] + [VMEM] * 6, out_specs=[V...]
    all_to_all x1, starting transfers between devices: 3.73 us -> 7.12 us  [local(): got = lax.all_to_all(sent, 'tile', split_axis=0, concat_axis=0, tiled=True)]
    ppermute x6, waiting for transfers between devices: 15.8 us -> 14.2 us  [summed(): lax.ppermute(x, axis, [(i, other(i, stride, by)) for i in range(size)])]
  transfers between devices with their start and end apart: 19 -> 19, of which waited for: 11 -> 12; matrix products, arithmetic and copies ran while one was open for 3% -> 2% of each run, Pallas kernels for 4% -> 1%
where the time goes in v6:
time: 144 us
  waiting for transfers between devices  54.9 us (38%)
  starting transfers between devices  47.9 us (33%)
  Pallas kernels  31.6 us (22%)
  other arithmetic  7.02 us (5%)
  between operations  1.49 us (1%)
    ppermute x10, waiting for transfers between devices, turned(): return lax.ppermute(x, axis, [(i, (i + by) % size) for i in range(size)])  27.6 us
    ppermute x10, starting transfers between devices, turned(): return lax.ppermute(x, axis, [(i, (i + by) % size) for i in range(size)])  25.5 us
    pallas_call x4, Pallas kernels, phase(): pl.pallas_call(functools.partial(phase_kernel, p, rows, cols), in_specs=[...  16.7 us
    ppermute x6, waiting for transfers between devices, summed(): lax.ppermute(x, axis, [(i, other(i, stride, by)) for i in range(size)])  14.2 us
    pallas_call x1, Pallas kernels, finish(): pl.pallas_call(functools.partial(finish_kernel, rows, cols), in_specs=[VM...  8.94 us
    ppermute x6, starting transfers between devices, summed(): lax.ppermute(x, axis, [(i, other(i, stride, by)) for i in range(size)])  8.71 us
    all_to_all x1, waiting for transfers between devices, local(): lax.all_to_all(predictor, 'tile', split_axis=0, concat_axis=0, tiled=True)  7.64 us
    all_to_all x1, starting transfers between devices, local(): got = lax.all_to_all(sent, 'tile', split_axis=0, concat_axis=0, tiled=True)  7.12 us
  transfers between devices with their start and end apart: 19, of which 12 were waited for; matrix products, arithmetic and copies ran while one was open for 2% of the time, Pallas kernels for 1%

profile of v6, /device:TPU:0, one launch (start us, length us, event | category | flops | bytes accessed | tf_op | source)
XLA Modules:
  0.0 143.7 jit_solution(6975235245994158378)
XLA Ops:
  0.6 0.7 convert_element_type.56
  1.3 1.3 pad_maximum_fusion.23
  2.7 2.0 %columns.1 = (f32[16,8,128]{2,1,0:T(8,128)}, f32[16,8,128]{2,1,0:T(8,128)}) custom-call(f32[8,16,2048]{2,1,0:T(8,128)} %refs_0_.3, f32[8,16,2048]{2,1,0:T(8,128)} %refs_1_.3, f32[8,16,2048]{2,1,0:T(8,128)} %refs_2_.3, f32[8,16,2048]{2,1,0:T(8,128)} %refs_3_.3, f32[8,16,2048]{2,1,0:T(8,128)} %refs_0_.3, f32[8,16,2048]{2,1,0:T(8,128)} %refs_1_.3, ...), custom_call_target="tpu_custom_call" | custom-call | tf_op jit(solution)/shard_map/columns/pallas_call | solution.py:48
  4.7 7.1 %all-to-all-start = ((f32[16,3,128]{2,1,0:T(4,128)}), f32[16,3,128]{2,1,0:T(4,128)S(1)}, u32[]{:S(2)}, u32[]{:S(2)}) async-start(f32[16,3,128]{2,1,0:T(4,128)} %pad_maximum_fusion.23), calls=%async_computation | async-start | bytes 65536 | tf_op jit(solution)/shard_map/all_to_all | solution.py:576
  11.8 0.0 collective-permute-start.10
  11.9 3.2 %collective-permute-start.11 = (f32[16,8,128]{2,1,0:T(8,128)}, f32[16,8,128]{2,1,0:T(8,128)S(1)}, u32[]{:S(2)}, u32[]{:S(2)}) collective-permute-start(f32[16,8,128]{2,1,0:T(8,128)} %get-tuple-element.163), channel_id=1, source_target_pairs={{0,7},{1,0},{2,1},{3,2},{4,3},{5,4},{6,5},{7,6},{8,15},{9,8},{10,9... | collective-permute-start | bytes 196616 | tf_op jit(solution)/shard_map/ppermute | solution.py:524
  15.1 0.1 add_convert_fusion.flags.refs_0_
  15.1 4.3 %all-to-all-done = f32[16,3,128]{2,1,0:T(4,128)S(1)} async-done(((f32[16,3,128]{2,1,0:T(4,128)}), f32[16,3,128]{2,1,0:T(4,128)S(1)}, u32[]{:S(2)}, u32[]{:S(2)}) %all-to-all-start) | async-done | bytes 24608 | tf_op jit(solution)/shard_map/all_to_all | solution.py:576
  19.5 0.0 collective-permute-done.10.left
  19.5 0.0 collective-permute-done.11.right
  19.5 0.0 copy-done
  19.5 0.0 copy-done.5
  19.5 0.0 copy-done.7
  19.5 2.4 %prepare.1 = (f32[16,8,2176]{2,1,0:T(8,128)S(1)}, f32[16,8,2176]{2,1,0:T(8,128)S(1)}, f32[16,8,2176]{2,1,0:T(8,128)S(1)}, f32[16,8,2176]{2,1,0:T(8,128)S(1)}, f3...) custom-call(f32[4]{0:T(128)S(1)} %add_convert_fusion.flags.refs_0_, f32[16,8,128]{2,1,0:T(8,128)S(1)} %collective-permute-done.10.left, ...), custom_call_target="tpu_custom_call" | custom-call | tf_op jit(solution)/shard_map/prepare/pallas_call | solution.py:104
  21.9 0.6 collective-permute-start.12
  22.6 4.8 %collective-permute-start.13 = (f32[12,8,2176]{2,1,0:T(8,128)S(1)}, f32[12,8,2176]{2,1,0:T(8,128)S(1)}, u32[]{:S(2)}, u32[]{:S(2)}) collective-permute-start(f32[12,8,2176]{2,1,0:T(8,128)S(1)} %get-tuple-element.165), channel_id=1, source_target_pairs={{0,120},{8,0},{16,8},{24,16},{32,24},{40,32},{48,40},{56,48},{64,5... | collective-permute-start | bytes 2506760 | tf_op jit(solution)/shard_map/ppermute | solution.py:524
  27.4 0.6 fusion.30
  27.9 0.6 compare_select_fusion.4
  28.6 0.7 broadcast_select_fusion.refs_1_
  29.3 15.2 %collective-permute-done.12.refs_2_ = f32[12,8,2176]{2,1,0:T(8,128)S(1)} collective-permute-done((f32[12,8,2176]{2,1,0:T(8,128)S(1)}, f32[12,8,2176]{2,1,0:T(8,128)S(1)}, u32[]{:S(2)}, u32[]{:S(2)}) %collective-permute-start.12) | collective-permute-done | bytes 835616 | tf_op jit(solution)/shard_map/ppermute | solution.py:524
  44.4 0.0 collective-permute-done.13.refs_3_
  44.4 4.5 %phase0.1 = (f32[24,8,2176]{2,1,0:T(8,128)S(1)}, f32[24,8,2176]{2,1,0:T(8,128)S(1)}, f32[24,8,2176]{2,1,0:T(8,128)S(1)}, f32[24,8,2176]{2,1,0:T(8,128)S(1)}, f32...) custom-call(f32[4]{0:T(128)S(1)} %add_convert_fusion.flags.refs_0_, ...), custom_call_target="tpu_custom_call" | custom-call | tf_op jit(solution)/shard_map/phase0/pallas_call | solution.py:291
  48.9 0.1 collective-permute-start.14
  49.0 5.3 %collective-permute-start.15 = (f32[4,8,2176]{2,1,0:T(8,128)S(1)}, f32[4,8,2176]{2,1,0:T(8,128)S(1)}, u32[]{:S(2)}, u32[]{:S(2)}) collective-permute-start(f32[4,8,2176]{2,1,0:T(8,128)S(1)} %get-tuple-element.171), channel_id=1, source_target_pairs={{0,120},{8,0},{16,8},{24,16},{32,24},{40,32},{48,40},{56,48},{64,5... | collective-permute-start | bytes 835592 | tf_op jit(solution)/shard_map/ppermute | solution.py:524
  54.4 4.5 %collective-permute-done.14.refs_2_ = f32[4,8,2176]{2,1,0:T(8,128)S(1)} collective-permute-done((f32[4,8,2176]{2,1,0:T(8,128)S(1)}, f32[4,8,2176]{2,1,0:T(8,128)S(1)}, u32[]{:S(2)}, u32[]{:S(2)}) %collective-permute-start.14) | collective-permute-done | bytes 278560 | tf_op jit(solution)/shard_map/ppermute | solution.py:524
  58.9 0.0 collective-permute-done.15.refs_3_
  58.9 4.5 %phase1.1 = (f32[24,8,2176]{2,1,0:T(8,128)S(1)}, f32[18,8,2176]{2,1,0:T(8,128)S(1)}, f32[16,8,2176]{2,1,0:T(8,128)S(1)}, f32[4,8,2176]{2,1,0:T(8,128)S(1)}, f32[...) custom-call(f32[4]{0:T(128)S(1)} %add_convert_fusion.flags.refs_0_, f32[8,128]{1,0:T(8,128)S(1)} %broadcast_select_fusion.refs_1_, ...), custom_call_target="tpu_custom_call" | custom-call | tf_op jit(solution)/shard_map/phase1/pallas_call | solution.py:291
  63.4 0.1 collective-permute-start.16
  63.5 5.6 %collective-permute-start.17 = (f32[4,8,2176]{2,1,0:T(8,128)S(1)}, f32[4,8,2176]{2,1,0:T(8,128)S(1)}, u32[]{:S(2)}, u32[]{:S(2)}) collective-permute-start(f32[4,8,2176]{2,1,0:T(8,128)S(1)} %get-tuple-element.179), channel_id=1, source_target_pairs={{0,120},{8,0},{16,8},{24,16},{32,24},{40,32},{48,40},{56,48},{64,5... | collective-permute-start | bytes 835592 | tf_op jit(solution)/shard_map/ppermute | solution.py:524
  69.1 4.3 %collective-permute-done.16.refs_2_ = f32[4,8,2176]{2,1,0:T(8,128)S(1)} collective-permute-done((f32[4,8,2176]{2,1,0:T(8,128)S(1)}, f32[4,8,2176]{2,1,0:T(8,128)S(1)}, u32[]{:S(2)}, u32[]{:S(2)}) %collective-permute-start.16) | collective-permute-done | bytes 278560 | tf_op jit(solution)/shard_map/ppermute | solution.py:524
  73.4 0.0 collective-permute-done.17.refs_3_
  73.4 4.4 %phase2.1 = (f32[24,8,2176]{2,1,0:T(8,128)S(1)}, f32[18,8,2176]{2,1,0:T(8,128)S(1)}, f32[16,8,2176]{2,1,0:T(8,128)S(1)}, f32[3,8,2176]{2,1,0:T(8,128)S(1)}, f32[...) custom-call(f32[4]{0:T(128)S(1)} %add_convert_fusion.flags.refs_0_, f32[8,128]{1,0:T(8,128)S(1)} %broadcast_select_fusion.refs_1_, ...), custom_call_target="tpu_custom_call" | custom-call | tf_op jit(solution)/shard_map/phase2/pallas_call | solution.py:291
  77.8 0.1 collective-permute-start.18
  77.9 5.7 %collective-permute-start.19 = (f32[3,8,2176]{2,1,0:T(8,128)S(1)}, f32[3,8,2176]{2,1,0:T(8,128)S(1)}, u32[]{:S(2)}, u32[]{:S(2)}) collective-permute-start(f32[3,8,2176]{2,1,0:T(8,128)S(1)} %get-tuple-element.184), channel_id=1, source_target_pairs={{0,120},{8,0},{16,8},{24,16},{32,24},{40,32},{48,40},{56,48},{64,5... | collective-permute-start | bytes 626696 | tf_op jit(solution)/shard_map/ppermute | solution.py:524
  83.6 3.7 %collective-permute-done.18.refs_2_ = f32[3,8,2176]{2,1,0:T(8,128)S(1)} collective-permute-done((f32[3,8,2176]{2,1,0:T(8,128)S(1)}, f32[3,8,2176]{2,1,0:T(8,128)S(1)}, u32[]{:S(2)}, u32[]{:S(2)}) %collective-permute-start.18) | collective-permute-done | bytes 208928 | tf_op jit(solution)/shard_map/ppermute | solution.py:524
  87.2 0.0 collective-permute-done.19.refs_3_
  87.2 3.2 %phase3.1 = (f32[1,128]{1,0:T(1,128)S(1)}, f32[24,8,2176]{2,1,0:T(8,128)S(1)}, f32[18,8,2176]{2,1,0:T(8,128)S(1)}) custom-call(f32[4]{0:T(128)S(1)} %add_convert_fusion.flags.refs_0_, f32[8,128]{1,0:T(8,128)S(1)} %broadcast_select_fusion.refs_1_, f32[3,8,2176]{2,1,0:T(8,128)S(1)} %collective-permute-done.18.refs_2_, ...), custom_call_target="tpu_custom_call" | custom-call | tf_op jit(solution)/shard_map/phase3/pallas_call | solution.py:291
  90.5 0.0 collective-permute-start.20
  90.5 1.1 collective-permute-done.20
  91.6 1.9 %collective-permute-start.21 = (f32[1,128]{1,0:T(1,128)S(1)}, f32[1,128]{1,0:T(1,128)S(1)}, u32[]{:S(2)}, u32[]{:S(2)}) collective-permute-start(f32[1,128]{1,0:T(1,128)S(1)} %add.114), channel_id=1, source_target_pairs={{0,2},{1,3},{2,0},{3,1},{4,6},{5,7},{6,4},{7,5},{8,10},{9,11},{10,... | collective-permute-start | bytes 1544 | tf_op jit(solution)/shard_map/ppermute | solution.py:532
  93.5 1.6 %collective-permute-done.21 = f32[1,128]{1,0:T(1,128)S(1)} collective-permute-done((f32[1,128]{1,0:T(1,128)S(1)}, f32[1,128]{1,0:T(1,128)S(1)}, u32[]{:S(2)}, u32[]{:S(2)}) %collective-permute-start.21) | collective-permute-done | bytes 544 | tf_op jit(solution)/shard_map/ppermute | solution.py:532
  95.2 3.8 %collective-permute-start.22 = (f32[1,128]{1,0:T(1,128)S(1)}, f32[1,128]{1,0:T(1,128)S(1)}, u32[]{:S(2)}, u32[]{:S(2)}) collective-permute-start(f32[1,128]{1,0:T(1,128)S(1)} %add.115), channel_id=1, source_target_pairs={{0,6},{1,7},{2,4},{3,5},{4,2},{5,3},{6,0},{7,1},{8,14},{9,15},{10,... | collective-permute-start | bytes 1544 | tf_op jit(solution)/shard_map/ppermute | solution.py:532
  99.0 1.5 %collective-permute-done.22 = f32[1,128]{1,0:T(1,128)S(1)} collective-permute-done((f32[1,128]{1,0:T(1,128)S(1)}, f32[1,128]{1,0:T(1,128)S(1)}, u32[]{:S(2)}, u32[]{:S(2)}) %collective-permute-start.22) | collective-permute-done | bytes 544 | tf_op jit(solution)/shard_map/ppermute | solution.py:532
  100.5 0.0 collective-permute-start.23
  100.5 3.5 %collective-permute-done.23 = f32[1,128]{1,0:T(1,128)S(1)} collective-permute-done((f32[1,128]{1,0:T(1,128)S(1)}, f32[1,128]{1,0:T(1,128)S(1)}, u32[]{:S(2)}, u32[]{:S(2)}) %collective-permute-start.23) | collective-permute-done | bytes 544 | tf_op jit(solution)/shard_map/ppermute | solution.py:532
  104.1 0.2 collective-permute-start.24
  104.3 4.5 %collective-permute-done.24 = f32[1,128]{1,0:T(1,128)S(1)} collective-permute-done((f32[1,128]{1,0:T(1,128)S(1)}, f32[1,128]{1,0:T(1,128)S(1)}, u32[]{:S(2)}, u32[]{:S(2)}) %collective-permute-start.24) | collective-permute-done | bytes 544 | tf_op jit(solution)/shard_map/ppermute | solution.py:532
  108.8 0.0 collective-permute-start.25
  108.8 0.0 copy-done.14
  108.8 0.6 convert_bitcast_fusion
  109.4 2.9 %collective-permute-done.25 = f32[1,128]{1,0:T(1,128)S(1)} collective-permute-done((f32[1,128]{1,0:T(1,128)S(1)}, f32[1,128]{1,0:T(1,128)S(1)}, u32[]{:S(2)}, u32[]{:S(2)}) %collective-permute-start.25) | collective-permute-done | bytes 544 | tf_op jit(solution)/shard_map/ppermute | solution.py:532
  112.4 2.7 %collective-permute-start.26 = (f32[1,128]{1,0:T(1,128)S(1)}, f32[1,128]{1,0:T(1,128)S(1)}, u32[]{:S(2)}, u32[]{:S(2)}) collective-permute-start(f32[1,128]{1,0:T(1,128)S(1)} %add.119), channel_id=1, source_target_pairs={{0,96},{8,104},{16,112},{24,120},{32,64},{40,72},{48,80},{56,88},{... | collective-permute-start | bytes 1544 | tf_op jit(solution)/shard_map/ppermute | solution.py:532
  115.1 0.0 copy-done.15
  115.1 0.7 fusion.23
  115.8 1.5 %columns_hot.1.hot = bf16[2048,2048]{1,0:T(8,128)(2,1)S(1)} custom-call(s32[1,2048]{1,0:T(1,128)S(1)} %bitcast.104), custom_call_target="tpu_custom_call" | custom-call | tf_op jit(solution)/shard_map/columns_hot/pallas_call | solution.py:368
  117.3 0.0 collective-permute-done.26
  117.3 8.9 %finish.1 = (f32[8,16,2048]{2,1,0:T(8,128)}, f32[128,128]{1,0:T(8,128)}, f32[8,128]{1,0:T(8,128)S(1)}) custom-call(f32[1,128]{1,0:T(1,128)S(1)} %add.120.line, s32[1,2048]{1,0:T(1,128)S(1)} %get-tuple-element.305.cells, f32[1,2048]{1,0:T(1,128)S(1)} %get-tuple-element.303.row_frac, f32[1,2048]{1,0:T(1,128)S(1)} %get-tuple-element.304.col_frac, ...), custom_call_target="tpu_custom_call" | custom-call | tf_op jit(solution)/shard_map/finish/pallas_call | solution.py:438
  126.3 0.7 compare_reduce_fusion
  127.6 0.0 copy-start.16
  127.6 0.2 while.28
  127.8 6.6 %all-to-all-start.1 = ((f32[16,8,128]{2,1,0:T(8,128)}), f32[16,8,128]{2,1,0:T(8,128)S(1)}, u32[]{:S(2)}, u32[]{:S(2)}) async-start(f32[16,8,128]{2,1,0:T(8,128)} %bitcast.111), calls=%async_computation.1 | async-start | bytes 131072 | tf_op jit(solution)/shard_map/all_to_all | solution.py:611
  134.5 7.6 %all-to-all-done.1 = f32[16,8,128]{2,1,0:T(8,128)S(1)} async-done(((f32[16,8,128]{2,1,0:T(8,128)}), f32[16,8,128]{2,1,0:T(8,128)S(1)}, u32[]{:S(2)}, u32[]{:S(2)}) %all-to-all-start.1) | async-done | bytes 65568 | tf_op jit(solution)/shard_map/all_to_all | solution.py:611
  142.1 0.0 copy-done.13
  142.1 1.6 %fusion.22 = f32[1,1,16,8,128]{4,3,2,1,0:T(8,128)} fusion(s32[1,1,16,8,128]{4,3,2,1,0:T(8,128)} %param.27, f32[16,8,128]{2,1,0:T(8,128)S(1)} %all-to-all-done.1, s32[1,1,16,8,128]{4,3,2,1,0:T(8,128)} %param.26, f32[16,128]{1,0:T(8,128)S(1)} %copy-done.13, f32[8]{0:T(128)S(1)} %subtract_log_fusion, f32[16,128]{1,0:T(8,128)S(1)} %copy-done.12), kind=kLoop, calls=%fused_computation.86 | loop fusion | flops 245760 | bytes 278560 | tf_op jit(solution)/shard_map/broadcast_in_dim | solution.py:625
  (19 shorter events, 0.1 us)
Async XLA Ops:
  2.7 16.8 %copy-start = (f32[8,16,2048]{2,1,0:T(8,128)S(1)}, f32[8,16,2048]{2,1,0:T(8,128)}, u32[]{:S(2)}) copy-start(f32[8,16,2048]{2,1,0:T(8,128)} %refs_1_.3) | copy-start | bytes 3145732
  2.7 16.8 %copy-start.5 = (f32[8,16,2048]{2,1,0:T(8,128)S(1)}, f32[8,16,2048]{2,1,0:T(8,128)}, u32[]{:S(2)}) copy-start(f32[8,16,2048]{2,1,0:T(8,128)} %refs_2_.3) | copy-start | bytes 3145732
  2.7 16.8 %copy-start.7 = (f32[8,16,2048]{2,1,0:T(8,128)S(1)}, f32[8,16,2048]{2,1,0:T(8,128)}, u32[]{:S(2)}) copy-start(f32[8,16,2048]{2,1,0:T(8,128)} %refs_0_.3) | copy-start | bytes 3145732
  4.7 14.7 %all-to-all-start = ((f32[16,3,128]{2,1,0:T(4,128)}), f32[16,3,128]{2,1,0:T(4,128)S(1)}, u32[]{:S(2)}, u32[]{:S(2)}) async-start(f32[16,3,128]{2,1,0:T(4,128)} %pad_maximum_fusion.23), calls=%async_computation | async-start | bytes 65536 | tf_op jit(solution)/shard_map/all_to_all | solution.py:576
  11.8 7.6 %collective-permute-start.10 = (f32[16,8,128]{2,1,0:T(8,128)}, f32[16,8,128]{2,1,0:T(8,128)S(1)}, u32[]{:S(2)}, u32[]{:S(2)}) collective-permute-start(f32[16,8,128]{2,1,0:T(8,128)} %get-tuple-element.162), channel_id=1, source_target_pairs={{0,1},{1,2},{2,3},{3,4},{4,5},{5,6},{6,7},{7,0},{8,9},{9,10},{10,1... | collective-permute-start | bytes 196616 | tf_op jit(solution)/shard_map/ppermute | solution.py:524
  11.9 7.6 %collective-permute-start.11 = (f32[16,8,128]{2,1,0:T(8,128)}, f32[16,8,128]{2,1,0:T(8,128)S(1)}, u32[]{:S(2)}, u32[]{:S(2)}) collective-permute-start(f32[16,8,128]{2,1,0:T(8,128)} %get-tuple-element.163), channel_id=1, source_target_pairs={{0,7},{1,0},{2,1},{3,2},{4,3},{5,4},{6,5},{7,6},{8,15},{9,8},{10,9... | collective-permute-start | bytes 196616 | tf_op jit(solution)/shard_map/ppermute | solution.py:524
  21.9 22.5 %collective-permute-start.12 = (f32[12,8,2176]{2,1,0:T(8,128)S(1)}, f32[12,8,2176]{2,1,0:T(8,128)S(1)}, u32[]{:S(2)}, u32[]{:S(2)}) collective-permute-start(f32[12,8,2176]{2,1,0:T(8,128)S(1)} %get-tuple-element.164), channel_id=1, source_target_pairs={{0,8},{8,16},{16,24},{24,32},{32,40},{40,48},{48,56},{56,64},{64,7... | collective-permute-start | bytes 2506760 | tf_op jit(solution)/shard_map/ppermute | solution.py:524
  22.6 21.9 %collective-permute-start.13 = (f32[12,8,2176]{2,1,0:T(8,128)S(1)}, f32[12,8,2176]{2,1,0:T(8,128)S(1)}, u32[]{:S(2)}, u32[]{:S(2)}) collective-permute-start(f32[12,8,2176]{2,1,0:T(8,128)S(1)} %get-tuple-element.165), channel_id=1, source_target_pairs={{0,120},{8,0},{16,8},{24,16},{32,24},{40,32},{48,40},{56,48},{64,5... | collective-permute-start | bytes 2506760 | tf_op jit(solution)/shard_map/ppermute | solution.py:524
  48.9 9.9 %collective-permute-start.14 = (f32[4,8,2176]{2,1,0:T(8,128)S(1)}, f32[4,8,2176]{2,1,0:T(8,128)S(1)}, u32[]{:S(2)}, u32[]{:S(2)}) collective-permute-start(f32[4,8,2176]{2,1,0:T(8,128)S(1)} %get-tuple-element.170), channel_id=1, source_target_pairs={{0,8},{8,16},{16,24},{24,32},{32,40},{40,48},{48,56},{56,64},{64,7... | collective-permute-start | bytes 835592 | tf_op jit(solution)/shard_map/ppermute | solution.py:524
  49.0 9.9 %collective-permute-start.15 = (f32[4,8,2176]{2,1,0:T(8,128)S(1)}, f32[4,8,2176]{2,1,0:T(8,128)S(1)}, u32[]{:S(2)}, u32[]{:S(2)}) collective-permute-start(f32[4,8,2176]{2,1,0:T(8,128)S(1)} %get-tuple-element.171), channel_id=1, source_target_pairs={{0,120},{8,0},{16,8},{24,16},{32,24},{40,32},{48,40},{56,48},{64,5... | collective-permute-start | bytes 835592 | tf_op jit(solution)/shard_map/ppermute | solution.py:524
  63.4 9.9 %collective-permute-start.16 = (f32[4,8,2176]{2,1,0:T(8,128)S(1)}, f32[4,8,2176]{2,1,0:T(8,128)S(1)}, u32[]{:S(2)}, u32[]{:S(2)}) collective-permute-start(f32[4,8,2176]{2,1,0:T(8,128)S(1)} %get-tuple-element.178), channel_id=1, source_target_pairs={{0,8},{8,16},{16,24},{24,32},{32,40},{40,48},{48,56},{56,64},{64,7... | collective-permute-start | bytes 835592 | tf_op jit(solution)/shard_map/ppermute | solution.py:524
  63.5 9.9 %collective-permute-start.17 = (f32[4,8,2176]{2,1,0:T(8,128)S(1)}, f32[4,8,2176]{2,1,0:T(8,128)S(1)}, u32[]{:S(2)}, u32[]{:S(2)}) collective-permute-start(f32[4,8,2176]{2,1,0:T(8,128)S(1)} %get-tuple-element.179), channel_id=1, source_target_pairs={{0,120},{8,0},{16,8},{24,16},{32,24},{40,32},{48,40},{56,48},{64,5... | collective-permute-start | bytes 835592 | tf_op jit(solution)/shard_map/ppermute | solution.py:524
  77.8 9.4 %collective-permute-start.18 = (f32[3,8,2176]{2,1,0:T(8,128)S(1)}, f32[3,8,2176]{2,1,0:T(8,128)S(1)}, u32[]{:S(2)}, u32[]{:S(2)}) collective-permute-start(f32[3,8,2176]{2,1,0:T(8,128)S(1)} %get-tuple-element.183), channel_id=1, source_target_pairs={{0,8},{8,16},{16,24},{24,32},{32,40},{40,48},{48,56},{56,64},{64,7... | collective-permute-start | bytes 626696 | tf_op jit(solution)/shard_map/ppermute | solution.py:524
  77.9 9.4 %collective-permute-start.19 = (f32[3,8,2176]{2,1,0:T(8,128)S(1)}, f32[3,8,2176]{2,1,0:T(8,128)S(1)}, u32[]{:S(2)}, u32[]{:S(2)}) collective-permute-start(f32[3,8,2176]{2,1,0:T(8,128)S(1)} %get-tuple-element.184), channel_id=1, source_target_pairs={{0,120},{8,0},{16,8},{24,16},{32,24},{40,32},{48,40},{56,48},{64,5... | collective-permute-start | bytes 626696 | tf_op jit(solution)/shard_map/ppermute | solution.py:524
  87.2 21.6 %copy-start.14 = (s32[1,1,16,128]{3,2,1,0:T(8,128)S(1)}, s32[1,1,16,128]{3,2,1,0:T(8,128)}, u32[]{:S(2)}) copy-start(s32[1,1,16,128]{3,2,1,0:T(8,128)} %param.25) | copy-start | bytes 24580
  87.2 27.9 %copy-start.15 = (s32[1,1,16]{2,1,0:T(1,128)S(1)}, s32[1,1,16]{2,1,0:T(1,128)}, u32[]{:S(2)}) copy-start(s32[1,1,16]{2,1,0:T(1,128)} %param.24) | copy-start | bytes 196
  90.5 1.1 collective-permute-start.20
  91.6 3.5 %collective-permute-start.21 = (f32[1,128]{1,0:T(1,128)S(1)}, f32[1,128]{1,0:T(1,128)S(1)}, u32[]{:S(2)}, u32[]{:S(2)}) collective-permute-start(f32[1,128]{1,0:T(1,128)S(1)} %add.114), channel_id=1, source_target_pairs={{0,2},{1,3},{2,0},{3,1},{4,6},{5,7},{6,4},{7,5},{8,10},{9,11},{10,... | collective-permute-start | bytes 1544 | tf_op jit(solution)/shard_map/ppermute | solution.py:532
  95.2 5.4 %collective-permute-start.22 = (f32[1,128]{1,0:T(1,128)S(1)}, f32[1,128]{1,0:T(1,128)S(1)}, u32[]{:S(2)}, u32[]{:S(2)}) collective-permute-start(f32[1,128]{1,0:T(1,128)S(1)} %add.115), channel_id=1, source_target_pairs={{0,6},{1,7},{2,4},{3,5},{4,2},{5,3},{6,0},{7,1},{8,14},{9,15},{10,... | collective-permute-start | bytes 1544 | tf_op jit(solution)/shard_map/ppermute | solution.py:532
  100.5 3.5 %collective-permute-start.23 = (f32[1,128]{1,0:T(1,128)S(1)}, f32[1,128]{1,0:T(1,128)S(1)}, u32[]{:S(2)}, u32[]{:S(2)}) collective-permute-start(f32[1,128]{1,0:T(1,128)S(1)} %add.116), channel_id=1, source_target_pairs={{0,8},{8,0},{16,24},{24,16},{32,40},{40,32},{48,56},{56,48},{64,72... | collective-permute-start | bytes 1544 | tf_op jit(solution)/shard_map/ppermute | solution.py:532
  104.1 4.8 %collective-permute-start.24 = (f32[1,128]{1,0:T(1,128)S(1)}, f32[1,128]{1,0:T(1,128)S(1)}, u32[]{:S(2)}, u32[]{:S(2)}) collective-permute-start(f32[1,128]{1,0:T(1,128)S(1)} %add.117), channel_id=1, source_target_pairs={{0,24},{8,16},{16,8},{24,0},{32,56},{40,48},{48,40},{56,32},{64,88... | collective-permute-start | bytes 1544 | tf_op jit(solution)/shard_map/ppermute | solution.py:532
  108.8 3.5 %collective-permute-start.25 = (f32[1,128]{1,0:T(1,128)S(1)}, f32[1,128]{1,0:T(1,128)S(1)}, u32[]{:S(2)}, u32[]{:S(2)}) collective-permute-start(f32[1,128]{1,0:T(1,128)S(1)} %add.118), channel_id=1, source_target_pairs={{0,32},{8,40},{16,48},{24,56},{32,0},{40,8},{48,16},{56,24},{64,96... | collective-permute-start | bytes 1544 | tf_op jit(solution)/shard_map/ppermute | solution.py:532
  112.4 4.9 %collective-permute-start.26 = (f32[1,128]{1,0:T(1,128)S(1)}, f32[1,128]{1,0:T(1,128)S(1)}, u32[]{:S(2)}, u32[]{:S(2)}) collective-permute-start(f32[1,128]{1,0:T(1,128)S(1)} %add.119), channel_id=1, source_target_pairs={{0,96},{8,104},{16,112},{24,120},{32,64},{40,72},{48,80},{56,88},{... | collective-permute-start | bytes 1544 | tf_op jit(solution)/shard_map/ppermute | solution.py:532
  127.6 6.9 %copy-start.16 = (f32[8]{0:T(128)S(1)}, f32[8]{0:T(128)}, u32[]{:S(2)}) copy-start(f32[8]{0:T(128)} %param.21) | copy-start | bytes 100
  127.6 14.5 %copy-start.12 = (f32[16,128]{1,0:T(8,128)S(1)}, f32[16,128]{1,0:T(8,128)}, u32[]{:S(2)}) copy-start(f32[16,128]{1,0:T(8,128)} %convert_bitcast_fusion) | copy-start | bytes 24580
  127.6 14.5 %copy-start.13 = (f32[16,128]{1,0:T(8,128)S(1)}, f32[16,128]{1,0:T(8,128)}, u32[]{:S(2)}) copy-start(f32[16,128]{1,0:T(8,128)} %fusion.23) | copy-start | bytes 24580
  127.8 14.3 %all-to-all-start.1 = ((f32[16,8,128]{2,1,0:T(8,128)}), f32[16,8,128]{2,1,0:T(8,128)S(1)}, u32[]{:S(2)}, u32[]{:S(2)}) async-start(f32[16,8,128]{2,1,0:T(8,128)} %bitcast.111), calls=%async_computation.1 | async-start | bytes 131072 | tf_op jit(solution)/shard_map/all_to_all | solution.py:611

commit v7 on v6

--- a/solution.py
+++ b/solution.py
@@ -26,7 +26,10 @@
 
 
 def columns_kernel(*refs):
-    firsts, lasts, (to_left, to_right) = refs[0:4], refs[4:8], refs[8:]
+    firsts, lasts, (cells, offsets, to_left, to_right, sent) = refs[0:4], refs[4:8], refs[8:]
+    for i in range(cells.shape[0]):
+        sent[i, 0:1] = cells[i : i + 1].astype(jnp.float32)
+        sent[i, 1:3] = offsets[i]
     lane = lax.broadcasted_iota(jnp.int32, (16, F, LANES), 2)
     for out, blocks, start in ((to_left, firsts, 0), (to_right, lasts, LANES - SIDE)):
         packed = jnp.zeros((16, F, LANES), jnp.float32)
@@ -39,20 +42,25 @@
         out[...] = packed
 
 
-def columns_of(fields):
+def columns_of(fields, cells, offsets):
     rows, cols = fields[0].shape[1:]
     first = pl.BlockSpec((F, rows, LANES), lambda i: (0, 0, 0))
     last = pl.BlockSpec((F, rows, LANES), lambda i: (0, 0, cols // LANES - 1))
     out = pl.BlockSpec((rows, F, LANES), lambda i: (0, 0, 0))
     shape = jax.ShapeDtypeStruct((rows, F, LANES), jnp.float32)
+    sent = (cells.shape[0], 3, cells.shape[1])
+
+    def whole(shape):
+        return pl.BlockSpec(shape, lambda i: (0,) * len(shape))
+
     return pl.pallas_call(
         columns_kernel,
         grid=(1,),
-        in_specs=[first] * 4 + [last] * 4,
-        out_specs=[out, out],
-        out_shape=[shape, shape],
+        in_specs=[first] * 4 + [last] * 4 + [whole(cells.shape), whole(offsets.shape)],
+        out_specs=[out, out, whole(sent)],
+        out_shape=[shape, shape, jax.ShapeDtypeStruct(sent, jnp.float32)],
         name="columns",
-    )(*fields, *fields)
+    )(*fields, *fields, cells, offsets)
 
 
 DEPTHS = (4, 3, 3, 2)
@@ -143,39 +151,30 @@
     return lax.fori_loop(0, (high - low) // 2, lambda i, carry: body(low + 2 * i, carry), carry, unroll=True)
 
 
-def phase_kernel(p, rows, cols, *refs):
+class Rows:
+    def __init__(self, ref, shift):
+        self.ref, self.shift = ref, shift
+
+    def __getitem__(self, key):
+        return self.ref[(key[0] + self.shift, *key[1:])]
+
+    def __setitem__(self, key, value):
+        self.ref[(key[0] + self.shift, *key[1:])] = value
+
+
+def rows_of(ref, shift):
+    return None if ref is None else Rows(ref, shift)
+
+
+INSIDE = dict(scale=[(1, 15)], first=[(2, 14)], again=[(3, 13)], second=[(4, 12)])
+OUTSIDE = dict(
+    scale=[(-3, 3), (13, 19)], first=[(0, 2), (14, 16)], again=[(-1, 5), (11, 17)], second=[(0, 4), (12, 16)]
+)
+
+
+def apply_twice(p, cols, where, ring, mask, current, kap, tau, cur, older, old, scaled, one, middle, newest):
     first, last = p == 0, p == ITERS // 2 - 1
-    refs = list(refs)
-    take = lambda n: [refs.pop(0) for _ in range(n)]
-    flags, mask, up, down = take(4)
-    if first:
-        mains = take(4)
-    else:
-        own, kap, tau, cur, older, old = take(6)
-    if last:
-        earlier = take(ITERS // 2 - 1)
-        line, current, middle = take(3)
-    elif first:
-        kap, tau, cur, current, middle, newest, to_up, to_down, sums = take(9)
-    else:
-        current, middle, newest, to_up, to_down, sums = take(6)
-    scaled, one = refs
     wide = cols + LANES
-    own_low, own_high = PAD, PAD + rows
-
-    work = (current, kap, tau, cur)
-    if first:
-        for a, source in enumerate(mains):
-            work[a][own_low:own_high] = source[...]
-    else:
-        current[own_low:own_high] = own[...]
-    base = 0
-    for a, depth in enumerate(DEPTHS if first else (up.shape[0],)):
-        for i in range(depth):
-            work[a][own_low - depth + i] = up[base + i] * flags[2]
-            work[a][own_high + i] = down[base + i] * flags[3]
-        base += depth
-
     zero = jnp.zeros((F, LANES), jnp.float32)
 
     def scale(ref, low, high):
@@ -195,23 +194,24 @@
                 out.append(new * mask[...] if at.start == cols else new)
             yield at, out
 
-    reach = 2 if last else 3
-    scale(current, own_low - reach, own_high + reach)
-    for r, flag, inner in ((own_low - 2, flags[2], 1), (own_high, flags[3], 0)):
+    for low, high in where["scale"]:
+        scale(current, low, high)
+    for r, flag, inner in ring:
         for at, new in image(current, r):
             for i in range(2):
                 value = new[i] * flag
                 one[r + i, :, at] = value
                 if i == inner:
-                    middle[r + i - SKIP, :, at] = value if first else 2.0 * value - old[r + i - SKIP, :, at]
+                    middle[r + i, :, at] = value if first else 2.0 * value - old[r + i, :, at]
 
     def first_rows(r, carry):
         cross = square = start = zero
         for at, new in image(current, r):
             for i in range(2):
-                one[r + i, :, at] = new[i]
-                value = new[i] if first else 2.0 * new[i] - old[r + i - SKIP, :, at]
-                middle[r + i - SKIP, :, at] = value
+                if not last:
+                    one[r + i, :, at] = new[i]
+                value = new[i] if first else 2.0 * new[i] - old[r + i, :, at]
+                middle[r + i, :, at] = value
                 if at.start < cols:
                     source = current[r + i, :, at]
                     cross += value * source
@@ -221,39 +221,27 @@
         out = (carry[0] + cross, carry[1] + square)
         return out + ((carry[2] + start,) if first else ())
 
-    found = pairs(own_low, own_high, first_rows, (zero,) * (3 if first else 2))
+    found = (zero,) * (3 if first else 2)
+    for low, high in where["first"]:
+        found = pairs(low, high, first_rows, found)
 
     if last:
-
         def final_rows(r, carry):
             total = zero
-            for at, v, near in walk(middle, r - SKIP, 2, wide):
+            for at, v, near in walk(middle, r, 2, wide):
                 if at.start < cols:
                     for i in range(2):
                         k = kap[r + i, :, at] * v[i] - near[i]
                         total += tau[r + i, :, at] * k * k + cur[r + i, :, at] * v[i] * v[i]
             return carry + total
 
-        found += (pairs(own_low, own_high, final_rows, zero),)
-        entries = [earlier[0][4]]
-        for s in earlier:
-            entries += [s[i] for i in range(4)]
-        lane = lax.broadcasted_iota(jnp.int32, (F, LANES), 1)
-        table = zero
-        for k, entry in enumerate(entries + list(found)):
-            table = jnp.where(lane == k, jnp.sum(entry, axis=1, keepdims=True), table)
-        total = table[0:1]
-        for f in range(1, F):
-            total = total + pltpu.roll(table[f : f + 1], 2 * ITERS * f, 1)
-        line[...] = total
-        return
-
-    sums[0] = found[0]
-    sums[1] = found[1]
-    if first:
-        sums[4] = found[2]
-
-    scale(one, own_low - 1, own_high + 1)
+        total = zero
+        for low, high in where["second"]:
+            total = pairs(low, high, final_rows, total)
+        return [*found, total]
+
+    for low, high in where["again"]:
+        scale(one, low, high)
 
     def second_rows(r, carry):
         cross = square = zero
@@ -262,13 +250,93 @@
                 value = 2.0 * new[i] - current[r + i, :, at]
                 if not first:
                     value = 2.0 * value - older[r + i, :, at]
-                newest[r + i - PAD, :, at] = value
+                newest[r + i, :, at] = value
                 if at.start < cols:
-                    cross += value * middle[r + i - SKIP, :, at]
+                    cross += value * middle[r + i, :, at]
                     square += value * value
         return carry[0] + cross, carry[1] + square
 
-    sums[2], sums[3] = pairs(own_low, own_high, second_rows, (zero, zero))
+    more = (zero, zero)
+    for low, high in where["second"]:
+        more = pairs(low, high, second_rows, more)
+    return [found[0], found[1], *more, *found[2:]]
+
+
+def inside_kernel(p, cols, *refs):
+    first, last = p == 0, p == ITERS // 2 - 1
+    refs = list(refs)
+    take = lambda n: [refs.pop(0) for _ in range(n)]
+    mask, own, kap, tau, cur = take(5)
+    older, old = (None, None) if first else take(2)
+    shift = 0 if first else PAD
+    coefs = [Rows(x, shift) for x in (kap, tau, cur)]
+    older, old = rows_of(older, PAD), rows_of(old, 1)
+    (middle,) = take(1)
+    one, newest = (None, None) if last else take(2)
+    sums, scaled = refs
+    found = apply_twice(
+        p, cols, INSIDE, (), mask, Rows(own, 0), *coefs, older, old, Rows(scaled, 0),
+        rows_of(one, -2), Rows(middle, -2), rows_of(newest, -4),
+    )
+    for i, total in enumerate(found):
+        sums[i] = total
+
+
+def outside_kernel(p, rows, cols, *refs):
+    first, last = p == 0, p == ITERS // 2 - 1
+    refs = list(refs)
+    take = lambda n: [refs.pop(0) for _ in range(n)]
+    flags, mask, up, down, own, kap_in, tau_in, cur_in = take(8)
+    older, old = (None, None) if first else take(2)
+    (middle_in,) = take(1)
+    one_in, newest_in = (None, None) if last else take(2)
+    (part,) = take(1)
+    if last:
+        earlier = take(ITERS // 2 - 1)
+        (line,) = take(1)
+    current, middle = take(2)
+    kap, tau, cur = take(3) if first else (kap_in, tau_in, cur_in)
+    if not last:
+        newest, to_up, to_down, sums = take(4)
+    scaled, one = refs
+    own_low, own_high = PAD, PAD + rows
+
+    work = (current, kap, tau, cur)
+    for a, source in enumerate((own, kap_in, tau_in, cur_in) if first else (own,)):
+        work[a][own_low:own_high] = source[...]
+    base = 0
+    for a, depth in enumerate(DEPTHS if first else (up.shape[0],)):
+        for i in range(depth):
+            work[a][own_low - depth + i] = up[base + i] * flags[2]
+            work[a][own_high + i] = down[base + i] * flags[3]
+        base += depth
+    middle[1 + 2 : 1 + rows - 2] = middle_in[...]
+    if not last:
+        one[own_low + 2 : own_low + 6] = one_in[:4]
+        one[own_high - 6 : own_high - 2] = one_in[8:]
+        newest[4 : rows - 4] = newest_in[...]
+
+    found = apply_twice(
+        p, cols, OUTSIDE, ((-2, flags[2], 1), (rows, flags[3], 0)), mask,
+        *[Rows(x, PAD) for x in (current, kap, tau, cur)], rows_of(older, PAD), rows_of(old, 1),
+        Rows(scaled, PAD), Rows(one, PAD), Rows(middle, 1), None if last else Rows(newest, 0),
+    )
+    found = [x + part[i] for i, x in enumerate(found)]
+    if last:
+        entries = [earlier[0][4]]
+        for s in earlier:
+            entries += [s[i] for i in range(4)]
+        lane = lax.broadcasted_iota(jnp.int32, (F, LANES), 1)
+        table = jnp.zeros((F, LANES), jnp.float32)
+        for k, entry in enumerate(entries + found):
+            table = jnp.where(lane == k, jnp.sum(entry, axis=1, keepdims=True), table)
+        total = table[0:1]
+        for f in range(1, F):
+            total = total + pltpu.roll(table[f : f + 1], 2 * ITERS * f, 1)
+        line[...] = total
+        return
+    for i, total in enumerate(found):
+        sums[i] = total
     depth = to_up.shape[0]
     to_up[...] = newest[:depth]
     to_down[...] = newest[rows - depth :]
@@ -279,24 +347,39 @@
     f32 = jnp.float32
     wide = cols + LANES
     ext = (rows + 2 * PAD, F, wide)
-    out_shape = [pltpu.VMEM(ext, f32)] * (4 if first else 1) + [pltpu.VMEM((rows + 2, F, wide), f32)]
+    state = [held(x) for x in state]
+    counted = jax.ShapeDtypeStruct((5 if first else 3 if last else 4, F, LANES), f32)
+    part_shape = [pltpu.VMEM((rows - 4, F, wide), f32)]
+    if not last:
+        part_shape += [pltpu.VMEM((rows - 4, F, wide), f32), pltpu.VMEM((rows - 8, F, wide), f32)]
+    inside = pl.pallas_call(
+        functools.partial(inside_kernel, p, cols),
+        in_specs=[VMEM] * (1 + len(state)),
+        out_specs=[VMEM] * (len(part_shape) + 1),
+        out_shape=part_shape + [counted],
+        scratch_shapes=[pltpu.VMEM((rows, F, wide), f32)],
+        compiler_params=PARAMS,
+        cost_estimate=pl.CostEstimate(flops=100_000_000, bytes_accessed=8_000_000, transcendentals=0),
+        name=f"inside{p}",
+    )(mask, *state)
+    out_shape = [pltpu.VMEM(ext, f32), pltpu.VMEM((rows + 2, F, wide), f32)]
+    if first:
+        out_shape += [pltpu.VMEM(ext, f32)] * 3
     if last:
         out_shape = [jax.ShapeDtypeStruct((1, LANES), f32)] + out_shape
     else:
         out_shape += [pltpu.VMEM((rows, F, wide), f32)]
         depth = PAD - 1 if p == ITERS // 2 - 2 else PAD
-        out_shape += [jax.ShapeDtypeStruct((depth, F, wide), f32)] * 2
-        out_shape += [jax.ShapeDtypeStruct((5 if first else 4, F, LANES), f32)]
-    operands = [held(x) for x in state]
+        out_shape += [jax.ShapeDtypeStruct((depth, F, wide), f32)] * 2 + [counted]
     return pl.pallas_call(
-        functools.partial(phase_kernel, p, rows, cols),
-        in_specs=[SMEM] + [VMEM] * (3 + len(operands) + len(earlier)),
+        functools.partial(outside_kernel, p, rows, cols),
+        in_specs=[SMEM] + [VMEM] * (3 + len(state) + len(inside) + len(earlier)),
         out_specs=[VMEM] * len(out_shape),
         out_shape=out_shape,
         scratch_shapes=[pltpu.VMEM(ext, f32), pltpu.VMEM(ext, f32)],
         compiler_params=PARAMS,
-        name=f"phase{p}",
-    )(flags, mask, up, down, *operands, *earlier)
+        name=f"outside{p}",
+    )(flags, mask, up, down, *state, *[held(x) for x in inside[:-1]], inside[-1], *earlier)
 
 
 def coefficients(line):
@@ -567,10 +650,8 @@
     mask = jnp.where(lane < SIDE, flags[1], jnp.where(lane >= LANES - SIDE, flags[0], 0.0))
 
     fields = (right_side, kappa_field, tau_field, curvature)
-    to_left, to_right = columns_of(fields)
     cells = site_cells[0, 0]
-    sent = jnp.concatenate([cells.astype(jnp.float32)[:, None], site_offsets[0, 0]], axis=1)
-    sent, to_left, to_right = lax.optimization_barrier((sent, to_left, to_right))
+    to_left, to_right, sent = columns_of(fields, cells, site_offsets[0, 0])
     from_right = turned(to_left, "field", -1)
     from_left = turned(to_right, "field", 1)
     got = lax.all_to_all(sent, "tile", split_axis=0, concat_axis=0, tiled=True)
@@ -585,9 +666,7 @@
         return turned(to_down, "tile", 1), turned(to_up, "tile", -1)
 
     up, down = exchanged(to_up, to_down)
-    *coefs, older, old, own, to_up, to_down, part = phase(
-        0, *common, up, down, mains
-    )
+    older, old, *coefs, own, to_up, to_down, part = phase(0, *common, up, down, mains)
     basis, sums = [older, old], [part]
     for p in range(1, ITERS // 2 - 1):
         up, down = exchanged(to_up, to_down)

time: 144 us -> 136 us (0.944)
  waiting for transfers between devices: 54.9 us -> 46 us
  Pallas kernels: 31.6 us -> 34 us
  other arithmetic: 7.02 us -> 5.01 us
    ppermute x10, waiting for transfers between devices: 27.6 us -> 18.8 us  [turned(): return lax.ppermute(x, axis, [(i, (i + by) % size) for i in range(size)])]
    pallas_call x4 -> x8, Pallas kernels: 16.7 us -> 19.1 us  [the longest x4 10.3 us: phase(): pl.pallas_call(functools.partial(outside_kernel, p, rows, cols), in_specs...]
  transfers between devices with their start and end apart: 19 -> 19, of which waited for: 12 -> 12; matrix products, arithmetic and copies ran while one was open for 2% -> 2% of each run, Pallas kernels for 1% -> 8%
where the time goes in v7:
time: 136 us; the launch traced here: 135 us
  starting transfers between devices  47.9 us (35%)
  waiting for transfers between devices  46 us (34%)
  Pallas kernels  34 us (25%)
  other arithmetic  5.01 us (4%)
  between operations  1.55 us (1%)
    ppermute x10, starting transfers between devices, turned(): return lax.ppermute(x, axis, [(i, (i + by) % size) for i in range(size)])  25.5 us
    ppermute x10, waiting for transfers between devices, turned(): return lax.ppermute(x, axis, [(i, (i + by) % size) for i in range(size)])  18.8 us
    ppermute x6, waiting for transfers between devices, summed(): lax.ppermute(x, axis, [(i, other(i, stride, by)) for i in range(size)])  14.2 us
    pallas_call x4, Pallas kernels, phase(): pl.pallas_call(functools.partial(outside_kernel, p, rows, cols), in_specs...  10.3 us
    pallas_call x1, Pallas kernels, finish(): pl.pallas_call(functools.partial(finish_kernel, rows, cols), in_specs=[VM...  8.89 us
    pallas_call x4, Pallas kernels, phase(): pl.pallas_call(functools.partial(inside_kernel, p, cols), in_specs=[VMEM]...  8.79 us
    ppermute x6, starting transfers between devices, summed(): lax.ppermute(x, axis, [(i, other(i, stride, by)) for i in range(size)])  8.71 us
    all_to_all x1, waiting for transfers between devices, local(): lax.all_to_all(predictor, 'tile', split_axis=0, concat_axis=0, tiled=True)  7.64 us
  transfers between devices with their start and end apart: 19, of which 12 were waited for; matrix products, arithmetic and copies ran while one was open for 2% of the time, Pallas kernels for 8%

profile of v7, /device:TPU:0, one launch (start us, length us, event | category | flops | bytes accessed | tf_op | source)
XLA Modules:
  0.0 135.3 jit_solution(86047404701602017)
XLA Ops:
  0.6 0.0 copy-start
  0.6 0.0 copy-start.3
  0.7 0.0 copy-start.5
  0.7 2.1 %columns.1 = (f32[16,8,128]{2,1,0:T(8,128)}, f32[16,8,128]{2,1,0:T(8,128)}, f32[16,3,128]{2,1,0:T(4,128)}) custom-call(f32[8,16,2048]{2,1,0:T(8,128)} %refs_0_.3, f32[8,16,2048]{2,1,0:T(8,128)} %refs_1_.3, f32[8,16,2048]{2,1,0:T(8,128)} %refs_2_.3, f32[8,16,2048]{2,1,0:T(8,128)} %refs_3_.3, f32[8,16,2048]{2,1,0:T(8,128)} %refs_0_.3, f32[8,16,2048]{2,1,0:T(8,128)} %refs_1_.3, ...), custom_call_target="tpu_custom_call" | custom-call | tf_op jit(solution)/shard_map/columns/pallas_call | solution.py:56
  2.7 7.1 %all-to-all-start = ((f32[16,3,128]{2,1,0:T(4,128)}), f32[16,3,128]{2,1,0:T(4,128)S(1)}, u32[]{:S(2)}, u32[]{:S(2)}) async-start(f32[16,3,128]{2,1,0:T(4,128)} %get-tuple-element.170), calls=%async_computation | async-start | bytes 65536 | tf_op jit(solution)/shard_map/all_to_all | solution.py:657
  9.8 0.0 collective-permute-start.10
  9.9 3.2 %collective-permute-start.11 = (f32[16,8,128]{2,1,0:T(8,128)}, f32[16,8,128]{2,1,0:T(8,128)S(1)}, u32[]{:S(2)}, u32[]{:S(2)}) collective-permute-start(f32[16,8,128]{2,1,0:T(8,128)} %get-tuple-element.173), channel_id=1, source_target_pairs={{0,7},{1,0},{2,1},{3,2},{4,3},{5,4},{6,5},{7,6},{8,15},{9,8},{10,9... | collective-permute-start | bytes 196616 | tf_op jit(solution)/shard_map/ppermute | solution.py:607
  13.1 0.1 add_convert_fusion.flags.refs_0_
  13.2 4.3 %all-to-all-done = f32[16,3,128]{2,1,0:T(4,128)S(1)} async-done(((f32[16,3,128]{2,1,0:T(4,128)}), f32[16,3,128]{2,1,0:T(4,128)S(1)}, u32[]{:S(2)}, u32[]{:S(2)}) %all-to-all-start) | async-done | bytes 24608 | tf_op jit(solution)/shard_map/all_to_all | solution.py:657
  17.5 0.0 collective-permute-done.10.left
  17.5 0.0 collective-permute-done.11.right
  17.5 0.0 copy-done.3
  17.5 2.4 %prepare.1 = (f32[16,8,2176]{2,1,0:T(8,128)S(1)}, f32[16,8,2176]{2,1,0:T(8,128)S(1)}, f32[16,8,2176]{2,1,0:T(8,128)S(1)}, f32[16,8,2176]{2,1,0:T(8,128)S(1)}, f3...) custom-call(f32[4]{0:T(128)S(1)} %add_convert_fusion.flags.refs_0_, f32[16,8,128]{2,1,0:T(8,128)S(1)} %collective-permute-done.10.left, ...), custom_call_target="tpu_custom_call" | custom-call | tf_op jit(solution)/shard_map/prepare/pallas_call | solution.py:112
  20.0 0.6 collective-permute-start.12
  20.6 4.8 %collective-permute-start.13 = (f32[12,8,2176]{2,1,0:T(8,128)S(1)}, f32[12,8,2176]{2,1,0:T(8,128)S(1)}, u32[]{:S(2)}, u32[]{:S(2)}) collective-permute-start(f32[12,8,2176]{2,1,0:T(8,128)S(1)} %get-tuple-element.175), channel_id=1, source_target_pairs={{0,120},{8,0},{16,8},{24,16},{32,24},{40,32},{48,40},{56,48},{64,5... | collective-permute-start | bytes 2506760 | tf_op jit(solution)/shard_map/ppermute | solution.py:607
  25.4 0.6 fusion.30
  26.0 0.6 compare_select_fusion.4
  26.6 0.7 broadcast_select_fusion.refs_0_.refs_1_
  27.3 2.4 %inside0.1 = (f32[12,8,2176]{2,1,0:T(8,128)S(1)}, f32[12,8,2176]{2,1,0:T(8,128)S(1)}, f32[8,8,2176]{2,1,0:T(8,128)S(1)}, f32[5,8,128]{2,1,0:T(8,128)S(1)}) custom-call(f32[8,128]{1,0:T(8,128)S(1)} %broadcast_select_fusion.refs_0_.refs_1_, f32[16,8,2176]{2,1,0:T(8,128)S(1)} %get-tuple-element.176.refs_1_.refs_4_, ...), custom_call_target="tpu_custom_call" | custom-call | flops 100000000 | bytes 8000000 | tf_op jit(solution)/shard_map/inside0/pallas_call | solution.py:355
  29.7 12.8 %collective-permute-done.12.refs_2_ = f32[12,8,2176]{2,1,0:T(8,128)S(1)} collective-permute-done((f32[12,8,2176]{2,1,0:T(8,128)S(1)}, f32[12,8,2176]{2,1,0:T(8,128)S(1)}, u32[]{:S(2)}, u32[]{:S(2)}) %collective-permute-start.12) | collective-permute-done | bytes 835616 | tf_op jit(solution)/shard_map/ppermute | solution.py:607
  42.4 0.0 collective-permute-done.13.refs_3_
  42.4 2.8 %outside0.1 = (f32[24,8,2176]{2,1,0:T(8,128)S(1)}, f32[18,8,2176]{2,1,0:T(8,128)S(1)}, f32[24,8,2176]{2,1,0:T(8,128)S(1)}, f32[24,8,2176]{2,1,0:T(8,128)S(1)}, f...) custom-call(f32[4]{0:T(128)S(1)} %add_convert_fusion.flags.refs_0_, ...), custom_call_target="tpu_custom_call" | custom-call | tf_op jit(solution)/shard_map/outside0/pallas_call | solution.py:374
  45.3 0.1 collective-permute-start.14
  45.4 5.3 %collective-permute-start.15 = (f32[4,8,2176]{2,1,0:T(8,128)S(1)}, f32[4,8,2176]{2,1,0:T(8,128)S(1)}, u32[]{:S(2)}, u32[]{:S(2)}) collective-permute-start(f32[4,8,2176]{2,1,0:T(8,128)S(1)} %get-tuple-element.185), channel_id=1, source_target_pairs={{0,120},{8,0},{16,8},{24,16},{32,24},{40,32},{48,40},{56,48},{64,5... | collective-permute-start | bytes 835592 | tf_op jit(solution)/shard_map/ppermute | solution.py:607
  50.7 2.3 %inside1.1 = (f32[12,8,2176]{2,1,0:T(8,128)S(1)}, f32[12,8,2176]{2,1,0:T(8,128)S(1)}, f32[8,8,2176]{2,1,0:T(8,128)S(1)}, f32[4,8,128]{2,1,0:T(8,128)S(1)}) custom-call(f32[8,128]{1,0:T(8,128)S(1)} %broadcast_select_fusion.refs_0_.refs_1_, f32[16,8,2176]{2,1,0:T(8,128)S(1)} %get-tuple-element.186.refs_1_.refs_4_, ...), custom_call_target="tpu_custom_call" | custom-call | flops 100000000 | bytes 8000000 | tf_op jit(solution)/shard_map/inside1/pallas_call | solution.py:355
  53.0 2.2 %collective-permute-done.14.refs_2_ = f32[4,8,2176]{2,1,0:T(8,128)S(1)} collective-permute-done((f32[4,8,2176]{2,1,0:T(8,128)S(1)}, f32[4,8,2176]{2,1,0:T(8,128)S(1)}, u32[]{:S(2)}, u32[]{:S(2)}) %collective-permute-start.14) | collective-permute-done | bytes 278560 | tf_op jit(solution)/shard_map/ppermute | solution.py:607
  55.2 0.0 collective-permute-done.15.refs_3_
  55.2 2.7 %outside1.1 = (f32[24,8,2176]{2,1,0:T(8,128)S(1)}, f32[18,8,2176]{2,1,0:T(8,128)S(1)}, f32[16,8,2176]{2,1,0:T(8,128)S(1)}, f32[4,8,2176]{2,1,0:T(8,128)S(1)}, f3...) custom-call(f32[4]{0:T(128)S(1)} %add_convert_fusion.flags.refs_0_, f32[8,128]{1,0:T(8,128)S(1)} %broadcast_select_fusion.refs_0_.refs_1_, ...), custom_call_target="tpu_custom_call" | custom-call | tf_op jit(solution)/shard_map/outside1/pallas_call | solution.py:374
  58.0 0.1 collective-permute-start.16
  58.1 5.6 %collective-permute-start.17 = (f32[4,8,2176]{2,1,0:T(8,128)S(1)}, f32[4,8,2176]{2,1,0:T(8,128)S(1)}, u32[]{:S(2)}, u32[]{:S(2)}) collective-permute-start(f32[4,8,2176]{2,1,0:T(8,128)S(1)} %get-tuple-element.197), channel_id=1, source_target_pairs={{0,120},{8,0},{16,8},{24,16},{32,24},{40,32},{48,40},{56,48},{64,5... | collective-permute-start | bytes 835592 | tf_op jit(solution)/shard_map/ppermute | solution.py:607
  63.6 2.3 %inside2.1 = (f32[12,8,2176]{2,1,0:T(8,128)S(1)}, f32[12,8,2176]{2,1,0:T(8,128)S(1)}, f32[8,8,2176]{2,1,0:T(8,128)S(1)}, f32[4,8,128]{2,1,0:T(8,128)S(1)}) custom-call(f32[8,128]{1,0:T(8,128)S(1)} %broadcast_select_fusion.refs_0_.refs_1_, f32[16,8,2176]{2,1,0:T(8,128)S(1)} %get-tuple-element.198.refs_1_.refs_4_, ...), custom_call_target="tpu_custom_call" | custom-call | flops 100000000 | bytes 8000000 | tf_op jit(solution)/shard_map/inside2/pallas_call | solution.py:355
  66.0 1.9 %collective-permute-done.16.refs_2_ = f32[4,8,2176]{2,1,0:T(8,128)S(1)} collective-permute-done((f32[4,8,2176]{2,1,0:T(8,128)S(1)}, f32[4,8,2176]{2,1,0:T(8,128)S(1)}, u32[]{:S(2)}, u32[]{:S(2)}) %collective-permute-start.16) | collective-permute-done | bytes 278560 | tf_op jit(solution)/shard_map/ppermute | solution.py:607
  67.9 0.0 collective-permute-done.17.refs_3_
  67.9 2.7 %outside2.1 = (f32[24,8,2176]{2,1,0:T(8,128)S(1)}, f32[18,8,2176]{2,1,0:T(8,128)S(1)}, f32[16,8,2176]{2,1,0:T(8,128)S(1)}, f32[3,8,2176]{2,1,0:T(8,128)S(1)}, f3...) custom-call(f32[4]{0:T(128)S(1)} %add_convert_fusion.flags.refs_0_, f32[8,128]{1,0:T(8,128)S(1)} %broadcast_select_fusion.refs_0_.refs_1_, ...), custom_call_target="tpu_custom_call" | custom-call | tf_op jit(solution)/shard_map/outside2/pallas_call | solution.py:374
  70.7 0.1 collective-permute-start.18
  70.7 5.7 %collective-permute-start.19 = (f32[3,8,2176]{2,1,0:T(8,128)S(1)}, f32[3,8,2176]{2,1,0:T(8,128)S(1)}, u32[]{:S(2)}, u32[]{:S(2)}) collective-permute-start(f32[3,8,2176]{2,1,0:T(8,128)S(1)} %get-tuple-element.206), channel_id=1, source_target_pairs={{0,120},{8,0},{16,8},{24,16},{32,24},{40,32},{48,40},{56,48},{64,5... | collective-permute-start | bytes 626696 | tf_op jit(solution)/shard_map/ppermute | solution.py:607
  76.4 1.8 %inside3.1 = (f32[12,8,2176]{2,1,0:T(8,128)S(1)}, f32[3,8,128]{2,1,0:T(8,128)S(1)}) custom-call(f32[8,128]{1,0:T(8,128)S(1)} %broadcast_select_fusion.refs_0_.refs_1_, f32[16,8,2176]{2,1,0:T(8,128)S(1)} %get-tuple-element.207.refs_1_.refs_4_, f32[24,8,2176]{2,1,0:T(8,128)S(1)} %get-tuple-element.187.refs_2_.refs_5_, ...), custom_call_target="tpu_custom_call" | custom-call | flops 100000000 | bytes 8000000 | tf_op jit(solution)/shard_map/inside3/pallas_call | solution.py:355
  78.2 1.9 %collective-permute-done.18.refs_2_ = f32[3,8,2176]{2,1,0:T(8,128)S(1)} collective-permute-done((f32[3,8,2176]{2,1,0:T(8,128)S(1)}, f32[3,8,2176]{2,1,0:T(8,128)S(1)}, u32[]{:S(2)}, u32[]{:S(2)}) %collective-permute-start.18) | collective-permute-done | bytes 208928 | tf_op jit(solution)/shard_map/ppermute | solution.py:607
  80.1 0.0 collective-permute-done.19.refs_3_
  80.1 2.0 %outside3.1 = (f32[1,128]{1,0:T(1,128)S(1)}, f32[24,8,2176]{2,1,0:T(8,128)S(1)}, f32[18,8,2176]{2,1,0:T(8,128)S(1)}) custom-call(f32[4]{0:T(128)S(1)} %add_convert_fusion.flags.refs_0_, f32[8,128]{1,0:T(8,128)S(1)} %broadcast_select_fusion.refs_0_.refs_1_, f32[3,8,2176]{2,1,0:T(8,128)S(1)} %collective-permute-done.18.refs_2_, ...), custom_call_target="tpu_custom_call" | custom-call | tf_op jit(solution)/shard_map/outside3/pallas_call | solution.py:374
  82.1 0.0 collective-permute-start.20
  82.1 1.1 collective-permute-done.20
  83.2 1.9 %collective-permute-start.21 = (f32[1,128]{1,0:T(1,128)S(1)}, f32[1,128]{1,0:T(1,128)S(1)}, u32[]{:S(2)}, u32[]{:S(2)}) collective-permute-start(f32[1,128]{1,0:T(1,128)S(1)} %add.114), channel_id=1, source_target_pairs={{0,2},{1,3},{2,0},{3,1},{4,6},{5,7},{6,4},{7,5},{8,10},{9,11},{10,... | collective-permute-start | bytes 1544 | tf_op jit(solution)/shard_map/ppermute | solution.py:615
  85.2 1.6 %collective-permute-done.21 = f32[1,128]{1,0:T(1,128)S(1)} collective-permute-done((f32[1,128]{1,0:T(1,128)S(1)}, f32[1,128]{1,0:T(1,128)S(1)}, u32[]{:S(2)}, u32[]{:S(2)}) %collective-permute-start.21) | collective-permute-done | bytes 544 | tf_op jit(solution)/shard_map/ppermute | solution.py:615
  86.8 3.8 %collective-permute-start.22 = (f32[1,128]{1,0:T(1,128)S(1)}, f32[1,128]{1,0:T(1,128)S(1)}, u32[]{:S(2)}, u32[]{:S(2)}) collective-permute-start(f32[1,128]{1,0:T(1,128)S(1)} %add.115), channel_id=1, source_target_pairs={{0,6},{1,7},{2,4},{3,5},{4,2},{5,3},{6,0},{7,1},{8,14},{9,15},{10,... | collective-permute-start | bytes 1544 | tf_op jit(solution)/shard_map/ppermute | solution.py:615
  90.6 1.5 %collective-permute-done.22 = f32[1,128]{1,0:T(1,128)S(1)} collective-permute-done((f32[1,128]{1,0:T(1,128)S(1)}, f32[1,128]{1,0:T(1,128)S(1)}, u32[]{:S(2)}, u32[]{:S(2)}) %collective-permute-start.22) | collective-permute-done | bytes 544 | tf_op jit(solution)/shard_map/ppermute | solution.py:615
  92.1 0.0 collective-permute-start.23
  92.1 3.5 %collective-permute-done.23 = f32[1,128]{1,0:T(1,128)S(1)} collective-permute-done((f32[1,128]{1,0:T(1,128)S(1)}, f32[1,128]{1,0:T(1,128)S(1)}, u32[]{:S(2)}, u32[]{:S(2)}) %collective-permute-start.23) | collective-permute-done | bytes 544 | tf_op jit(solution)/shard_map/ppermute | solution.py:615
  95.7 0.2 collective-permute-start.24
  95.9 4.6 %collective-permute-done.24 = f32[1,128]{1,0:T(1,128)S(1)} collective-permute-done((f32[1,128]{1,0:T(1,128)S(1)}, f32[1,128]{1,0:T(1,128)S(1)}, u32[]{:S(2)}, u32[]{:S(2)}) %collective-permute-start.24) | collective-permute-done | bytes 544 | tf_op jit(solution)/shard_map/ppermute | solution.py:615
  100.4 0.0 collective-permute-start.25
  100.5 0.6 convert_bitcast_fusion
  101.1 2.9 %collective-permute-done.25 = f32[1,128]{1,0:T(1,128)S(1)} collective-permute-done((f32[1,128]{1,0:T(1,128)S(1)}, f32[1,128]{1,0:T(1,128)S(1)}, u32[]{:S(2)}, u32[]{:S(2)}) %collective-permute-start.25) | collective-permute-done | bytes 544 | tf_op jit(solution)/shard_map/ppermute | solution.py:615
  104.0 2.7 %collective-permute-start.26 = (f32[1,128]{1,0:T(1,128)S(1)}, f32[1,128]{1,0:T(1,128)S(1)}, u32[]{:S(2)}, u32[]{:S(2)}) collective-permute-start(f32[1,128]{1,0:T(1,128)S(1)} %add.119), channel_id=1, source_target_pairs={{0,96},{8,104},{16,112},{24,120},{32,64},{40,72},{48,80},{56,88},{... | collective-permute-start | bytes 1544 | tf_op jit(solution)/shard_map/ppermute | solution.py:615
  106.7 0.7 fusion.23
  107.4 1.5 %columns_hot.1.hot = bf16[2048,2048]{1,0:T(8,128)(2,1)S(1)} custom-call(s32[1,2048]{1,0:T(1,128)S(1)} %bitcast.104), custom_call_target="tpu_custom_call" | custom-call | tf_op jit(solution)/shard_map/columns_hot/pallas_call | solution.py:451
  108.9 0.0 collective-permute-done.26
  109.0 8.9 %finish.1 = (f32[8,16,2048]{2,1,0:T(8,128)}, f32[128,128]{1,0:T(8,128)}, f32[8,128]{1,0:T(8,128)S(1)}) custom-call(f32[1,128]{1,0:T(1,128)S(1)} %add.120.line, s32[1,2048]{1,0:T(1,128)S(1)} %get-tuple-element.339.cells, f32[1,2048]{1,0:T(1,128)S(1)} %get-tuple-element.337.row_frac, f32[1,2048]{1,0:T(1,128)S(1)} %get-tuple-element.338.col_frac, ...), custom_call_target="tpu_custom_call" | custom-call | tf_op jit(solution)/shard_map/finish/pallas_call | solution.py:521
  117.8 0.7 compare_reduce_fusion
  119.2 0.0 copy-start.14
  119.2 0.2 while.28
  119.4 6.6 %all-to-all-start.1 = ((f32[16,8,128]{2,1,0:T(8,128)}), f32[16,8,128]{2,1,0:T(8,128)S(1)}, u32[]{:S(2)}, u32[]{:S(2)}) async-start(f32[16,8,128]{2,1,0:T(8,128)} %bitcast.111), calls=%async_computation.1 | async-start | bytes 131072 | tf_op jit(solution)/shard_map/all_to_all | solution.py:690
  126.1 7.6 %all-to-all-done.1 = f32[16,8,128]{2,1,0:T(8,128)S(1)} async-done(((f32[16,8,128]{2,1,0:T(8,128)}), f32[16,8,128]{2,1,0:T(8,128)S(1)}, u32[]{:S(2)}, u32[]{:S(2)}) %all-to-all-start.1) | async-done | bytes 65568 | tf_op jit(solution)/shard_map/all_to_all | solution.py:690
  133.7 1.6 %fusion.22 = f32[1,1,16,8,128]{4,3,2,1,0:T(8,128)} fusion(s32[1,1,16,8,128]{4,3,2,1,0:T(8,128)} %param.27, f32[16,8,128]{2,1,0:T(8,128)S(1)} %all-to-all-done.1, s32[1,1,16,8,128]{4,3,2,1,0:T(8,128)} %param.26, f32[16,128]{1,0:T(8,128)S(1)} %copy-done.11, f32[8]{0:T(128)S(1)} %subtract_log_fusion, f32[16,128]{1,0:T(8,128)S(1)} %copy-done.10), kind=kLoop, calls=%fused_computation.86 | loop fusion | flops 245760 | bytes 278560 | tf_op jit(solution)/shard_map/broadcast_in_dim | solution.py:704
  (25 shorter events, 0.1 us)
Async XLA Ops:
  0.6 16.8 %copy-start = (f32[8,16,2048]{2,1,0:T(8,128)S(1)}, f32[8,16,2048]{2,1,0:T(8,128)}, u32[]{:S(2)}) copy-start(f32[8,16,2048]{2,1,0:T(8,128)} %refs_1_.3) | copy-start | bytes 3145732
  0.6 16.8 %copy-start.3 = (f32[8,16,2048]{2,1,0:T(8,128)S(1)}, f32[8,16,2048]{2,1,0:T(8,128)}, u32[]{:S(2)}) copy-start(f32[8,16,2048]{2,1,0:T(8,128)} %refs_2_.3) | copy-start | bytes 3145732
  0.7 16.8 %copy-start.5 = (f32[8,16,2048]{2,1,0:T(8,128)S(1)}, f32[8,16,2048]{2,1,0:T(8,128)}, u32[]{:S(2)}) copy-start(f32[8,16,2048]{2,1,0:T(8,128)} %refs_3_.3) | copy-start | bytes 3145732
  2.7 14.7 %all-to-all-start = ((f32[16,3,128]{2,1,0:T(4,128)}), f32[16,3,128]{2,1,0:T(4,128)S(1)}, u32[]{:S(2)}, u32[]{:S(2)}) async-start(f32[16,3,128]{2,1,0:T(4,128)} %get-tuple-element.170), calls=%async_computation | async-start | bytes 65536 | tf_op jit(solution)/shard_map/all_to_all | solution.py:657
  9.8 7.6 %collective-permute-start.10 = (f32[16,8,128]{2,1,0:T(8,128)}, f32[16,8,128]{2,1,0:T(8,128)S(1)}, u32[]{:S(2)}, u32[]{:S(2)}) collective-permute-start(f32[16,8,128]{2,1,0:T(8,128)} %get-tuple-element.172), channel_id=1, source_target_pairs={{0,1},{1,2},{2,3},{3,4},{4,5},{5,6},{6,7},{7,0},{8,9},{9,10},{10,1... | collective-permute-start | bytes 196616 | tf_op jit(solution)/shard_map/ppermute | solution.py:607
  9.9 7.6 %collective-permute-start.11 = (f32[16,8,128]{2,1,0:T(8,128)}, f32[16,8,128]{2,1,0:T(8,128)S(1)}, u32[]{:S(2)}, u32[]{:S(2)}) collective-permute-start(f32[16,8,128]{2,1,0:T(8,128)} %get-tuple-element.173), channel_id=1, source_target_pairs={{0,7},{1,0},{2,1},{3,2},{4,3},{5,4},{6,5},{7,6},{8,15},{9,8},{10,9... | collective-permute-start | bytes 196616 | tf_op jit(solution)/shard_map/ppermute | solution.py:607
  20.0 22.5 %collective-permute-start.12 = (f32[12,8,2176]{2,1,0:T(8,128)S(1)}, f32[12,8,2176]{2,1,0:T(8,128)S(1)}, u32[]{:S(2)}, u32[]{:S(2)}) collective-permute-start(f32[12,8,2176]{2,1,0:T(8,128)S(1)} %get-tuple-element.174), channel_id=1, source_target_pairs={{0,8},{8,16},{16,24},{24,32},{32,40},{40,48},{48,56},{56,64},{64,7... | collective-permute-start | bytes 2506760 | tf_op jit(solution)/shard_map/ppermute | solution.py:607
  20.6 21.9 %collective-permute-start.13 = (f32[12,8,2176]{2,1,0:T(8,128)S(1)}, f32[12,8,2176]{2,1,0:T(8,128)S(1)}, u32[]{:S(2)}, u32[]{:S(2)}) collective-permute-start(f32[12,8,2176]{2,1,0:T(8,128)S(1)} %get-tuple-element.175), channel_id=1, source_target_pairs={{0,120},{8,0},{16,8},{24,16},{32,24},{40,32},{48,40},{56,48},{64,5... | collective-permute-start | bytes 2506760 | tf_op jit(solution)/shard_map/ppermute | solution.py:607
  45.3 9.9 %collective-permute-start.14 = (f32[4,8,2176]{2,1,0:T(8,128)S(1)}, f32[4,8,2176]{2,1,0:T(8,128)S(1)}, u32[]{:S(2)}, u32[]{:S(2)}) collective-permute-start(f32[4,8,2176]{2,1,0:T(8,128)S(1)} %get-tuple-element.184), channel_id=1, source_target_pairs={{0,8},{8,16},{16,24},{24,32},{32,40},{40,48},{48,56},{56,64},{64,7... | collective-permute-start | bytes 835592 | tf_op jit(solution)/shard_map/ppermute | solution.py:607
  45.4 9.9 %collective-permute-start.15 = (f32[4,8,2176]{2,1,0:T(8,128)S(1)}, f32[4,8,2176]{2,1,0:T(8,128)S(1)}, u32[]{:S(2)}, u32[]{:S(2)}) collective-permute-start(f32[4,8,2176]{2,1,0:T(8,128)S(1)} %get-tuple-element.185), channel_id=1, source_target_pairs={{0,120},{8,0},{16,8},{24,16},{32,24},{40,32},{48,40},{56,48},{64,5... | collective-permute-start | bytes 835592 | tf_op jit(solution)/shard_map/ppermute | solution.py:607
  58.0 9.9 %collective-permute-start.16 = (f32[4,8,2176]{2,1,0:T(8,128)S(1)}, f32[4,8,2176]{2,1,0:T(8,128)S(1)}, u32[]{:S(2)}, u32[]{:S(2)}) collective-permute-start(f32[4,8,2176]{2,1,0:T(8,128)S(1)} %get-tuple-element.196), channel_id=1, source_target_pairs={{0,8},{8,16},{16,24},{24,32},{32,40},{40,48},{48,56},{56,64},{64,7... | collective-permute-start | bytes 835592 | tf_op jit(solution)/shard_map/ppermute | solution.py:607
  58.1 9.9 %collective-permute-start.17 = (f32[4,8,2176]{2,1,0:T(8,128)S(1)}, f32[4,8,2176]{2,1,0:T(8,128)S(1)}, u32[]{:S(2)}, u32[]{:S(2)}) collective-permute-start(f32[4,8,2176]{2,1,0:T(8,128)S(1)} %get-tuple-element.197), channel_id=1, source_target_pairs={{0,120},{8,0},{16,8},{24,16},{32,24},{40,32},{48,40},{56,48},{64,5... | collective-permute-start | bytes 835592 | tf_op jit(solution)/shard_map/ppermute | solution.py:607
  70.7 9.4 %collective-permute-start.18 = (f32[3,8,2176]{2,1,0:T(8,128)S(1)}, f32[3,8,2176]{2,1,0:T(8,128)S(1)}, u32[]{:S(2)}, u32[]{:S(2)}) collective-permute-start(f32[3,8,2176]{2,1,0:T(8,128)S(1)} %get-tuple-element.205), channel_id=1, source_target_pairs={{0,8},{8,16},{16,24},{24,32},{32,40},{40,48},{48,56},{56,64},{64,7... | collective-permute-start | bytes 626696 | tf_op jit(solution)/shard_map/ppermute | solution.py:607
  70.7 9.4 %collective-permute-start.19 = (f32[3,8,2176]{2,1,0:T(8,128)S(1)}, f32[3,8,2176]{2,1,0:T(8,128)S(1)}, u32[]{:S(2)}, u32[]{:S(2)}) collective-permute-start(f32[3,8,2176]{2,1,0:T(8,128)S(1)} %get-tuple-element.206), channel_id=1, source_target_pairs={{0,120},{8,0},{16,8},{24,16},{32,24},{40,32},{48,40},{56,48},{64,5... | collective-permute-start | bytes 626696 | tf_op jit(solution)/shard_map/ppermute | solution.py:607
  76.4 31.0 %copy-start.8 = (s32[16,1,128]{2,1,0:T(1,128)}, s32[16,1,128]{2,1,0:T(1,128)S(1)}, u32[]{:S(2)}) copy-start(s32[16,1,128]{2,1,0:T(1,128)S(1)} %get-tuple-element.341) | copy-start | bytes 24580
  80.1 20.3 %copy-start.12 = (s32[1,1,16,128]{3,2,1,0:T(8,128)S(1)}, s32[1,1,16,128]{3,2,1,0:T(8,128)}, u32[]{:S(2)}) copy-start(s32[1,1,16,128]{3,2,1,0:T(8,128)} %param.25) | copy-start | bytes 24580
  80.1 26.6 %copy-start.13 = (s32[1,1,16]{2,1,0:T(1,128)S(1)}, s32[1,1,16]{2,1,0:T(1,128)}, u32[]{:S(2)}) copy-start(s32[1,1,16]{2,1,0:T(1,128)} %param.24) | copy-start | bytes 196
  82.1 1.1 collective-permute-start.20
  83.2 3.5 %collective-permute-start.21 = (f32[1,128]{1,0:T(1,128)S(1)}, f32[1,128]{1,0:T(1,128)S(1)}, u32[]{:S(2)}, u32[]{:S(2)}) collective-permute-start(f32[1,128]{1,0:T(1,128)S(1)} %add.114), channel_id=1, source_target_pairs={{0,2},{1,3},{2,0},{3,1},{4,6},{5,7},{6,4},{7,5},{8,10},{9,11},{10,... | collective-permute-start | bytes 1544 | tf_op jit(solution)/shard_map/ppermute | solution.py:615
  86.8 5.4 %collective-permute-start.22 = (f32[1,128]{1,0:T(1,128)S(1)}, f32[1,128]{1,0:T(1,128)S(1)}, u32[]{:S(2)}, u32[]{:S(2)}) collective-permute-start(f32[1,128]{1,0:T(1,128)S(1)} %add.115), channel_id=1, source_target_pairs={{0,6},{1,7},{2,4},{3,5},{4,2},{5,3},{6,0},{7,1},{8,14},{9,15},{10,... | collective-permute-start | bytes 1544 | tf_op jit(solution)/shard_map/ppermute | solution.py:615
  92.1 3.5 %collective-permute-start.23 = (f32[1,128]{1,0:T(1,128)S(1)}, f32[1,128]{1,0:T(1,128)S(1)}, u32[]{:S(2)}, u32[]{:S(2)}) collective-permute-start(f32[1,128]{1,0:T(1,128)S(1)} %add.116), channel_id=1, source_target_pairs={{0,8},{8,0},{16,24},{24,16},{32,40},{40,32},{48,56},{56,48},{64,72... | collective-permute-start | bytes 1544 | tf_op jit(solution)/shard_map/ppermute | solution.py:615
  95.7 4.8 %collective-permute-start.24 = (f32[1,128]{1,0:T(1,128)S(1)}, f32[1,128]{1,0:T(1,128)S(1)}, u32[]{:S(2)}, u32[]{:S(2)}) collective-permute-start(f32[1,128]{1,0:T(1,128)S(1)} %add.117), channel_id=1, source_target_pairs={{0,24},{8,16},{16,8},{24,0},{32,56},{40,48},{48,40},{56,32},{64,88... | collective-permute-start | bytes 1544 | tf_op jit(solution)/shard_map/ppermute | solution.py:615
  100.4 3.5 %collective-permute-start.25 = (f32[1,128]{1,0:T(1,128)S(1)}, f32[1,128]{1,0:T(1,128)S(1)}, u32[]{:S(2)}, u32[]{:S(2)}) collective-permute-start(f32[1,128]{1,0:T(1,128)S(1)} %add.118), channel_id=1, source_target_pairs={{0,32},{8,40},{16,48},{24,56},{32,0},{40,8},{48,16},{56,24},{64,96... | collective-permute-start | bytes 1544 | tf_op jit(solution)/shard_map/ppermute | solution.py:615
  104.0 4.9 %collective-permute-start.26 = (f32[1,128]{1,0:T(1,128)S(1)}, f32[1,128]{1,0:T(1,128)S(1)}, u32[]{:S(2)}, u32[]{:S(2)}) collective-permute-start(f32[1,128]{1,0:T(1,128)S(1)} %add.119), channel_id=1, source_target_pairs={{0,96},{8,104},{16,112},{24,120},{32,64},{40,72},{48,80},{56,88},{... | collective-permute-start | bytes 1544 | tf_op jit(solution)/shard_map/ppermute | solution.py:615
  108.9 10.2 %copy-start.9 = (s32[16,1,128]{2,1,0:T(1,128)S(1)}, s32[16,1,128]{2,1,0:T(1,128)}, u32[]{:S(2)}) copy-start(s32[16,1,128]{2,1,0:T(1,128)} %copy-done.8) | copy-start | bytes 24580
  119.2 6.9 %copy-start.14 = (f32[8]{0:T(128)S(1)}, f32[8]{0:T(128)}, u32[]{:S(2)}) copy-start(f32[8]{0:T(128)} %param.21) | copy-start | bytes 100
  119.2 14.5 %copy-start.10 = (f32[16,128]{1,0:T(8,128)S(1)}, f32[16,128]{1,0:T(8,128)}, u32[]{:S(2)}) copy-start(f32[16,128]{1,0:T(8,128)} %convert_bitcast_fusion) | copy-start | bytes 24580
  119.2 14.5 %copy-start.11 = (f32[16,128]{1,0:T(8,128)S(1)}, f32[16,128]{1,0:T(8,128)}, u32[]{:S(2)}) copy-start(f32[16,128]{1,0:T(8,128)} %fusion.23) | copy-start | bytes 24580
  119.4 14.3 %all-to-all-start.1 = ((f32[16,8,128]{2,1,0:T(8,128)}), f32[16,8,128]{2,1,0:T(8,128)S(1)}, u32[]{:S(2)}, u32[]{:S(2)}) async-start(f32[16,8,128]{2,1,0:T(8,128)} %bitcast.111), calls=%async_computation.1 | async-start | bytes 131072 | tf_op jit(solution)/shard_map/all_to_all | solution.py:690

commit v8 on v7

--- a/solution.py
+++ b/solution.py
@@ -460,8 +460,7 @@
 
 def finish_kernel(rows, cols, line, cells, row_frac, col_frac, hot, *refs):
     basis, refs = refs[:ITERS], refs[ITERS:]
-    latent, predictor, fine, parts, keep = refs
-    wide = cols + LANES
+    latent, predictor, fine, parts, keep, laid, sent = refs
     lat_in, good = coefficients(line[...])
     fine[...] = jnp.where(good, 1.0, 0.0)
     for k in range(ITERS):
@@ -475,26 +474,27 @@
         parts[base : base + tall, at] = part.reshape(tall, LANES)
         parts[base + tall : base + 2 * tall, at] = rest.reshape(tall, LANES)
 
-    def step(c, after):
-        c = wide // LANES - 1 - c
-        at = pl.ds(pl.multiple_of(c * LANES, LANES), LANES)
+    def combined(at):
         total = None
         for k in range(ITERS):
             begin = PAD - SKIP * (k % 2)
             term = keep[k] * basis[k][begin : begin + rows + 1, :, at]
             total = term if total is None else total + term
-        total = jnp.concatenate([total, jnp.zeros((1, F, LANES), jnp.float32)], axis=0)
+        return jnp.concatenate([total, jnp.zeros((1, F, LANES), jnp.float32)], axis=0)
+
+    def step(c, after):
+        at = pl.ds(pl.multiple_of((cols // LANES - 1 - c) * LANES, LANES), LANES)
+        total = combined(at)
         turned = pltpu.roll(total, LANES - 1, 2)
-
-        @pl.when(c < cols // LANES)
-        def _():
-            split(total, at, 0)
-            split(jnp.where(lane == LANES - 1, after, turned), at, 2 * tall)
-            latent[:, :, at] = jnp.swapaxes(total[:rows], 0, 1)
-
+        split(total, at, 0)
+        split(jnp.where(lane == LANES - 1, after, turned), at, 2 * tall)
+        laid[:, :, at] = jnp.swapaxes(total[:rows], 0, 1)
         return turned
 
-    lax.fori_loop(0, wide // LANES, step, jnp.zeros((rows + 2, F, LANES), jnp.float32))
+    beyond = pltpu.roll(combined(slice(cols, cols + LANES)), LANES - 1, 2)
+    lax.fori_loop(0, cols // LANES, step, beyond, unroll=2)
+    copy = pltpu.make_async_copy(laid, latent, sent)
+    copy.start()
     for c in range(0, cells.shape[1], CHUNK):
         at = slice(c, c + CHUNK)
         both = jnp.dot(parts[...], hot[:, at], preferred_element_type=jnp.float32)
@@ -513,23 +513,25 @@
         for i in range(CHUNK // LANES):
             base = (c // LANES + i) * F
             predictor[base : base + F] = out[:, i * LANES : (i + 1) * LANES]
+    copy.wait()
 
 
 def finish(rows, cols, line, cells, row_frac, col_frac, hot, basis):
     f32 = jnp.float32
-    wide = cols + LANES
     return pl.pallas_call(
         functools.partial(finish_kernel, rows, cols),
         in_specs=[VMEM] * (5 + ITERS),
-        out_specs=[VMEM] * 3,
+        out_specs=[HBM, VMEM, VMEM],
         out_shape=[
-            jax.ShapeDtypeStruct((F, rows, cols), f32),
+            pltpu.HBM((F, rows, cols), f32),
             jax.ShapeDtypeStruct((cells.shape[1] // LANES * F, LANES), f32),
             jax.ShapeDtypeStruct((F, LANES), f32),
         ],
         scratch_shapes=[
             pltpu.VMEM((4 * (rows + 2) * F, cols), jnp.bfloat16),
             pltpu.VMEM((ITERS, F, LANES), f32),
+            pltpu.VMEM((F, rows, cols), f32),
+            pltpu.SemaphoreType.DMA,
         ],
         compiler_params=PARAMS,
         name="finish",
@@ -679,7 +681,9 @@
 
     line, got_cells = lax.optimization_barrier((line, got_cells))
     hot = columns_hot(got_cells.reshape(1, -1), cols)
-    line = summed(summed(line, "field"), "tile")
+    line = summed(line, "field")
+    line, hot = lax.optimization_barrier((line, hot))
+    line = summed(line, "tile")
     latent, predictor, fine = finish(rows, cols, line, *sites, hot, basis)
     latent, predictor, _ = lax.while_loop(
         lambda state: state[2],

time: 136 us -> 136 us (level)
  no operation moved by 1% of the time
where the time goes in v8:
time: 136 us; the launch traced here: 135 us
  starting transfers between devices  48.1 us (35%)
  waiting for transfers between devices  45.9 us (34%)
  Pallas kernels  33.7 us (25%)
  other arithmetic  5.01 us (4%)
  between operations  1.55 us (1%)
    ppermute x10, starting transfers between devices, turned(): return lax.ppermute(x, axis, [(i, (i + by) % size) for i in range(size)])  25.5 us
    ppermute x10, waiting for transfers between devices, turned(): return lax.ppermute(x, axis, [(i, (i + by) % size) for i in range(size)])  18.8 us
    ppermute x6, waiting for transfers between devices, summed(): lax.ppermute(x, axis, [(i, other(i, stride, by)) for i in range(size)])  14.1 us
    pallas_call x4, Pallas kernels, phase(): pl.pallas_call(functools.partial(outside_kernel, p, rows, cols), in_specs...  10.3 us
    pallas_call x4, Pallas kernels, phase(): pl.pallas_call(functools.partial(inside_kernel, p, cols), in_specs=[VMEM]...  8.79 us
    ppermute x6, starting transfers between devices, summed(): lax.ppermute(x, axis, [(i, other(i, stride, by)) for i in range(size)])  8.7 us
    pallas_call x1, Pallas kernels, finish(): pl.pallas_call(functools.partial(finish_kernel, rows, cols), in_specs=[VM...  8.59 us
    all_to_all x1, waiting for transfers between devices, local(): lax.all_to_all(predictor, 'tile', split_axis=0, concat_axis=0, tiled=True)  7.64 us
  transfers between devices with their start and end apart: 19, of which 12 were waited for; matrix products, arithmetic and copies ran while one was open for 2% of the time, Pallas kernels for 8%

profile of v8, /device:TPU:0, one launch (start us, length us, event | category | flops | bytes accessed | tf_op | source)
XLA Modules:
  0.0 135.1 jit_solution(9654979076244669184)
XLA Ops:
  0.6 0.0 copy-start
  0.6 0.0 copy-start.3
  0.7 0.0 copy-start.5
  0.7 2.1 %columns.1 = (f32[16,8,128]{2,1,0:T(8,128)}, f32[16,8,128]{2,1,0:T(8,128)}, f32[16,3,128]{2,1,0:T(4,128)}) custom-call(f32[8,16,2048]{2,1,0:T(8,128)} %refs_0_.3, f32[8,16,2048]{2,1,0:T(8,128)} %refs_1_.3, f32[8,16,2048]{2,1,0:T(8,128)} %refs_2_.3, f32[8,16,2048]{2,1,0:T(8,128)} %refs_3_.3, f32[8,16,2048]{2,1,0:T(8,128)} %refs_0_.3, f32[8,16,2048]{2,1,0:T(8,128)} %refs_1_.3, ...), custom_call_target="tpu_custom_call" | custom-call | tf_op jit(solution)/shard_map/columns/pallas_call | solution.py:56
  2.7 7.1 %all-to-all-start = ((f32[16,3,128]{2,1,0:T(4,128)}), f32[16,3,128]{2,1,0:T(4,128)S(1)}, u32[]{:S(2)}, u32[]{:S(2)}) async-start(f32[16,3,128]{2,1,0:T(4,128)} %get-tuple-element.172), calls=%async_computation | async-start | bytes 65536 | tf_op jit(solution)/shard_map/all_to_all | solution.py:659
  9.8 0.0 collective-permute-start.10
  9.9 3.2 %collective-permute-start.11 = (f32[16,8,128]{2,1,0:T(8,128)}, f32[16,8,128]{2,1,0:T(8,128)S(1)}, u32[]{:S(2)}, u32[]{:S(2)}) collective-permute-start(f32[16,8,128]{2,1,0:T(8,128)} %get-tuple-element.175), channel_id=1, source_target_pairs={{0,7},{1,0},{2,1},{3,2},{4,3},{5,4},{6,5},{7,6},{8,15},{9,8},{10,9... | collective-permute-start | bytes 196616 | tf_op jit(solution)/shard_map/ppermute | solution.py:609
  13.1 0.1 add_convert_fusion.flags.refs_0_
  13.2 4.3 %all-to-all-done = f32[16,3,128]{2,1,0:T(4,128)S(1)} async-done(((f32[16,3,128]{2,1,0:T(4,128)}), f32[16,3,128]{2,1,0:T(4,128)S(1)}, u32[]{:S(2)}, u32[]{:S(2)}) %all-to-all-start) | async-done | bytes 24608 | tf_op jit(solution)/shard_map/all_to_all | solution.py:659
  17.5 0.0 collective-permute-done.10.left
  17.5 0.0 collective-permute-done.11.right
  17.5 0.0 copy-done.3
  17.5 2.4 %prepare.1 = (f32[16,8,2176]{2,1,0:T(8,128)S(1)}, f32[16,8,2176]{2,1,0:T(8,128)S(1)}, f32[16,8,2176]{2,1,0:T(8,128)S(1)}, f32[16,8,2176]{2,1,0:T(8,128)S(1)}, f3...) custom-call(f32[4]{0:T(128)S(1)} %add_convert_fusion.flags.refs_0_, f32[16,8,128]{2,1,0:T(8,128)S(1)} %collective-permute-done.10.left, ...), custom_call_target="tpu_custom_call" | custom-call | tf_op jit(solution)/shard_map/prepare/pallas_call | solution.py:112
  20.0 0.6 collective-permute-start.12
  20.6 4.8 %collective-permute-start.13 = (f32[12,8,2176]{2,1,0:T(8,128)S(1)}, f32[12,8,2176]{2,1,0:T(8,128)S(1)}, u32[]{:S(2)}, u32[]{:S(2)}) collective-permute-start(f32[12,8,2176]{2,1,0:T(8,128)S(1)} %get-tuple-element.177), channel_id=1, source_target_pairs={{0,120},{8,0},{16,8},{24,16},{32,24},{40,32},{48,40},{56,48},{64,5... | collective-permute-start | bytes 2506760 | tf_op jit(solution)/shard_map/ppermute | solution.py:609
  25.4 0.6 fusion.30
  26.0 0.6 compare_select_fusion.4
  26.6 0.7 broadcast_select_fusion.refs_0_.refs_1_
  27.3 2.4 %inside0.1 = (f32[12,8,2176]{2,1,0:T(8,128)S(1)}, f32[12,8,2176]{2,1,0:T(8,128)S(1)}, f32[8,8,2176]{2,1,0:T(8,128)S(1)}, f32[5,8,128]{2,1,0:T(8,128)S(1)}) custom-call(f32[8,128]{1,0:T(8,128)S(1)} %broadcast_select_fusion.refs_0_.refs_1_, f32[16,8,2176]{2,1,0:T(8,128)S(1)} %get-tuple-element.178.refs_1_.refs_4_, ...), custom_call_target="tpu_custom_call" | custom-call | flops 100000000 | bytes 8000000 | tf_op jit(solution)/shard_map/inside0/pallas_call | solution.py:355
  29.7 12.8 %collective-permute-done.12.refs_2_ = f32[12,8,2176]{2,1,0:T(8,128)S(1)} collective-permute-done((f32[12,8,2176]{2,1,0:T(8,128)S(1)}, f32[12,8,2176]{2,1,0:T(8,128)S(1)}, u32[]{:S(2)}, u32[]{:S(2)}) %collective-permute-start.12) | collective-permute-done | bytes 835616 | tf_op jit(solution)/shard_map/ppermute | solution.py:609
  42.4 0.0 collective-permute-done.13.refs_3_
  42.4 2.8 %outside0.1 = (f32[24,8,2176]{2,1,0:T(8,128)S(1)}, f32[18,8,2176]{2,1,0:T(8,128)S(1)}, f32[24,8,2176]{2,1,0:T(8,128)S(1)}, f32[24,8,2176]{2,1,0:T(8,128)S(1)}, f...) custom-call(f32[4]{0:T(128)S(1)} %add_convert_fusion.flags.refs_0_, ...), custom_call_target="tpu_custom_call" | custom-call | tf_op jit(solution)/shard_map/outside0/pallas_call | solution.py:374
  45.3 0.1 collective-permute-start.14
  45.4 5.3 %collective-permute-start.15 = (f32[4,8,2176]{2,1,0:T(8,128)S(1)}, f32[4,8,2176]{2,1,0:T(8,128)S(1)}, u32[]{:S(2)}, u32[]{:S(2)}) collective-permute-start(f32[4,8,2176]{2,1,0:T(8,128)S(1)} %get-tuple-element.187), channel_id=1, source_target_pairs={{0,120},{8,0},{16,8},{24,16},{32,24},{40,32},{48,40},{56,48},{64,5... | collective-permute-start | bytes 835592 | tf_op jit(solution)/shard_map/ppermute | solution.py:609
  50.7 2.3 %inside1.1 = (f32[12,8,2176]{2,1,0:T(8,128)S(1)}, f32[12,8,2176]{2,1,0:T(8,128)S(1)}, f32[8,8,2176]{2,1,0:T(8,128)S(1)}, f32[4,8,128]{2,1,0:T(8,128)S(1)}) custom-call(f32[8,128]{1,0:T(8,128)S(1)} %broadcast_select_fusion.refs_0_.refs_1_, f32[16,8,2176]{2,1,0:T(8,128)S(1)} %get-tuple-element.188.refs_1_.refs_4_, ...), custom_call_target="tpu_custom_call" | custom-call | flops 100000000 | bytes 8000000 | tf_op jit(solution)/shard_map/inside1/pallas_call | solution.py:355
  53.0 2.2 %collective-permute-done.14.refs_2_ = f32[4,8,2176]{2,1,0:T(8,128)S(1)} collective-permute-done((f32[4,8,2176]{2,1,0:T(8,128)S(1)}, f32[4,8,2176]{2,1,0:T(8,128)S(1)}, u32[]{:S(2)}, u32[]{:S(2)}) %collective-permute-start.14) | collective-permute-done | bytes 278560 | tf_op jit(solution)/shard_map/ppermute | solution.py:609
  55.2 0.0 collective-permute-done.15.refs_3_
  55.2 2.7 %outside1.1 = (f32[24,8,2176]{2,1,0:T(8,128)S(1)}, f32[18,8,2176]{2,1,0:T(8,128)S(1)}, f32[16,8,2176]{2,1,0:T(8,128)S(1)}, f32[4,8,2176]{2,1,0:T(8,128)S(1)}, f3...) custom-call(f32[4]{0:T(128)S(1)} %add_convert_fusion.flags.refs_0_, f32[8,128]{1,0:T(8,128)S(1)} %broadcast_select_fusion.refs_0_.refs_1_, ...), custom_call_target="tpu_custom_call" | custom-call | tf_op jit(solution)/shard_map/outside1/pallas_call | solution.py:374
  58.0 0.1 collective-permute-start.16
  58.1 5.6 %collective-permute-start.17 = (f32[4,8,2176]{2,1,0:T(8,128)S(1)}, f32[4,8,2176]{2,1,0:T(8,128)S(1)}, u32[]{:S(2)}, u32[]{:S(2)}) collective-permute-start(f32[4,8,2176]{2,1,0:T(8,128)S(1)} %get-tuple-element.199), channel_id=1, source_target_pairs={{0,120},{8,0},{16,8},{24,16},{32,24},{40,32},{48,40},{56,48},{64,5... | collective-permute-start | bytes 835592 | tf_op jit(solution)/shard_map/ppermute | solution.py:609
  63.6 2.3 %inside2.1 = (f32[12,8,2176]{2,1,0:T(8,128)S(1)}, f32[12,8,2176]{2,1,0:T(8,128)S(1)}, f32[8,8,2176]{2,1,0:T(8,128)S(1)}, f32[4,8,128]{2,1,0:T(8,128)S(1)}) custom-call(f32[8,128]{1,0:T(8,128)S(1)} %broadcast_select_fusion.refs_0_.refs_1_, f32[16,8,2176]{2,1,0:T(8,128)S(1)} %get-tuple-element.200.refs_1_.refs_4_, ...), custom_call_target="tpu_custom_call" | custom-call | flops 100000000 | bytes 8000000 | tf_op jit(solution)/shard_map/inside2/pallas_call | solution.py:355
  66.0 1.9 %collective-permute-done.16.refs_2_ = f32[4,8,2176]{2,1,0:T(8,128)S(1)} collective-permute-done((f32[4,8,2176]{2,1,0:T(8,128)S(1)}, f32[4,8,2176]{2,1,0:T(8,128)S(1)}, u32[]{:S(2)}, u32[]{:S(2)}) %collective-permute-start.16) | collective-permute-done | bytes 278560 | tf_op jit(solution)/shard_map/ppermute | solution.py:609
  67.9 0.0 collective-permute-done.17.refs_3_
  67.9 2.7 %outside2.1 = (f32[24,8,2176]{2,1,0:T(8,128)S(1)}, f32[18,8,2176]{2,1,0:T(8,128)S(1)}, f32[16,8,2176]{2,1,0:T(8,128)S(1)}, f32[3,8,2176]{2,1,0:T(8,128)S(1)}, f3...) custom-call(f32[4]{0:T(128)S(1)} %add_convert_fusion.flags.refs_0_, f32[8,128]{1,0:T(8,128)S(1)} %broadcast_select_fusion.refs_0_.refs_1_, ...), custom_call_target="tpu_custom_call" | custom-call | tf_op jit(solution)/shard_map/outside2/pallas_call | solution.py:374
  70.7 0.1 collective-permute-start.18
  70.7 5.7 %collective-permute-start.19 = (f32[3,8,2176]{2,1,0:T(8,128)S(1)}, f32[3,8,2176]{2,1,0:T(8,128)S(1)}, u32[]{:S(2)}, u32[]{:S(2)}) collective-permute-start(f32[3,8,2176]{2,1,0:T(8,128)S(1)} %get-tuple-element.208), channel_id=1, source_target_pairs={{0,120},{8,0},{16,8},{24,16},{32,24},{40,32},{48,40},{56,48},{64,5... | collective-permute-start | bytes 626696 | tf_op jit(solution)/shard_map/ppermute | solution.py:609
  76.4 1.8 %inside3.1 = (f32[12,8,2176]{2,1,0:T(8,128)S(1)}, f32[3,8,128]{2,1,0:T(8,128)S(1)}) custom-call(f32[8,128]{1,0:T(8,128)S(1)} %broadcast_select_fusion.refs_0_.refs_1_, f32[16,8,2176]{2,1,0:T(8,128)S(1)} %get-tuple-element.209.refs_1_.refs_4_, f32[24,8,2176]{2,1,0:T(8,128)S(1)} %get-tuple-element.189.refs_2_.refs_5_, ...), custom_call_target="tpu_custom_call" | custom-call | flops 100000000 | bytes 8000000 | tf_op jit(solution)/shard_map/inside3/pallas_call | solution.py:355
  78.2 1.9 %collective-permute-done.18.refs_2_ = f32[3,8,2176]{2,1,0:T(8,128)S(1)} collective-permute-done((f32[3,8,2176]{2,1,0:T(8,128)S(1)}, f32[3,8,2176]{2,1,0:T(8,128)S(1)}, u32[]{:S(2)}, u32[]{:S(2)}) %collective-permute-start.18) | collective-permute-done | bytes 208928 | tf_op jit(solution)/shard_map/ppermute | solution.py:609
  80.1 0.0 collective-permute-done.19.refs_3_
  80.1 2.0 %outside3.1 = (f32[1,128]{1,0:T(1,128)S(1)}, f32[24,8,2176]{2,1,0:T(8,128)S(1)}, f32[18,8,2176]{2,1,0:T(8,128)S(1)}) custom-call(f32[4]{0:T(128)S(1)} %add_convert_fusion.flags.refs_0_, f32[8,128]{1,0:T(8,128)S(1)} %broadcast_select_fusion.refs_0_.refs_1_, f32[3,8,2176]{2,1,0:T(8,128)S(1)} %collective-permute-done.18.refs_2_, ...), custom_call_target="tpu_custom_call" | custom-call | tf_op jit(solution)/shard_map/outside3/pallas_call | solution.py:374
  82.1 0.0 collective-permute-start.20
  82.1 1.1 collective-permute-done.20
  83.2 1.9 %collective-permute-start.21 = (f32[1,128]{1,0:T(1,128)S(1)}, f32[1,128]{1,0:T(1,128)S(1)}, u32[]{:S(2)}, u32[]{:S(2)}) collective-permute-start(f32[1,128]{1,0:T(1,128)S(1)} %add.114), channel_id=1, source_target_pairs={{0,2},{1,3},{2,0},{3,1},{4,6},{5,7},{6,4},{7,5},{8,10},{9,11},{10,... | collective-permute-start | bytes 1544 | tf_op jit(solution)/shard_map/ppermute | solution.py:617
  85.1 1.6 %collective-permute-done.21 = f32[1,128]{1,0:T(1,128)S(1)} collective-permute-done((f32[1,128]{1,0:T(1,128)S(1)}, f32[1,128]{1,0:T(1,128)S(1)}, u32[]{:S(2)}, u32[]{:S(2)}) %collective-permute-start.21) | collective-permute-done | bytes 544 | tf_op jit(solution)/shard_map/ppermute | solution.py:617
  86.8 3.8 %collective-permute-start.22 = (f32[1,128]{1,0:T(1,128)S(1)}, f32[1,128]{1,0:T(1,128)S(1)}, u32[]{:S(2)}, u32[]{:S(2)}) collective-permute-start(f32[1,128]{1,0:T(1,128)S(1)} %add.115), channel_id=1, source_target_pairs={{0,6},{1,7},{2,4},{3,5},{4,2},{5,3},{6,0},{7,1},{8,14},{9,15},{10,... | collective-permute-start | bytes 1544 | tf_op jit(solution)/shard_map/ppermute | solution.py:617
  90.6 1.5 %columns_hot.1.hot = bf16[2048,2048]{1,0:T(8,128)(2,1)S(1)} custom-call(s32[1,2048]{1,0:T(1,128)S(1)} %bitcast.104), custom_call_target="tpu_custom_call" | custom-call | tf_op jit(solution)/shard_map/columns_hot/pallas_call | solution.py:451
  92.1 0.0 collective-permute-done.22
  92.2 0.1 collective-permute-start.23
  92.2 3.5 %collective-permute-done.23 = f32[1,128]{1,0:T(1,128)S(1)} collective-permute-done((f32[1,128]{1,0:T(1,128)S(1)}, f32[1,128]{1,0:T(1,128)S(1)}, u32[]{:S(2)}, u32[]{:S(2)}) %collective-permute-start.23) | collective-permute-done | bytes 544 | tf_op jit(solution)/shard_map/ppermute | solution.py:617
  95.8 0.1 collective-permute-start.24
  95.9 4.6 %collective-permute-done.24 = f32[1,128]{1,0:T(1,128)S(1)} collective-permute-done((f32[1,128]{1,0:T(1,128)S(1)}, f32[1,128]{1,0:T(1,128)S(1)}, u32[]{:S(2)}, u32[]{:S(2)}) %collective-permute-start.24) | collective-permute-done | bytes 544 | tf_op jit(solution)/shard_map/ppermute | solution.py:617
  100.5 0.0 collective-permute-start.25
  100.5 0.6 convert_bitcast_fusion
  101.1 2.9 %collective-permute-done.25 = f32[1,128]{1,0:T(1,128)S(1)} collective-permute-done((f32[1,128]{1,0:T(1,128)S(1)}, f32[1,128]{1,0:T(1,128)S(1)}, u32[]{:S(2)}, u32[]{:S(2)}) %collective-permute-start.25) | collective-permute-done | bytes 544 | tf_op jit(solution)/shard_map/ppermute | solution.py:617
  104.1 2.7 %collective-permute-start.26 = (f32[1,128]{1,0:T(1,128)S(1)}, f32[1,128]{1,0:T(1,128)S(1)}, u32[]{:S(2)}, u32[]{:S(2)}) collective-permute-start(f32[1,128]{1,0:T(1,128)S(1)} %add.119), channel_id=1, source_target_pairs={{0,96},{8,104},{16,112},{24,120},{32,64},{40,72},{48,80},{56,88},{... | collective-permute-start | bytes 1544 | tf_op jit(solution)/shard_map/ppermute | solution.py:617
  106.8 0.7 fusion.23
  107.5 1.3 collective-permute-done.26
  108.8 8.6 %finish.1 = (f32[8,16,2048]{2,1,0:T(8,128)}, f32[128,128]{1,0:T(8,128)}, f32[8,128]{1,0:T(8,128)S(1)}) custom-call(f32[1,128]{1,0:T(1,128)S(1)} %add.120.line, s32[1,2048]{1,0:T(1,128)S(1)} %get-tuple-element.343.cells, f32[1,2048]{1,0:T(1,128)S(1)} %get-tuple-element.341.row_frac, f32[1,2048]{1,0:T(1,128)S(1)} %get-tuple-element.342.col_frac, ...), custom_call_target="tpu_custom_call" | custom-call | tf_op jit(solution)/shard_map/finish/pallas_call | solution.py:521
  117.4 0.7 compare_reduce_fusion
  118.8 0.0 copy-start.14
  118.8 0.2 while.28
  119.0 6.8 %all-to-all-start.1 = ((f32[16,8,128]{2,1,0:T(8,128)}), f32[16,8,128]{2,1,0:T(8,128)S(1)}, u32[]{:S(2)}, u32[]{:S(2)}) async-start(f32[16,8,128]{2,1,0:T(8,128)} %bitcast.111), calls=%async_computation.1 | async-start | bytes 131072 | tf_op jit(solution)/shard_map/all_to_all | solution.py:694
  125.9 7.6 %all-to-all-done.1 = f32[16,8,128]{2,1,0:T(8,128)S(1)} async-done(((f32[16,8,128]{2,1,0:T(8,128)}), f32[16,8,128]{2,1,0:T(8,128)S(1)}, u32[]{:S(2)}, u32[]{:S(2)}) %all-to-all-start.1) | async-done | bytes 65568 | tf_op jit(solution)/shard_map/all_to_all | solution.py:694
  133.5 1.6 %fusion.22 = f32[1,1,16,8,128]{4,3,2,1,0:T(8,128)} fusion(s32[1,1,16,8,128]{4,3,2,1,0:T(8,128)} %param.27, f32[16,8,128]{2,1,0:T(8,128)S(1)} %all-to-all-done.1, s32[1,1,16,8,128]{4,3,2,1,0:T(8,128)} %param.26, f32[16,128]{1,0:T(8,128)S(1)} %copy-done.11, f32[8]{0:T(128)S(1)} %subtract_log_fusion, f32[16,128]{1,0:T(8,128)S(1)} %copy-done.10), kind=kLoop, calls=%fused_computation.86 | loop fusion | flops 245760 | bytes 278560 | tf_op jit(solution)/shard_map/broadcast_in_dim | solution.py:708
  (25 shorter events, 0.1 us)
Async XLA Ops:
  0.6 16.8 %copy-start = (f32[8,16,2048]{2,1,0:T(8,128)S(1)}, f32[8,16,2048]{2,1,0:T(8,128)}, u32[]{:S(2)}) copy-start(f32[8,16,2048]{2,1,0:T(8,128)} %refs_1_.3) | copy-start | bytes 3145732
  0.6 16.8 %copy-start.3 = (f32[8,16,2048]{2,1,0:T(8,128)S(1)}, f32[8,16,2048]{2,1,0:T(8,128)}, u32[]{:S(2)}) copy-start(f32[8,16,2048]{2,1,0:T(8,128)} %refs_2_.3) | copy-start | bytes 3145732
  0.7 16.8 %copy-start.5 = (f32[8,16,2048]{2,1,0:T(8,128)S(1)}, f32[8,16,2048]{2,1,0:T(8,128)}, u32[]{:S(2)}) copy-start(f32[8,16,2048]{2,1,0:T(8,128)} %refs_3_.3) | copy-start | bytes 3145732
  2.7 14.7 %all-to-all-start = ((f32[16,3,128]{2,1,0:T(4,128)}), f32[16,3,128]{2,1,0:T(4,128)S(1)}, u32[]{:S(2)}, u32[]{:S(2)}) async-start(f32[16,3,128]{2,1,0:T(4,128)} %get-tuple-element.172), calls=%async_computation | async-start | bytes 65536 | tf_op jit(solution)/shard_map/all_to_all | solution.py:659
  9.8 7.6 %collective-permute-start.10 = (f32[16,8,128]{2,1,0:T(8,128)}, f32[16,8,128]{2,1,0:T(8,128)S(1)}, u32[]{:S(2)}, u32[]{:S(2)}) collective-permute-start(f32[16,8,128]{2,1,0:T(8,128)} %get-tuple-element.174), channel_id=1, source_target_pairs={{0,1},{1,2},{2,3},{3,4},{4,5},{5,6},{6,7},{7,0},{8,9},{9,10},{10,1... | collective-permute-start | bytes 196616 | tf_op jit(solution)/shard_map/ppermute | solution.py:609
  9.9 7.6 %collective-permute-start.11 = (f32[16,8,128]{2,1,0:T(8,128)}, f32[16,8,128]{2,1,0:T(8,128)S(1)}, u32[]{:S(2)}, u32[]{:S(2)}) collective-permute-start(f32[16,8,128]{2,1,0:T(8,128)} %get-tuple-element.175), channel_id=1, source_target_pairs={{0,7},{1,0},{2,1},{3,2},{4,3},{5,4},{6,5},{7,6},{8,15},{9,8},{10,9... | collective-permute-start | bytes 196616 | tf_op jit(solution)/shard_map/ppermute | solution.py:609
  20.0 22.5 %collective-permute-start.12 = (f32[12,8,2176]{2,1,0:T(8,128)S(1)}, f32[12,8,2176]{2,1,0:T(8,128)S(1)}, u32[]{:S(2)}, u32[]{:S(2)}) collective-permute-start(f32[12,8,2176]{2,1,0:T(8,128)S(1)} %get-tuple-element.176), channel_id=1, source_target_pairs={{0,8},{8,16},{16,24},{24,32},{32,40},{40,48},{48,56},{56,64},{64,7... | collective-permute-start | bytes 2506760 | tf_op jit(solution)/shard_map/ppermute | solution.py:609
  20.6 21.9 %collective-permute-start.13 = (f32[12,8,2176]{2,1,0:T(8,128)S(1)}, f32[12,8,2176]{2,1,0:T(8,128)S(1)}, u32[]{:S(2)}, u32[]{:S(2)}) collective-permute-start(f32[12,8,2176]{2,1,0:T(8,128)S(1)} %get-tuple-element.177), channel_id=1, source_target_pairs={{0,120},{8,0},{16,8},{24,16},{32,24},{40,32},{48,40},{56,48},{64,5... | collective-permute-start | bytes 2506760 | tf_op jit(solution)/shard_map/ppermute | solution.py:609
  45.3 9.9 %collective-permute-start.14 = (f32[4,8,2176]{2,1,0:T(8,128)S(1)}, f32[4,8,2176]{2,1,0:T(8,128)S(1)}, u32[]{:S(2)}, u32[]{:S(2)}) collective-permute-start(f32[4,8,2176]{2,1,0:T(8,128)S(1)} %get-tuple-element.186), channel_id=1, source_target_pairs={{0,8},{8,16},{16,24},{24,32},{32,40},{40,48},{48,56},{56,64},{64,7... | collective-permute-start | bytes 835592 | tf_op jit(solution)/shard_map/ppermute | solution.py:609
  45.4 9.9 %collective-permute-start.15 = (f32[4,8,2176]{2,1,0:T(8,128)S(1)}, f32[4,8,2176]{2,1,0:T(8,128)S(1)}, u32[]{:S(2)}, u32[]{:S(2)}) collective-permute-start(f32[4,8,2176]{2,1,0:T(8,128)S(1)} %get-tuple-element.187), channel_id=1, source_target_pairs={{0,120},{8,0},{16,8},{24,16},{32,24},{40,32},{48,40},{56,48},{64,5... | collective-permute-start | bytes 835592 | tf_op jit(solution)/shard_map/ppermute | solution.py:609
  58.0 9.9 %collective-permute-start.16 = (f32[4,8,2176]{2,1,0:T(8,128)S(1)}, f32[4,8,2176]{2,1,0:T(8,128)S(1)}, u32[]{:S(2)}, u32[]{:S(2)}) collective-permute-start(f32[4,8,2176]{2,1,0:T(8,128)S(1)} %get-tuple-element.198), channel_id=1, source_target_pairs={{0,8},{8,16},{16,24},{24,32},{32,40},{40,48},{48,56},{56,64},{64,7... | collective-permute-start | bytes 835592 | tf_op jit(solution)/shard_map/ppermute | solution.py:609
  58.1 9.9 %collective-permute-start.17 = (f32[4,8,2176]{2,1,0:T(8,128)S(1)}, f32[4,8,2176]{2,1,0:T(8,128)S(1)}, u32[]{:S(2)}, u32[]{:S(2)}) collective-permute-start(f32[4,8,2176]{2,1,0:T(8,128)S(1)} %get-tuple-element.199), channel_id=1, source_target_pairs={{0,120},{8,0},{16,8},{24,16},{32,24},{40,32},{48,40},{56,48},{64,5... | collective-permute-start | bytes 835592 | tf_op jit(solution)/shard_map/ppermute | solution.py:609
  70.7 9.4 %collective-permute-start.18 = (f32[3,8,2176]{2,1,0:T(8,128)S(1)}, f32[3,8,2176]{2,1,0:T(8,128)S(1)}, u32[]{:S(2)}, u32[]{:S(2)}) collective-permute-start(f32[3,8,2176]{2,1,0:T(8,128)S(1)} %get-tuple-element.207), channel_id=1, source_target_pairs={{0,8},{8,16},{16,24},{24,32},{32,40},{40,48},{48,56},{56,64},{64,7... | collective-permute-start | bytes 626696 | tf_op jit(solution)/shard_map/ppermute | solution.py:609
  70.7 9.4 %collective-permute-start.19 = (f32[3,8,2176]{2,1,0:T(8,128)S(1)}, f32[3,8,2176]{2,1,0:T(8,128)S(1)}, u32[]{:S(2)}, u32[]{:S(2)}) collective-permute-start(f32[3,8,2176]{2,1,0:T(8,128)S(1)} %get-tuple-element.208), channel_id=1, source_target_pairs={{0,120},{8,0},{16,8},{24,16},{32,24},{40,32},{48,40},{56,48},{64,5... | collective-permute-start | bytes 626696 | tf_op jit(solution)/shard_map/ppermute | solution.py:609
  76.4 14.2 %copy-start.8 = (s32[16,1,128]{2,1,0:T(1,128)}, s32[16,1,128]{2,1,0:T(1,128)S(1)}, u32[]{:S(2)}) copy-start(s32[16,1,128]{2,1,0:T(1,128)S(1)} %get-tuple-element.345) | copy-start | bytes 24580
  82.1 1.1 collective-permute-start.20
  83.2 3.5 %collective-permute-start.21 = (f32[1,128]{1,0:T(1,128)S(1)}, f32[1,128]{1,0:T(1,128)S(1)}, u32[]{:S(2)}, u32[]{:S(2)}) collective-permute-start(f32[1,128]{1,0:T(1,128)S(1)} %add.114), channel_id=1, source_target_pairs={{0,2},{1,3},{2,0},{3,1},{4,6},{5,7},{6,4},{7,5},{8,10},{9,11},{10,... | collective-permute-start | bytes 1544 | tf_op jit(solution)/shard_map/ppermute | solution.py:617
  86.8 5.4 %collective-permute-start.22 = (f32[1,128]{1,0:T(1,128)S(1)}, f32[1,128]{1,0:T(1,128)S(1)}, u32[]{:S(2)}, u32[]{:S(2)}) collective-permute-start(f32[1,128]{1,0:T(1,128)S(1)} %add.115), channel_id=1, source_target_pairs={{0,6},{1,7},{2,4},{3,5},{4,2},{5,3},{6,0},{7,1},{8,14},{9,15},{10,... | collective-permute-start | bytes 1544 | tf_op jit(solution)/shard_map/ppermute | solution.py:617
  90.6 9.9 %copy-start.12 = (s32[1,1,16,128]{3,2,1,0:T(8,128)S(1)}, s32[1,1,16,128]{3,2,1,0:T(8,128)}, u32[]{:S(2)}) copy-start(s32[1,1,16,128]{3,2,1,0:T(8,128)} %param.25) | copy-start | bytes 24580
  90.6 16.2 %copy-start.13 = (s32[1,1,16]{2,1,0:T(1,128)S(1)}, s32[1,1,16]{2,1,0:T(1,128)}, u32[]{:S(2)}) copy-start(s32[1,1,16]{2,1,0:T(1,128)} %param.24) | copy-start | bytes 196
  92.2 3.6 %collective-permute-start.23 = (f32[1,128]{1,0:T(1,128)S(1)}, f32[1,128]{1,0:T(1,128)S(1)}, u32[]{:S(2)}, u32[]{:S(2)}) collective-permute-start(f32[1,128]{1,0:T(1,128)S(1)} %add.116), channel_id=1, source_target_pairs={{0,8},{8,0},{16,24},{24,16},{32,40},{40,32},{48,56},{56,48},{64,72... | collective-permute-start | bytes 1544 | tf_op jit(solution)/shard_map/ppermute | solution.py:617
  95.8 4.8 %collective-permute-start.24 = (f32[1,128]{1,0:T(1,128)S(1)}, f32[1,128]{1,0:T(1,128)S(1)}, u32[]{:S(2)}, u32[]{:S(2)}) collective-permute-start(f32[1,128]{1,0:T(1,128)S(1)} %add.117), channel_id=1, source_target_pairs={{0,24},{8,16},{16,8},{24,0},{32,56},{40,48},{48,40},{56,32},{64,88... | collective-permute-start | bytes 1544 | tf_op jit(solution)/shard_map/ppermute | solution.py:617
  100.5 3.5 %collective-permute-start.25 = (f32[1,128]{1,0:T(1,128)S(1)}, f32[1,128]{1,0:T(1,128)S(1)}, u32[]{:S(2)}, u32[]{:S(2)}) collective-permute-start(f32[1,128]{1,0:T(1,128)S(1)} %add.118), channel_id=1, source_target_pairs={{0,32},{8,40},{16,48},{24,56},{32,0},{40,8},{48,16},{56,24},{64,96... | collective-permute-start | bytes 1544 | tf_op jit(solution)/shard_map/ppermute | solution.py:617
  104.1 4.8 %collective-permute-start.26 = (f32[1,128]{1,0:T(1,128)S(1)}, f32[1,128]{1,0:T(1,128)S(1)}, u32[]{:S(2)}, u32[]{:S(2)}) collective-permute-start(f32[1,128]{1,0:T(1,128)S(1)} %add.119), channel_id=1, source_target_pairs={{0,96},{8,104},{16,112},{24,120},{32,64},{40,72},{48,80},{56,88},{... | collective-permute-start | bytes 1544 | tf_op jit(solution)/shard_map/ppermute | solution.py:617
  108.8 9.9 %copy-start.9 = (s32[16,1,128]{2,1,0:T(1,128)S(1)}, s32[16,1,128]{2,1,0:T(1,128)}, u32[]{:S(2)}) copy-start(s32[16,1,128]{2,1,0:T(1,128)} %copy-done.8) | copy-start | bytes 24580
  118.8 7.1 %copy-start.14 = (f32[8]{0:T(128)S(1)}, f32[8]{0:T(128)}, u32[]{:S(2)}) copy-start(f32[8]{0:T(128)} %param.21) | copy-start | bytes 100
  118.8 14.7 %copy-start.10 = (f32[16,128]{1,0:T(8,128)S(1)}, f32[16,128]{1,0:T(8,128)}, u32[]{:S(2)}) copy-start(f32[16,128]{1,0:T(8,128)} %convert_bitcast_fusion) | copy-start | bytes 24580
  118.8 14.7 %copy-start.11 = (f32[16,128]{1,0:T(8,128)S(1)}, f32[16,128]{1,0:T(8,128)}, u32[]{:S(2)}) copy-start(f32[16,128]{1,0:T(8,128)} %fusion.23) | copy-start | bytes 24580
  119.0 14.5 %all-to-all-start.1 = ((f32[16,8,128]{2,1,0:T(8,128)}), f32[16,8,128]{2,1,0:T(8,128)S(1)}, u32[]{:S(2)}, u32[]{:S(2)}) async-start(f32[16,8,128]{2,1,0:T(8,128)} %bitcast.111), calls=%async_computation.1 | async-start | bytes 131072 | tf_op jit(solution)/shard_map/all_to_all | solution.py:694

commit v9 on v8

--- a/solution.py
+++ b/solution.py
@@ -656,12 +656,13 @@
     to_left, to_right, sent = columns_of(fields, cells, site_offsets[0, 0])
     from_right = turned(to_left, "field", -1)
     from_left = turned(to_right, "field", 1)
+    *mains, to_up, to_down = prepare(flags, from_left, from_right, fields)
+    sent, to_up, to_down = lax.optimization_barrier((sent, to_up, to_down))
     got = lax.all_to_all(sent, "tile", split_axis=0, concat_axis=0, tiled=True)
     flags, got = lax.optimization_barrier((flags, got))
     got_cells = got[:, 0].astype(jnp.int32)
     got_row, got_col = got[:, 1], got[:, 2]
     sites = (got_cells.reshape(1, -1), got_row.reshape(1, -1), got_col.reshape(1, -1))
-    *mains, to_up, to_down = prepare(flags, from_left, from_right, fields)
     common = (rows, cols, flags, mask)
 
     def exchanged(to_up, to_down):

time: 136 us -> 141 us (1.037)
  local copies, waits for them, and re-layouts: 0.63 us -> 10.2 us
  waiting for transfers between devices: 45.9 us -> 41 us
  Pallas kernels: 33.7 us -> 36.6 us
  starting transfers between devices: 48.1 us -> 45.6 us
    unnamed x20 -> x34, local copies, waits for them, and re-layouts: 0.05 us -> 9.59 us
    ppermute x10, waiting for transfers between devices: 18.8 us -> 9.57 us  [turned(): return lax.ppermute(x, axis, [(i, (i + by) % size) for i in range(size)])]
    all_to_all x1, waiting for transfers between devices: 4.31 us -> 8.5 us  [local(): got = lax.all_to_all(sent, 'tile', split_axis=0, concat_axis=0, tiled=True)]
    all_to_all x1, starting transfers between devices: 7.12 us -> 3.73 us  [local(): got = lax.all_to_all(sent, 'tile', split_axis=0, concat_axis=0, tiled=True)]
    pallas_call x1, Pallas kernels: 2.45 us -> 4.54 us  [prepare(): pl.pallas_call(prepare_kernel, in_specs=[SMEM] + [VMEM] * 6, out_specs=[V...]
  transfers between devices with their start and end apart: 19 -> 19, of which waited for: 12 -> 13; matrix products, arithmetic and copies ran while one was open for 2% -> 2% of each run, Pallas kernels for 8% -> 7%
where the time goes in v9:
time: 141 us; the launch traced here: 140 us
  starting transfers between devices  45.6 us (32%)
  waiting for transfers between devices  41 us (29%)
  Pallas kernels  36.6 us (26%)
  local copies, waits for them, and re-layouts  10.2 us (7%)
  other arithmetic  5.03 us (4%)
  between operations  1.54 us (1%)
    ppermute x10, starting transfers between devices, turned(): return lax.ppermute(x, axis, [(i, (i + by) % size) for i in range(size)])  25.1 us
    ppermute x6, waiting for transfers between devices, summed(): lax.ppermute(x, axis, [(i, other(i, stride, by)) for i in range(size)])  14.1 us
    pallas_call x4, Pallas kernels, phase(): pl.pallas_call(functools.partial(outside_kernel, p, rows, cols), in_specs...  11.1 us
    ppermute x6, starting transfers between devices, summed(): lax.ppermute(x, axis, [(i, other(i, stride, by)) for i in range(size)])  9.94 us
    unnamed x34, local copies, waits for them, and re-layouts  9.59 us
    ppermute x10, waiting for transfers between devices, turned(): return lax.ppermute(x, axis, [(i, (i + by) % size) for i in range(size)])  9.57 us
    pallas_call x4, Pallas kernels, phase(): pl.pallas_call(functools.partial(inside_kernel, p, cols), in_specs=[VMEM]...  8.87 us
    pallas_call x1, Pallas kernels, finish(): pl.pallas_call(functools.partial(finish_kernel, rows, cols), in_specs=[VM...  8.67 us
  transfers between devices with their start and end apart: 19, of which 13 were waited for; matrix products, arithmetic and copies ran while one was open for 2% of the time, Pallas kernels for 7%

profile of v9, /device:TPU:0, one launch (start us, length us, event | category | flops | bytes accessed | tf_op | source)
XLA Modules:
  0.0 140.1 jit_solution(1350527810270823328)
XLA Ops:
  0.6 1.9 %columns.1 = (f32[16,8,128]{2,1,0:T(8,128)}, f32[16,8,128]{2,1,0:T(8,128)}, f32[16,3,128]{2,1,0:T(4,128)}) custom-call(f32[8,16,2048]{2,1,0:T(8,128)} %refs_0_.3, f32[8,16,2048]{2,1,0:T(8,128)} %refs_1_.3, f32[8,16,2048]{2,1,0:T(8,128)} %refs_2_.3, f32[8,16,2048]{2,1,0:T(8,128)} %refs_3_.3, f32[8,16,2048]{2,1,0:T(8,128)} %refs_0_.3, f32[8,16,2048]{2,1,0:T(8,128)} %refs_1_.3, ...), custom_call_target="tpu_custom_call" | custom-call | tf_op jit(solution)/shard_map/columns/pallas_call | solution.py:56
  2.5 3.6 %collective-permute-start.11 = (f32[16,8,128]{2,1,0:T(8,128)}, f32[16,8,128]{2,1,0:T(8,128)S(1)}, u32[]{:S(2)}, u32[]{:S(2)}) collective-permute-start(f32[16,8,128]{2,1,0:T(8,128)} %get-tuple-element.177), channel_id=1, source_target_pairs={{0,7},{1,0},{2,1},{3,2},{4,3},{5,4},{6,5},{7,6},{8,15},{9,8},{10,9... | collective-permute-start | bytes 196616 | tf_op jit(solution)/shard_map/ppermute | solution.py:609
  6.1 0.1 add_convert_fusion.flags.refs_0_
  6.2 2.1 %collective-permute-done.10.left = f32[16,8,128]{2,1,0:T(8,128)S(1)} collective-permute-done((f32[16,8,128]{2,1,0:T(8,128)}, f32[16,8,128]{2,1,0:T(8,128)S(1)}, u32[]{:S(2)}, u32[]{:S(2)}) %collective-permute-start.10) | collective-permute-done | bytes 65568 | tf_op jit(solution)/shard_map/ppermute | solution.py:609
  8.3 0.1 collective-permute-done.11.right
  8.3 4.5 %prepare.1 = (f32[16,8,2176]{2,1,0:T(8,128)S(1)}, f32[16,8,2176]{2,1,0:T(8,128)S(1)}, f32[16,8,2176]{2,1,0:T(8,128)S(1)}, f32[16,8,2176]{2,1,0:T(8,128)S(1)}, f3...) custom-call(f32[4]{0:T(128)S(1)} %add_convert_fusion.flags.refs_0_, f32[16,8,128]{2,1,0:T(8,128)S(1)} %collective-permute-done.10.left, ...), custom_call_target="tpu_custom_call" | custom-call | tf_op jit(solution)/shard_map/prepare/pallas_call | solution.py:112
  12.9 1.0 copy-done
  13.9 1.6 %collective-permute-start.12 = (f32[12,8,2176]{2,1,0:T(8,128)}, f32[12,8,2176]{2,1,0:T(8,128)}, u32[]{:S(2)}, u32[]{:S(2)}) collective-permute-start(f32[12,8,2176]{2,1,0:T(8,128)} %get-tuple-element.182), channel_id=1, source_target_pairs={{0,8},{8,16},{16,24},{24,32},{32,40},{40,48},{48,56},{56,64},{64,7... | collective-permute-start | bytes 2506760 | tf_op jit(solution)/shard_map/ppermute | solution.py:609
  15.5 3.8 %collective-permute-start.13 = (f32[12,8,2176]{2,1,0:T(8,128)}, f32[12,8,2176]{2,1,0:T(8,128)}, u32[]{:S(2)}, u32[]{:S(2)}) collective-permute-start(f32[12,8,2176]{2,1,0:T(8,128)} %get-tuple-element.183), channel_id=1, source_target_pairs={{0,120},{8,0},{16,8},{24,16},{32,24},{40,32},{48,40},{56,48},{64,5... | collective-permute-start | bytes 2506760 | tf_op jit(solution)/shard_map/ppermute | solution.py:609
  19.3 0.6 fusion.30
  19.9 0.7 compare_select_fusion.4
  20.6 3.7 %all-to-all-start = ((f32[16,3,128]{2,1,0:T(4,128)}), f32[16,3,128]{2,1,0:T(4,128)S(1)}, u32[]{:S(2)}, u32[]{:S(2)}) async-start(f32[16,3,128]{2,1,0:T(4,128)} %get-tuple-element.180), calls=%async_computation | async-start | bytes 65536 | tf_op jit(solution)/shard_map/all_to_all | solution.py:661
  24.3 0.7 broadcast_select_fusion.refs_0_.refs_1_
  25.0 1.2 copy-done.1
  26.2 2.3 %inside0.1 = (f32[12,8,2176]{2,1,0:T(8,128)S(1)}, f32[12,8,2176]{2,1,0:T(8,128)S(1)}, f32[8,8,2176]{2,1,0:T(8,128)S(1)}, f32[5,8,128]{2,1,0:T(8,128)S(1)}) custom-call(f32[8,128]{1,0:T(8,128)S(1)} %broadcast_select_fusion.refs_0_.refs_1_, f32[16,8,2176]{2,1,0:T(8,128)S(1)} %get-tuple-element.184.refs_1_.refs_4_, ...), custom_call_target="tpu_custom_call" | custom-call | flops 100000000 | bytes 8000000 | tf_op jit(solution)/shard_map/inside0/pallas_call | solution.py:355
  28.5 0.9 copy-done.3
  29.4 0.9 copy-done.5
  30.4 0.8 copy-done.7
  31.2 8.5 %all-to-all-done = f32[16,3,128]{2,1,0:T(4,128)S(1)} async-done(((f32[16,3,128]{2,1,0:T(4,128)}), f32[16,3,128]{2,1,0:T(4,128)S(1)}, u32[]{:S(2)}, u32[]{:S(2)}) %all-to-all-start) | async-done | bytes 24608 | tf_op jit(solution)/shard_map/all_to_all | solution.py:661
  39.7 0.0 collective-permute-done.13.refs_3_
  39.7 1.2 copy-done.2
  40.9 1.1 copy-done.4
  42.1 1.1 copy-done.6
  43.2 1.1 copy-done.8
  44.3 3.6 %outside0.1 = (f32[24,8,2176]{2,1,0:T(8,128)S(1)}, f32[18,8,2176]{2,1,0:T(8,128)S(1)}, f32[24,8,2176]{2,1,0:T(8,128)S(1)}, f32[24,8,2176]{2,1,0:T(8,128)S(1)}, f...) custom-call(f32[4]{0:T(128)S(1)} %add_convert_fusion.flags.refs_0_, ...), custom_call_target="tpu_custom_call" | custom-call | tf_op jit(solution)/shard_map/outside0/pallas_call | solution.py:374
  47.9 0.8 collective-permute-start.14
  48.8 4.6 %collective-permute-start.15 = (f32[4,8,2176]{2,1,0:T(8,128)S(1)}, f32[4,8,2176]{2,1,0:T(8,128)S(1)}, u32[]{:S(2)}, u32[]{:S(2)}) collective-permute-start(f32[4,8,2176]{2,1,0:T(8,128)S(1)} %get-tuple-element.193), channel_id=1, source_target_pairs={{0,120},{8,0},{16,8},{24,16},{32,24},{40,32},{48,40},{56,48},{64,5... | collective-permute-start | bytes 835592 | tf_op jit(solution)/shard_map/ppermute | solution.py:609
  53.4 2.3 %inside1.1 = (f32[12,8,2176]{2,1,0:T(8,128)S(1)}, f32[12,8,2176]{2,1,0:T(8,128)S(1)}, f32[8,8,2176]{2,1,0:T(8,128)S(1)}, f32[4,8,128]{2,1,0:T(8,128)S(1)}) custom-call(f32[8,128]{1,0:T(8,128)S(1)} %broadcast_select_fusion.refs_0_.refs_1_, f32[16,8,2176]{2,1,0:T(8,128)S(1)} %get-tuple-element.194.refs_1_.refs_4_, ...), custom_call_target="tpu_custom_call" | custom-call | flops 100000000 | bytes 8000000 | tf_op jit(solution)/shard_map/inside1/pallas_call | solution.py:355
  55.7 3.3 %collective-permute-done.14.refs_2_ = f32[4,8,2176]{2,1,0:T(8,128)S(1)} collective-permute-done((f32[4,8,2176]{2,1,0:T(8,128)S(1)}, f32[4,8,2176]{2,1,0:T(8,128)S(1)}, u32[]{:S(2)}, u32[]{:S(2)}) %collective-permute-start.14) | collective-permute-done | bytes 278560 | tf_op jit(solution)/shard_map/ppermute | solution.py:609
  59.0 0.0 collective-permute-done.15.refs_3_
  59.0 2.8 %outside1.1 = (f32[24,8,2176]{2,1,0:T(8,128)S(1)}, f32[18,8,2176]{2,1,0:T(8,128)S(1)}, f32[16,8,2176]{2,1,0:T(8,128)S(1)}, f32[4,8,2176]{2,1,0:T(8,128)S(1)}, f3...) custom-call(f32[4]{0:T(128)S(1)} %add_convert_fusion.flags.refs_0_, f32[8,128]{1,0:T(8,128)S(1)} %broadcast_select_fusion.refs_0_.refs_1_, ...), custom_call_target="tpu_custom_call" | custom-call | tf_op jit(solution)/shard_map/outside1/pallas_call | solution.py:374
  61.7 0.1 collective-permute-start.16
  61.8 5.3 %collective-permute-start.17 = (f32[4,8,2176]{2,1,0:T(8,128)S(1)}, f32[4,8,2176]{2,1,0:T(8,128)S(1)}, u32[]{:S(2)}, u32[]{:S(2)}) collective-permute-start(f32[4,8,2176]{2,1,0:T(8,128)S(1)} %get-tuple-element.205), channel_id=1, source_target_pairs={{0,120},{8,0},{16,8},{24,16},{32,24},{40,32},{48,40},{56,48},{64,5... | collective-permute-start | bytes 835592 | tf_op jit(solution)/shard_map/ppermute | solution.py:609
  67.2 2.4 %inside2.1 = (f32[12,8,2176]{2,1,0:T(8,128)S(1)}, f32[12,8,2176]{2,1,0:T(8,128)S(1)}, f32[8,8,2176]{2,1,0:T(8,128)S(1)}, f32[4,8,128]{2,1,0:T(8,128)S(1)}) custom-call(f32[8,128]{1,0:T(8,128)S(1)} %broadcast_select_fusion.refs_0_.refs_1_, f32[16,8,2176]{2,1,0:T(8,128)S(1)} %get-tuple-element.206.refs_1_.refs_4_, ...), custom_call_target="tpu_custom_call" | custom-call | flops 100000000 | bytes 8000000 | tf_op jit(solution)/shard_map/inside2/pallas_call | solution.py:355
  69.6 2.2 %collective-permute-done.16.refs_2_ = f32[4,8,2176]{2,1,0:T(8,128)S(1)} collective-permute-done((f32[4,8,2176]{2,1,0:T(8,128)S(1)}, f32[4,8,2176]{2,1,0:T(8,128)S(1)}, u32[]{:S(2)}, u32[]{:S(2)}) %collective-permute-start.16) | collective-permute-done | bytes 278560 | tf_op jit(solution)/shard_map/ppermute | solution.py:609
  71.8 0.0 collective-permute-done.17.refs_3_
  71.8 2.8 %outside2.1 = (f32[24,8,2176]{2,1,0:T(8,128)S(1)}, f32[18,8,2176]{2,1,0:T(8,128)S(1)}, f32[16,8,2176]{2,1,0:T(8,128)S(1)}, f32[3,8,2176]{2,1,0:T(8,128)S(1)}, f3...) custom-call(f32[4]{0:T(128)S(1)} %add_convert_fusion.flags.refs_0_, f32[8,128]{1,0:T(8,128)S(1)} %broadcast_select_fusion.refs_0_.refs_1_, ...), custom_call_target="tpu_custom_call" | custom-call | tf_op jit(solution)/shard_map/outside2/pallas_call | solution.py:374
  74.6 0.1 collective-permute-start.18
  74.7 5.3 %collective-permute-start.19 = (f32[3,8,2176]{2,1,0:T(8,128)S(1)}, f32[3,8,2176]{2,1,0:T(8,128)S(1)}, u32[]{:S(2)}, u32[]{:S(2)}) collective-permute-start(f32[3,8,2176]{2,1,0:T(8,128)S(1)} %get-tuple-element.214), channel_id=1, source_target_pairs={{0,120},{8,0},{16,8},{24,16},{32,24},{40,32},{48,40},{56,48},{64,5... | collective-permute-start | bytes 626696 | tf_op jit(solution)/shard_map/ppermute | solution.py:609
  80.1 1.8 %inside3.1 = (f32[12,8,2176]{2,1,0:T(8,128)S(1)}, f32[3,8,128]{2,1,0:T(8,128)S(1)}) custom-call(f32[8,128]{1,0:T(8,128)S(1)} %broadcast_select_fusion.refs_0_.refs_1_, f32[16,8,2176]{2,1,0:T(8,128)S(1)} %get-tuple-element.215.refs_1_.refs_4_, f32[24,8,2176]{2,1,0:T(8,128)S(1)} %get-tuple-element.195.refs_2_.refs_5_, ...), custom_call_target="tpu_custom_call" | custom-call | flops 100000000 | bytes 8000000 | tf_op jit(solution)/shard_map/inside3/pallas_call | solution.py:355
  81.9 1.9 %collective-permute-done.18.refs_2_ = f32[3,8,2176]{2,1,0:T(8,128)S(1)} collective-permute-done((f32[3,8,2176]{2,1,0:T(8,128)S(1)}, f32[3,8,2176]{2,1,0:T(8,128)S(1)}, u32[]{:S(2)}, u32[]{:S(2)}) %collective-permute-start.18) | collective-permute-done | bytes 208928 | tf_op jit(solution)/shard_map/ppermute | solution.py:609
  83.8 1.9 %outside3.1 = (f32[1,128]{1,0:T(1,128)S(1)}, f32[24,8,2176]{2,1,0:T(8,128)S(1)}, f32[18,8,2176]{2,1,0:T(8,128)S(1)}) custom-call(f32[4]{0:T(128)S(1)} %add_convert_fusion.flags.refs_0_, f32[8,128]{1,0:T(8,128)S(1)} %broadcast_select_fusion.refs_0_.refs_1_, f32[3,8,2176]{2,1,0:T(8,128)S(1)} %collective-permute-done.18.refs_2_, ...), custom_call_target="tpu_custom_call" | custom-call | tf_op jit(solution)/shard_map/outside3/pallas_call | solution.py:374
  85.7 0.0 collective-permute-start.20
  85.8 1.1 collective-permute-done.20
  86.9 3.9 %collective-permute-start.21 = (f32[1,128]{1,0:T(1,128)S(1)}, f32[1,128]{1,0:T(1,128)S(1)}, u32[]{:S(2)}, u32[]{:S(2)}) collective-permute-start(f32[1,128]{1,0:T(1,128)S(1)} %add.114), channel_id=1, source_target_pairs={{0,2},{1,3},{2,0},{3,1},{4,6},{5,7},{6,4},{7,5},{8,10},{9,11},{10,... | collective-permute-start | bytes 1544 | tf_op jit(solution)/shard_map/ppermute | solution.py:617
  90.8 1.5 %collective-permute-done.21 = f32[1,128]{1,0:T(1,128)S(1)} collective-permute-done((f32[1,128]{1,0:T(1,128)S(1)}, f32[1,128]{1,0:T(1,128)S(1)}, u32[]{:S(2)}, u32[]{:S(2)}) %collective-permute-start.21) | collective-permute-done | bytes 544 | tf_op jit(solution)/shard_map/ppermute | solution.py:617
  92.4 3.2 %collective-permute-start.22 = (f32[1,128]{1,0:T(1,128)S(1)}, f32[1,128]{1,0:T(1,128)S(1)}, u32[]{:S(2)}, u32[]{:S(2)}) collective-permute-start(f32[1,128]{1,0:T(1,128)S(1)} %add.115), channel_id=1, source_target_pairs={{0,6},{1,7},{2,4},{3,5},{4,2},{5,3},{6,0},{7,1},{8,14},{9,15},{10,... | collective-permute-start | bytes 1544 | tf_op jit(solution)/shard_map/ppermute | solution.py:617
  95.6 1.5 %columns_hot.1.hot = bf16[2048,2048]{1,0:T(8,128)(2,1)S(1)} custom-call(s32[1,2048]{1,0:T(1,128)S(1)} %bitcast.104), custom_call_target="tpu_custom_call" | custom-call | tf_op jit(solution)/shard_map/columns_hot/pallas_call | solution.py:451
  97.1 0.0 collective-permute-done.22
  97.1 0.1 collective-permute-start.23
  97.2 3.5 %collective-permute-done.23 = f32[1,128]{1,0:T(1,128)S(1)} collective-permute-done((f32[1,128]{1,0:T(1,128)S(1)}, f32[1,128]{1,0:T(1,128)S(1)}, u32[]{:S(2)}, u32[]{:S(2)}) %collective-permute-start.23) | collective-permute-done | bytes 544 | tf_op jit(solution)/shard_map/ppermute | solution.py:617
  100.8 4.7 %collective-permute-done.24 = f32[1,128]{1,0:T(1,128)S(1)} collective-permute-done((f32[1,128]{1,0:T(1,128)S(1)}, f32[1,128]{1,0:T(1,128)S(1)}, u32[]{:S(2)}, u32[]{:S(2)}) %collective-permute-start.24) | collective-permute-done | bytes 544 | tf_op jit(solution)/shard_map/ppermute | solution.py:617
  105.5 0.6 convert_bitcast_fusion
  106.1 2.9 %collective-permute-done.25 = f32[1,128]{1,0:T(1,128)S(1)} collective-permute-done((f32[1,128]{1,0:T(1,128)S(1)}, f32[1,128]{1,0:T(1,128)S(1)}, u32[]{:S(2)}, u32[]{:S(2)}) %collective-permute-start.25) | collective-permute-done | bytes 544 | tf_op jit(solution)/shard_map/ppermute | solution.py:617
  109.1 2.7 %collective-permute-start.26 = (f32[1,128]{1,0:T(1,128)S(1)}, f32[1,128]{1,0:T(1,128)S(1)}, u32[]{:S(2)}, u32[]{:S(2)}) collective-permute-start(f32[1,128]{1,0:T(1,128)S(1)} %add.119), channel_id=1, source_target_pairs={{0,96},{8,104},{16,112},{24,120},{32,64},{40,72},{48,80},{56,88},{... | collective-permute-start | bytes 1544 | tf_op jit(solution)/shard_map/ppermute | solution.py:617
  111.7 0.7 fusion.23
  112.4 1.4 %collective-permute-done.26 = f32[1,128]{1,0:T(1,128)S(1)} collective-permute-done((f32[1,128]{1,0:T(1,128)S(1)}, f32[1,128]{1,0:T(1,128)S(1)}, u32[]{:S(2)}, u32[]{:S(2)}) %collective-permute-start.26) | collective-permute-done | bytes 544 | tf_op jit(solution)/shard_map/ppermute | solution.py:617
  113.8 8.7 %finish.1 = (f32[8,16,2048]{2,1,0:T(8,128)}, f32[128,128]{1,0:T(8,128)}, f32[8,128]{1,0:T(8,128)S(1)}) custom-call(f32[1,128]{1,0:T(1,128)S(1)} %add.120.line, s32[1,2048]{1,0:T(1,128)S(1)} %get-tuple-element.349.cells, f32[1,2048]{1,0:T(1,128)S(1)} %get-tuple-element.347.row_frac, f32[1,2048]{1,0:T(1,128)S(1)} %get-tuple-element.348.col_frac, ...), custom_call_target="tpu_custom_call" | custom-call | tf_op jit(solution)/shard_map/finish/pallas_call | solution.py:521
  122.5 0.7 compare_reduce_fusion
  123.8 0.0 copy-start.20
  123.9 0.2 while.28
  124.1 6.7 %all-to-all-start.1 = ((f32[16,8,128]{2,1,0:T(8,128)}), f32[16,8,128]{2,1,0:T(8,128)S(1)}, u32[]{:S(2)}, u32[]{:S(2)}) async-start(f32[16,8,128]{2,1,0:T(8,128)} %bitcast.111), calls=%async_computation.1 | async-start | bytes 131072 | tf_op jit(solution)/shard_map/all_to_all | solution.py:695
  130.9 7.6 %all-to-all-done.1 = f32[16,8,128]{2,1,0:T(8,128)S(1)} async-done(((f32[16,8,128]{2,1,0:T(8,128)}), f32[16,8,128]{2,1,0:T(8,128)S(1)}, u32[]{:S(2)}, u32[]{:S(2)}) %all-to-all-start.1) | async-done | bytes 65568 | tf_op jit(solution)/shard_map/all_to_all | solution.py:695
  138.5 1.6 %fusion.22 = f32[1,1,16,8,128]{4,3,2,1,0:T(8,128)} fusion(s32[1,1,16,8,128]{4,3,2,1,0:T(8,128)} %param.27, f32[16,8,128]{2,1,0:T(8,128)S(1)} %all-to-all-done.1, s32[1,1,16,8,128]{4,3,2,1,0:T(8,128)} %param.26, f32[16,128]{1,0:T(8,128)S(1)} %copy-done.17, f32[8]{0:T(128)S(1)} %subtract_log_fusion, f32[16,128]{1,0:T(8,128)S(1)} %copy-done.16), kind=kLoop, calls=%fused_computation.86 | loop fusion | flops 245760 | bytes 278560 | tf_op jit(solution)/shard_map/broadcast_in_dim | solution.py:709
  (39 shorter events, 0.1 us)
Async XLA Ops:
  2.5 5.7 %collective-permute-start.10 = (f32[16,8,128]{2,1,0:T(8,128)}, f32[16,8,128]{2,1,0:T(8,128)S(1)}, u32[]{:S(2)}, u32[]{:S(2)}) collective-permute-start(f32[16,8,128]{2,1,0:T(8,128)} %get-tuple-element.176), channel_id=1, source_target_pairs={{0,1},{1,2},{2,3},{3,4},{4,5},{5,6},{6,7},{7,0},{8,9},{9,10},{10,1... | collective-permute-start | bytes 196616 | tf_op jit(solution)/shard_map/ppermute | solution.py:609
  2.5 5.8 %collective-permute-start.11 = (f32[16,8,128]{2,1,0:T(8,128)}, f32[16,8,128]{2,1,0:T(8,128)S(1)}, u32[]{:S(2)}, u32[]{:S(2)}) collective-permute-start(f32[16,8,128]{2,1,0:T(8,128)} %get-tuple-element.177), channel_id=1, source_target_pairs={{0,7},{1,0},{2,1},{3,2},{4,3},{5,4},{6,5},{7,6},{8,15},{9,8},{10,9... | collective-permute-start | bytes 196616 | tf_op jit(solution)/shard_map/ppermute | solution.py:609
  12.9 1.0 copy-start
  13.9 25.8 %collective-permute-start.12 = (f32[12,8,2176]{2,1,0:T(8,128)}, f32[12,8,2176]{2,1,0:T(8,128)}, u32[]{:S(2)}, u32[]{:S(2)}) collective-permute-start(f32[12,8,2176]{2,1,0:T(8,128)} %get-tuple-element.182), channel_id=1, source_target_pairs={{0,8},{8,16},{16,24},{24,32},{32,40},{40,48},{48,56},{56,64},{64,7... | collective-permute-start | bytes 2506760 | tf_op jit(solution)/shard_map/ppermute | solution.py:609
  15.5 24.2 %collective-permute-start.13 = (f32[12,8,2176]{2,1,0:T(8,128)}, f32[12,8,2176]{2,1,0:T(8,128)}, u32[]{:S(2)}, u32[]{:S(2)}) collective-permute-start(f32[12,8,2176]{2,1,0:T(8,128)} %get-tuple-element.183), channel_id=1, source_target_pairs={{0,120},{8,0},{16,8},{24,16},{32,24},{40,32},{48,40},{56,48},{64,5... | collective-permute-start | bytes 2506760 | tf_op jit(solution)/shard_map/ppermute | solution.py:609
  20.6 19.1 %all-to-all-start = ((f32[16,3,128]{2,1,0:T(4,128)}), f32[16,3,128]{2,1,0:T(4,128)S(1)}, u32[]{:S(2)}, u32[]{:S(2)}) async-start(f32[16,3,128]{2,1,0:T(4,128)} %get-tuple-element.180), calls=%async_computation | async-start | bytes 65536 | tf_op jit(solution)/shard_map/all_to_all | solution.py:661
  25.0 1.2 copy-start.1
  28.5 0.9 copy-start.3
  29.4 0.9 copy-start.5
  30.4 0.8 copy-start.7
  39.7 1.2 copy-start.2
  40.9 1.1 copy-start.4
  42.1 1.1 copy-start.6
  43.2 1.1 copy-start.8
  47.9 11.0 %collective-permute-start.14 = (f32[4,8,2176]{2,1,0:T(8,128)S(1)}, f32[4,8,2176]{2,1,0:T(8,128)S(1)}, u32[]{:S(2)}, u32[]{:S(2)}) collective-permute-start(f32[4,8,2176]{2,1,0:T(8,128)S(1)} %get-tuple-element.192), channel_id=1, source_target_pairs={{0,8},{8,16},{16,24},{24,32},{32,40},{40,48},{48,56},{56,64},{64,7... | collective-permute-start | bytes 835592 | tf_op jit(solution)/shard_map/ppermute | solution.py:609
  48.8 10.2 %collective-permute-start.15 = (f32[4,8,2176]{2,1,0:T(8,128)S(1)}, f32[4,8,2176]{2,1,0:T(8,128)S(1)}, u32[]{:S(2)}, u32[]{:S(2)}) collective-permute-start(f32[4,8,2176]{2,1,0:T(8,128)S(1)} %get-tuple-element.193), channel_id=1, source_target_pairs={{0,120},{8,0},{16,8},{24,16},{32,24},{40,32},{48,40},{56,48},{64,5... | collective-permute-start | bytes 835592 | tf_op jit(solution)/shard_map/ppermute | solution.py:609
  61.7 10.1 %collective-permute-start.16 = (f32[4,8,2176]{2,1,0:T(8,128)S(1)}, f32[4,8,2176]{2,1,0:T(8,128)S(1)}, u32[]{:S(2)}, u32[]{:S(2)}) collective-permute-start(f32[4,8,2176]{2,1,0:T(8,128)S(1)} %get-tuple-element.204), channel_id=1, source_target_pairs={{0,8},{8,16},{16,24},{24,32},{32,40},{40,48},{48,56},{56,64},{64,7... | collective-permute-start | bytes 835592 | tf_op jit(solution)/shard_map/ppermute | solution.py:609
  61.8 10.0 %collective-permute-start.17 = (f32[4,8,2176]{2,1,0:T(8,128)S(1)}, f32[4,8,2176]{2,1,0:T(8,128)S(1)}, u32[]{:S(2)}, u32[]{:S(2)}) collective-permute-start(f32[4,8,2176]{2,1,0:T(8,128)S(1)} %get-tuple-element.205), channel_id=1, source_target_pairs={{0,120},{8,0},{16,8},{24,16},{32,24},{40,32},{48,40},{56,48},{64,5... | collective-permute-start | bytes 835592 | tf_op jit(solution)/shard_map/ppermute | solution.py:609
  74.6 9.2 %collective-permute-start.18 = (f32[3,8,2176]{2,1,0:T(8,128)S(1)}, f32[3,8,2176]{2,1,0:T(8,128)S(1)}, u32[]{:S(2)}, u32[]{:S(2)}) collective-permute-start(f32[3,8,2176]{2,1,0:T(8,128)S(1)} %get-tuple-element.213), channel_id=1, source_target_pairs={{0,8},{8,16},{16,24},{24,32},{32,40},{40,48},{48,56},{56,64},{64,7... | collective-permute-start | bytes 626696 | tf_op jit(solution)/shard_map/ppermute | solution.py:609
  74.7 9.1 %collective-permute-start.19 = (f32[3,8,2176]{2,1,0:T(8,128)S(1)}, f32[3,8,2176]{2,1,0:T(8,128)S(1)}, u32[]{:S(2)}, u32[]{:S(2)}) collective-permute-start(f32[3,8,2176]{2,1,0:T(8,128)S(1)} %get-tuple-element.214), channel_id=1, source_target_pairs={{0,120},{8,0},{16,8},{24,16},{32,24},{40,32},{48,40},{56,48},{64,5... | collective-permute-start | bytes 626696 | tf_op jit(solution)/shard_map/ppermute | solution.py:609
  80.1 15.5 %copy-start.14 = (s32[16,1,128]{2,1,0:T(1,128)}, s32[16,1,128]{2,1,0:T(1,128)S(1)}, u32[]{:S(2)}) copy-start(s32[16,1,128]{2,1,0:T(1,128)S(1)} %get-tuple-element.351) | copy-start | bytes 24580
  85.7 1.1 collective-permute-start.20
  86.9 5.5 %collective-permute-start.21 = (f32[1,128]{1,0:T(1,128)S(1)}, f32[1,128]{1,0:T(1,128)S(1)}, u32[]{:S(2)}, u32[]{:S(2)}) collective-permute-start(f32[1,128]{1,0:T(1,128)S(1)} %add.114), channel_id=1, source_target_pairs={{0,2},{1,3},{2,0},{3,1},{4,6},{5,7},{6,4},{7,5},{8,10},{9,11},{10,... | collective-permute-start | bytes 1544 | tf_op jit(solution)/shard_map/ppermute | solution.py:617
  92.4 4.8 %collective-permute-start.22 = (f32[1,128]{1,0:T(1,128)S(1)}, f32[1,128]{1,0:T(1,128)S(1)}, u32[]{:S(2)}, u32[]{:S(2)}) collective-permute-start(f32[1,128]{1,0:T(1,128)S(1)} %add.115), channel_id=1, source_target_pairs={{0,6},{1,7},{2,4},{3,5},{4,2},{5,3},{6,0},{7,1},{8,14},{9,15},{10,... | collective-permute-start | bytes 1544 | tf_op jit(solution)/shard_map/ppermute | solution.py:617
  95.6 9.9 %copy-start.18 = (s32[1,1,16,128]{3,2,1,0:T(8,128)S(1)}, s32[1,1,16,128]{3,2,1,0:T(8,128)}, u32[]{:S(2)}) copy-start(s32[1,1,16,128]{3,2,1,0:T(8,128)} %param.25) | copy-start | bytes 24580
  95.6 16.1 %copy-start.19 = (s32[1,1,16]{2,1,0:T(1,128)S(1)}, s32[1,1,16]{2,1,0:T(1,128)}, u32[]{:S(2)}) copy-start(s32[1,1,16]{2,1,0:T(1,128)} %param.24) | copy-start | bytes 196
  97.1 3.6 %collective-permute-start.23 = (f32[1,128]{1,0:T(1,128)S(1)}, f32[1,128]{1,0:T(1,128)S(1)}, u32[]{:S(2)}, u32[]{:S(2)}) collective-permute-start(f32[1,128]{1,0:T(1,128)S(1)} %add.116), channel_id=1, source_target_pairs={{0,8},{8,0},{16,24},{24,16},{32,40},{40,32},{48,56},{56,48},{64,72... | collective-permute-start | bytes 1544 | tf_op jit(solution)/shard_map/ppermute | solution.py:617
  100.8 4.8 %collective-permute-start.24 = (f32[1,128]{1,0:T(1,128)S(1)}, f32[1,128]{1,0:T(1,128)S(1)}, u32[]{:S(2)}, u32[]{:S(2)}) collective-permute-start(f32[1,128]{1,0:T(1,128)S(1)} %add.117), channel_id=1, source_target_pairs={{0,24},{8,16},{16,8},{24,0},{32,56},{40,48},{48,40},{56,32},{64,88... | collective-permute-start | bytes 1544 | tf_op jit(solution)/shard_map/ppermute | solution.py:617
  105.5 3.5 %collective-permute-start.25 = (f32[1,128]{1,0:T(1,128)S(1)}, f32[1,128]{1,0:T(1,128)S(1)}, u32[]{:S(2)}, u32[]{:S(2)}) collective-permute-start(f32[1,128]{1,0:T(1,128)S(1)} %add.118), channel_id=1, source_target_pairs={{0,32},{8,40},{16,48},{24,56},{32,0},{40,8},{48,16},{56,24},{64,96... | collective-permute-start | bytes 1544 | tf_op jit(solution)/shard_map/ppermute | solution.py:617
  109.1 4.8 %collective-permute-start.26 = (f32[1,128]{1,0:T(1,128)S(1)}, f32[1,128]{1,0:T(1,128)S(1)}, u32[]{:S(2)}, u32[]{:S(2)}) collective-permute-start(f32[1,128]{1,0:T(1,128)S(1)} %add.119), channel_id=1, source_target_pairs={{0,96},{8,104},{16,112},{24,120},{32,64},{40,72},{48,80},{56,88},{... | collective-permute-start | bytes 1544 | tf_op jit(solution)/shard_map/ppermute | solution.py:617
  113.8 10.0 %copy-start.12 = (f32[8,16,2048]{2,1,0:T(8,128)S(1)}, f32[8,16,2048]{2,1,0:T(8,128)}, u32[]{:S(2)}) copy-start(f32[8,16,2048]{2,1,0:T(8,128)} %refs_0_.3) | copy-start | bytes 3145732
  113.8 10.0 %copy-start.15 = (s32[16,1,128]{2,1,0:T(1,128)S(1)}, s32[16,1,128]{2,1,0:T(1,128)}, u32[]{:S(2)}) copy-start(s32[16,1,128]{2,1,0:T(1,128)} %copy-done.14) | copy-start | bytes 24580
  123.8 7.0 %copy-start.20 = (f32[8]{0:T(128)S(1)}, f32[8]{0:T(128)}, u32[]{:S(2)}) copy-start(f32[8]{0:T(128)} %param.21) | copy-start | bytes 100
  123.8 14.7 %copy-start.16 = (f32[16,128]{1,0:T(8,128)S(1)}, f32[16,128]{1,0:T(8,128)}, u32[]{:S(2)}) copy-start(f32[16,128]{1,0:T(8,128)} %convert_bitcast_fusion) | copy-start | bytes 24580
  123.8 14.7 %copy-start.17 = (f32[16,128]{1,0:T(8,128)S(1)}, f32[16,128]{1,0:T(8,128)}, u32[]{:S(2)}) copy-start(f32[16,128]{1,0:T(8,128)} %fusion.23) | copy-start | bytes 24580
  124.1 14.4 %all-to-all-start.1 = ((f32[16,8,128]{2,1,0:T(8,128)}), f32[16,8,128]{2,1,0:T(8,128)S(1)}, u32[]{:S(2)}, u32[]{:S(2)}) async-start(f32[16,8,128]{2,1,0:T(8,128)} %bitcast.111), calls=%async_computation.1 | async-start | bytes 131072 | tf_op jit(solution)/shard_map/all_to_all | solution.py:695
